TPU v7x, 256 devices: a whole 4x4x8 slice. The times are simulated.
256 devices in a mesh: pts: 32 (over z_hi, x, core), modes: 8 (over y, z_lo).
Axes of the slice: x: 4, y: 4, z: 8 (z_hi: 4, z_lo: 2; z = z_hi * 2 + z_lo), core: 2. Of those that a mesh axis runs over, the one named last changes fastest.
Arguments:
- features: bfloat16 [131072, 128], P('pts'), may hold values from -6 to 6
- coords: float32 [3, 131072], P(None, 'pts'), may hold values from 0 to 1
- quad_weight: float32 [131072], P('pts'), may hold values from 0.5 to 6, as said below
- mode_table: int32 [3, 8192], replicated, may hold values from -8 to 31, as said below
- mode_weight: bfloat16 [8192, 2, 128, 128], P(('pts', 'modes')), may hold values from -5 to 5
- lin_weight: bfloat16 [128, 128], replicated, may hold values from -0.5 to 0.5
- bias: float32 [128], replicated, may hold values from -3 to 3
Outputs:
- output: bfloat16 [131072, 128], P(('pts', 'modes'))
Inputs may be any that keep to these rules, and one draw needn't show every extreme that they name: `mode_table`: each column is a distinct triple (kx, ky, kz) with -8 <= kx < 8, -8 <= ky < 8, 0 <= kz < 32; every such triple appears exactly once, in an order drawn from the seed. `quad_weight`: Positive.
All inputs are finite; a program needn't handle non-finite values.
Results may differ from a plain program's by a relative error of at most 0.018.
Values may be sent and summed in bfloat16 or wider, within the bound.
No kernel may reach another device: no remote copies, remote signals or barrier semaphores. Data moves between devices by JAX's collectives and lax.ppermute only.
A program may use at most 64 MiB of HBM per device.

v0:
```python
import math

import jax
import jax.numpy as jnp
from jax import lax
from jax.sharding import PartitionSpec as P


def phase_basis(coords, wave):
    turns = coords[0][:, None] * wave[0][None, :] + coords[1][:, None] * wave[1][None, :]
    turns = turns + coords[2][:, None] * wave[2][None, :]
    angle = 2.0 * math.pi * turns
    return jnp.concatenate([jnp.cos(angle), -jnp.sin(angle)], axis=1).astype(jnp.bfloat16)


def on_device(features, coords, quad_weight, mode_table, mode_weight, lin_weight, bias):
    width = features.shape[1]
    local_pts = features.shape[0]
    own_modes = mode_weight.shape[0]
    n_pts = lax.axis_size("pts")
    n_groups = lax.axis_size("modes")
    group = lax.axis_index("modes")
    group_modes = n_pts * own_modes
    weighted = (quad_weight[:, None] * features.astype(jnp.float32)).astype(jnp.bfloat16)
    total = lax.psum(jnp.sum(quad_weight), "pts")
    wave_all = mode_table.astype(jnp.float32)
    grouped = wave_all.reshape(3, n_pts, n_groups, own_modes)
    wave_group = lax.dynamic_slice_in_dim(grouped, group, 1, 2).reshape(3, group_modes)
    basis_all = phase_basis(coords, wave_group)

    def pick_columns(rows):
        cosine = lax.slice_in_dim(basis_all, 0, rows, axis=1)
        sine = lax.dynamic_slice_in_dim(basis_all, group_modes, rows, 1)
        return jnp.concatenate([cosine, sine], axis=1)

    basis = pick_columns(lax.axis_size("pts") * own_modes)
    term = lax.dot_general(
        basis, weighted, (((0,), (0,)), ((), ())), preferred_element_type=jnp.float32
    )
    coef = lax.psum_scatter(
        term.reshape(2, lax.axis_size("pts") * own_modes, width)
        .transpose(1, 0, 2)
        .reshape(lax.axis_size("pts") * own_modes, 2 * width)
        .astype(jnp.bfloat16),
        "pts",
        scatter_dimension=0,
        tiled=True,
    )
    real_in = coef[:, :width]
    imag_in = coef[:, width:]
    w_real = mode_weight[:, 0]
    w_imag = mode_weight[:, 1]
    real_out = jnp.einsum(
        "mc,mcd->md", real_in, w_real, preferred_element_type=jnp.float32
    ) - jnp.einsum("mc,mcd->md", imag_in, w_imag, preferred_element_type=jnp.float32)
    imag_out = jnp.einsum(
        "mc,mcd->md", real_in, w_imag, preferred_element_type=jnp.float32
    ) + jnp.einsum("mc,mcd->md", imag_in, w_real, preferred_element_type=jnp.float32)
    filtered = jnp.concatenate([real_out, imag_out], axis=1).astype(jnp.bfloat16)
    out_rows = local_pts // n_groups
    my_features = lax.dynamic_slice_in_dim(features, group * out_rows, out_rows, 0)
    piece = lax.all_gather(filtered, "pts", axis=0, tiled=True)
    basis = pick_columns(piece.shape[0])
    rhs = jnp.concatenate([piece[:, :width], piece[:, width:]], axis=0)
    field = jnp.dot(basis, rhs, preferred_element_type=jnp.float32)
    spectral = lax.psum_scatter(
        field.astype(jnp.bfloat16), "modes", scatter_dimension=0, tiled=True
    ).astype(jnp.float32)
    linear = jnp.dot(my_features, lin_weight, preferred_element_type=jnp.float32)
    pre = spectral / total + linear + bias[None, :]
    return jax.nn.gelu(pre, approximate=False).astype(jnp.bfloat16)


def solution(mesh):
    return jax.shard_map(
        on_device,
        mesh=mesh,
        in_specs=(
            P("pts", None),
            P(None, "pts"),
            P("pts"),
            P(),
            P(("pts", "modes"), None, None, None),
            P(),
            P(),
        ),
        out_specs=P(("pts", "modes"), None),
        check_vma=False,
    )
```

profile of v0, /device:TPU:1, one launch (start us, length us, event | category | flops | bytes accessed | tf_op | source)
XLA Modules:
  0.0 317.3 jit_solution(12225409190686408662)
XLA Ops:
  6.5 0.0 copy-start
  6.5 0.0 reduce-scatter.7.cloned.1.call-start
  6.5 0.9 convert_element_type.32
  7.5 0.2 reshape.19
  7.6 0.2 dynamic-slice_reduce_fusion.2
  7.8 0.1 mul.85
  7.9 0.1 mul.90
  8.0 0.1 mul.95
  8.0 1.0 fusion.36
  9.0 0.0 copy-start.4
  9.0 68.2 %cosine_convert_fusion = (bf16[4096,1024]{1,0:T(8,128)(2,1)S(1)}, bf16[4096,1024]{1,0:T(8,128)(2,1)S(1)}) fusion(f32[1024]{0:T(1024)S(1)} %mul.95, f32[4096]{0:T(1024)S(1)} %bitcast.42, f32[1024]{0:T(1024)S(1)} %mul.90, f32[4096]{0:T(1024)S(1)} %bitcast.43, f32[1024]{0:T(1024)S(1)} %mul.85, f32[4096]{0:T(1024)S(1)} %bitcast.41), kind=kLoop, calls=%fused_computation.2 | loop fusion | flops 37748736 | bytes 16838656 | tf_op jit(solution)/shard_map/convert.2
  77.2 0.0 copy-start.1
  77.2 0.0 copy-start.2
  77.3 0.0 copy-done.4
  77.3 0.0 copy-start.3
  77.3 8.5 %fusion.3 = bf16[2048,128]{1,0:T(8,128)(2,1)} fusion(bf16[4096,1024]{1,0:T(8,128)(2,1)S(1)} %get-tuple-element.14, bf16[4096,1024]{1,0:T(8,128)(2,1)S(1)} %get-tuple-element.13, bf16[4096,128]{1,0:T(8,128)(2,1)} %param.7, f32[4096]{0:T(1024)S(1)} %copy-done.4), kind=kOutput, calls=%fused_computation.7 | convolution fusion | flops 2182873088 | bytes 18366464 | tf_op jit(solution)/shard_map/dot_general | solution.py:37
  85.8 0.0 copy-done.1
  85.8 0.0 copy-done.2
  85.8 1.2 copy.9
  87.1 1.0 copy.16
  88.1 0.0 reduce-scatter.7.cloned.1.call-update
  88.1 0.2 reduce-scatter.5.cloned.1.call-start
  88.3 90.1 %reduce-scatter.7.cloned.1.call-done = bf16[32,256]{1,0:T(8,128)(2,1)} async-done(((bf16[1024,256]{1,0:T(8,128)(2,1)}), bf16[32,256]{1,0:T(8,128)(2,1)}) %reduce-scatter.7.cloned.1.call-update) | async-done | bytes 16400
  178.4 0.7 fusion.37
  179.1 0.1 copy.19
  179.2 0.1 copy.12
  179.3 0.0 copy-done.3
  179.3 0.4 fusion.7
  179.7 0.4 fusion.9
  180.1 0.1 copy.18
  180.2 0.1 copy.10
  180.3 0.4 fusion.5
  180.7 0.4 fusion.11
  181.1 46.4 %all_gather.3 = bf16[1024,256]{1,0:T(8,128)(2,1)S(1)} all-gather(bf16[32,256]{1,0:T(8,128)(2,1)S(1)} %pad_maximum_fusion.7), channel_id=1, replica_groups=mesh['pts'=32,'modes'=8] {'pts'}, dimensions={0}, use_global_device_ids=true | all-gather | bytes 540672 | tf_op jit(solution)/shard_map/all_gather | solution.py:62
  227.5 0.0 copy-start.5
  227.5 9.0 %fusion.2 = bf16[4096,128]{1,0:T(8,128)(2,1)} fusion(bf16[4096,1024]{1,0:T(8,128)(2,1)} %copy-done.2, bf16[4096,1024]{1,0:T(8,128)(2,1)} %copy-done.1, bf16[1024,128]{1,0:T(8,128)(2,1)S(1)} %get-tuple-element.9, bf16[1024,128]{1,0:T(8,128)(2,1)S(1)} %get-tuple-element.8), kind=kOutput, calls=%fused_computation.6 | convolution fusion | flops 2182610944 | bytes 18350080 | tf_op jit(solution)/shard_map/dot_general | solution.py:65
  236.6 0.0 reduce-scatter.5.cloned.1.call-update
  236.6 0.6 reduce_sum.9
  237.2 70.3 %psum.7 = f32[]{:T(128)} all-reduce(f32[]{:T(128)} %reduce_sum.9), channel_id=1, replica_groups=mesh['pts'=32,'modes'=8] {'pts'}, use_global_device_ids=true, to_apply=%region_3.0 | all-reduce | flops 1 | bytes 8 | tf_op jit(solution)/shard_map/psum | solution.py:25
  307.5 0.0 reduce-scatter.5.cloned.1.call-done
  307.5 0.0 copy-done
  307.5 0.0 copy-done.5
  307.5 2.9 fusion.23
  (3 shorter events, 0.0 us)
Async XLA Ops:
  6.5 301.0 %copy-start = (bf16[128,128]{1,0:T(8,128)(2,1)S(1)}, bf16[128,128]{1,0:T(8,128)(2,1)}, u32[]{:S(2)}) copy-start(bf16[128,128]{1,0:T(8,128)(2,1)} %param.12) | copy-start | bytes 98308
  6.5 171.8 %reduce-scatter.7.cloned.1.call-start = ((), (), s32[]{:S(2)}) async-start(), calls=%async_computation.3 | async-start | bytes 540672
  9.0 68.2 %copy-start.4 = (f32[4096]{0:T(1024)S(1)}, f32[4096]{0:T(1024)}, u32[]{:S(2)}) copy-start(f32[4096]{0:T(1024)} %param.9) | copy-start | bytes 49156
  77.2 8.6 %copy-start.1 = (bf16[4096,1024]{1,0:T(8,128)(2,1)}, bf16[4096,1024]{1,0:T(8,128)(2,1)S(1)}, u32[]{:S(2)}) copy-start(bf16[4096,1024]{1,0:T(8,128)(2,1)S(1)} %get-tuple-element.13) | copy-start | bytes 25165828
  77.2 8.6 %copy-start.2 = (bf16[4096,1024]{1,0:T(8,128)(2,1)}, bf16[4096,1024]{1,0:T(8,128)(2,1)S(1)}, u32[]{:S(2)}) copy-start(bf16[4096,1024]{1,0:T(8,128)(2,1)S(1)} %get-tuple-element.14) | copy-start | bytes 25165828
  77.3 102.0 %copy-start.3 = (bf16[32,2,128,128]{3,2,1,0:T(8,128)(2,1)S(1)}, bf16[32,2,128,128]{3,2,1,0:T(8,128)(2,1)}, u32[]{:S(2)}) copy-start(bf16[32,2,128,128]{3,2,1,0:T(8,128)(2,1)} %param.11) | copy-start | bytes 6291460
  88.1 219.4 %reduce-scatter.5.cloned.1.call-start = ((), (), s32[]{:S(2)}) async-start(), calls=%async_computation.2 | async-start | bytes 1179648 | tf_op jit(solution)/shard_map/reduce_scatter | solution.py:66
  227.5 80.0 %copy-start.5 = (f32[128]{0:T(128)S(1)}, f32[128]{0:T(128)}, u32[]{:S(2)}) copy-start(f32[128]{0:T(128)} %param.13) | copy-start | bytes 1540
Sparse Core Ops, SparseCore 0:
  88.2 90.1 reduce-scatter.6
  236.7 35.1 reduce-scatter.4
where the time goes:
time: 318 us; the launch traced here: 317 us
  blocking collectives  117 us (37%)
  waiting for transfers between devices  90.1 us (28%)
  other arithmetic  69.7 us (22%)
  matrix products  22 us (7%)
  between operations  13.5 us (4%)
  local copies, waits for them, and re-layouts  4.98 us (2%)
    unnamed x3, waiting for transfers between devices  90.1 us
    psum x1, blocking collectives, on_device(): total = lax.psum(jnp.sum(quad_weight), 'pts')  70.3 us
    another operation x2, other arithmetic  68.2 us
    all_gather x1, blocking collectives, on_device(): piece = lax.all_gather(filtered, 'pts', axis=0, tiled=True)  46.4 us
    dot_general x1, matrix products, on_device(): field = jnp.dot(basis, rhs, preferred_element_type=jnp.float32)  9.03 us
    dot_general x1, matrix products, on_device(): lax.dot_general(basis, weighted, (((0,), (0,)), ((), ())), preferred_elem...  8.53 us
  transfers between devices with their start and end apart: 2, of which 1 were waited for; matrix products, arithmetic and copies ran while one was open for 0% of the time, Pallas kernels for 0%

commit v1 on v0

v1 whole, which is shorter than its diff:
```python
import math

import jax
import jax.numpy as jnp
from jax import lax
from jax.sharding import Mesh, PartitionSpec as P

SIZES = {"z_hi": 4, "x": 4, "core": 2, "y": 4, "z_lo": 2}
PTS = ("z_hi", "x", "core")
GRP = ("y", "z_lo")
ALL = PTS + GRP


def phase_basis(coords, wave):
    turns = coords[0][:, None] * wave[0][None, :] + coords[1][:, None] * wave[1][None, :]
    turns = turns + coords[2][:, None] * wave[2][None, :]
    angle = 2.0 * math.pi * turns
    return jnp.concatenate([jnp.cos(angle), -jnp.sin(angle)], axis=1).astype(jnp.bfloat16)


def send(value, axes, shift):
    n = 1
    for a in axes:
        n *= SIZES[a]
    return lax.ppermute(value, axes, [(j, (j + shift) % n) for j in range(n)])


def split3(value):
    hi = value.astype(jnp.bfloat16)
    rest = value - hi.astype(jnp.float32)
    mid = rest.astype(jnp.bfloat16)
    low = (rest - mid.astype(jnp.float32)).astype(jnp.bfloat16)
    lane = lax.broadcasted_iota(jnp.int32, (16, 256), 1)
    return jnp.where(lane == 0, hi, jnp.where(lane == 1, mid, jnp.where(lane == 2, low, jnp.bfloat16(0))))


def join3(rows):
    return jnp.sum(rows[0, :3].astype(jnp.float32))


def reduce_over(own, parts, total, axes, n):
    tail = split3(total)
    got = [send(jnp.concatenate([parts[s - 1], tail]), axes, s) for s in range(1, n)]
    acc = own.astype(jnp.float32)
    for g in got:
        acc = acc + g[:-16].astype(jnp.float32)
        total = total + join3(g[-16:])
    return acc.astype(jnp.bfloat16), total


def gather_over(piece, axes, n):
    return jnp.concatenate([piece] + [send(piece, axes, n - s) for s in range(1, n)])


def on_device(features, coords, quad_weight, mode_table, mode_weight, lin_weight, bias):
    width = features.shape[1]
    local_pts = features.shape[0]
    own_modes = mode_weight.shape[0]
    z, x, core = (lax.axis_index(a) for a in PTS)
    group = lax.axis_index(GRP)
    weighted = (quad_weight[:, None] * features.astype(jnp.float32)).astype(jnp.bfloat16)
    total = jnp.sum(quad_weight)
    grouped = mode_table.astype(jnp.float32).reshape(3, 4, 4, 2, 8, own_modes)
    wave = lax.dynamic_index_in_dim(grouped, group, 4, keepdims=False)
    wave = jnp.roll(wave, (-z, -x, -core), (1, 2, 3)).transpose(0, 3, 2, 1, 4).reshape(3, -1)
    modes = wave.shape[1]
    basis = phase_basis(coords, wave)
    term = lax.dot_general(
        basis, weighted, (((0,), (0,)), ((), ())), preferred_element_type=jnp.float32
    )
    term = jnp.concatenate([term[:modes], term[modes:]], axis=1).astype(jnp.bfloat16)
    half = modes // 2
    coef, total = reduce_over(term[:half], [term[half:]], total, ("core",), 2)
    q = half // 4
    coef, total = reduce_over(coef[:q], [coef[q * s : q * (s + 1)] for s in (1, 2, 3)], total, ("x",), 4)
    q = q // 4
    coef, total = reduce_over(coef[:q], [coef[q * s : q * (s + 1)] for s in (1, 2, 3)], total, ("z_hi",), 4)
    real_in = coef[:, :width]
    imag_in = coef[:, width:]
    w_real = mode_weight[:, 0]
    w_imag = mode_weight[:, 1]
    real_out = jnp.einsum(
        "mc,mcd->md", real_in, w_real, preferred_element_type=jnp.float32
    ) - jnp.einsum("mc,mcd->md", imag_in, w_imag, preferred_element_type=jnp.float32)
    imag_out = jnp.einsum(
        "mc,mcd->md", real_in, w_imag, preferred_element_type=jnp.float32
    ) + jnp.einsum("mc,mcd->md", imag_in, w_real, preferred_element_type=jnp.float32)
    filtered = jnp.concatenate([real_out, imag_out], axis=1).astype(jnp.bfloat16)
    piece = gather_over(filtered, ("z_hi",), 4)
    piece = gather_over(piece, ("x",), 4)
    piece = gather_over(piece, ("core",), 2)
    rhs = jnp.concatenate([piece[:, :width], piece[:, width:]], axis=0)
    field = jnp.dot(basis, rhs, preferred_element_type=jnp.float32).astype(jnp.bfloat16)
    out_rows = local_pts // 8
    blocks = field.reshape(8, out_rows, width)
    take = lambda a, i: lax.dynamic_index_in_dim(a, i, 0, keepdims=False)
    spectral = take(blocks, group).astype(jnp.float32)
    got = [send(take(blocks, lax.rem(group + s, 8)), GRP, s) for s in range(1, 8)]
    for g in got:
        spectral = spectral + g.astype(jnp.float32)
    my_features = lax.dynamic_slice_in_dim(features, group * out_rows, out_rows, 0)
    linear = jnp.dot(my_features, lin_weight, preferred_element_type=jnp.float32)
    pre = spectral / total + linear + bias[None, :]
    return jax.nn.gelu(pre, approximate=False).astype(jnp.bfloat16)


def solution(mesh):
    fine = Mesh(mesh.devices.reshape([SIZES[a] for a in ALL]), ALL)
    return jax.shard_map(
        on_device,
        mesh=fine,
        in_specs=(
            P(PTS, None),
            P(None, PTS),
            P(PTS),
            P(),
            P(ALL, None, None, None),
            P(),
            P(),
        ),
        out_specs=P(ALL, None),
        check_vma=False,
    )
```

time: 318 us -> 173 us (0.54)
  blocking collectives: 117 us -> 0 us
  waiting for transfers between devices: 90.1 us -> 23.4 us
  starting transfers between devices: 0.22 us -> 40.5 us
  between operations: 13.5 us -> 6.92 us
  other arithmetic: 69.7 us -> 75.4 us
    unnamed x3 -> x0, waiting for transfers between devices: 90.1 us -> none
    psum x1 -> x0, blocking collectives: 70.3 us -> none  [on_device(): total = lax.psum(jnp.sum(quad_weight), 'pts')]
    all_gather x1 -> x0, blocking collectives: 46.4 us -> none  [on_device(): piece = lax.all_gather(filtered, 'pts', axis=0, tiled=True)]
    ppermute x0 -> x21, starting transfers between devices: none -> 40.5 us  [send(): return lax.ppermute(value, axes, [(j, (j + shift) % n) for j in range(n)])]
    ppermute x0 -> x21, waiting for transfers between devices: none -> 23.4 us  [send(): return lax.ppermute(value, axes, [(j, (j + shift) % n) for j in range(n)])]
    reduce_sum x1 -> x8, other arithmetic: 0.6 us -> 5.08 us  [the longest x7 4.47 us: join3(): return jnp.sum(rows[0, :3].astype(jnp.float32))]
    another operation x2 -> x3, other arithmetic: 68.2 us -> 68.3 us
  transfers between devices with their start and end apart: 2 -> 21, of which waited for: 1 -> 13; matrix products, arithmetic and copies ran while one was open for 0% -> 2% of each run, Pallas kernels for 0% -> 0%
where the time goes in v1:
time: 173 us; the launch traced here: 172 us
  other arithmetic  75.4 us (44%)
  starting transfers between devices  40.5 us (23%)
  waiting for transfers between devices  23.4 us (14%)
  matrix products  22.9 us (13%)
  between operations  6.92 us (4%)
  local copies, waits for them, and re-layouts  3.07 us (2%)
    another operation x3, other arithmetic  68.3 us
    ppermute x21, starting transfers between devices, send(): return lax.ppermute(value, axes, [(j, (j + shift) % n) for j in range(n)])  40.5 us
    ppermute x21, waiting for transfers between devices, send(): return lax.ppermute(value, axes, [(j, (j + shift) % n) for j in range(n)])  23.4 us
    dot_general x1, matrix products, on_device(): jnp.dot(basis, rhs, preferred_element_type=jnp.float32).astype(jnp.bfloat16)  8.23 us
    dot_general x1, matrix products, on_device(): lax.dot_general(basis, weighted, (((0,), (0,)), ((), ())), preferred_elem...  5.88 us
    reduce_sum x7, other arithmetic, join3(): return jnp.sum(rows[0, :3].astype(jnp.float32))  4.47 us
  transfers between devices with their start and end apart: 21, of which 13 were waited for; matrix products, arithmetic and copies ran while one was open for 2% of the time, Pallas kernels for 0%

profile of v1, /device:TPU:1, one launch (start us, length us, event | category | flops | bytes accessed | tf_op | source)
XLA Modules:
  0.0 172.2 jit_solution(15957818897506891574)
XLA Ops:
  0.0 0.9 convert_element_type.157
  1.6 1.0 fusion.59
  2.7 68.3 %cosine_convert_fusion = (bf16[4096,1024]{1,0:T(8,128)(2,1)S(1)}, bf16[4096,1024]{1,0:T(8,128)(2,1)S(1)}) fusion(f32[1024]{0:T(1024)S(1)} %mul.99, f32[4096]{0:T(1024)S(1)} %bitcast.61, f32[1024]{0:T(1024)S(1)} %mul.94, f32[4096]{0:T(1024)S(1)} %bitcast.62, f32[1024]{0:T(1024)S(1)} %mul.89, f32[4096]{0:T(1024)S(1)} %bitcast.60), kind=kLoop, calls=%fused_computation.2 | loop fusion | flops 37748736 | bytes 16838656 | tf_op jit(solution)/shard_map/convert.7
  71.0 5.9 %fusion.3 = bf16[2048,128]{0,1:T(8,128)(2,1)} fusion(bf16[4096,1024]{1,0:T(8,128)(2,1)S(1)} %get-tuple-element.40, bf16[4096,1024]{1,0:T(8,128)(2,1)S(1)} %get-tuple-element.39, bf16[4096,128]{1,0:T(8,128)(2,1)} %param.7, f32[4096]{0:T(1024)S(1)} %copy-done.3), kind=kOutput, calls=%fused_computation.7 | convolution fusion | flops 2182873088 | bytes 18366464 | tf_op jit(solution)/shard_map/dot_general | solution.py:68
  76.9 1.1 fusion.56
  78.0 0.6 reduce_sum.72
  79.9 0.2 select_select_fusion.2
  80.1 3.3 %collective-permute-start = (bf16[528,256]{0,1:T(8,128)(2,1)S(1)}, bf16[528,256]{0,1:T(8,128)(2,1)S(1)}, u32[]{:S(2)}, u32[]{:S(2)}) collective-permute-start(bf16[528,256]{0,1:T(8,128)(2,1)S(1)} %fusion.20), channel_id=1, source_target_pairs={{0,8},{8,0},{1,9},{9,1},{2,10},{10,2},{3,11},{11,3},{4,12},{12,4},... | collective-permute-start | bytes 811016 | tf_op jit(solution)/shard_map/ppermute | solution.py:25
  83.4 1.3 collective-permute-done
  84.8 0.7 convert_reduce_fusion.6
  87.1 1.9 %collective-permute-start.2 = (bf16[144,256]{0,1:T(8,128)(2,1)S(1)}, bf16[144,256]{0,1:T(8,128)(2,1)S(1)}, u32[]{:S(2)}, u32[]{:S(2)}) collective-permute-start(bf16[144,256]{0,1:T(8,128)(2,1)S(1)} %get-tuple-element.34), channel_id=1, source_target_pairs={{0,32},{16,48},{32,0},{48,16},{1,33},{17,49},{33,1},{49,17},{2,34}... | collective-permute-start | bytes 221192 | tf_op jit(solution)/shard_map/ppermute | solution.py:25
  89.0 1.2 collective-permute-start.3
  90.2 3.6 %collective-permute-done.1 = bf16[144,256]{0,1:T(8,128)(2,1)S(1)} collective-permute-done((bf16[144,256]{0,1:T(8,128)(2,1)S(1)}, bf16[144,256]{0,1:T(8,128)(2,1)S(1)}, u32[]{:S(2)}, u32[]{:S(2)}) %collective-permute-start.1) | collective-permute-done | bytes 73760 | tf_op jit(solution)/shard_map/ppermute | solution.py:25
  93.7 0.6 convert_reduce_fusion.5
  95.1 0.6 convert_reduce_fusion.4
  96.4 0.6 convert_reduce_fusion.3
  98.1 3.2 %collective-permute-start.4 = (bf16[48,256]{0,1:T(8,128)(2,1)S(1)}, bf16[48,256]{0,1:T(8,128)(2,1)S(1)}, u32[]{:S(2)}, u32[]{:S(2)}) collective-permute-start(bf16[48,256]{0,1:T(8,128)(2,1)S(1)} %get-tuple-element.27), channel_id=1, source_target_pairs={{0,64},{64,128},{128,192},{192,0},{1,65},{65,129},{129,193},{193,1... | collective-permute-start | bytes 73736 | tf_op jit(solution)/shard_map/ppermute | solution.py:25
  101.3 5.1 %collective-permute-start.5 = (bf16[48,256]{0,1:T(8,128)(2,1)S(1)}, bf16[48,256]{0,1:T(8,128)(2,1)S(1)}, u32[]{:S(2)}, u32[]{:S(2)}) collective-permute-start(bf16[48,256]{0,1:T(8,128)(2,1)S(1)} %get-tuple-element.28), channel_id=1, source_target_pairs={{0,128},{64,192},{128,0},{192,64},{1,129},{65,193},{129,1},{193,65... | collective-permute-start | bytes 73736 | tf_op jit(solution)/shard_map/ppermute | solution.py:25
  106.4 2.4 %collective-permute-start.6 = (bf16[48,256]{0,1:T(8,128)(2,1)S(1)}, bf16[48,256]{0,1:T(8,128)(2,1)S(1)}, u32[]{:S(2)}, u32[]{:S(2)}) collective-permute-start(bf16[48,256]{0,1:T(8,128)(2,1)S(1)} %get-tuple-element.29), channel_id=1, source_target_pairs={{0,192},{64,0},{128,64},{192,128},{1,193},{65,1},{129,65},{193,129... | collective-permute-start | bytes 73736 | tf_op jit(solution)/shard_map/ppermute | solution.py:25
  108.9 4.8 %collective-permute-done.6 = bf16[48,256]{0,1:T(8,128)(2,1)S(1)} collective-permute-done((bf16[48,256]{0,1:T(8,128)(2,1)S(1)}, bf16[48,256]{0,1:T(8,128)(2,1)S(1)}, u32[]{:S(2)}, u32[]{:S(2)}) %collective-permute-start.6) | collective-permute-done | bytes 24608 | tf_op jit(solution)/shard_map/ppermute | solution.py:25
  113.8 1.6 fusion.10
  115.4 1.6 fusion.4
  117.2 1.6 fusion.6
  118.8 1.6 fusion.8
  120.4 2.0 %collective-permute-start.7 = (bf16[32,256]{1,0:T(8,128)(2,1)S(1)}, bf16[32,256]{1,0:T(8,128)(2,1)S(1)}, u32[]{:S(2)}, u32[]{:S(2)}) collective-permute-start(bf16[32,256]{1,0:T(8,128)(2,1)S(1)} %get-tuple-element.52), channel_id=1, source_target_pairs={{0,192},{64,0},{128,64},{192,128},{1,193},{65,1},{129,65},{193,129... | collective-permute-start | bytes 49160 | tf_op jit(solution)/shard_map/ppermute | solution.py:25
  122.5 1.5 collective-permute-start.8
  124.0 2.3 %collective-permute-start.9 = (bf16[32,256]{1,0:T(8,128)(2,1)S(1)}, bf16[32,256]{1,0:T(8,128)(2,1)S(1)}, u32[]{:S(2)}, u32[]{:S(2)}) collective-permute-start(bf16[32,256]{1,0:T(8,128)(2,1)S(1)} %get-tuple-element.52), channel_id=1, source_target_pairs={{0,64},{64,128},{128,192},{192,0},{1,65},{65,129},{129,193},{193,1... | collective-permute-start | bytes 49160 | tf_op jit(solution)/shard_map/ppermute | solution.py:25
  126.3 2.7 %collective-permute-done.8 = bf16[32,256]{1,0:T(8,128)(2,1)S(1)} collective-permute-done((bf16[32,256]{1,0:T(8,128)(2,1)S(1)}, bf16[32,256]{1,0:T(8,128)(2,1)S(1)}, u32[]{:S(2)}, u32[]{:S(2)}) %collective-permute-start.8) | collective-permute-done | bytes 16416 | tf_op jit(solution)/shard_map/ppermute | solution.py:25
  129.0 1.9 %collective-permute-start.10 = (bf16[128,256]{1,0:T(8,128)(2,1)S(1)}, bf16[128,256]{1,0:T(8,128)(2,1)S(1)}, u32[]{:S(2)}, u32[]{:S(2)}) collective-permute-start(bf16[128,256]{1,0:T(8,128)(2,1)S(1)} %pad_maximum_fusion.14), channel_id=1, source_target_pairs={{0,48},{16,0},{32,16},{48,32},{1,49},{17,1},{33,17},{49,33},{2,50}... | collective-permute-start | bytes 196616 | tf_op jit(solution)/shard_map/ppermute | solution.py:25
  130.9 0.7 collective-permute-start.12
  131.6 1.2 collective-permute-done.10
  132.8 2.8 %collective-permute-done.11 = bf16[128,256]{1,0:T(8,128)(2,1)S(1)} collective-permute-done((bf16[128,256]{1,0:T(8,128)(2,1)S(1)}, bf16[128,256]{1,0:T(8,128)(2,1)S(1)}, u32[]{:S(2)}, u32[]{:S(2)}) %collective-permute-start.11) | collective-permute-done | bytes 65568 | tf_op jit(solution)/shard_map/ppermute | solution.py:25
  135.6 0.3 collective-permute-done.12
  135.9 5.3 %collective-permute-start.13 = (bf16[512,256]{1,0:T(8,128)(2,1)S(1)}, bf16[512,256]{1,0:T(8,128)(2,1)S(1)}, u32[]{:S(2)}, u32[]{:S(2)}) collective-permute-start(bf16[512,256]{1,0:T(8,128)(2,1)S(1)} %get-tuple-element.19), channel_id=1, source_target_pairs={{0,8},{8,0},{1,9},{9,1},{2,10},{10,2},{3,11},{11,3},{4,12},{12,4},... | collective-permute-start | bytes 786440 | tf_op jit(solution)/shard_map/ppermute | solution.py:25
  141.2 1.2 collective-permute-done.13
  142.4 8.2 %fusion.2 = bf16[4096,128]{1,0:T(8,128)(2,1)S(1)} fusion(bf16[4096,1024]{1,0:T(8,128)(2,1)} %copy-done.2, bf16[4096,1024]{1,0:T(8,128)(2,1)} %copy-done.1, bf16[1024,128]{1,0:T(8,128)(2,1)S(1)} %get-tuple-element.13, bf16[1024,128]{1,0:T(8,128)(2,1)S(1)} %get-tuple-element.12), kind=kOutput, calls=%fused_computation.6 | convolution fusion | flops 2182610944 | bytes 18350080 | tf_op jit(solution)/shard_map/dot_general | solution.py:93
  150.8 1.4 collective-permute-start.15
  152.2 0.7 convert_reduce_fusion.2
  152.9 3.1 %collective-permute-start.16 = (bf16[512,128]{1,0:T(8,128)(2,1)S(1)}, bf16[512,128]{1,0:T(8,128)(2,1)S(1)}, u32[]{:S(2)}, u32[]{:S(2)}) collective-permute-start(bf16[512,128]{1,0:T(8,128)(2,1)S(1)} %get-tuple-element.10), channel_id=1, source_target_pairs={{0,3},{1,4},{2,5},{3,6},{4,7},{5,0},{6,1},{7,2},{8,11},{9,12},{10,... | collective-permute-start | bytes 393224 | tf_op jit(solution)/shard_map/ppermute | solution.py:25
  156.0 1.6 collective-permute-start.17
  157.6 1.8 %collective-permute-start.18 = (bf16[512,128]{1,0:T(8,128)(2,1)S(1)}, bf16[512,128]{1,0:T(8,128)(2,1)S(1)}, u32[]{:S(2)}, u32[]{:S(2)}) collective-permute-start(bf16[512,128]{1,0:T(8,128)(2,1)S(1)} %get-tuple-element.8), channel_id=1, source_target_pairs={{0,5},{1,6},{2,7},{3,0},{4,1},{5,2},{6,3},{7,4},{8,13},{9,14},{10,... | collective-permute-start | bytes 393224 | tf_op jit(solution)/shard_map/ppermute | solution.py:25
  159.4 1.1 collective-permute-start.19
  160.6 0.6 collective-permute-start.20
  161.2 0.7 convert_reduce_fusion.1
  163.2 0.7 convert_reduce_fusion
  164.5 2.0 %collective-permute-done.17 = bf16[512,128]{1,0:T(8,128)(2,1)S(1)} collective-permute-done((bf16[512,128]{1,0:T(8,128)(2,1)S(1)}, bf16[512,128]{1,0:T(8,128)(2,1)S(1)}, u32[]{:S(2)}, u32[]{:S(2)}) %collective-permute-start.17) | collective-permute-done | bytes 131104 | tf_op jit(solution)/shard_map/ppermute | solution.py:25
  166.5 3.2 %collective-permute-done.19 = bf16[512,128]{1,0:T(8,128)(2,1)S(1)} collective-permute-done((bf16[512,128]{1,0:T(8,128)(2,1)S(1)}, bf16[512,128]{1,0:T(8,128)(2,1)S(1)}, u32[]{:S(2)}, u32[]{:S(2)}) %collective-permute-start.19) | collective-permute-done | bytes 131104 | tf_op jit(solution)/shard_map/ppermute | solution.py:25
  169.8 2.4 %fusion.23 = bf16[512,128]{1,0:T(8,128)(2,1)} fusion(bf16[512,128]{1,0:T(8,128)(2,1)S(1)} %collective-permute-done.20, bf16[512,128]{1,0:T(8,128)(2,1)S(1)} %collective-permute-done.19, bf16[512,128]{1,0:T(8,128)(2,1)S(1)} %collective-permute-done.18, bf16[512,128]{1,0:T(8,128)(2,1)S(1)} %collective-permute-done.17, ...), kind=kOutput, calls=%fused_computation.33 | convolution fusion | flops 22216704 | bytes 1344012 | tf_op jit(solution)/shard_map/dot_general | solution.py:102
  (64 shorter events, 2.4 us)
Async XLA Ops:
  0.0 169.8 %copy-start = (bf16[128,128]{1,0:T(8,128)(2,1)S(1)}, bf16[128,128]{1,0:T(8,128)(2,1)}, u32[]{:S(2)}) copy-start(bf16[128,128]{1,0:T(8,128)(2,1)} %param.12) | copy-start | bytes 98308
  2.6 68.4 %copy-start.3 = (f32[4096]{0:T(1024)S(1)}, f32[4096]{0:T(1024)}, u32[]{:S(2)}) copy-start(f32[4096]{0:T(1024)} %param.9) | copy-start | bytes 49156
  71.0 5.9 %copy-start.1 = (bf16[4096,1024]{1,0:T(8,128)(2,1)}, bf16[4096,1024]{1,0:T(8,128)(2,1)S(1)}, u32[]{:S(2)}) copy-start(bf16[4096,1024]{1,0:T(8,128)(2,1)S(1)} %get-tuple-element.39) | copy-start | bytes 25165828
  71.0 5.9 %copy-start.2 = (bf16[4096,1024]{1,0:T(8,128)(2,1)}, bf16[4096,1024]{1,0:T(8,128)(2,1)S(1)}, u32[]{:S(2)}) copy-start(bf16[4096,1024]{1,0:T(8,128)(2,1)S(1)} %get-tuple-element.40) | copy-start | bytes 25165828
  80.1 4.6 %collective-permute-start = (bf16[528,256]{0,1:T(8,128)(2,1)S(1)}, bf16[528,256]{0,1:T(8,128)(2,1)S(1)}, u32[]{:S(2)}, u32[]{:S(2)}) collective-permute-start(bf16[528,256]{0,1:T(8,128)(2,1)S(1)} %fusion.20), channel_id=1, source_target_pairs={{0,8},{8,0},{1,9},{9,1},{2,10},{10,2},{3,11},{11,3},{4,12},{12,4},... | collective-permute-start | bytes 811016 | tf_op jit(solution)/shard_map/ppermute | solution.py:25
  87.0 6.7 %collective-permute-start.1 = (bf16[144,256]{0,1:T(8,128)(2,1)S(1)}, bf16[144,256]{0,1:T(8,128)(2,1)S(1)}, u32[]{:S(2)}, u32[]{:S(2)}) collective-permute-start(bf16[144,256]{0,1:T(8,128)(2,1)S(1)} %get-tuple-element.33), channel_id=1, source_target_pairs={{0,16},{16,32},{32,48},{48,0},{1,17},{17,33},{33,49},{49,1},{2,18}... | collective-permute-start | bytes 221192 | tf_op jit(solution)/shard_map/ppermute | solution.py:25
  87.1 8.0 %collective-permute-start.2 = (bf16[144,256]{0,1:T(8,128)(2,1)S(1)}, bf16[144,256]{0,1:T(8,128)(2,1)S(1)}, u32[]{:S(2)}, u32[]{:S(2)}) collective-permute-start(bf16[144,256]{0,1:T(8,128)(2,1)S(1)} %get-tuple-element.34), channel_id=1, source_target_pairs={{0,32},{16,48},{32,0},{48,16},{1,33},{17,49},{33,1},{49,17},{2,34}... | collective-permute-start | bytes 221192 | tf_op jit(solution)/shard_map/ppermute | solution.py:25
  89.0 7.4 %collective-permute-start.3 = (bf16[144,256]{0,1:T(8,128)(2,1)S(1)}, bf16[144,256]{0,1:T(8,128)(2,1)S(1)}, u32[]{:S(2)}, u32[]{:S(2)}) collective-permute-start(bf16[144,256]{0,1:T(8,128)(2,1)S(1)} %get-tuple-element.35), channel_id=1, source_target_pairs={{0,48},{16,0},{32,16},{48,32},{1,49},{17,1},{33,17},{49,33},{2,50}... | collective-permute-start | bytes 221192 | tf_op jit(solution)/shard_map/ppermute | solution.py:25
  98.1 10.7 %collective-permute-start.4 = (bf16[48,256]{0,1:T(8,128)(2,1)S(1)}, bf16[48,256]{0,1:T(8,128)(2,1)S(1)}, u32[]{:S(2)}, u32[]{:S(2)}) collective-permute-start(bf16[48,256]{0,1:T(8,128)(2,1)S(1)} %get-tuple-element.27), channel_id=1, source_target_pairs={{0,64},{64,128},{128,192},{192,0},{1,65},{65,129},{129,193},{193,1... | collective-permute-start | bytes 73736 | tf_op jit(solution)/shard_map/ppermute | solution.py:25
  101.3 7.6 %collective-permute-start.5 = (bf16[48,256]{0,1:T(8,128)(2,1)S(1)}, bf16[48,256]{0,1:T(8,128)(2,1)S(1)}, u32[]{:S(2)}, u32[]{:S(2)}) collective-permute-start(bf16[48,256]{0,1:T(8,128)(2,1)S(1)} %get-tuple-element.28), channel_id=1, source_target_pairs={{0,128},{64,192},{128,0},{192,64},{1,129},{65,193},{129,1},{193,65... | collective-permute-start | bytes 73736 | tf_op jit(solution)/shard_map/ppermute | solution.py:25
  106.4 7.2 %collective-permute-start.6 = (bf16[48,256]{0,1:T(8,128)(2,1)S(1)}, bf16[48,256]{0,1:T(8,128)(2,1)S(1)}, u32[]{:S(2)}, u32[]{:S(2)}) collective-permute-start(bf16[48,256]{0,1:T(8,128)(2,1)S(1)} %get-tuple-element.29), channel_id=1, source_target_pairs={{0,192},{64,0},{128,64},{192,128},{1,193},{65,1},{129,65},{193,129... | collective-permute-start | bytes 73736 | tf_op jit(solution)/shard_map/ppermute | solution.py:25
  120.4 5.8 %collective-permute-start.7 = (bf16[32,256]{1,0:T(8,128)(2,1)S(1)}, bf16[32,256]{1,0:T(8,128)(2,1)S(1)}, u32[]{:S(2)}, u32[]{:S(2)}) collective-permute-start(bf16[32,256]{1,0:T(8,128)(2,1)S(1)} %get-tuple-element.52), channel_id=1, source_target_pairs={{0,192},{64,0},{128,64},{192,128},{1,193},{65,1},{129,65},{193,129... | collective-permute-start | bytes 49160 | tf_op jit(solution)/shard_map/ppermute | solution.py:25
  122.5 6.5 %collective-permute-start.8 = (bf16[32,256]{1,0:T(8,128)(2,1)S(1)}, bf16[32,256]{1,0:T(8,128)(2,1)S(1)}, u32[]{:S(2)}, u32[]{:S(2)}) collective-permute-start(bf16[32,256]{1,0:T(8,128)(2,1)S(1)} %get-tuple-element.52), channel_id=1, source_target_pairs={{0,128},{64,192},{128,0},{192,64},{1,129},{65,193},{129,1},{193,65... | collective-permute-start | bytes 49160 | tf_op jit(solution)/shard_map/ppermute | solution.py:25
  124.0 5.0 %collective-permute-start.9 = (bf16[32,256]{1,0:T(8,128)(2,1)S(1)}, bf16[32,256]{1,0:T(8,128)(2,1)S(1)}, u32[]{:S(2)}, u32[]{:S(2)}) collective-permute-start(bf16[32,256]{1,0:T(8,128)(2,1)S(1)} %get-tuple-element.52), channel_id=1, source_target_pairs={{0,64},{64,128},{128,192},{192,0},{1,65},{65,129},{129,193},{193,1... | collective-permute-start | bytes 49160 | tf_op jit(solution)/shard_map/ppermute | solution.py:25
  129.0 3.8 %collective-permute-start.10 = (bf16[128,256]{1,0:T(8,128)(2,1)S(1)}, bf16[128,256]{1,0:T(8,128)(2,1)S(1)}, u32[]{:S(2)}, u32[]{:S(2)}) collective-permute-start(bf16[128,256]{1,0:T(8,128)(2,1)S(1)} %pad_maximum_fusion.14), channel_id=1, source_target_pairs={{0,48},{16,0},{32,16},{48,32},{1,49},{17,1},{33,17},{49,33},{2,50}... | collective-permute-start | bytes 196616 | tf_op jit(solution)/shard_map/ppermute | solution.py:25
  130.9 4.7 %collective-permute-start.11 = (bf16[128,256]{1,0:T(8,128)(2,1)S(1)}, bf16[128,256]{1,0:T(8,128)(2,1)S(1)}, u32[]{:S(2)}, u32[]{:S(2)}) collective-permute-start(bf16[128,256]{1,0:T(8,128)(2,1)S(1)} %pad_maximum_fusion.14), channel_id=1, source_target_pairs={{0,32},{16,48},{32,0},{48,16},{1,33},{17,49},{33,1},{49,17},{2,34}... | collective-permute-start | bytes 196616 | tf_op jit(solution)/shard_map/ppermute | solution.py:25
  130.9 5.0 %collective-permute-start.12 = (bf16[128,256]{1,0:T(8,128)(2,1)S(1)}, bf16[128,256]{1,0:T(8,128)(2,1)S(1)}, u32[]{:S(2)}, u32[]{:S(2)}) collective-permute-start(bf16[128,256]{1,0:T(8,128)(2,1)S(1)} %pad_maximum_fusion.14), channel_id=1, source_target_pairs={{0,16},{16,32},{32,48},{48,0},{1,17},{17,33},{33,49},{49,1},{2,18}... | collective-permute-start | bytes 196616 | tf_op jit(solution)/shard_map/ppermute | solution.py:25
  135.9 6.4 %collective-permute-start.13 = (bf16[512,256]{1,0:T(8,128)(2,1)S(1)}, bf16[512,256]{1,0:T(8,128)(2,1)S(1)}, u32[]{:S(2)}, u32[]{:S(2)}) collective-permute-start(bf16[512,256]{1,0:T(8,128)(2,1)S(1)} %get-tuple-element.19), channel_id=1, source_target_pairs={{0,8},{8,0},{1,9},{9,1},{2,10},{10,2},{3,11},{11,3},{4,12},{12,4},... | collective-permute-start | bytes 786440 | tf_op jit(solution)/shard_map/ppermute | solution.py:25
  142.4 27.4 %copy-start.4 = (f32[128]{0:T(128)S(1)}, f32[128]{0:T(128)}, u32[]{:S(2)}) copy-start(f32[128]{0:T(128)} %param.13) | copy-start | bytes 1540
  150.7 8.6 %collective-permute-start.14 = (bf16[512,128]{1,0:T(8,128)(2,1)S(1)}, bf16[512,128]{1,0:T(8,128)(2,1)S(1)}, u32[]{:S(2)}, u32[]{:S(2)}) collective-permute-start(bf16[512,128]{1,0:T(8,128)(2,1)S(1)} %get-tuple-element.5), channel_id=1, source_target_pairs={{0,1},{1,2},{2,3},{3,4},{4,5},{5,6},{6,7},{7,0},{8,9},{9,10},{10,1... | collective-permute-start | bytes 393224 | tf_op jit(solution)/shard_map/ppermute | solution.py:25
  150.8 9.7 %collective-permute-start.15 = (bf16[512,128]{1,0:T(8,128)(2,1)S(1)}, bf16[512,128]{1,0:T(8,128)(2,1)S(1)}, u32[]{:S(2)}, u32[]{:S(2)}) collective-permute-start(bf16[512,128]{1,0:T(8,128)(2,1)S(1)} %get-tuple-element.11), channel_id=1, source_target_pairs={{0,2},{1,3},{2,4},{3,5},{4,6},{5,7},{6,0},{7,1},{8,10},{9,11},{10,... | collective-permute-start | bytes 393224 | tf_op jit(solution)/shard_map/ppermute | solution.py:25
  152.9 11.6 %collective-permute-start.16 = (bf16[512,128]{1,0:T(8,128)(2,1)S(1)}, bf16[512,128]{1,0:T(8,128)(2,1)S(1)}, u32[]{:S(2)}, u32[]{:S(2)}) collective-permute-start(bf16[512,128]{1,0:T(8,128)(2,1)S(1)} %get-tuple-element.10), channel_id=1, source_target_pairs={{0,3},{1,4},{2,5},{3,6},{4,7},{5,0},{6,1},{7,2},{8,11},{9,12},{10,... | collective-permute-start | bytes 393224 | tf_op jit(solution)/shard_map/ppermute | solution.py:25
  156.0 10.5 %collective-permute-start.17 = (bf16[512,128]{1,0:T(8,128)(2,1)S(1)}, bf16[512,128]{1,0:T(8,128)(2,1)S(1)}, u32[]{:S(2)}, u32[]{:S(2)}) collective-permute-start(bf16[512,128]{1,0:T(8,128)(2,1)S(1)} %get-tuple-element.9), channel_id=1, source_target_pairs={{0,4},{1,5},{2,6},{3,7},{4,0},{5,1},{6,2},{7,3},{8,12},{9,13},{10,... | collective-permute-start | bytes 393224 | tf_op jit(solution)/shard_map/ppermute | solution.py:25
  157.6 9.0 %collective-permute-start.18 = (bf16[512,128]{1,0:T(8,128)(2,1)S(1)}, bf16[512,128]{1,0:T(8,128)(2,1)S(1)}, u32[]{:S(2)}, u32[]{:S(2)}) collective-permute-start(bf16[512,128]{1,0:T(8,128)(2,1)S(1)} %get-tuple-element.8), channel_id=1, source_target_pairs={{0,5},{1,6},{2,7},{3,0},{4,1},{5,2},{6,3},{7,4},{8,13},{9,14},{10,... | collective-permute-start | bytes 393224 | tf_op jit(solution)/shard_map/ppermute | solution.py:25
  159.4 10.4 %collective-permute-start.19 = (bf16[512,128]{1,0:T(8,128)(2,1)S(1)}, bf16[512,128]{1,0:T(8,128)(2,1)S(1)}, u32[]{:S(2)}, u32[]{:S(2)}) collective-permute-start(bf16[512,128]{1,0:T(8,128)(2,1)S(1)} %get-tuple-element.7), channel_id=1, source_target_pairs={{0,6},{1,7},{2,0},{3,1},{4,2},{5,3},{6,4},{7,5},{8,14},{9,15},{10,... | collective-permute-start | bytes 393224 | tf_op jit(solution)/shard_map/ppermute | solution.py:25
  160.6 9.2 %collective-permute-start.20 = (bf16[512,128]{1,0:T(8,128)(2,1)S(1)}, bf16[512,128]{1,0:T(8,128)(2,1)S(1)}, u32[]{:S(2)}, u32[]{:S(2)}) collective-permute-start(bf16[512,128]{1,0:T(8,128)(2,1)S(1)} %get-tuple-element.6), channel_id=1, source_target_pairs={{0,7},{1,0},{2,1},{3,2},{4,3},{5,4},{6,5},{7,6},{8,15},{9,8},{10,9... | collective-permute-start | bytes 393224 | tf_op jit(solution)/shard_map/ppermute | solution.py:25

commit v2 on v1

v2 whole, which is shorter than its diff:
```python
import functools
import math

import jax
import jax.numpy as jnp
from jax import lax
from jax.experimental import pallas as pl
from jax.experimental.pallas import tpu as pltpu
from jax.sharding import Mesh, PartitionSpec as P

SIZES = {"z_hi": 4, "x": 4, "core": 2, "y": 4, "z_lo": 2}
PTS = ("z_hi", "x", "core")
GRP = ("y", "z_lo")
ALL = PTS + GRP
C = 128
PITCH = C + 1
ROWS = 32
BF, F32 = jnp.bfloat16, jnp.float32
VM = pl.BlockSpec(memory_space=pltpu.VMEM)
SM = pl.BlockSpec(memory_space=pltpu.SMEM)


def call(body, n_in, out_shape, name, scratch=(), smem=0, flops=0, limit=None):
    many = isinstance(out_shape, (list, tuple))
    return pl.pallas_call(
        body,
        in_specs=[SM] * smem + [VM] * n_in,
        out_specs=[VM] * len(out_shape) if many else VM,
        out_shape=out_shape,
        scratch_shapes=list(scratch),
        compiler_params=pltpu.CompilerParams(vmem_limit_bytes=(limit or 16) * 2**20),
        cost_estimate=pl.CostEstimate(flops=flops, bytes_accessed=2**20, transcendentals=0),
        name=name,
    )


def send(value, axes, shift):
    n = 1
    for a in axes:
        n *= SIZES[a]
    return lax.ppermute(value, axes, [(j, (j + shift) % n) for j in range(n)])


def turn(x):
    h = math.pi * (x - jnp.round(x))
    q = h * h
    s = c = None
    for k in range(6, -1, -1):
        a = (-1) ** k / math.factorial(2 * k + 1)
        s = a if s is None else s * q + a
    for k in range(7, -1, -1):
        a = (-1) ** k / math.factorial(2 * k)
        c = a if c is None else c * q + a
    s = s * h
    return 1.0 - 2.0 * s * s, -2.0 * s * c


def times(a, b):
    return a[0] * b[0] - a[1] * b[1], a[0] * b[1] + a[1] * b[0]


def powers(x, n):
    one = turn(x)
    out = [(jnp.ones_like(x), jnp.zeros_like(x)), one]
    for k in range(2, n):
        out.append(times(out[k // 2], out[k - k // 2]))
    return out


def build_tables(coords, exy, ez, sl):
    for k, v in enumerate(powers(coords[2, sl], 32)):
        ez[k, 0, sl], ez[k, 1, sl] = v
    px, py = powers(coords[0, sl], 9), powers(coords[1, sl], 9)
    signed = lambda p, k: p[k] if k >= 0 else (p[-k][0], -p[-k][1])
    for kx in range(-8, 8):
        for ky in range(-8, 8):
            k = (kx + 8) * 16 + ky + 8
            exy[k, 0, sl], exy[k, 1, sl] = times(signed(px, kx), signed(py, ky))


def lanes3(value):
    hi = value.astype(BF).astype(F32)
    mid = (value - hi).astype(BF).astype(F32)
    low = value - hi - mid
    lane = lax.broadcasted_iota(jnp.int32, (16, C), 1)
    return jnp.where(lane == 0, hi, jnp.where(lane == 1, mid, jnp.where(lane == 2, low, 0.0))).astype(BF)


def total_of(rows):
    lane = lax.broadcasted_iota(jnp.int32, (1, C), 1)
    return jnp.sum(jnp.where(lane < 3, rows[:1], 0.0), axis=1, keepdims=True)


def analyse(flip, index, coef, basis, exy, ez, wt, total, scr):
    z, x, core = (lax.axis_index(a) for a in PTS)
    core = lax.rem(core + flip, 2)

    def block(dx):
        across = lax.rem(x + dx, 4)

        def some(it):
            own = (lax.rem(z + it // 2, 4) * 4 + across) * 2 + core
            for u in range(16):
                m = it * 16 + u
                k = index[own * 32 + lax.rem(it, 2) * 16 + u]
                ixy, iz = lax.shift_right_logical(k, 5), lax.bitwise_and(k, 31)
                for j in range(ROWS // 8):
                    sl = pl.ds(8 * j, 8)
                    re, im = times((exy[ixy, 0, sl], exy[ixy, 1, sl]), (ez[iz, 0, sl], ez[iz, 1, sl]))
                    scr[pl.ds(8 * j * PITCH + m, 8, stride=PITCH), :] = re
                    scr[pl.ds((ROWS + 8 * j) * PITCH + m, 8, stride=PITCH), :] = im

        pl.loop(0, C // 16)(some)
        at = pl.ds(pl.multiple_of(dx * C, C), C)
        acc = None
        for k in range(4):
            cols = pl.ds(k * 1024, 1024)
            both = []
            for part in range(2):
                rows = [scr[pl.ds((part * ROWS + k * 8 + h) * PITCH, C), :].astype(BF) for h in range(8)]
                both.append(jnp.concatenate(rows, axis=1))
                basis[part, at, cols] = both[-1]
            term = lax.dot_general(
                wt[:, cols], jnp.concatenate(both, axis=0), (((1,), (1,)), ((), ())), preferred_element_type=F32
            )
            acc = term if acc is None else acc + term
        coef[pl.ds(0, C), at] = acc[:, :C].astype(BF)
        coef[pl.ds(C, C), at] = acc[:, C:].astype(BF)
        coef[pl.ds(2 * C, 16), at] = lanes3(total)

    pl.loop(0, 4)(block)


def first_body(index, features, quad, coords, coef, basis, exy, ez, wt, scr):
    @pl.loop(0, ROWS)
    def _(o):
        at = pl.ds(pl.multiple_of(o * C, C), C)
        wt[:, at] = (features[at, :].astype(F32).T * quad[pl.ds(o, 1), :]).astype(BF)

    @pl.loop(0, ROWS // 8)
    def _(o):
        build_tables(coords, exy, ez, pl.ds(pl.multiple_of(8 * o, 8), 8))

    total = jnp.sum(jnp.sum(quad[...], axis=0, keepdims=True), axis=1, keepdims=True)
    analyse(1, index, coef, basis, exy, ez, wt, total, scr)


def second_body(index, quad, exy, ez, wt, coef, basis, scr):
    total = jnp.sum(jnp.sum(quad[...], axis=0, keepdims=True), axis=1, keepdims=True)
    analyse(0, index, coef, basis, exy, ez, wt, total, scr)


def pair_body(own, got, keep, out1, out2, out3):
    for s, ref in enumerate((keep, out1, out2, out3)):
        at = pl.ds(s * C, C)
        summed = own[pl.ds(0, 2 * C), at].astype(F32) + got[pl.ds(0, 2 * C), at].astype(F32)
        ref[pl.ds(0, 2 * C), :] = summed.astype(ref.dtype)
        tail = total_of(own[pl.ds(2 * C, 16), at].astype(F32) + got[pl.ds(2 * C, 16), at].astype(F32))
        ref[pl.ds(2 * C, 16), :] = lanes3(tail).astype(ref.dtype)


def across_body(own, got1, got2, got3, keep, out1, out2, out3):
    rows = pl.ds(2 * C, 16)
    tail = own[rows, :]
    for g in (got1, got2, got3):
        tail = tail + g[rows, :].astype(F32)
    tail = lanes3(total_of(tail))
    for part in range(2):
        rows = pl.ds(part * C, C)
        summed = own[rows, :]
        for g in (got1, got2, got3):
            summed = summed + g[rows, :].astype(F32)
        summed = summed.T
        for s, ref in enumerate((keep, out1, out2, out3)):
            ref[pl.ds(0, 32), pl.ds(part * C, C)] = summed[s * 32 : s * 32 + 32].astype(ref.dtype)
            ref[pl.ds(32, 16), pl.ds(part * C, C)] = tail.astype(ref.dtype)


def filter_body(own, got1, got2, got3, weight, out, total):
    summed = own[...]
    for g in (got1, got2, got3):
        summed = summed + g[...].astype(F32)
    total[...] = jnp.broadcast_to(total_of(summed[32:, :C]), total.shape)
    row = lax.rem(lax.broadcasted_iota(jnp.int32, (16, 2 * C), 0), 8)
    for g in range(4):
        block = summed[8 * g : 8 * g + 8]
        lhs = jnp.concatenate([block[:, :C], block[:, C:]], axis=0).astype(BF)
        picked = jnp.zeros((16, 2 * C), F32)
        for i in range(8):
            m = 8 * g + i
            both = jnp.concatenate([weight[m, 0], weight[m, 1]], axis=1)
            picked = jnp.where(row == i, jnp.dot(lhs, both, preferred_element_type=F32), picked)
        real = picked[:8, :C] - picked[8:, C:]
        imag = picked[:8, C:] + picked[8:, :C]
        out[pl.ds(8 * g, 8), :] = jnp.concatenate([real, imag], axis=1).astype(BF)


def turned_body(own, far, out0, out1):
    for src, out in ((own, out0), (far, out1)):
        for part in range(2):
            for s in range(4):
                block = src[pl.ds(s * C, C), pl.ds(part * C, C)].astype(F32).T
                out[:, pl.ds((part * 4 + s) * C, C)] = block.astype(BF)


def synthesis_body(shifts, own, far, basis0, basis1, *outs):
    group = lax.axis_index("y") * 2 + lax.axis_index("z_lo")
    for s, out in zip(shifts, outs, strict=True):
        at = pl.ds(pl.multiple_of(lax.rem(group + s, 8) * 512, 512), 512)
        acc = None
        for f, b in ((own, basis0), (far, basis1)):
            for part in range(2):
                term = jnp.dot(f[:, pl.ds(part * 512, 512)], b[part, :, at], preferred_element_type=F32)
                acc = term if acc is None else acc + term
        out[...] = acc.astype(BF)


def finish_body(total, features, lin, bias, *rest):
    *blocks, out = rest
    summed = blocks[0][...].astype(F32)
    for b in blocks[1:]:
        summed = summed + b[...].astype(F32)
    scaled = summed / total[0:1, 0:1]
    for k in range(4):
        rows = pl.ds(k * C, C)
        pre = scaled[:, k * C : k * C + C].T + jnp.dot(features[rows, :], lin[...], preferred_element_type=F32) + bias[...]
        out[rows, :] = (0.5 * pre * (1.0 + lax.erf(pre * math.sqrt(0.5)))).astype(BF)


def gather_over(piece, axes, n):
    return jnp.concatenate([piece] + [send(piece, axes, n - s) for s in range(1, n)])


def on_device(features, coords, quad_weight, mode_table, mode_weight, lin_weight, bias):
    pts = features.shape[0]
    group = lax.axis_index(GRP)
    table = mode_table.reshape(3, 32, 8, 32)
    table = lax.dynamic_index_in_dim(table, group, 2, keepdims=False)
    index = (((table[0] + 8) * 16 + table[1] + 8) * 32 + table[2]).reshape(1024)
    quad = quad_weight.reshape(ROWS, C)
    coords = coords.reshape(3, ROWS, C)
    scr = pltpu.VMEM((2 * ROWS * PITCH, C), F32)
    shape = jax.ShapeDtypeStruct
    coef_shape = shape((2 * C + 16, 512), BF)
    basis_shape = pltpu.VMEM((2, 512, pts), BF)
    half = 2 * 2 * 512 * pts * C
    far, basis1, exy, ez, wt = call(
        first_body, 3,
        [coef_shape, basis_shape, pltpu.VMEM((256, 2, ROWS, C), F32), pltpu.VMEM((32, 2, ROWS, C), F32), pltpu.VMEM((C, pts), BF)],
        "first_half", [scr], 1, 4 * half,
    )(index, features, quad, coords)
    near, basis0 = call(second_body, 4, [coef_shape, basis_shape], "second_half", [scr], 1, 3 * half)(
        index, quad, exy, ez, wt
    )
    got = send(far, ("core",), 1)
    one = lambda rows, cols, dt: shape((rows, cols), dt)
    keep, *outs = call(pair_body, 2, [one(272, C, F32)] + [one(272, C, BF)] * 3, "pair_sum")(near, got)
    got = [send(o, ("x",), s) for s, o in zip((1, 2, 3), outs)]
    keep, *outs = call(across_body, 4, [one(48, 2 * C, F32)] + [one(48, 2 * C, BF)] * 3, "x_sum")(keep, *got)
    got = [send(o, ("z_hi",), s) for s, o in zip((1, 2, 3), outs)]
    piece, total = call(filter_body, 5, [one(32, 2 * C, BF), one(8, C, F32)], "filter")(keep, *got, mode_weight)
    piece = gather_over(piece, ("z_hi",), 4)
    piece = gather_over(piece, ("x",), 4)
    other = send(piece, ("core",), 1)
    own, other = call(turned_body, 2, [one(C, 1024, BF)] * 2, "turned")(piece, other)
    fields = []
    for shifts in ((1, 2, 3), (4, 5), (6, 7), (0,)):
        out = [one(C, 512, BF)] * len(shifts)
        outs = call(functools.partial(synthesis_body, shifts), 4, out, "synthesis", flops=len(shifts) * half // 4)(
            own, other, basis0, basis1
        )
        fields += [send(o, GRP, s) if s else o for s, o in zip(shifts, outs)]
    rows = pts // 8
    mine = lax.dynamic_slice_in_dim(features, group * rows, rows, 0)
    return call(finish_body, 12, shape((rows, C), BF), "finish")(
        total, mine, lin_weight, bias.reshape(1, C), *fields
    )


def solution(mesh):
    fine = Mesh(mesh.devices.reshape([SIZES[a] for a in ALL]), ALL)
    return jax.shard_map(
        on_device,
        mesh=fine,
        in_specs=(
            P(PTS, None),
            P(None, PTS),
            P(PTS),
            P(),
            P(ALL, None, None, None),
            P(),
            P(),
        ),
        out_specs=P(ALL, None),
        check_vma=False,
    )
```

time: 173 us -> 99.5 us (0.58)
  other arithmetic: 75.4 us -> 0.1 us
  matrix products: 22.9 us -> 0 us
  Pallas kernels: 0 us -> 22.9 us
  local copies, waits for them, and re-layouts: 3.07 us -> 11.7 us
  between operations: 6.92 us -> 0.21 us
    another operation x3 -> x0, other arithmetic: 68.3 us -> none
    dot_general x7 -> x0, matrix products: 22.9 us -> none  [the longest x1 8.23 us: on_device(): jnp.dot(basis, rhs, preferred_element_type=jnp.float32).astype(jnp.bfloat16)]
    pallas_call x0 -> x11, Pallas kernels: none -> 22.9 us  [the longest x1 11.5 us: on_device(): call(first_body, 3, [coef_shape, basis_shape, pltpu.VMEM((256, 2, ROWS, C...]
    unnamed x15 -> x26, local copies, waits for them, and re-layouts: 0.05 us -> 9.6 us
    reduce_sum x8 -> x0, other arithmetic: 5.08 us -> none  [the longest x7 4.47 us: join3(): return jnp.sum(rows[0, :3].astype(jnp.float32))]
    slice x9 -> x0, local copies, waits for them, and re-layouts: 2.45 us -> none  [the longest x1 1.06 us: on_device(): term[:modes]]
  transfers between devices with their start and end apart: 21 -> 21, of which waited for: 13 -> 10; matrix products, arithmetic and copies ran while one was open for 2% -> 1% of each run, Pallas kernels for 0% -> 9%
where the time goes in v2:
time: 99.5 us; the launch traced here: 99.2 us
  starting transfers between devices  40.5 us (41%)
  waiting for transfers between devices  23.7 us (24%)
  Pallas kernels  22.9 us (23%)
  local copies, waits for them, and re-layouts  11.7 us (12%)
    ppermute x21, starting transfers between devices, send(): return lax.ppermute(value, axes, [(j, (j + shift) % n) for j in range(n)])  40.5 us
    ppermute x21, waiting for transfers between devices, send(): return lax.ppermute(value, axes, [(j, (j + shift) % n) for j in range(n)])  23.7 us
    pallas_call x1, Pallas kernels, on_device(): call(first_body, 3, [coef_shape, basis_shape, pltpu.VMEM((256, 2, ROWS, C...  11.5 us
    unnamed x26, local copies, waits for them, and re-layouts  9.6 us
    pallas_call x1, Pallas kernels, on_device(): call(second_body, 4, [coef_shape, basis_shape], 'second_half', [scr], 1,...  6.68 us
    pallas_call x4, Pallas kernels, on_device(): call(functools.partial(synthesis_body, shifts), 4, out, 'synthesis', flop...  2.99 us
  transfers between devices with their start and end apart: 21, of which 10 were waited for; matrix products, arithmetic and copies ran while one was open for 1% of the time, Pallas kernels for 9%

profile of v2, /device:TPU:1, one launch (start us, length us, event | category | flops | bytes accessed | tf_op | source)
XLA Modules:
  0.0 99.2 jit_solution(10486814150486478001)
XLA Ops:
  0.0 1.1 %reshape.29 = s32[3,32,8,32]{3,2,1,0:T(8,128)S(1)} reshape(s32[3,8192]{1,0:T(4,128)} %param.10) | data formatting | bytes 196608 | tf_op jit(solution)/shard_map/reshape | solution.py:237
  1.1 0.1 fusion
  1.3 0.8 copy.10
  2.1 1.2 %copy-done.6 = bf16[4096,128]{1,0:T(8,128)(2,1)S(1)} copy-done((bf16[4096,128]{1,0:T(8,128)(2,1)S(1)}, bf16[4096,128]{1,0:T(8,128)(2,1)}, u32[]{:S(2)}) %copy-start.6) | copy-done | bytes 1048600
  3.3 0.7 copy-done.8
  4.0 11.5 %first_half.1 = (bf16[272,512]{1,0:T(8,128)(2,1)S(1)}, bf16[2,512,4096]{2,1,0:T(8,128)(2,1)S(1)}, f32[256,2,32,128]{3,2,1,0:T(8,128)S(1)}, f32[32,2,32,128]{3,2,1,0:T(8,128)S(1)}, bf16[128,4096]{1,0:T(8,128)(2,1)S(1)}) custom-call(s32[1024]{0:T(1024)S(1)} %reshape.35.index, bf16[4096,128]{1,0:T(8,128)(2,1)S(1)} %copy-done.6, f32[32,128]{1,0:T(8,128)S(1)} %bitcast.8, ...), custom_call_target="tpu_custom_call" | custom-call | flops 4294967296 | bytes 1048576 | tf_op jit(solution)/shard_map/first_half/pallas_call | solution.py:247
  15.6 3.3 %collective-permute-start = (bf16[272,512]{1,0:T(8,128)(2,1)S(1)}, bf16[272,512]{1,0:T(8,128)(2,1)S(1)}, u32[]{:S(2)}, u32[]{:S(2)}) collective-permute-start(bf16[272,512]{1,0:T(8,128)(2,1)S(1)} %get-tuple-element.35), channel_id=1, source_target_pairs={{0,8},{8,0},{1,9},{9,1},{2,10},{10,2},{3,11},{11,3},{4,12},{12,4},... | collective-permute-start | bytes 835592 | tf_op jit(solution)/shard_map/ppermute | solution.py:41
  18.9 6.7 %second_half.1 = (bf16[272,512]{1,0:T(8,128)(2,1)S(1)}, bf16[2,512,4096]{2,1,0:T(8,128)(2,1)S(1)}) custom-call(s32[1024]{0:T(1024)S(1)} %reshape.35.index, f32[32,128]{1,0:T(8,128)S(1)} %bitcast.9, f32[256,2,32,128]{3,2,1,0:T(8,128)S(1)} %get-tuple-element.31.exy, f32[32,2,32,128]{3,2,1,0:T(8,128)S(1)} %get-tuple-element.32.ez, ...), custom_call_target="tpu_custom_call" | custom-call | flops 3221225472 | bytes 1048576 | tf_op jit(solution)/shard_map/second_half/pallas_call | solution.py:252
  25.6 0.1 pair_sum.1
  25.8 1.9 %collective-permute-start.2 = (bf16[272,128]{1,0:T(8,128)(2,1)S(1)}, bf16[272,128]{1,0:T(8,128)(2,1)S(1)}, u32[]{:S(2)}, u32[]{:S(2)}) collective-permute-start(bf16[272,128]{1,0:T(8,128)(2,1)S(1)} %get-tuple-element.38), channel_id=1, source_target_pairs={{0,32},{16,48},{32,0},{48,16},{1,33},{17,49},{33,1},{49,17},{2,34}... | collective-permute-start | bytes 208904 | tf_op jit(solution)/shard_map/ppermute | solution.py:41
  27.8 1.1 %collective-permute-start.3 = (bf16[272,128]{1,0:T(8,128)(2,1)S(1)}, bf16[272,128]{1,0:T(8,128)(2,1)S(1)}, u32[]{:S(2)}, u32[]{:S(2)}) collective-permute-start(bf16[272,128]{1,0:T(8,128)(2,1)S(1)} %get-tuple-element.39), channel_id=1, source_target_pairs={{0,48},{16,0},{32,16},{48,32},{1,49},{17,1},{33,17},{49,33},{2,50}... | collective-permute-start | bytes 208904 | tf_op jit(solution)/shard_map/ppermute | solution.py:41
  28.9 3.4 %collective-permute-done.1.got1 = bf16[272,128]{1,0:T(8,128)(2,1)S(1)} collective-permute-done((bf16[272,128]{1,0:T(8,128)(2,1)S(1)}, bf16[272,128]{1,0:T(8,128)(2,1)S(1)}, u32[]{:S(2)}, u32[]{:S(2)}) %collective-permute-start.1) | collective-permute-done | bytes 69664 | tf_op jit(solution)/shard_map/ppermute | solution.py:41
  32.3 0.2 collective-permute-done.3.got3
  32.6 0.1 x_sum.1
  32.7 2.1 %collective-permute-start.4 = (bf16[48,256]{1,0:T(8,128)(2,1)S(1)}, bf16[48,256]{1,0:T(8,128)(2,1)S(1)}, u32[]{:S(2)}, u32[]{:S(2)}) collective-permute-start(bf16[48,256]{1,0:T(8,128)(2,1)S(1)} %get-tuple-element.41), channel_id=1, source_target_pairs={{0,64},{64,128},{128,192},{192,0},{1,65},{65,129},{129,193},{193,1... | collective-permute-start | bytes 73736 | tf_op jit(solution)/shard_map/ppermute | solution.py:41
  34.8 5.1 %collective-permute-start.5 = (bf16[48,256]{1,0:T(8,128)(2,1)S(1)}, bf16[48,256]{1,0:T(8,128)(2,1)S(1)}, u32[]{:S(2)}, u32[]{:S(2)}) collective-permute-start(bf16[48,256]{1,0:T(8,128)(2,1)S(1)} %get-tuple-element.42), channel_id=1, source_target_pairs={{0,128},{64,192},{128,0},{192,64},{1,129},{65,193},{129,1},{193,65... | collective-permute-start | bytes 73736 | tf_op jit(solution)/shard_map/ppermute | solution.py:41
  39.9 2.4 %collective-permute-start.6 = (bf16[48,256]{1,0:T(8,128)(2,1)S(1)}, bf16[48,256]{1,0:T(8,128)(2,1)S(1)}, u32[]{:S(2)}, u32[]{:S(2)}) collective-permute-start(bf16[48,256]{1,0:T(8,128)(2,1)S(1)} %get-tuple-element.43), channel_id=1, source_target_pairs={{0,192},{64,0},{128,64},{192,128},{1,193},{65,1},{129,65},{193,129... | collective-permute-start | bytes 73736 | tf_op jit(solution)/shard_map/ppermute | solution.py:41
  42.3 1.2 %collective-permute-done.6.got3 = bf16[48,256]{1,0:T(8,128)(2,1)S(1)} collective-permute-done((bf16[48,256]{1,0:T(8,128)(2,1)S(1)}, bf16[48,256]{1,0:T(8,128)(2,1)S(1)}, u32[]{:S(2)}, u32[]{:S(2)}) %collective-permute-start.6) | collective-permute-done | bytes 24608 | tf_op jit(solution)/shard_map/ppermute | solution.py:41
  43.5 0.4 filter.1
  43.9 4.1 %collective-permute-start.7 = (bf16[32,256]{1,0:T(8,128)(2,1)S(1)}, bf16[32,256]{1,0:T(8,128)(2,1)S(1)}, u32[]{:S(2)}, u32[]{:S(2)}) collective-permute-start(bf16[32,256]{1,0:T(8,128)(2,1)S(1)} %get-tuple-element.45), channel_id=1, source_target_pairs={{0,192},{64,0},{128,64},{192,128},{1,193},{65,1},{129,65},{193,129... | collective-permute-start | bytes 49160 | tf_op jit(solution)/shard_map/ppermute | solution.py:41
  48.0 1.3 %collective-permute-start.8 = (bf16[32,256]{1,0:T(8,128)(2,1)S(1)}, bf16[32,256]{1,0:T(8,128)(2,1)S(1)}, u32[]{:S(2)}, u32[]{:S(2)}) collective-permute-start(bf16[32,256]{1,0:T(8,128)(2,1)S(1)} %get-tuple-element.45), channel_id=1, source_target_pairs={{0,128},{64,192},{128,0},{192,64},{1,129},{65,193},{129,1},{193,65... | collective-permute-start | bytes 49160 | tf_op jit(solution)/shard_map/ppermute | solution.py:41
  49.3 0.9 collective-permute-start.9
  50.2 4.3 %collective-permute-done.8 = bf16[32,256]{1,0:T(8,128)(2,1)S(1)} collective-permute-done((bf16[32,256]{1,0:T(8,128)(2,1)S(1)}, bf16[32,256]{1,0:T(8,128)(2,1)S(1)}, u32[]{:S(2)}, u32[]{:S(2)}) %collective-permute-start.8) | collective-permute-done | bytes 16416 | tf_op jit(solution)/shard_map/ppermute | solution.py:41
  54.5 2.1 %collective-permute-start.10 = (bf16[128,256]{1,0:T(8,128)(2,1)S(1)}, bf16[128,256]{1,0:T(8,128)(2,1)S(1)}, u32[]{:S(2)}, u32[]{:S(2)}) collective-permute-start(bf16[128,256]{1,0:T(8,128)(2,1)S(1)} %get-tuple-element.57), channel_id=1, source_target_pairs={{0,48},{16,0},{32,16},{48,32},{1,49},{17,1},{33,17},{49,33},{2,50}... | collective-permute-start | bytes 196616 | tf_op jit(solution)/shard_map/ppermute | solution.py:41
  56.6 0.1 collective-permute-start.11
  56.7 0.8 collective-permute-start.12
  57.5 0.5 collective-permute-done.10
  58.0 3.3 %collective-permute-done.11 = bf16[128,256]{1,0:T(8,128)(2,1)S(1)} collective-permute-done((bf16[128,256]{1,0:T(8,128)(2,1)S(1)}, bf16[128,256]{1,0:T(8,128)(2,1)S(1)}, u32[]{:S(2)}, u32[]{:S(2)}) %collective-permute-start.11) | collective-permute-done | bytes 65568 | tf_op jit(solution)/shard_map/ppermute | solution.py:41
  61.3 0.4 collective-permute-done.12
  61.8 5.8 %collective-permute-start.13 = (bf16[512,256]{1,0:T(8,128)(2,1)S(1)}, bf16[512,256]{1,0:T(8,128)(2,1)S(1)}, u32[]{:S(2)}, u32[]{:S(2)}) collective-permute-start(bf16[512,256]{1,0:T(8,128)(2,1)S(1)} %constant_dynamic-update-slice_fusion.4.own), channel_id=1, source_target_pairs={{0,8},{8,0},{1,9},{9,1},{2,10},{10,2},{3,11},{11,3},{4,12},{12,4},... | collective-permute-start | bytes 786440 | tf_op jit(solution)/shard_map/ppermute | solution.py:41
  67.6 1.2 %collective-permute-done.13.far = bf16[512,256]{1,0:T(8,128)(2,1)S(1)} collective-permute-done((bf16[512,256]{1,0:T(8,128)(2,1)S(1)}, bf16[512,256]{1,0:T(8,128)(2,1)S(1)}, u32[]{:S(2)}, u32[]{:S(2)}) %collective-permute-start.13) | collective-permute-done | bytes 262176 | tf_op jit(solution)/shard_map/ppermute | solution.py:41
  68.8 0.2 turned.1
  69.0 0.8 synthesis.6
  69.8 2.8 %collective-permute-start.19 = (bf16[128,512]{1,0:T(8,128)(2,1)S(1)}, bf16[128,512]{1,0:T(8,128)(2,1)S(1)}, u32[]{:S(2)}, u32[]{:S(2)}) collective-permute-start(bf16[128,512]{1,0:T(8,128)(2,1)S(1)} %get-tuple-element.55), channel_id=1, source_target_pairs={{0,6},{1,7},{2,0},{3,1},{4,2},{5,3},{6,4},{7,5},{8,14},{9,15},{10,... | collective-permute-start | bytes 393224 | tf_op jit(solution)/shard_map/ppermute | solution.py:41
  72.6 0.7 collective-permute-start.20
  73.3 3.4 %copy-done.1 = bf16[2,512,4096]{2,1,0:T(8,128)(2,1)S(1)} copy-done((bf16[2,512,4096]{2,1,0:T(8,128)(2,1)S(1)}, bf16[2,512,4096]{2,1,0:T(8,128)(2,1)}, u32[]{:S(2)}) %copy-start.1) | copy-done | bytes 8388632
  76.7 3.4 %copy-done.3 = bf16[2,512,4096]{2,1,0:T(8,128)(2,1)S(1)} copy-done((bf16[2,512,4096]{2,1,0:T(8,128)(2,1)S(1)}, bf16[2,512,4096]{2,1,0:T(8,128)(2,1)}, u32[]{:S(2)}) %copy-start.3) | copy-done | bytes 8388632
  80.1 0.7 synthesis.5
  80.8 0.1 collective-permute-start.17
  81.0 3.4 %collective-permute-start.18 = (bf16[128,512]{1,0:T(8,128)(2,1)S(1)}, bf16[128,512]{1,0:T(8,128)(2,1)S(1)}, u32[]{:S(2)}, u32[]{:S(2)}) collective-permute-start(bf16[128,512]{1,0:T(8,128)(2,1)S(1)} %get-tuple-element.54), channel_id=1, source_target_pairs={{0,5},{1,6},{2,7},{3,0},{4,1},{5,2},{6,3},{7,4},{8,13},{9,14},{10,... | collective-permute-start | bytes 393224 | tf_op jit(solution)/shard_map/ppermute | solution.py:41
  84.3 1.0 %synthesis.4 = (bf16[128,512]{1,0:T(8,128)(2,1)S(1)}, bf16[128,512]{1,0:T(8,128)(2,1)S(1)}, bf16[128,512]{1,0:T(8,128)(2,1)S(1)}) custom-call(bf16[128,1024]{1,0:T(8,128)(2,1)S(1)} %get-tuple-element.46.own, bf16[128,1024]{1,0:T(8,128)(2,1)S(1)} %get-tuple-element.47.far, bf16[2,512,4096]{2,1,0:T(8,128)(2,1)S(1)} %copy-done.3, ...), custom_call_target="tpu_custom_call" | custom-call | flops 805306368 | bytes 1048576 | tf_op jit(solution)/shard_map/synthesis/pallas_call | solution.py:269
  85.4 1.2 %collective-permute-start.14 = (bf16[128,512]{1,0:T(8,128)(2,1)S(1)}, bf16[128,512]{1,0:T(8,128)(2,1)S(1)}, u32[]{:S(2)}, u32[]{:S(2)}) collective-permute-start(bf16[128,512]{1,0:T(8,128)(2,1)S(1)} %get-tuple-element.50), channel_id=1, source_target_pairs={{0,1},{1,2},{2,3},{3,4},{4,5},{5,6},{6,7},{7,0},{8,9},{9,10},{10,1... | collective-permute-start | bytes 393224 | tf_op jit(solution)/shard_map/ppermute | solution.py:41
  86.6 1.1 %collective-permute-start.16 = (bf16[128,512]{1,0:T(8,128)(2,1)S(1)}, bf16[128,512]{1,0:T(8,128)(2,1)S(1)}, u32[]{:S(2)}, u32[]{:S(2)}) collective-permute-start(bf16[128,512]{1,0:T(8,128)(2,1)S(1)} %get-tuple-element.52), channel_id=1, source_target_pairs={{0,3},{1,4},{2,5},{3,6},{4,7},{5,0},{6,1},{7,2},{8,11},{9,12},{10,... | collective-permute-start | bytes 393224 | tf_op jit(solution)/shard_map/ppermute | solution.py:41
  87.7 0.9 constant_dynamic-slice_fusion.features
  88.6 0.5 synthesis.7.rest_7_
  89.1 2.4 %collective-permute-done.14.rest_0_ = bf16[128,512]{1,0:T(8,128)(2,1)S(1)} collective-permute-done((bf16[128,512]{1,0:T(8,128)(2,1)S(1)}, bf16[128,512]{1,0:T(8,128)(2,1)S(1)}, u32[]{:S(2)}, u32[]{:S(2)}) %collective-permute-start.14) | collective-permute-done | bytes 131104 | tf_op jit(solution)/shard_map/ppermute | solution.py:41
  91.5 6.8 %collective-permute-done.15.rest_1_ = bf16[128,512]{1,0:T(8,128)(2,1)S(1)} collective-permute-done((bf16[128,512]{1,0:T(8,128)(2,1)S(1)}, bf16[128,512]{1,0:T(8,128)(2,1)S(1)}, u32[]{:S(2)}, u32[]{:S(2)}) %collective-permute-start.15) | collective-permute-done | bytes 131104 | tf_op jit(solution)/shard_map/ppermute | solution.py:41
  98.3 0.9 finish.1
  (37 shorter events, 0.3 us)
Async XLA Ops:
  0.0 18.9 %copy-start.9 = (f32[4096]{0:T(1024)S(1)}, f32[4096]{0:T(1024)}, u32[]{:S(2)}) copy-start(f32[4096]{0:T(1024)} %param.9) | copy-start | bytes 49156
  2.1 1.2 %copy-start.6 = (bf16[4096,128]{1,0:T(8,128)(2,1)S(1)}, bf16[4096,128]{1,0:T(8,128)(2,1)}, u32[]{:S(2)}) copy-start(bf16[4096,128]{1,0:T(8,128)(2,1)} %features.1) | copy-start | bytes 3145732
  3.3 0.7 copy-start.8
  15.6 54.2 %copy-start = (bf16[2,512,4096]{2,1,0:T(8,128)(2,1)}, bf16[2,512,4096]{2,1,0:T(8,128)(2,1)S(1)}, u32[]{:S(2)}) copy-start(bf16[2,512,4096]{2,1,0:T(8,128)(2,1)S(1)} %get-tuple-element.49.basis1) | copy-start | bytes 25165828
  15.6 27.9 %copy-start.4 = (bf16[32,2,128,128]{3,2,1,0:T(8,128)(2,1)S(1)}, bf16[32,2,128,128]{3,2,1,0:T(8,128)(2,1)}, u32[]{:S(2)}) copy-start(bf16[32,2,128,128]{3,2,1,0:T(8,128)(2,1)} %weight.1) | copy-start | bytes 6291460
  15.6 10.0 %collective-permute-start = (bf16[272,512]{1,0:T(8,128)(2,1)S(1)}, bf16[272,512]{1,0:T(8,128)(2,1)S(1)}, u32[]{:S(2)}, u32[]{:S(2)}) collective-permute-start(bf16[272,512]{1,0:T(8,128)(2,1)S(1)} %get-tuple-element.35), channel_id=1, source_target_pairs={{0,8},{8,0},{1,9},{9,1},{2,10},{10,2},{3,11},{11,3},{4,12},{12,4},... | collective-permute-start | bytes 835592 | tf_op jit(solution)/shard_map/ppermute | solution.py:41
  25.6 44.2 %copy-start.2 = (bf16[2,512,4096]{2,1,0:T(8,128)(2,1)}, bf16[2,512,4096]{2,1,0:T(8,128)(2,1)S(1)}, u32[]{:S(2)}) copy-start(bf16[2,512,4096]{2,1,0:T(8,128)(2,1)S(1)} %get-tuple-element.48.basis0) | copy-start | bytes 25165828
  25.7 6.6 %collective-permute-start.1 = (bf16[272,128]{1,0:T(8,128)(2,1)S(1)}, bf16[272,128]{1,0:T(8,128)(2,1)S(1)}, u32[]{:S(2)}, u32[]{:S(2)}) collective-permute-start(bf16[272,128]{1,0:T(8,128)(2,1)S(1)} %get-tuple-element.37), channel_id=1, source_target_pairs={{0,16},{16,32},{32,48},{48,0},{1,17},{17,33},{33,49},{49,1},{2,18}... | collective-permute-start | bytes 208904 | tf_op jit(solution)/shard_map/ppermute | solution.py:41
  25.8 6.5 %collective-permute-start.2 = (bf16[272,128]{1,0:T(8,128)(2,1)S(1)}, bf16[272,128]{1,0:T(8,128)(2,1)S(1)}, u32[]{:S(2)}, u32[]{:S(2)}) collective-permute-start(bf16[272,128]{1,0:T(8,128)(2,1)S(1)} %get-tuple-element.38), channel_id=1, source_target_pairs={{0,32},{16,48},{32,0},{48,16},{1,33},{17,49},{33,1},{49,17},{2,34}... | collective-permute-start | bytes 208904 | tf_op jit(solution)/shard_map/ppermute | solution.py:41
  27.8 4.8 %collective-permute-start.3 = (bf16[272,128]{1,0:T(8,128)(2,1)S(1)}, bf16[272,128]{1,0:T(8,128)(2,1)S(1)}, u32[]{:S(2)}, u32[]{:S(2)}) collective-permute-start(bf16[272,128]{1,0:T(8,128)(2,1)S(1)} %get-tuple-element.39), channel_id=1, source_target_pairs={{0,48},{16,0},{32,16},{48,32},{1,49},{17,1},{33,17},{49,33},{2,50}... | collective-permute-start | bytes 208904 | tf_op jit(solution)/shard_map/ppermute | solution.py:41
  32.7 9.6 %collective-permute-start.4 = (bf16[48,256]{1,0:T(8,128)(2,1)S(1)}, bf16[48,256]{1,0:T(8,128)(2,1)S(1)}, u32[]{:S(2)}, u32[]{:S(2)}) collective-permute-start(bf16[48,256]{1,0:T(8,128)(2,1)S(1)} %get-tuple-element.41), channel_id=1, source_target_pairs={{0,64},{64,128},{128,192},{192,0},{1,65},{65,129},{129,193},{193,1... | collective-permute-start | bytes 73736 | tf_op jit(solution)/shard_map/ppermute | solution.py:41
  34.8 7.5 %collective-permute-start.5 = (bf16[48,256]{1,0:T(8,128)(2,1)S(1)}, bf16[48,256]{1,0:T(8,128)(2,1)S(1)}, u32[]{:S(2)}, u32[]{:S(2)}) collective-permute-start(bf16[48,256]{1,0:T(8,128)(2,1)S(1)} %get-tuple-element.42), channel_id=1, source_target_pairs={{0,128},{64,192},{128,0},{192,64},{1,129},{65,193},{129,1},{193,65... | collective-permute-start | bytes 73736 | tf_op jit(solution)/shard_map/ppermute | solution.py:41
  39.9 3.6 %collective-permute-start.6 = (bf16[48,256]{1,0:T(8,128)(2,1)S(1)}, bf16[48,256]{1,0:T(8,128)(2,1)S(1)}, u32[]{:S(2)}, u32[]{:S(2)}) collective-permute-start(bf16[48,256]{1,0:T(8,128)(2,1)S(1)} %get-tuple-element.43), channel_id=1, source_target_pairs={{0,192},{64,0},{128,64},{192,128},{1,193},{65,1},{129,65},{193,129... | collective-permute-start | bytes 73736 | tf_op jit(solution)/shard_map/ppermute | solution.py:41
  43.9 6.3 %collective-permute-start.7 = (bf16[32,256]{1,0:T(8,128)(2,1)S(1)}, bf16[32,256]{1,0:T(8,128)(2,1)S(1)}, u32[]{:S(2)}, u32[]{:S(2)}) collective-permute-start(bf16[32,256]{1,0:T(8,128)(2,1)S(1)} %get-tuple-element.45), channel_id=1, source_target_pairs={{0,192},{64,0},{128,64},{192,128},{1,193},{65,1},{129,65},{193,129... | collective-permute-start | bytes 49160 | tf_op jit(solution)/shard_map/ppermute | solution.py:41
  48.0 6.5 %collective-permute-start.8 = (bf16[32,256]{1,0:T(8,128)(2,1)S(1)}, bf16[32,256]{1,0:T(8,128)(2,1)S(1)}, u32[]{:S(2)}, u32[]{:S(2)}) collective-permute-start(bf16[32,256]{1,0:T(8,128)(2,1)S(1)} %get-tuple-element.45), channel_id=1, source_target_pairs={{0,128},{64,192},{128,0},{192,64},{1,129},{65,193},{129,1},{193,65... | collective-permute-start | bytes 49160 | tf_op jit(solution)/shard_map/ppermute | solution.py:41
  49.3 5.2 %collective-permute-start.9 = (bf16[32,256]{1,0:T(8,128)(2,1)S(1)}, bf16[32,256]{1,0:T(8,128)(2,1)S(1)}, u32[]{:S(2)}, u32[]{:S(2)}) collective-permute-start(bf16[32,256]{1,0:T(8,128)(2,1)S(1)} %get-tuple-element.45), channel_id=1, source_target_pairs={{0,64},{64,128},{128,192},{192,0},{1,65},{65,129},{129,193},{193,1... | collective-permute-start | bytes 49160 | tf_op jit(solution)/shard_map/ppermute | solution.py:41
  54.5 3.5 %collective-permute-start.10 = (bf16[128,256]{1,0:T(8,128)(2,1)S(1)}, bf16[128,256]{1,0:T(8,128)(2,1)S(1)}, u32[]{:S(2)}, u32[]{:S(2)}) collective-permute-start(bf16[128,256]{1,0:T(8,128)(2,1)S(1)} %get-tuple-element.57), channel_id=1, source_target_pairs={{0,48},{16,0},{32,16},{48,32},{1,49},{17,1},{33,17},{49,33},{2,50}... | collective-permute-start | bytes 196616 | tf_op jit(solution)/shard_map/ppermute | solution.py:41
  56.6 4.7 %collective-permute-start.11 = (bf16[128,256]{1,0:T(8,128)(2,1)S(1)}, bf16[128,256]{1,0:T(8,128)(2,1)S(1)}, u32[]{:S(2)}, u32[]{:S(2)}) collective-permute-start(bf16[128,256]{1,0:T(8,128)(2,1)S(1)} %get-tuple-element.57), channel_id=1, source_target_pairs={{0,32},{16,48},{32,0},{48,16},{1,33},{17,49},{33,1},{49,17},{2,34}... | collective-permute-start | bytes 196616 | tf_op jit(solution)/shard_map/ppermute | solution.py:41
  56.7 5.0 %collective-permute-start.12 = (bf16[128,256]{1,0:T(8,128)(2,1)S(1)}, bf16[128,256]{1,0:T(8,128)(2,1)S(1)}, u32[]{:S(2)}, u32[]{:S(2)}) collective-permute-start(bf16[128,256]{1,0:T(8,128)(2,1)S(1)} %get-tuple-element.57), channel_id=1, source_target_pairs={{0,16},{16,32},{32,48},{48,0},{1,17},{17,33},{33,49},{49,1},{2,18}... | collective-permute-start | bytes 196616 | tf_op jit(solution)/shard_map/ppermute | solution.py:41
  61.8 7.0 %collective-permute-start.13 = (bf16[512,256]{1,0:T(8,128)(2,1)S(1)}, bf16[512,256]{1,0:T(8,128)(2,1)S(1)}, u32[]{:S(2)}, u32[]{:S(2)}) collective-permute-start(bf16[512,256]{1,0:T(8,128)(2,1)S(1)} %constant_dynamic-update-slice_fusion.4.own), channel_id=1, source_target_pairs={{0,8},{8,0},{1,9},{9,1},{2,10},{10,2},{3,11},{11,3},{4,12},{12,4},... | collective-permute-start | bytes 786440 | tf_op jit(solution)/shard_map/ppermute | solution.py:41
  69.8 16.8 %collective-permute-start.19 = (bf16[128,512]{1,0:T(8,128)(2,1)S(1)}, bf16[128,512]{1,0:T(8,128)(2,1)S(1)}, u32[]{:S(2)}, u32[]{:S(2)}) collective-permute-start(bf16[128,512]{1,0:T(8,128)(2,1)S(1)} %get-tuple-element.55), channel_id=1, source_target_pairs={{0,6},{1,7},{2,0},{3,1},{4,2},{5,3},{6,4},{7,5},{8,14},{9,15},{10,... | collective-permute-start | bytes 393224 | tf_op jit(solution)/shard_map/ppermute | solution.py:41
  72.6 14.0 %collective-permute-start.20 = (bf16[128,512]{1,0:T(8,128)(2,1)S(1)}, bf16[128,512]{1,0:T(8,128)(2,1)S(1)}, u32[]{:S(2)}, u32[]{:S(2)}) collective-permute-start(bf16[128,512]{1,0:T(8,128)(2,1)S(1)} %get-tuple-element.56), channel_id=1, source_target_pairs={{0,7},{1,0},{2,1},{3,2},{4,3},{5,4},{6,5},{7,6},{8,15},{9,8},{10,9... | collective-permute-start | bytes 393224 | tf_op jit(solution)/shard_map/ppermute | solution.py:41
  73.3 3.4 %copy-start.1 = (bf16[2,512,4096]{2,1,0:T(8,128)(2,1)S(1)}, bf16[2,512,4096]{2,1,0:T(8,128)(2,1)}, u32[]{:S(2)}) copy-start(bf16[2,512,4096]{2,1,0:T(8,128)(2,1)} %copy-done) | copy-start | bytes 25165828
  76.7 3.4 %copy-start.3 = (bf16[2,512,4096]{2,1,0:T(8,128)(2,1)S(1)}, bf16[2,512,4096]{2,1,0:T(8,128)(2,1)}, u32[]{:S(2)}) copy-start(bf16[2,512,4096]{2,1,0:T(8,128)(2,1)} %copy-done.2) | copy-start | bytes 25165828
  80.8 8.3 %collective-permute-start.17 = (bf16[128,512]{1,0:T(8,128)(2,1)S(1)}, bf16[128,512]{1,0:T(8,128)(2,1)S(1)}, u32[]{:S(2)}, u32[]{:S(2)}) collective-permute-start(bf16[128,512]{1,0:T(8,128)(2,1)S(1)} %get-tuple-element.53), channel_id=1, source_target_pairs={{0,4},{1,5},{2,6},{3,7},{4,0},{5,1},{6,2},{7,3},{8,12},{9,13},{10,... | collective-permute-start | bytes 393224 | tf_op jit(solution)/shard_map/ppermute | solution.py:41
  81.0 8.1 %collective-permute-start.18 = (bf16[128,512]{1,0:T(8,128)(2,1)S(1)}, bf16[128,512]{1,0:T(8,128)(2,1)S(1)}, u32[]{:S(2)}, u32[]{:S(2)}) collective-permute-start(bf16[128,512]{1,0:T(8,128)(2,1)S(1)} %get-tuple-element.54), channel_id=1, source_target_pairs={{0,5},{1,6},{2,7},{3,0},{4,1},{5,2},{6,3},{7,4},{8,13},{9,14},{10,... | collective-permute-start | bytes 393224 | tf_op jit(solution)/shard_map/ppermute | solution.py:41
  85.4 6.1 %collective-permute-start.14 = (bf16[128,512]{1,0:T(8,128)(2,1)S(1)}, bf16[128,512]{1,0:T(8,128)(2,1)S(1)}, u32[]{:S(2)}, u32[]{:S(2)}) collective-permute-start(bf16[128,512]{1,0:T(8,128)(2,1)S(1)} %get-tuple-element.50), channel_id=1, source_target_pairs={{0,1},{1,2},{2,3},{3,4},{4,5},{5,6},{6,7},{7,0},{8,9},{9,10},{10,1... | collective-permute-start | bytes 393224 | tf_op jit(solution)/shard_map/ppermute | solution.py:41
  86.6 11.7 %collective-permute-start.15 = (bf16[128,512]{1,0:T(8,128)(2,1)S(1)}, bf16[128,512]{1,0:T(8,128)(2,1)S(1)}, u32[]{:S(2)}, u32[]{:S(2)}) collective-permute-start(bf16[128,512]{1,0:T(8,128)(2,1)S(1)} %get-tuple-element.51), channel_id=1, source_target_pairs={{0,2},{1,3},{2,4},{3,5},{4,6},{5,7},{6,0},{7,1},{8,10},{9,11},{10,... | collective-permute-start | bytes 393224 | tf_op jit(solution)/shard_map/ppermute | solution.py:41
  86.6 11.7 %collective-permute-start.16 = (bf16[128,512]{1,0:T(8,128)(2,1)S(1)}, bf16[128,512]{1,0:T(8,128)(2,1)S(1)}, u32[]{:S(2)}, u32[]{:S(2)}) collective-permute-start(bf16[128,512]{1,0:T(8,128)(2,1)S(1)} %get-tuple-element.52), channel_id=1, source_target_pairs={{0,3},{1,4},{2,5},{3,6},{4,7},{5,0},{6,1},{7,2},{8,11},{9,12},{10,... | collective-permute-start | bytes 393224 | tf_op jit(solution)/shard_map/ppermute | solution.py:41
  88.6 9.6 %copy-start.5 = (bf16[128,128]{1,0:T(8,128)(2,1)S(1)}, bf16[128,128]{1,0:T(8,128)(2,1)}, u32[]{:S(2)}) copy-start(bf16[128,128]{1,0:T(8,128)(2,1)} %lin.1) | copy-start | bytes 98308
  88.6 9.6 %copy-start.7 = (f32[128]{0:T(128)S(1)}, f32[128]{0:T(128)}, u32[]{:S(2)}) copy-start(f32[128]{0:T(128)} %param.13) | copy-start | bytes 1540

commit v3 on v2

v3 whole, which is shorter than its diff:
```python
import functools
import math

import jax
import jax.numpy as jnp
from jax import lax
from jax.experimental import pallas as pl
from jax.experimental.pallas import tpu as pltpu
from jax.sharding import Mesh, PartitionSpec as P

SIZES = {"z_hi": 4, "x": 4, "core": 2, "y": 4, "z_lo": 2}
PTS = ("z_hi", "x", "core")
GRP = ("y", "z_lo")
ALL = PTS + GRP
C = 128
PITCH = C + 1
ROWS = 32
BF, F32 = jnp.bfloat16, jnp.float32
VM = pl.BlockSpec(memory_space=pltpu.VMEM)
SM = pl.BlockSpec(memory_space=pltpu.SMEM)


def call(body, n_in, out_shape, name, scratch=(), smem=0, flops=0, aliases={}, last=(), room=16):
    many = isinstance(out_shape, (list, tuple))
    return pl.pallas_call(
        body,
        in_specs=[SM] * smem + [VM] * n_in + [pl.BlockSpec(memory_space=m) for m in last],
        out_specs=[VM] * len(out_shape) if many else VM,
        out_shape=out_shape,
        scratch_shapes=list(scratch),
        compiler_params=pltpu.CompilerParams(vmem_limit_bytes=room * 2**20),
        input_output_aliases=aliases,
        cost_estimate=pl.CostEstimate(flops=flops, bytes_accessed=2**20, transcendentals=0),
        name=name,
    )


def send(value, axes, shift):
    n = 1
    for a in axes:
        n *= SIZES[a]
    return lax.ppermute(value, axes, [(j, (j + shift) % n) for j in range(n)])


def turn(x):
    h = math.pi * (x - jnp.round(x))
    q = h * h
    s = c = None
    for k in range(6, -1, -1):
        a = (-1) ** k / math.factorial(2 * k + 1)
        s = a if s is None else s * q + a
    for k in range(7, -1, -1):
        a = (-1) ** k / math.factorial(2 * k)
        c = a if c is None else c * q + a
    s = s * h
    return 1.0 - 2.0 * s * s, -2.0 * s * c


def times(a, b):
    return a[0] * b[0] - a[1] * b[1], a[0] * b[1] + a[1] * b[0]


def powers(x, n):
    one = turn(x)
    out = [(jnp.ones_like(x), jnp.zeros_like(x)), one]
    for k in range(2, n):
        out.append(times(out[k // 2], out[k - k // 2]))
    return out


def build_tables(coords, exy, ez, sl):
    for k, v in enumerate(powers(coords[2], 32)):
        ez[k, 0, sl], ez[k, 1, sl] = v
    px, py = powers(coords[0], 9), powers(coords[1], 9)
    signed = lambda p, k: p[k] if k >= 0 else (p[-k][0], -p[-k][1])
    for kx in range(-8, 8):
        for ky in range(-8, 8):
            k = (kx + 8) * 16 + ky + 8
            exy[k, 0, sl], exy[k, 1, sl] = times(signed(px, kx), signed(py, ky))


def lanes3(value):
    hi = value.astype(BF).astype(F32)
    mid = (value - hi).astype(BF).astype(F32)
    low = value - hi - mid
    lane = lax.broadcasted_iota(jnp.int32, (16, C), 1)
    return jnp.where(lane == 0, hi, jnp.where(lane == 1, mid, jnp.where(lane == 2, low, 0.0))).astype(BF)


def total_of(rows):
    lane = lax.broadcasted_iota(jnp.int32, (1, C), 1)
    return jnp.sum(jnp.where(lane < 3, rows[:1], 0.0), axis=1, keepdims=True)


def analyse(flip, dz, index, put_coef, put_basis, exy, ez, wt, total, scr):
    z, x, core = (lax.axis_index(a) for a in PTS)
    start = lax.rem(z + dz, 4) * 8 + lax.rem(core + flip, 2)

    @pl.loop(0, C // 16)
    def _(it):
        own = start + lax.rem(x + it // 2, 4) * 2
        base = own * 32 + lax.rem(it, 2) * 16
        for u in range(16):
            m = it * 16 + u
            k = index[base + u]
            ixy, iz = lax.shift_right_logical(k, 5), lax.bitwise_and(k, 31)
            for j in range(ROWS // 8):
                sl = pl.ds(8 * j, 8)
                re, im = times((exy[ixy, 0, sl], exy[ixy, 1, sl]), (ez[iz, 0, sl], ez[iz, 1, sl]))
                scr[pl.ds(8 * j * PITCH + m, 8, stride=PITCH), :] = re
                scr[pl.ds((ROWS + 8 * j) * PITCH + m, 8, stride=PITCH), :] = im

    acc = None
    for k in range(4):
        cols = pl.ds(k * 1024, 1024)
        both = []
        for part in range(2):
            rows = [scr[pl.ds((part * ROWS + k * 8 + h) * PITCH, C), :].astype(BF) for h in range(8)]
            both.append(jnp.concatenate(rows, axis=1))
        both = jnp.concatenate(both, axis=0)
        put_basis(cols, both)
        term = lax.dot_general(wt[:, cols], both, (((1,), (1,)), ((), ())), preferred_element_type=F32)
        acc = term if acc is None else acc + term
    put_coef(jnp.concatenate([acc[:, :C].astype(BF), acc[:, C:].astype(BF), lanes3(total)], axis=0))


def sum_all(quad):
    return jnp.sum(jnp.sum(quad[...], axis=0, keepdims=True), axis=1, keepdims=True)


def first_body(index, *refs):
    given, (coef, basis, exy, ez, wt, linear, quad, scr), here, sems = refs[:5], refs[5:13], refs[13:17], refs[17]
    here = (here[0], quad, *here[1:])
    loads = [pltpu.make_async_copy(src, dst, sems.at[i]) for i, (src, dst) in enumerate(zip(given, here))]
    for load in loads:
        load.start()
    coords, quad, lin, bias, f = here
    loads[0].wait()

    @pl.loop(0, ROWS // 8)
    def _(o):
        row = lambda i, r: coords[pl.ds(i, 1), pl.ds(pl.multiple_of((8 * o + r) * C, C), C)]
        at = [jnp.concatenate([row(i, r) for r in range(8)], axis=0) for i in range(3)]
        build_tables(at, exy, ez, pl.ds(pl.multiple_of(8 * o, 8), 8))

    for load in loads[1:]:
        load.wait()
    same = lax.broadcasted_iota(jnp.int32, (C, C), 0) == lax.broadcasted_iota(jnp.int32, (C, C), 1)
    unit = jnp.where(same, 1.0, 0.0).astype(BF)
    for o in range(ROWS // 8):
        turned = lax.dot_general(
            unit, f[pl.ds(o * 8 * C, 8 * C), :], (((1,), (1,)), ((), ())), preferred_element_type=F32
        )
        for r in range(8):
            at = pl.ds((8 * o + r) * C, C)
            wt[:, at] = (turned[:, r * C : r * C + C] * quad[pl.ds(8 * o + r, 1), :]).astype(BF)
    group = lax.axis_index("y") * 2 + lax.axis_index("z_lo")
    mine = f[pl.ds(pl.multiple_of(group * 512, 512), 512), :]
    linear[...] = jnp.dot(mine, lin[...], preferred_element_type=F32) + bias[...]
    total = sum_all(quad)

    @pl.loop(0, 3)
    def _(s):
        def put_coef(value):
            coef[:, pl.ds(pl.multiple_of(s * C, C), C)] = value

        def put_basis(cols, value):
            basis[s, :, cols] = value

        analyse(1, s + 1, index, put_coef, put_basis, exy, ez, wt, total, scr)


def slab_body(flip, dz, index, quad, exy, ez, wt, after, coef, basis, scr):
    def put_coef(value):
        coef[...] = value

    def put_basis(cols, value):
        basis[:, cols] = value

    analyse(flip, dz, index, put_coef, put_basis, exy, ez, wt, sum_all(quad), scr)


def pair_body(s, own, got, out):
    at = pl.ds(s * C, C)
    summed = own[...].astype(F32) + got[:, at].astype(F32)
    out[pl.ds(0, 2 * C), :] = summed[: 2 * C].astype(BF)
    out[pl.ds(2 * C, 16), :] = lanes3(total_of(summed[2 * C :]))


def z_body(own, got0, got1, got2, got3, keep, out1, out2, out3):
    summed = own[...].astype(F32)
    for g in (got0, got1, got2, got3):
        summed = summed + g[...].astype(F32)
    tail = lanes3(total_of(summed[2 * C :]))
    for part in range(2):
        rows = summed[part * C : part * C + C].T
        for s, ref in enumerate((keep, out1, out2, out3)):
            ref[pl.ds(0, 32), pl.ds(part * C, C)] = rows[s * 32 : s * 32 + 32].astype(ref.dtype)
            ref[pl.ds(32, 16), pl.ds(part * C, C)] = tail.astype(ref.dtype)


def filter_body(own, got1, got2, got3, weight, out, total):
    summed = own[...]
    for g in (got1, got2, got3):
        summed = summed + g[...].astype(F32)
    total[...] = jnp.broadcast_to(total_of(summed[32:, :C]), total.shape)
    row = lax.rem(lax.broadcasted_iota(jnp.int32, (16, 2 * C), 0), 8)
    for g in range(4):
        block = summed[8 * g : 8 * g + 8]
        lhs = jnp.concatenate([block[:, :C], block[:, C:]], axis=0).astype(BF)
        picked = jnp.zeros((16, 2 * C), F32)
        for i in range(8):
            m = 8 * g + i
            both = jnp.concatenate([weight[m, 0], weight[m, 1]], axis=1)
            picked = jnp.where(row == i, jnp.dot(lhs, both, preferred_element_type=F32), picked)
        real = picked[:8, :C] - picked[8:, C:]
        imag = picked[:8, C:] + picked[8:, :C]
        out[pl.ds(8 * g, 8), :] = jnp.concatenate([real, imag], axis=1).astype(BF)


def turned_body(own, far, out):
    for flip, src in enumerate((own, far)):
        for dz in range(4):
            for part in range(2):
                cols = pl.ds(part * C, C)
                block = jnp.concatenate([src[pl.ds(dx * C + dz * 32, 32), cols].astype(F32) for dx in range(4)], axis=0)
                out[:, pl.ds(((flip * 4 + dz) * 2 + part) * C, C)] = block.T.astype(BF)


def synthesis_body(shifts, f, n0, n1, n2, n3, f0, f123, *outs):
    group = lax.axis_index("y") * 2 + lax.axis_index("z_lo")
    for s, out in zip(shifts, outs[: len(shifts)], strict=True):
        at = pl.ds(pl.multiple_of(lax.rem(group + s, 8) * 512, 512), 512)
        acc = None
        for i, b in enumerate((n0, n1, n2, n3, f0, f123.at[0], f123.at[1], f123.at[2])):
            term = jnp.dot(f[:, pl.ds(i * 2 * C, 2 * C)], b[:, at], preferred_element_type=F32)
            acc = term if acc is None else acc + term
        out[...] = acc.astype(BF)


def finish_body(total, linear, *rest):
    *blocks, out = rest
    summed = blocks[0][...].astype(F32)
    for b in blocks[1:]:
        summed = summed + b[...].astype(F32)
    scaled = summed / total[0:1, 0:1]
    for k in range(4):
        rows = pl.ds(k * C, C)
        pre = scaled[:, k * C : k * C + C].T + linear[rows, :]
        out[rows, :] = (0.5 * pre * (1.0 + lax.erf(pre * math.sqrt(0.5)))).astype(BF)


def gather_over(piece, axes, n):
    return jnp.concatenate([piece] + [send(piece, axes, n - s) for s in range(1, n)])


def on_device(features, coords, quad_weight, mode_table, mode_weight, lin_weight, bias):
    pts = features.shape[0]
    group = lax.axis_index(GRP)
    packed = ((mode_table[0] + 8) * 16 + mode_table[1] + 8) * 32 + mode_table[2]
    packed = lax.dynamic_index_in_dim(packed.reshape(32, 2, C), group // 4, 1, keepdims=False)
    index = lax.dynamic_slice_in_dim(packed, lax.rem(group, 4) * 32, 32, 1).reshape(1024)
    scr = pltpu.VMEM((2 * ROWS * PITCH, C), F32)
    one = lambda rows, cols, dt: jax.ShapeDtypeStruct((rows, cols), dt)
    tail = 2 * C + 16
    slab = 2 * 2 * C * pts * C
    far, f123, exy, ez, wt, linear, quad = call(
        first_body, 0,
        [pltpu.VMEM((tail, 3 * C), BF), pltpu.VMEM((3, 2 * C, pts), BF), pltpu.VMEM((256, 2, ROWS, C), F32),
         pltpu.VMEM((32, 2, ROWS, C), F32), pltpu.VMEM((C, pts), BF), pltpu.VMEM((pts // 8, C), F32), pltpu.VMEM((ROWS, C), F32)],
        "first",
        [scr, pltpu.VMEM((3, pts), F32), pltpu.VMEM((C, C), BF), pltpu.VMEM((1, C), F32), pltpu.VMEM((pts, C), BF),
         pltpu.SemaphoreType.DMA((5,))],
        1, 6 * slab, last=[pltpu.HBM] * 5, room=42,
    )(index, coords, quad_weight.reshape(ROWS, C), lin_weight, bias.reshape(1, C), features)
    got = send(far, ("core",), 1)

    def near(flip, dz, after):
        return call(
            functools.partial(slab_body, flip, dz), 4, [one(tail, C, BF), pltpu.VMEM((2 * C, pts), BF)],
            "slab", [scr], 1, 2 * slab, last=[pl.ANY],
        )(index, quad, exy, ez, wt, after)

    across, bases = {}, {}
    after = linear
    for dz in (2, 1, 3):
        mine, bases[dz] = near(0, dz, after)
        after = call(functools.partial(pair_body, dz - 1), 2, one(tail, C, BF), "pair")(mine, got)
        across[dz] = send(after, ("z_hi",), dz)
    far, f0 = near(1, 0, after)
    got = send(far, ("core",), 1)
    mine, bases[0] = near(0, 0, far)
    keep, *outs = call(z_body, 5, [one(48, 2 * C, F32)] + [one(48, 2 * C, BF)] * 3, "z_sum")(
        mine, got, across[1], across[2], across[3]
    )
    got = [send(o, ("x",), s) for s, o in zip((1, 2, 3), outs)]
    piece, total = call(filter_body, 5, [one(32, 2 * C, BF), one(8, C, F32)], "filter")(keep, *got, mode_weight)
    piece = gather_over(piece, ("z_hi",), 4)
    piece = gather_over(piece, ("x",), 4)
    other = send(piece, ("core",), 1)
    f = call(turned_body, 2, one(C, 2048, BF), "turned")(piece, other)
    fields = []
    bases = [bases[0], bases[1], bases[2], bases[3], f0, f123]
    for shifts in ((4, 3), (5, 2, 6), (1, 7, 0)):
        on = 0 not in shifts
        out = [one(C, 512, BF)] * len(shifts) + [pltpu.VMEM(b.shape, BF) for b in bases if on]
        outs = call(
            functools.partial(synthesis_body, shifts), 7, out, "synthesis", flops=len(shifts) * slab,
            aliases={i + 1: len(shifts) + i for i in range(6 if on else 0)},
        )(f, *bases)
        if on:
            bases = outs[len(shifts) :]
        fields += [send(o, GRP, s) if s else o for s, o in zip(shifts, outs)]
    return call(finish_body, 10, one(pts // 8, C, BF), "finish")(total, linear, *fields)


def solution(mesh):
    fine = Mesh(mesh.devices.reshape([SIZES[a] for a in ALL]), ALL)
    return jax.shard_map(
        on_device,
        mesh=fine,
        in_specs=(
            P(PTS, None),
            P(None, PTS),
            P(PTS),
            P(),
            P(ALL, None, None, None),
            P(),
            P(),
        ),
        out_specs=P(ALL, None),
        check_vma=False,
    )
```

time: 99.5 us -> 85.7 us (0.86)
  the two profiles are of different devices: /device:TPU:1 before, /device:TPU:22 now
where the time goes in v3:
time: 85.7 us; the launch traced here: 85.6 us
  starting transfers between devices  34.9 us (41%)
  waiting for transfers between devices  24.5 us (29%)
  Pallas kernels  24 us (28%)
  other arithmetic  1.16 us (1%)
    ppermute x22, starting transfers between devices, send(): return lax.ppermute(value, axes, [(j, (j + shift) % n) for j in range(n)])  34.9 us
    ppermute x22, waiting for transfers between devices, send(): return lax.ppermute(value, axes, [(j, (j + shift) % n) for j in range(n)])  24.5 us
    pallas_call x5, Pallas kernels, near(): call(functools.partial(slab_body, flip, dz), 4, [one(tail, C, BF), pltpu....  10.9 us
    pallas_call x1, Pallas kernels, on_device(): call(first_body, 0, [pltpu.VMEM((tail, 3 * C), BF), pltpu.VMEM((3, 2 * C,...  8.34 us
    pallas_call x3, Pallas kernels, on_device(): call(functools.partial(synthesis_body, shifts), 7, out, 'synthesis', flop...  2.84 us
  transfers between devices with their start and end apart: 22, of which 11 were waited for; matrix products, arithmetic and copies ran while one was open for 0% of the time, Pallas kernels for 15%

profile of v3, /device:TPU:22, one launch (start us, length us, event | category | flops | bytes accessed | tf_op | source)
XLA Modules:
  0.0 85.6 jit_solution(14414173666942182404)
XLA Ops:
  0.0 1.2 %multiply_add_fusion = s32[1,8192]{1,0:T(1,128)S(1)} fusion(s32[3,8192]{1,0:T(4,128)} %param.10), kind=kLoop, calls=%fused_computation | loop fusion | flops 49152 | bytes 131072 | tf_op jit(solution)/shard_map/add | solution.py:260
  1.2 0.1 dynamic-slice_reduce_fusion
  1.3 0.7 reshape.22.index
  2.0 8.3 %first.1 = (bf16[272,384]{1,0:T(8,128)(2,1)S(1)}, bf16[3,256,4096]{2,1,0:T(8,128)(2,1)S(1)}, f32[256,2,32,128]{3,2,1,0:T(8,128)S(1)}, f32[32,2,32,128]{3,2,1,0:T...) custom-call(s32[1024]{0:T(1024)} %reshape.22.index, f32[3,4096]{1,0:T(4,128)} %refs_0_.1, ...), custom_call_target="tpu_custom_call" | custom-call | flops 1610612736 | bytes 1048576 | tf_op jit(solution)/shard_map/first/pallas_call | solution.py:267
  10.3 0.1 collective-permute-start
  10.4 2.2 %slab.5 = (bf16[272,128]{1,0:T(8,128)(2,1)S(1)}, bf16[256,4096]{1,0:T(8,128)(2,1)S(1)}) custom-call(s32[1024]{0:T(1024)S(1)} %copy-done.1, f32[32,128]{1,0:T(8,128)S(1)} %get-tuple-element.48.quad, f32[256,2,32,128]{3,2,1,0:T(8,128)S(1)} %get-tuple-element.49.exy, f32[32,2,32,128]{3,2,1,0:T(8,128)S(1)} %get-tuple-element.50.ez, ...), custom_call_target="tpu_custom_call" | custom-call | flops 536870912 | bytes 1048576 | tf_op jit(solution)/shard_map/slab/pallas_call | solution.py:279
  12.6 0.1 pair.3.after
  12.7 7.2 %collective-permute-start.3 = (bf16[272,128]{1,0:T(8,128)(2,1)S(1)}, bf16[272,128]{1,0:T(8,128)(2,1)S(1)}, u32[]{:S(2)}, u32[]{:S(2)}) collective-permute-start(bf16[272,128]{1,0:T(8,128)(2,1)S(1)} %pair.3.after), channel_id=1, source_target_pairs={{0,128},{64,192},{128,0},{192,64},{1,129},{65,193},{129,1},{193,65... | collective-permute-start | bytes 208904 | tf_op jit(solution)/shard_map/ppermute | solution.py:42
  19.9 2.2 %slab.6 = (bf16[272,128]{1,0:T(8,128)(2,1)S(1)}, bf16[256,4096]{1,0:T(8,128)(2,1)S(1)}) custom-call(s32[1024]{0:T(1024)S(1)} %copy-done.1, f32[32,128]{1,0:T(8,128)S(1)} %get-tuple-element.48.quad, f32[256,2,32,128]{3,2,1,0:T(8,128)S(1)} %get-tuple-element.49.exy, f32[32,2,32,128]{3,2,1,0:T(8,128)S(1)} %get-tuple-element.50.ez, ...), custom_call_target="tpu_custom_call" | custom-call | flops 536870912 | bytes 1048576 | tf_op jit(solution)/shard_map/slab/pallas_call | solution.py:279
  22.1 0.1 pair.4.after
  22.2 1.5 %collective-permute-start.2 = (bf16[272,128]{1,0:T(8,128)(2,1)S(1)}, bf16[272,128]{1,0:T(8,128)(2,1)S(1)}, u32[]{:S(2)}, u32[]{:S(2)}) collective-permute-start(bf16[272,128]{1,0:T(8,128)(2,1)S(1)} %pair.4.after), channel_id=1, source_target_pairs={{0,64},{64,128},{128,192},{192,0},{1,65},{65,129},{129,193},{193,1... | collective-permute-start | bytes 208904 | tf_op jit(solution)/shard_map/ppermute | solution.py:42
  23.7 2.2 %slab.7 = (bf16[272,128]{1,0:T(8,128)(2,1)S(1)}, bf16[256,4096]{1,0:T(8,128)(2,1)S(1)}) custom-call(s32[1024]{0:T(1024)S(1)} %copy-done.1, f32[32,128]{1,0:T(8,128)S(1)} %get-tuple-element.48.quad, f32[256,2,32,128]{3,2,1,0:T(8,128)S(1)} %get-tuple-element.49.exy, f32[32,2,32,128]{3,2,1,0:T(8,128)S(1)} %get-tuple-element.50.ez, ...), custom_call_target="tpu_custom_call" | custom-call | flops 536870912 | bytes 1048576 | tf_op jit(solution)/shard_map/slab/pallas_call | solution.py:279
  25.9 0.1 pair.5.after
  26.0 2.7 %collective-permute-start.4 = (bf16[272,128]{1,0:T(8,128)(2,1)S(1)}, bf16[272,128]{1,0:T(8,128)(2,1)S(1)}, u32[]{:S(2)}, u32[]{:S(2)}) collective-permute-start(bf16[272,128]{1,0:T(8,128)(2,1)S(1)} %pair.5.after), channel_id=1, source_target_pairs={{0,192},{64,0},{128,64},{192,128},{1,193},{65,1},{129,65},{193,129... | collective-permute-start | bytes 208904 | tf_op jit(solution)/shard_map/ppermute | solution.py:42
  28.6 2.2 %slab.8 = (bf16[272,128]{1,0:T(8,128)(2,1)S(1)}, bf16[256,4096]{1,0:T(8,128)(2,1)S(1)}) custom-call(s32[1024]{0:T(1024)S(1)} %copy-done.1, f32[32,128]{1,0:T(8,128)S(1)} %get-tuple-element.48.quad, f32[256,2,32,128]{3,2,1,0:T(8,128)S(1)} %get-tuple-element.49.exy, f32[32,2,32,128]{3,2,1,0:T(8,128)S(1)} %get-tuple-element.50.ez, ...), custom_call_target="tpu_custom_call" | custom-call | flops 536870912 | bytes 1048576 | tf_op jit(solution)/shard_map/slab/pallas_call | solution.py:279
  30.8 0.1 collective-permute-start.1
  30.9 2.2 %slab.9 = (bf16[272,128]{1,0:T(8,128)(2,1)S(1)}, bf16[256,4096]{1,0:T(8,128)(2,1)S(1)}) custom-call(s32[1024]{0:T(1024)S(1)} %copy-done.1, f32[32,128]{1,0:T(8,128)S(1)} %get-tuple-element.48.quad, f32[256,2,32,128]{3,2,1,0:T(8,128)S(1)} %get-tuple-element.49.exy, f32[32,2,32,128]{3,2,1,0:T(8,128)S(1)} %get-tuple-element.50.ez, ...), custom_call_target="tpu_custom_call" | custom-call | flops 536870912 | bytes 1048576 | tf_op jit(solution)/shard_map/slab/pallas_call | solution.py:279
  33.2 0.1 z_sum.1
  33.3 0.6 collective-permute-start.5
  33.8 2.4 %collective-permute-start.6 = (bf16[48,256]{1,0:T(8,128)(2,1)S(1)}, bf16[48,256]{1,0:T(8,128)(2,1)S(1)}, u32[]{:S(2)}, u32[]{:S(2)}) collective-permute-start(bf16[48,256]{1,0:T(8,128)(2,1)S(1)} %get-tuple-element.61), channel_id=1, source_target_pairs={{0,32},{16,48},{32,0},{48,16},{1,33},{17,49},{33,1},{49,17},{2,34}... | collective-permute-start | bytes 73736 | tf_op jit(solution)/shard_map/ppermute | solution.py:42
  36.3 1.1 %collective-permute-done.5.got1 = bf16[48,256]{1,0:T(8,128)(2,1)S(1)} collective-permute-done((bf16[48,256]{1,0:T(8,128)(2,1)S(1)}, bf16[48,256]{1,0:T(8,128)(2,1)S(1)}, u32[]{:S(2)}, u32[]{:S(2)}) %collective-permute-start.5) | collective-permute-done | bytes 24608 | tf_op jit(solution)/shard_map/ppermute | solution.py:42
  37.4 1.8 %collective-permute-done.6.got2 = bf16[48,256]{1,0:T(8,128)(2,1)S(1)} collective-permute-done((bf16[48,256]{1,0:T(8,128)(2,1)S(1)}, bf16[48,256]{1,0:T(8,128)(2,1)S(1)}, u32[]{:S(2)}, u32[]{:S(2)}) %collective-permute-start.6) | collective-permute-done | bytes 24608 | tf_op jit(solution)/shard_map/ppermute | solution.py:42
  39.2 2.1 %collective-permute-done.7.got3 = bf16[48,256]{1,0:T(8,128)(2,1)S(1)} collective-permute-done((bf16[48,256]{1,0:T(8,128)(2,1)S(1)}, bf16[48,256]{1,0:T(8,128)(2,1)S(1)}, u32[]{:S(2)}, u32[]{:S(2)}) %collective-permute-start.7) | collective-permute-done | bytes 24608 | tf_op jit(solution)/shard_map/ppermute | solution.py:42
  41.3 0.4 filter.1
  41.7 0.8 collective-permute-start.10
  42.5 4.7 %collective-permute-start.9 = (bf16[32,256]{1,0:T(8,128)(2,1)S(1)}, bf16[32,256]{1,0:T(8,128)(2,1)S(1)}, u32[]{:S(2)}, u32[]{:S(2)}) collective-permute-start(bf16[32,256]{1,0:T(8,128)(2,1)S(1)} %get-tuple-element.64), channel_id=1, source_target_pairs={{0,128},{64,192},{128,0},{192,64},{1,129},{65,193},{129,1},{193,65... | collective-permute-start | bytes 49160 | tf_op jit(solution)/shard_map/ppermute | solution.py:42
  47.2 0.3 collective-permute-start.8
  47.5 4.4 %collective-permute-done.8 = bf16[32,256]{1,0:T(8,128)(2,1)S(1)} collective-permute-done((bf16[32,256]{1,0:T(8,128)(2,1)S(1)}, bf16[32,256]{1,0:T(8,128)(2,1)S(1)}, u32[]{:S(2)}, u32[]{:S(2)}) %collective-permute-start.8) | collective-permute-done | bytes 16416 | tf_op jit(solution)/shard_map/ppermute | solution.py:42
  52.1 3.2 %collective-permute-start.13 = (bf16[128,256]{1,0:T(8,128)(2,1)S(1)}, bf16[128,256]{1,0:T(8,128)(2,1)S(1)}, u32[]{:S(2)}, u32[]{:S(2)}) collective-permute-start(bf16[128,256]{1,0:T(8,128)(2,1)S(1)} %get-tuple-element.91), channel_id=1, source_target_pairs={{0,16},{16,32},{32,48},{48,0},{1,17},{17,33},{33,49},{49,1},{2,18}... | collective-permute-start | bytes 196616 | tf_op jit(solution)/shard_map/ppermute | solution.py:42
  55.3 2.2 %collective-permute-done.11 = bf16[128,256]{1,0:T(8,128)(2,1)S(1)} collective-permute-done((bf16[128,256]{1,0:T(8,128)(2,1)S(1)}, bf16[128,256]{1,0:T(8,128)(2,1)S(1)}, u32[]{:S(2)}, u32[]{:S(2)}) %collective-permute-start.11) | collective-permute-done | bytes 65568 | tf_op jit(solution)/shard_map/ppermute | solution.py:42
  57.5 3.5 %collective-permute-done.12 = bf16[128,256]{1,0:T(8,128)(2,1)S(1)} collective-permute-done((bf16[128,256]{1,0:T(8,128)(2,1)S(1)}, bf16[128,256]{1,0:T(8,128)(2,1)S(1)}, u32[]{:S(2)}, u32[]{:S(2)}) %collective-permute-start.12) | collective-permute-done | bytes 65568 | tf_op jit(solution)/shard_map/ppermute | solution.py:42
  61.1 0.1 collective-permute-start.14
  61.2 1.5 %collective-permute-done.14.far = bf16[512,256]{1,0:T(8,128)(2,1)S(1)} collective-permute-done((bf16[512,256]{1,0:T(8,128)(2,1)S(1)}, bf16[512,256]{1,0:T(8,128)(2,1)S(1)}, u32[]{:S(2)}, u32[]{:S(2)}) %collective-permute-start.14) | collective-permute-done | bytes 262176 | tf_op jit(solution)/shard_map/ppermute | solution.py:42
  62.7 0.2 turned.1.f
  62.9 0.8 synthesis.3
  63.7 0.4 collective-permute-start.15
  64.1 2.0 %collective-permute-start.16 = (bf16[128,512]{1,0:T(8,128)(2,1)S(1)}, bf16[128,512]{1,0:T(8,128)(2,1)S(1)}, u32[]{:S(2)}, u32[]{:S(2)}) collective-permute-start(bf16[128,512]{1,0:T(8,128)(2,1)S(1)} %get-tuple-element.72), channel_id=1, source_target_pairs={{0,3},{1,4},{2,5},{3,6},{4,7},{5,0},{6,1},{7,2},{8,11},{9,12},{10,... | collective-permute-start | bytes 393224 | tf_op jit(solution)/shard_map/ppermute | solution.py:42
  66.1 1.0 %synthesis.4 = (bf16[128,512]{1,0:T(8,128)(2,1)S(1)}, bf16[128,512]{1,0:T(8,128)(2,1)S(1)}, bf16[128,512]{1,0:T(8,128)(2,1)S(1)}, bf16[256,4096]{1,0:T(8,128)(2,...) custom-call(bf16[128,2048]{1,0:T(8,128)(2,1)S(1)} %turned.1.f, ...), custom_call_target="tpu_custom_call", output_to_operand_aliasing={{3}: (1, {}), {4}: (2, {}), {5}: (3, {}), {6}: (4, {}), {7}... | custom-call | flops 805306368 | bytes 1048576 | tf_op jit(solution)/shard_map/synthesis/pallas_call | solution.py:307
  67.2 2.5 %collective-permute-start.17 = (bf16[128,512]{1,0:T(8,128)(2,1)S(1)}, bf16[128,512]{1,0:T(8,128)(2,1)S(1)}, u32[]{:S(2)}, u32[]{:S(2)}) collective-permute-start(bf16[128,512]{1,0:T(8,128)(2,1)S(1)} %get-tuple-element.79), channel_id=1, source_target_pairs={{0,5},{1,6},{2,7},{3,0},{4,1},{5,2},{6,3},{7,4},{8,13},{9,14},{10,... | collective-permute-start | bytes 393224 | tf_op jit(solution)/shard_map/ppermute | solution.py:42
  69.7 2.2 %collective-permute-start.18 = (bf16[128,512]{1,0:T(8,128)(2,1)S(1)}, bf16[128,512]{1,0:T(8,128)(2,1)S(1)}, u32[]{:S(2)}, u32[]{:S(2)}) collective-permute-start(bf16[128,512]{1,0:T(8,128)(2,1)S(1)} %get-tuple-element.80), channel_id=1, source_target_pairs={{0,2},{1,3},{2,4},{3,5},{4,6},{5,7},{6,0},{7,1},{8,10},{9,11},{10,... | collective-permute-start | bytes 393224 | tf_op jit(solution)/shard_map/ppermute | solution.py:42
  71.9 0.2 collective-permute-start.19
  72.1 1.0 %synthesis.5 = (bf16[128,512]{1,0:T(8,128)(2,1)S(1)}, bf16[128,512]{1,0:T(8,128)(2,1)S(1)}, bf16[128,512]{1,0:T(8,128)(2,1)S(1)}) custom-call(bf16[128,2048]{1,0:T(8,128)(2,1)S(1)} %turned.1.f, bf16[256,4096]{1,0:T(8,128)(2,1)S(1)} %get-tuple-element.82.n0, bf16[256,4096]{1,0:T(8,128)(2,1)S(1)} %get-tuple-element.83.n1, ...), custom_call_target="tpu_custom_call" | custom-call | flops 805306368 | bytes 1048576 | tf_op jit(solution)/shard_map/synthesis/pallas_call | solution.py:307
  73.1 0.6 collective-permute-done.15.rest_0_
  73.8 3.8 %collective-permute-start.20 = (bf16[128,512]{1,0:T(8,128)(2,1)S(1)}, bf16[128,512]{1,0:T(8,128)(2,1)S(1)}, u32[]{:S(2)}, u32[]{:S(2)}) collective-permute-start(bf16[128,512]{1,0:T(8,128)(2,1)S(1)} %get-tuple-element.88), channel_id=1, source_target_pairs={{0,1},{1,2},{2,3},{3,4},{4,5},{5,6},{6,7},{7,0},{8,9},{9,10},{10,1... | collective-permute-start | bytes 393224 | tf_op jit(solution)/shard_map/ppermute | solution.py:42
  77.7 0.7 collective-permute-done.19.rest_4_
  78.4 2.3 %collective-permute-done.20.rest_5_ = bf16[128,512]{1,0:T(8,128)(2,1)S(1)} collective-permute-done((bf16[128,512]{1,0:T(8,128)(2,1)S(1)}, bf16[128,512]{1,0:T(8,128)(2,1)S(1)}, u32[]{:S(2)}, u32[]{:S(2)}) %collective-permute-start.20) | collective-permute-done | bytes 131104 | tf_op jit(solution)/shard_map/ppermute | solution.py:42
  80.7 4.0 %collective-permute-done.21.rest_6_ = bf16[128,512]{1,0:T(8,128)(2,1)S(1)} collective-permute-done((bf16[128,512]{1,0:T(8,128)(2,1)S(1)}, bf16[128,512]{1,0:T(8,128)(2,1)S(1)}, u32[]{:S(2)}, u32[]{:S(2)}) %collective-permute-start.21) | collective-permute-done | bytes 131104 | tf_op jit(solution)/shard_map/ppermute | solution.py:42
  84.7 0.9 %finish.1 = bf16[512,128]{1,0:T(8,128)(2,1)} custom-call(f32[8,128]{1,0:T(8,128)S(1)} %get-tuple-element.63.total, f32[512,128]{1,0:T(8,128)S(1)} %get-tuple-element.52.after.linear, bf16[128,512]{1,0:T(8,128)(2,1)S(1)} %collective-permute-done.15.rest_0_, bf16[128,512]{1,0:T(8,128)(2,1)S(1)} %collective-permute-done.16.rest_1_, ...), custom_call_target="tpu_custom_call" | custom-call | bytes 1048576 | tf_op jit(solution)/shard_map/finish/pallas_call | solution.py:314
  (26 shorter events, 0.2 us)
Async XLA Ops:
  2.0 8.5 %copy-start.1 = (s32[1024]{0:T(1024)S(1)}, s32[1024]{0:T(1024)}, u32[]{:S(2)}) copy-start(s32[1024]{0:T(1024)} %reshape.22.index) | copy-start | bytes 12292
  10.3 2.3 %collective-permute-start = (bf16[272,384]{1,0:T(8,128)(2,1)S(1)}, bf16[272,384]{1,0:T(8,128)(2,1)S(1)}, u32[]{:S(2)}, u32[]{:S(2)}) collective-permute-start(bf16[272,384]{1,0:T(8,128)(2,1)S(1)} %get-tuple-element.54), channel_id=1, source_target_pairs={{0,8},{8,0},{1,9},{9,1},{2,10},{10,2},{3,11},{11,3},{4,12},{12,4},... | collective-permute-start | bytes 626696 | tf_op jit(solution)/shard_map/ppermute | solution.py:42
  12.7 20.4 %collective-permute-start.3 = (bf16[272,128]{1,0:T(8,128)(2,1)S(1)}, bf16[272,128]{1,0:T(8,128)(2,1)S(1)}, u32[]{:S(2)}, u32[]{:S(2)}) collective-permute-start(bf16[272,128]{1,0:T(8,128)(2,1)S(1)} %pair.3.after), channel_id=1, source_target_pairs={{0,128},{64,192},{128,0},{192,64},{1,129},{65,193},{129,1},{193,65... | collective-permute-start | bytes 208904 | tf_op jit(solution)/shard_map/ppermute | solution.py:42
  22.2 10.9 %collective-permute-start.2 = (bf16[272,128]{1,0:T(8,128)(2,1)S(1)}, bf16[272,128]{1,0:T(8,128)(2,1)S(1)}, u32[]{:S(2)}, u32[]{:S(2)}) collective-permute-start(bf16[272,128]{1,0:T(8,128)(2,1)S(1)} %pair.4.after), channel_id=1, source_target_pairs={{0,64},{64,128},{128,192},{192,0},{1,65},{65,129},{129,193},{193,1... | collective-permute-start | bytes 208904 | tf_op jit(solution)/shard_map/ppermute | solution.py:42
  26.0 7.2 %collective-permute-start.4 = (bf16[272,128]{1,0:T(8,128)(2,1)S(1)}, bf16[272,128]{1,0:T(8,128)(2,1)S(1)}, u32[]{:S(2)}, u32[]{:S(2)}) collective-permute-start(bf16[272,128]{1,0:T(8,128)(2,1)S(1)} %pair.5.after), channel_id=1, source_target_pairs={{0,192},{64,0},{128,64},{192,128},{1,193},{65,1},{129,65},{193,129... | collective-permute-start | bytes 208904 | tf_op jit(solution)/shard_map/ppermute | solution.py:42
  30.8 10.5 %copy-start = (bf16[32,2,128,128]{3,2,1,0:T(8,128)(2,1)S(1)}, bf16[32,2,128,128]{3,2,1,0:T(8,128)(2,1)}, u32[]{:S(2)}) copy-start(bf16[32,2,128,128]{3,2,1,0:T(8,128)(2,1)} %weight.1) | copy-start | bytes 6291460
  30.8 2.3 %collective-permute-start.1 = (bf16[272,128]{1,0:T(8,128)(2,1)S(1)}, bf16[272,128]{1,0:T(8,128)(2,1)S(1)}, u32[]{:S(2)}, u32[]{:S(2)}) collective-permute-start(bf16[272,128]{1,0:T(8,128)(2,1)S(1)} %get-tuple-element.57.after), channel_id=1, source_target_pairs={{0,8},{8,0},{1,9},{9,1},{2,10},{10,2},{3,11},{11,3},{4,12},{12,4},... | collective-permute-start | bytes 208904 | tf_op jit(solution)/shard_map/ppermute | solution.py:42
  33.3 4.1 %collective-permute-start.5 = (bf16[48,256]{1,0:T(8,128)(2,1)S(1)}, bf16[48,256]{1,0:T(8,128)(2,1)S(1)}, u32[]{:S(2)}, u32[]{:S(2)}) collective-permute-start(bf16[48,256]{1,0:T(8,128)(2,1)S(1)} %get-tuple-element.60), channel_id=1, source_target_pairs={{0,16},{16,32},{32,48},{48,0},{1,17},{17,33},{33,49},{49,1},{2,18}... | collective-permute-start | bytes 73736 | tf_op jit(solution)/shard_map/ppermute | solution.py:42
  33.8 5.3 %collective-permute-start.6 = (bf16[48,256]{1,0:T(8,128)(2,1)S(1)}, bf16[48,256]{1,0:T(8,128)(2,1)S(1)}, u32[]{:S(2)}, u32[]{:S(2)}) collective-permute-start(bf16[48,256]{1,0:T(8,128)(2,1)S(1)} %get-tuple-element.61), channel_id=1, source_target_pairs={{0,32},{16,48},{32,0},{48,16},{1,33},{17,49},{33,1},{49,17},{2,34}... | collective-permute-start | bytes 73736 | tf_op jit(solution)/shard_map/ppermute | solution.py:42
  36.3 5.0 %collective-permute-start.7 = (bf16[48,256]{1,0:T(8,128)(2,1)S(1)}, bf16[48,256]{1,0:T(8,128)(2,1)S(1)}, u32[]{:S(2)}, u32[]{:S(2)}) collective-permute-start(bf16[48,256]{1,0:T(8,128)(2,1)S(1)} %get-tuple-element.62), channel_id=1, source_target_pairs={{0,48},{16,0},{32,16},{48,32},{1,49},{17,1},{33,17},{49,33},{2,50}... | collective-permute-start | bytes 73736 | tf_op jit(solution)/shard_map/ppermute | solution.py:42
  41.7 10.3 %collective-permute-start.10 = (bf16[32,256]{1,0:T(8,128)(2,1)S(1)}, bf16[32,256]{1,0:T(8,128)(2,1)S(1)}, u32[]{:S(2)}, u32[]{:S(2)}) collective-permute-start(bf16[32,256]{1,0:T(8,128)(2,1)S(1)} %get-tuple-element.64), channel_id=1, source_target_pairs={{0,64},{64,128},{128,192},{192,0},{1,65},{65,129},{129,193},{193,1... | collective-permute-start | bytes 49160 | tf_op jit(solution)/shard_map/ppermute | solution.py:42
  42.5 9.5 %collective-permute-start.9 = (bf16[32,256]{1,0:T(8,128)(2,1)S(1)}, bf16[32,256]{1,0:T(8,128)(2,1)S(1)}, u32[]{:S(2)}, u32[]{:S(2)}) collective-permute-start(bf16[32,256]{1,0:T(8,128)(2,1)S(1)} %get-tuple-element.64), channel_id=1, source_target_pairs={{0,128},{64,192},{128,0},{192,64},{1,129},{65,193},{129,1},{193,65... | collective-permute-start | bytes 49160 | tf_op jit(solution)/shard_map/ppermute | solution.py:42
  47.2 4.7 %collective-permute-start.8 = (bf16[32,256]{1,0:T(8,128)(2,1)S(1)}, bf16[32,256]{1,0:T(8,128)(2,1)S(1)}, u32[]{:S(2)}, u32[]{:S(2)}) collective-permute-start(bf16[32,256]{1,0:T(8,128)(2,1)S(1)} %get-tuple-element.64), channel_id=1, source_target_pairs={{0,192},{64,0},{128,64},{192,128},{1,193},{65,1},{129,65},{193,129... | collective-permute-start | bytes 49160 | tf_op jit(solution)/shard_map/ppermute | solution.py:42
  52.0 5.6 %collective-permute-start.11 = (bf16[128,256]{1,0:T(8,128)(2,1)S(1)}, bf16[128,256]{1,0:T(8,128)(2,1)S(1)}, u32[]{:S(2)}, u32[]{:S(2)}) collective-permute-start(bf16[128,256]{1,0:T(8,128)(2,1)S(1)} %get-tuple-element.91), channel_id=1, source_target_pairs={{0,48},{16,0},{32,16},{48,32},{1,49},{17,1},{33,17},{49,33},{2,50}... | collective-permute-start | bytes 196616 | tf_op jit(solution)/shard_map/ppermute | solution.py:42
  52.1 9.0 %collective-permute-start.13 = (bf16[128,256]{1,0:T(8,128)(2,1)S(1)}, bf16[128,256]{1,0:T(8,128)(2,1)S(1)}, u32[]{:S(2)}, u32[]{:S(2)}) collective-permute-start(bf16[128,256]{1,0:T(8,128)(2,1)S(1)} %get-tuple-element.91), channel_id=1, source_target_pairs={{0,16},{16,32},{32,48},{48,0},{1,17},{17,33},{33,49},{49,1},{2,18}... | collective-permute-start | bytes 196616 | tf_op jit(solution)/shard_map/ppermute | solution.py:42
  55.3 5.8 %collective-permute-start.12 = (bf16[128,256]{1,0:T(8,128)(2,1)S(1)}, bf16[128,256]{1,0:T(8,128)(2,1)S(1)}, u32[]{:S(2)}, u32[]{:S(2)}) collective-permute-start(bf16[128,256]{1,0:T(8,128)(2,1)S(1)} %get-tuple-element.91), channel_id=1, source_target_pairs={{0,32},{16,48},{32,0},{48,16},{1,33},{17,49},{33,1},{49,17},{2,34}... | collective-permute-start | bytes 196616 | tf_op jit(solution)/shard_map/ppermute | solution.py:42
  61.1 1.6 %collective-permute-start.14 = (bf16[512,256]{1,0:T(8,128)(2,1)S(1)}, bf16[512,256]{1,0:T(8,128)(2,1)S(1)}, u32[]{:S(2)}, u32[]{:S(2)}) collective-permute-start(bf16[512,256]{1,0:T(8,128)(2,1)S(1)} %constant_dynamic-update-slice_fusion.4.own), channel_id=1, source_target_pairs={{0,8},{8,0},{1,9},{9,1},{2,10},{10,2},{3,11},{11,3},{4,12},{12,4},... | collective-permute-start | bytes 786440 | tf_op jit(solution)/shard_map/ppermute | solution.py:42
  63.7 10.1 %collective-permute-start.15 = (bf16[128,512]{1,0:T(8,128)(2,1)S(1)}, bf16[128,512]{1,0:T(8,128)(2,1)S(1)}, u32[]{:S(2)}, u32[]{:S(2)}) collective-permute-start(bf16[128,512]{1,0:T(8,128)(2,1)S(1)} %get-tuple-element.71), channel_id=1, source_target_pairs={{0,4},{1,5},{2,6},{3,7},{4,0},{5,1},{6,2},{7,3},{8,12},{9,13},{10,... | collective-permute-start | bytes 393224 | tf_op jit(solution)/shard_map/ppermute | solution.py:42
  64.1 13.5 %collective-permute-start.16 = (bf16[128,512]{1,0:T(8,128)(2,1)S(1)}, bf16[128,512]{1,0:T(8,128)(2,1)S(1)}, u32[]{:S(2)}, u32[]{:S(2)}) collective-permute-start(bf16[128,512]{1,0:T(8,128)(2,1)S(1)} %get-tuple-element.72), channel_id=1, source_target_pairs={{0,3},{1,4},{2,5},{3,6},{4,7},{5,0},{6,1},{7,2},{8,11},{9,12},{10,... | collective-permute-start | bytes 393224 | tf_op jit(solution)/shard_map/ppermute | solution.py:42
  67.2 10.5 %collective-permute-start.17 = (bf16[128,512]{1,0:T(8,128)(2,1)S(1)}, bf16[128,512]{1,0:T(8,128)(2,1)S(1)}, u32[]{:S(2)}, u32[]{:S(2)}) collective-permute-start(bf16[128,512]{1,0:T(8,128)(2,1)S(1)} %get-tuple-element.79), channel_id=1, source_target_pairs={{0,5},{1,6},{2,7},{3,0},{4,1},{5,2},{6,3},{7,4},{8,13},{9,14},{10,... | collective-permute-start | bytes 393224 | tf_op jit(solution)/shard_map/ppermute | solution.py:42
  69.7 8.0 %collective-permute-start.18 = (bf16[128,512]{1,0:T(8,128)(2,1)S(1)}, bf16[128,512]{1,0:T(8,128)(2,1)S(1)}, u32[]{:S(2)}, u32[]{:S(2)}) collective-permute-start(bf16[128,512]{1,0:T(8,128)(2,1)S(1)} %get-tuple-element.80), channel_id=1, source_target_pairs={{0,2},{1,3},{2,4},{3,5},{4,6},{5,7},{6,0},{7,1},{8,10},{9,11},{10,... | collective-permute-start | bytes 393224 | tf_op jit(solution)/shard_map/ppermute | solution.py:42
  71.9 6.5 %collective-permute-start.19 = (bf16[128,512]{1,0:T(8,128)(2,1)S(1)}, bf16[128,512]{1,0:T(8,128)(2,1)S(1)}, u32[]{:S(2)}, u32[]{:S(2)}) collective-permute-start(bf16[128,512]{1,0:T(8,128)(2,1)S(1)} %get-tuple-element.81), channel_id=1, source_target_pairs={{0,6},{1,7},{2,0},{3,1},{4,2},{5,3},{6,4},{7,5},{8,14},{9,15},{10,... | collective-permute-start | bytes 393224 | tf_op jit(solution)/shard_map/ppermute | solution.py:42
  73.8 6.9 %collective-permute-start.20 = (bf16[128,512]{1,0:T(8,128)(2,1)S(1)}, bf16[128,512]{1,0:T(8,128)(2,1)S(1)}, u32[]{:S(2)}, u32[]{:S(2)}) collective-permute-start(bf16[128,512]{1,0:T(8,128)(2,1)S(1)} %get-tuple-element.88), channel_id=1, source_target_pairs={{0,1},{1,2},{2,3},{3,4},{4,5},{5,6},{6,7},{7,0},{8,9},{9,10},{10,1... | collective-permute-start | bytes 393224 | tf_op jit(solution)/shard_map/ppermute | solution.py:42
  77.6 7.1 %collective-permute-start.21 = (bf16[128,512]{1,0:T(8,128)(2,1)S(1)}, bf16[128,512]{1,0:T(8,128)(2,1)S(1)}, u32[]{:S(2)}, u32[]{:S(2)}) collective-permute-start(bf16[128,512]{1,0:T(8,128)(2,1)S(1)} %get-tuple-element.89), channel_id=1, source_target_pairs={{0,7},{1,0},{2,1},{3,2},{4,3},{5,4},{6,5},{7,6},{8,15},{9,8},{10,9... | collective-permute-start | bytes 393224 | tf_op jit(solution)/shard_map/ppermute | solution.py:42

commit v4 on v3

v4 whole, which is shorter than its diff:
```python
import functools
import math

import jax
import jax.numpy as jnp
from jax import lax
from jax.experimental import pallas as pl
from jax.experimental.pallas import tpu as pltpu
from jax.sharding import Mesh, PartitionSpec as P

SIZES = {"z_hi": 4, "x": 4, "core": 2, "y": 4, "z_lo": 2}
PTS = ("z_hi", "x", "core")
GRP = ("y", "z_lo")
ALL = PTS + GRP
C = 128
PITCH = C + 1
ROWS = 32
BF, F32 = jnp.bfloat16, jnp.float32
VM = pl.BlockSpec(memory_space=pltpu.VMEM)
SM = pl.BlockSpec(memory_space=pltpu.SMEM)


def call(body, n_in, out_shape, name, scratch=(), smem=0, flops=0, aliases={}, last=(), room=16):
    many = isinstance(out_shape, (list, tuple))
    return pl.pallas_call(
        body,
        in_specs=[SM] * smem + [VM] * n_in + [pl.BlockSpec(memory_space=m) for m in last],
        out_specs=[VM] * len(out_shape) if many else VM,
        out_shape=out_shape,
        scratch_shapes=list(scratch),
        compiler_params=pltpu.CompilerParams(vmem_limit_bytes=room * 2**20),
        input_output_aliases=aliases,
        cost_estimate=pl.CostEstimate(flops=flops, bytes_accessed=2**20, transcendentals=0),
        name=name,
    )


def send(value, axes, shift):
    n = 1
    for a in axes:
        n *= SIZES[a]
    return lax.ppermute(value, axes, [(j, (j + shift) % n) for j in range(n)])


def turn(x):
    h = math.pi * (x - jnp.round(x))
    q = h * h
    s = c = None
    for k in range(6, -1, -1):
        a = (-1) ** k / math.factorial(2 * k + 1)
        s = a if s is None else s * q + a
    for k in range(7, -1, -1):
        a = (-1) ** k / math.factorial(2 * k)
        c = a if c is None else c * q + a
    s = s * h
    return 1.0 - 2.0 * s * s, -2.0 * s * c


def times(a, b):
    return a[0] * b[0] - a[1] * b[1], a[0] * b[1] + a[1] * b[0]


def powers(x, n):
    one = turn(x)
    out = [(jnp.ones_like(x), jnp.zeros_like(x)), one]
    for k in range(2, n):
        out.append(times(out[k // 2], out[k - k // 2]))
    return out


def build_tables(coords, exy, ez, sl):
    for k, v in enumerate(powers(coords[2], 32)):
        ez[k, 0, sl], ez[k, 1, sl] = v
    px, py = powers(coords[0], 9), powers(coords[1], 9)
    signed = lambda p, k: p[k] if k >= 0 else (p[-k][0], -p[-k][1])
    for kx in range(-8, 8):
        for ky in range(-8, 8):
            k = (kx + 8) * 16 + ky + 8
            exy[k, 0, sl], exy[k, 1, sl] = times(signed(px, kx), signed(py, ky))


def lanes3(value):
    hi = value.astype(BF).astype(F32)
    mid = (value - hi).astype(BF).astype(F32)
    low = value - hi - mid
    lane = lax.broadcasted_iota(jnp.int32, (16, C), 1)
    return jnp.where(lane == 0, hi, jnp.where(lane == 1, mid, jnp.where(lane == 2, low, 0.0))).astype(BF)


def total_of(rows):
    lane = lax.broadcasted_iota(jnp.int32, (1, C), 1)
    return jnp.sum(jnp.where(lane < 3, rows[:1], 0.0), axis=1, keepdims=True)


def analyse(index, row, put_coef, put_basis, exy, ez, w, scr):
    @pl.loop(0, C // 16)
    def _(it):
        for u in range(16):
            m = it * 16 + u
            k = index[row, m]
            ixy, iz = lax.shift_right_logical(k, 5), lax.bitwise_and(k, 31)
            for j in range(ROWS // 8):
                sl = pl.ds(8 * j, 8)
                re, im = times((exy[ixy, 0, sl], exy[ixy, 1, sl]), (ez[iz, 0, sl], ez[iz, 1, sl]))
                scr[pl.ds(8 * j * PITCH + m, 8, stride=PITCH), :] = re
                scr[pl.ds((ROWS + 8 * j) * PITCH + m, 8, stride=PITCH), :] = im

    acc = None
    for k in range(4):
        cols = pl.ds(k * 1024, 1024)
        both = []
        for part in range(2):
            rows = [scr[pl.ds((part * ROWS + k * 8 + h) * PITCH, C), :].astype(BF) for h in range(8)]
            both.append(jnp.concatenate(rows, axis=1))
        both = jnp.concatenate(both, axis=0)
        put_basis(cols, both)
        term = jnp.dot(both, w[cols, :], preferred_element_type=F32)
        acc = term if acc is None else acc + term
    put_coef(acc.astype(BF))


def slabs(count, first, index, coef, basis, exy, ez, w, quad, scr):
    @pl.loop(0, count)
    def _(s):
        def put_coef(value):
            coef[pl.ds(pl.multiple_of(s * 2 * C, 2 * C), 2 * C), :] = value

        def put_basis(cols, value):
            basis[s, :, cols] = value

        analyse(index, first + s, put_coef, put_basis, exy, ez, w, scr)

    total = jnp.sum(jnp.sum(quad[...], axis=0, keepdims=True), axis=1, keepdims=True)
    coef[pl.ds(count * 2 * C, 16), :] = lanes3(total)


def pack_index(table, index):
    z, x, core = (lax.axis_index(a) for a in PTS)
    group = lax.axis_index("y") * 2 + lax.axis_index("z_lo")
    tile, within = group // 4, lax.rem(group, 4)
    part = lax.broadcasted_iota(jnp.int32, (1, C), 1) // 32
    for flip in range(2):
        for dz in range(4):
            row = jnp.zeros((1, C), jnp.int32)
            for dx in range(4):
                own = (lax.rem(z + dz, 4) * 4 + lax.rem(x + dx, 4)) * 2 + lax.rem(core + flip, 2)
                v = table[:, pl.ds(pl.multiple_of(own * 256 + tile * C, C), C)]
                k = ((v[0:1] + 8) * 16 + v[1:2] + 8) * 32 + v[2:3]
                k = pltpu.roll(k, lax.rem(dx - within + 4, 4) * 32, 1)
                row = jnp.where(part == dx, k, row)
            index[pl.ds(flip * 4 + dz, 1), :] = row


def first_body(*refs):
    given, (coef, basis, exy, ez, w, linear, quad, index) = refs[:6], refs[6:14]
    scr, coords, table, lin, bias, f, held, sems = refs[14:]
    here = (coords, table, quad, lin, bias, f)
    loads = [pltpu.make_async_copy(src, dst, sems.at[i]) for i, (src, dst) in enumerate(zip(given, here))]
    for load in loads:
        load.start()
    loads[0].wait()

    @pl.loop(0, ROWS // 8)
    def _(o):
        row = lambda i, r: coords[pl.ds(i, 1), pl.ds(pl.multiple_of((8 * o + r) * C, C), C)]
        at = [jnp.concatenate([row(i, r) for r in range(8)], axis=0) for i in range(3)]
        build_tables(at, exy, ez, pl.ds(pl.multiple_of(8 * o, 8), 8))

    loads[1].wait()
    pack_index(table, index)
    hold = pltpu.make_async_copy(index, held, sems.at[6])
    hold.start()
    for load in loads[2:]:
        load.wait()
    columns = quad[...].T
    for o in range(ROWS):
        rows = pl.ds(o * C, C)
        w[rows, :] = (f[rows, :].astype(F32) * columns[:, o : o + 1]).astype(BF)
    group = lax.axis_index("y") * 2 + lax.axis_index("z_lo")
    mine = f[pl.ds(pl.multiple_of(group * 512, 512), 512), :]
    linear[...] = jnp.dot(mine, lin[...], preferred_element_type=F32) + bias[...]
    hold.wait()
    slabs(4, 4, held, coef, basis, exy, ez, w, quad, scr)


def near_body(count, first, index, quad, exy, ez, w, after, coef, basis, scr):
    slabs(count, first, index, coef, basis, exy, ez, w, quad, scr)


def pair_body(own, got, *outs):
    tail = total_of(own[pl.ds(6 * C, 16), :].astype(F32) + got[pl.ds(8 * C, 16), :].astype(F32))
    for s, out in enumerate(outs):
        summed = own[pl.ds(s * 2 * C, 2 * C), :].astype(F32) + got[pl.ds((s + 1) * 2 * C, 2 * C), :].astype(F32)
        out[pl.ds(0, 2 * C), :] = summed.astype(BF)
        out[pl.ds(2 * C, 16), :] = lanes3(tail)


def z_body(own, got0, got1, got2, got3, keep, out1, out2, out3):
    body, rest = pl.ds(0, 2 * C), pl.ds(2 * C, 16)
    summed = own[body, :].astype(F32) + got0[body, :].astype(F32)
    tail = own[rest, :].astype(F32) + got0[pl.ds(8 * C, 16), :].astype(F32)
    for g in (got1, got2, got3):
        summed = summed + g[body, :].astype(F32)
        tail = tail + g[rest, :].astype(F32)
    tail = lanes3(total_of(tail))
    for part in range(2):
        cols = pl.ds(part * C, C)
        for s, ref in enumerate((keep, out1, out2, out3)):
            at = part * C + s * 32
            ref[pl.ds(0, 32), cols] = summed[at : at + 32].astype(ref.dtype)
            ref[pl.ds(32, 16), cols] = tail.astype(ref.dtype)


def filter_body(own, got1, got2, got3, weight, out, total):
    summed = own[...]
    for g in (got1, got2, got3):
        summed = summed + g[...].astype(F32)
    total[...] = jnp.broadcast_to(total_of(summed[32:, :C]), total.shape)
    row = lax.rem(lax.broadcasted_iota(jnp.int32, (16, 2 * C), 0), 8)
    for g in range(4):
        block = summed[8 * g : 8 * g + 8]
        lhs = jnp.concatenate([block[:, :C], block[:, C:]], axis=0).astype(BF)
        picked = jnp.zeros((16, 2 * C), F32)
        for i in range(8):
            m = 8 * g + i
            both = jnp.concatenate([weight[m, 0], weight[m, 1]], axis=1)
            picked = jnp.where(row == i, jnp.dot(lhs, both, preferred_element_type=F32), picked)
        real = picked[:8, :C] - picked[8:, C:]
        imag = picked[:8, C:] + picked[8:, :C]
        out[pl.ds(8 * g, 8), :] = jnp.concatenate([real, imag], axis=1).astype(BF)


def turned_body(src, out):
    for dz in range(4):
        for part in range(2):
            cols = pl.ds(part * C, C)
            block = jnp.concatenate([src[pl.ds(dx * C + dz * 32, 32), cols].astype(F32) for dx in range(4)], axis=0)
            out[:, pl.ds((dz * 2 + part) * C, C)] = block.T.astype(BF)


def near_field_body(src, n0, n123, part, f):
    turned_body(src, f)

    @pl.loop(0, 8)
    def _(k):
        at = pl.ds(pl.multiple_of(k * 512, 512), 512)
        acc = None
        for i, b in enumerate((n0.at[0], n123.at[0], n123.at[1], n123.at[2])):
            term = jnp.dot(f[:, pl.ds(i * 2 * C, 2 * C)], b[:, at], preferred_element_type=F32)
            acc = term if acc is None else acc + term
        part[:, at] = acc


def synthesis_body(shifts, f, basis, part, *outs):
    group = lax.axis_index("y") * 2 + lax.axis_index("z_lo")
    for s, out in zip(shifts, outs[: len(shifts)], strict=True):
        at = pl.ds(pl.multiple_of(lax.rem(group + s, 8) * 512, 512), 512)
        acc = part[:, at]
        for i in range(4):
            acc = acc + jnp.dot(f[:, pl.ds(i * 2 * C, 2 * C)], basis[i, :, at], preferred_element_type=F32)
        out[...] = acc.astype(BF)


def finish_body(total, linear, *rest):
    *blocks, out = rest
    summed = blocks[0][...].astype(F32)
    for b in blocks[1:]:
        summed = summed + b[...].astype(F32)
    scaled = summed / total[0:1, 0:1]
    for k in range(4):
        rows = pl.ds(k * C, C)
        pre = scaled[:, k * C : k * C + C].T + linear[rows, :]
        out[rows, :] = (0.5 * pre * (1.0 + lax.erf(pre * math.sqrt(0.5)))).astype(BF)


def gather_over(piece, axes, n):
    return jnp.concatenate([piece] + [send(piece, axes, n - s) for s in range(1, n)])


def on_device(features, coords, quad_weight, mode_table, mode_weight, lin_weight, bias):
    pts = features.shape[0]
    scr = pltpu.VMEM((2 * ROWS * PITCH, C), F32)
    one = lambda rows, cols, dt: jax.ShapeDtypeStruct((rows, cols), dt)
    slab = 2 * 2 * C * pts * C
    far, far_basis, exy, ez, w, linear, quad, index = call(
        first_body, 0,
        [pltpu.VMEM((8 * C + 16, C), BF), pltpu.VMEM((4, 2 * C, pts), BF), pltpu.VMEM((256, 2, ROWS, C), F32),
         pltpu.VMEM((32, 2, ROWS, C), F32), pltpu.VMEM((pts, C), BF), pltpu.VMEM((pts // 8, C), F32),
         pltpu.VMEM((ROWS, C), F32), pltpu.VMEM((8, C), jnp.int32)],
        "first",
        [scr, pltpu.VMEM((3, pts), F32), pltpu.VMEM((3, 8192), jnp.int32), pltpu.VMEM((C, C), BF), pltpu.VMEM((1, C), F32),
         pltpu.VMEM((pts, C), BF), pltpu.SMEM((8, C), jnp.int32), pltpu.SemaphoreType.DMA((7,))],
        0, 8 * slab, last=[pltpu.HBM] * 6, room=42,
    )(coords, mode_table, quad_weight.reshape(ROWS, C), lin_weight, bias.reshape(1, C), features)
    got = send(far, ("core",), 1)

    def near(count, first, after):
        return call(
            functools.partial(near_body, count, first), 4,
            [pltpu.VMEM((count * 2 * C + 16, C), BF), pltpu.VMEM((count, 2 * C, pts), BF)],
            "near", [scr], 1, 2 * count * slab, last=[pl.ANY],
        )(index, quad, exy, ez, w, after)

    mine, n123 = near(3, 1, linear)
    outs = call(pair_body, 2, [one(2 * C + 16, C, BF)] * 3, "pair")(mine, got)
    across = {s: send(outs[s - 1], ("z_hi",), s) for s in (2, 1, 3)}
    mine, n0 = near(1, 0, outs[0])
    keep, *outs = call(z_body, 5, [one(48, 2 * C, F32)] + [one(48, 2 * C, BF)] * 3, "z_sum")(
        mine, got, across[1], across[2], across[3]
    )
    got = [send(o, ("x",), s) for s, o in zip((1, 2, 3), outs)]
    piece, total = call(filter_body, 5, [one(32, 2 * C, BF), one(8, C, F32)], "filter")(keep, *got, mode_weight)
    piece = gather_over(piece, ("z_hi",), 4)
    piece = gather_over(piece, ("x",), 4)
    other = send(piece, ("core",), 1)
    part = call(
        near_field_body, 3, pltpu.VMEM((C, pts), F32), "near_field", [pltpu.VMEM((C, 8 * C), BF)], flops=4 * slab
    )(piece, n0, n123)
    f = call(turned_body, 1, one(C, 8 * C, BF), "turned")(other)
    fields = []
    for shifts in ((4, 3), (5, 2, 6), (1, 7, 0)):
        count = len(shifts)
        chain = [pltpu.VMEM(v.shape, v.dtype) for v in (far_basis, part)] if 0 not in shifts else []
        outs = call(
            functools.partial(synthesis_body, shifts), 3, [one(C, 512, BF)] * count + chain, "synthesis",
            flops=count * slab // 2, aliases={1: count, 2: count + 1} if chain else {},
        )(f, far_basis, part)
        if chain:
            far_basis, part = outs[count:]
        fields += [send(o, GRP, s) if s else o for s, o in zip(shifts, outs)]
    return call(finish_body, 10, one(pts // 8, C, BF), "finish")(total, linear, *fields)


def solution(mesh):
    fine = Mesh(mesh.devices.reshape([SIZES[a] for a in ALL]), ALL)
    return jax.shard_map(
        on_device,
        mesh=fine,
        in_specs=(
            P(PTS, None),
            P(None, PTS),
            P(PTS),
            P(),
            P(ALL, None, None, None),
            P(),
            P(),
        ),
        out_specs=P(ALL, None),
        check_vma=False,
    )
```

time: 85.7 us -> 83 us (0.968)
  the two profiles are of different devices: /device:TPU:22 before, /device:TPU:1 now
where the time goes in v4:
time: 83 us; the launch traced here: 82.9 us
  starting transfers between devices  42.6 us (51%)
  Pallas kernels  21.3 us (26%)
  waiting for transfers between devices  18.9 us (23%)
    ppermute x21, starting transfers between devices, send(): return lax.ppermute(value, axes, [(j, (j + shift) % n) for j in range(n)])  42.6 us
    ppermute x21, waiting for transfers between devices, send(): return lax.ppermute(value, axes, [(j, (j + shift) % n) for j in range(n)])  18.9 us
    pallas_call x1, Pallas kernels, on_device(): call(first_body, 0, [pltpu.VMEM((8 * C + 16, C), BF), pltpu.VMEM((4, 2 *...  8.85 us
    pallas_call x2, Pallas kernels, near(): call(functools.partial(near_body, count, first), 4, [pltpu.VMEM((count *...  6.43 us
    pallas_call x1, Pallas kernels, on_device(): call(near_field_body, 3, pltpu.VMEM((C, pts), F32), 'near_field', [pltpu....  2.68 us
    pallas_call x3, Pallas kernels, on_device(): call(functools.partial(synthesis_body, shifts), 3, [one(C, 512, BF)] * co...  1.75 us
  transfers between devices with their start and end apart: 21, of which 9 were waited for; matrix products, arithmetic and copies ran while one was open for 0% of the time, Pallas kernels for 13%

profile of v4, /device:TPU:1, one launch (start us, length us, event | category | flops | bytes accessed | tf_op | source)
XLA Modules:
  0.0 82.9 jit_solution(15526806935687532054)
XLA Ops:
  0.0 8.9 %first.1 = (bf16[1040,128]{1,0:T(8,128)(2,1)S(1)}, bf16[4,256,4096]{2,1,0:T(8,128)(2,1)S(1)}, f32[256,2,32,128]{3,2,1,0:T(8,128)S(1)}, f32[32,2,32,128]{3,2,1,0:...) custom-call(f32[3,4096]{1,0:T(4,128)} %refs_0_.1, ...), custom_call_target="tpu_custom_call" | custom-call | flops 2147483648 | bytes 1048576 | tf_op jit(solution)/shard_map/first/pallas_call | solution.py:285
  8.9 3.3 %collective-permute-start = (bf16[1040,128]{1,0:T(8,128)(2,1)S(1)}, bf16[1040,128]{1,0:T(8,128)(2,1)S(1)}, u32[]{:S(2)}, u32[]{:S(2)}) collective-permute-start(bf16[1040,128]{1,0:T(8,128)(2,1)S(1)} %get-tuple-element.45), channel_id=1, source_target_pairs={{0,8},{8,0},{1,9},{9,1},{2,10},{10,2},{3,11},{11,3},{4,12},{12,4},... | collective-permute-start | bytes 798728 | tf_op jit(solution)/shard_map/ppermute | solution.py:42
  12.2 4.6 %near.2 = (bf16[784,128]{1,0:T(8,128)(2,1)S(1)}, bf16[3,256,4096]{2,1,0:T(8,128)(2,1)S(1)}) custom-call(s32[8,128]{1,0:T(8,128)S(1)} %get-tuple-element.38.index, f32[32,128]{1,0:T(8,128)S(1)} %get-tuple-element.39.quad, f32[256,2,32,128]{3,2,1,0:T(8,128)S(1)} %get-tuple-element.40.exy, f32[32,2,32,128]{3,2,1,0:T(8,128)S(1)} %get-tuple-element.41.ez, ...), custom_call_target="tpu_custom_call" | custom-call | flops 1610612736 | bytes 1048576 | tf_op jit(solution)/shard_map/near/pallas_call | solution.py:298
  16.8 0.0 collective-permute-done.got.got0
  16.8 0.1 pair.1
  16.9 5.2 %collective-permute-start.2 = (bf16[272,128]{1,0:T(8,128)(2,1)S(1)}, bf16[272,128]{1,0:T(8,128)(2,1)S(1)}, u32[]{:S(2)}, u32[]{:S(2)}) collective-permute-start(bf16[272,128]{1,0:T(8,128)(2,1)S(1)} %get-tuple-element.48), channel_id=1, source_target_pairs={{0,128},{64,192},{128,0},{192,64},{1,129},{65,193},{129,1},{193,65... | collective-permute-start | bytes 208904 | tf_op jit(solution)/shard_map/ppermute | solution.py:42
  22.1 0.0 collective-permute-start.3
  22.1 2.4 %collective-permute-start.1 = (bf16[272,128]{1,0:T(8,128)(2,1)S(1)}, bf16[272,128]{1,0:T(8,128)(2,1)S(1)}, u32[]{:S(2)}, u32[]{:S(2)}) collective-permute-start(bf16[272,128]{1,0:T(8,128)(2,1)S(1)} %get-tuple-element.46.after), channel_id=1, source_target_pairs={{0,64},{64,128},{128,192},{192,0},{1,65},{65,129},{129,193},{193,1... | collective-permute-start | bytes 208904 | tf_op jit(solution)/shard_map/ppermute | solution.py:42
  24.5 1.8 %near.3 = (bf16[272,128]{1,0:T(8,128)(2,1)S(1)}, bf16[1,256,4096]{2,1,0:T(8,128)(2,1)S(1)}) custom-call(s32[8,128]{1,0:T(8,128)S(1)} %get-tuple-element.38.index, f32[32,128]{1,0:T(8,128)S(1)} %get-tuple-element.39.quad, f32[256,2,32,128]{3,2,1,0:T(8,128)S(1)} %get-tuple-element.40.exy, f32[32,2,32,128]{3,2,1,0:T(8,128)S(1)} %get-tuple-element.41.ez, ...), custom_call_target="tpu_custom_call" | custom-call | flops 536870912 | bytes 1048576 | tf_op jit(solution)/shard_map/near/pallas_call | solution.py:298
  26.3 0.0 collective-permute-done.2.got2
  26.3 3.4 %collective-permute-done.3.got3 = bf16[272,128]{1,0:T(8,128)(2,1)S(1)} collective-permute-done((bf16[272,128]{1,0:T(8,128)(2,1)S(1)}, bf16[272,128]{1,0:T(8,128)(2,1)S(1)}, u32[]{:S(2)}, u32[]{:S(2)}) %collective-permute-start.3) | collective-permute-done | bytes 69664 | tf_op jit(solution)/shard_map/ppermute | solution.py:42
  29.7 0.0 collective-permute-done.1.got1
  29.7 0.1 z_sum.1
  29.8 1.3 %collective-permute-start.4 = (bf16[48,256]{1,0:T(8,128)(2,1)S(1)}, bf16[48,256]{1,0:T(8,128)(2,1)S(1)}, u32[]{:S(2)}, u32[]{:S(2)}) collective-permute-start(bf16[48,256]{1,0:T(8,128)(2,1)S(1)} %get-tuple-element.51), channel_id=1, source_target_pairs={{0,16},{16,32},{32,48},{48,0},{1,17},{17,33},{33,49},{49,1},{2,18}... | collective-permute-start | bytes 73736 | tf_op jit(solution)/shard_map/ppermute | solution.py:42
  31.1 2.4 %collective-permute-start.5 = (bf16[48,256]{1,0:T(8,128)(2,1)S(1)}, bf16[48,256]{1,0:T(8,128)(2,1)S(1)}, u32[]{:S(2)}, u32[]{:S(2)}) collective-permute-start(bf16[48,256]{1,0:T(8,128)(2,1)S(1)} %get-tuple-element.52), channel_id=1, source_target_pairs={{0,32},{16,48},{32,0},{48,16},{1,33},{17,49},{33,1},{49,17},{2,34}... | collective-permute-start | bytes 73736 | tf_op jit(solution)/shard_map/ppermute | solution.py:42
  33.6 1.2 %collective-permute-start.6 = (bf16[48,256]{1,0:T(8,128)(2,1)S(1)}, bf16[48,256]{1,0:T(8,128)(2,1)S(1)}, u32[]{:S(2)}, u32[]{:S(2)}) collective-permute-start(bf16[48,256]{1,0:T(8,128)(2,1)S(1)} %get-tuple-element.53), channel_id=1, source_target_pairs={{0,48},{16,0},{32,16},{48,32},{1,49},{17,1},{33,17},{49,33},{2,50}... | collective-permute-start | bytes 73736 | tf_op jit(solution)/shard_map/ppermute | solution.py:42
  34.7 0.6 collective-permute-done.5.got2
  35.3 1.2 %collective-permute-done.6.got3 = bf16[48,256]{1,0:T(8,128)(2,1)S(1)} collective-permute-done((bf16[48,256]{1,0:T(8,128)(2,1)S(1)}, bf16[48,256]{1,0:T(8,128)(2,1)S(1)}, u32[]{:S(2)}, u32[]{:S(2)}) %collective-permute-start.6) | collective-permute-done | bytes 24608 | tf_op jit(solution)/shard_map/ppermute | solution.py:42
  36.5 0.4 filter.1
  36.9 1.0 %collective-permute-start.9 = (bf16[32,256]{1,0:T(8,128)(2,1)S(1)}, bf16[32,256]{1,0:T(8,128)(2,1)S(1)}, u32[]{:S(2)}, u32[]{:S(2)}) collective-permute-start(bf16[32,256]{1,0:T(8,128)(2,1)S(1)} %get-tuple-element.55), channel_id=1, source_target_pairs={{0,64},{64,128},{128,192},{192,0},{1,65},{65,129},{129,193},{193,1... | collective-permute-start | bytes 49160 | tf_op jit(solution)/shard_map/ppermute | solution.py:42
  37.9 3.5 %collective-permute-start.8 = (bf16[32,256]{1,0:T(8,128)(2,1)S(1)}, bf16[32,256]{1,0:T(8,128)(2,1)S(1)}, u32[]{:S(2)}, u32[]{:S(2)}) collective-permute-start(bf16[32,256]{1,0:T(8,128)(2,1)S(1)} %get-tuple-element.55), channel_id=1, source_target_pairs={{0,128},{64,192},{128,0},{192,64},{1,129},{65,193},{129,1},{193,65... | collective-permute-start | bytes 49160 | tf_op jit(solution)/shard_map/ppermute | solution.py:42
  41.5 1.5 %collective-permute-start.7 = (bf16[32,256]{1,0:T(8,128)(2,1)S(1)}, bf16[32,256]{1,0:T(8,128)(2,1)S(1)}, u32[]{:S(2)}, u32[]{:S(2)}) collective-permute-start(bf16[32,256]{1,0:T(8,128)(2,1)S(1)} %get-tuple-element.55), channel_id=1, source_target_pairs={{0,192},{64,0},{128,64},{192,128},{1,193},{65,1},{129,65},{193,129... | collective-permute-start | bytes 49160 | tf_op jit(solution)/shard_map/ppermute | solution.py:42
  43.0 2.0 %collective-permute-done.7 = bf16[32,256]{1,0:T(8,128)(2,1)S(1)} collective-permute-done((bf16[32,256]{1,0:T(8,128)(2,1)S(1)}, bf16[32,256]{1,0:T(8,128)(2,1)S(1)}, u32[]{:S(2)}, u32[]{:S(2)}) %collective-permute-start.7) | collective-permute-done | bytes 16416 | tf_op jit(solution)/shard_map/ppermute | solution.py:42
  45.0 0.0 collective-permute-done.8
  45.0 0.0 collective-permute-done.9
  45.0 2.4 %collective-permute-start.10 = (bf16[128,256]{1,0:T(8,128)(2,1)S(1)}, bf16[128,256]{1,0:T(8,128)(2,1)S(1)}, u32[]{:S(2)}, u32[]{:S(2)}) collective-permute-start(bf16[128,256]{1,0:T(8,128)(2,1)S(1)} %get-tuple-element.71), channel_id=1, source_target_pairs={{0,48},{16,0},{32,16},{48,32},{1,49},{17,1},{33,17},{49,33},{2,50}... | collective-permute-start | bytes 196616 | tf_op jit(solution)/shard_map/ppermute | solution.py:42
  47.4 0.0 collective-permute-start.12
  47.4 1.5 %collective-permute-start.11 = (bf16[128,256]{1,0:T(8,128)(2,1)S(1)}, bf16[128,256]{1,0:T(8,128)(2,1)S(1)}, u32[]{:S(2)}, u32[]{:S(2)}) collective-permute-start(bf16[128,256]{1,0:T(8,128)(2,1)S(1)} %get-tuple-element.71), channel_id=1, source_target_pairs={{0,32},{16,48},{32,0},{48,16},{1,33},{17,49},{33,1},{49,17},{2,34}... | collective-permute-start | bytes 196616 | tf_op jit(solution)/shard_map/ppermute | solution.py:42
  48.9 3.3 %collective-permute-done.11 = bf16[128,256]{1,0:T(8,128)(2,1)S(1)} collective-permute-done((bf16[128,256]{1,0:T(8,128)(2,1)S(1)}, bf16[128,256]{1,0:T(8,128)(2,1)S(1)}, u32[]{:S(2)}, u32[]{:S(2)}) %collective-permute-start.11) | collective-permute-done | bytes 65568 | tf_op jit(solution)/shard_map/ppermute | solution.py:42
  52.1 0.3 collective-permute-done.12
  52.4 5.8 %collective-permute-start.13 = (bf16[512,256]{1,0:T(8,128)(2,1)S(1)}, bf16[512,256]{1,0:T(8,128)(2,1)S(1)}, u32[]{:S(2)}, u32[]{:S(2)}) collective-permute-start(bf16[512,256]{1,0:T(8,128)(2,1)S(1)} %constant_dynamic-update-slice_fusion.4.src), channel_id=1, source_target_pairs={{0,8},{8,0},{1,9},{9,1},{2,10},{10,2},{3,11},{11,3},{4,12},{12,4},... | collective-permute-start | bytes 786440 | tf_op jit(solution)/shard_map/ppermute | solution.py:42
  58.2 2.7 %near_field.1.part = f32[128,4096]{1,0:T(8,128)S(1)} custom-call(bf16[512,256]{1,0:T(8,128)(2,1)S(1)} %constant_dynamic-update-slice_fusion.4.src, bf16[1,256,4096]{2,1,0:T(8,128)(2,1)S(1)} %get-tuple-element.57.n0, bf16[3,256,4096]{2,1,0:T(8,128)(2,1)S(1)} %get-tuple-element.58.n123), custom_call_target="tpu_custom_call" | custom-call | flops 1073741824 | bytes 1048576 | tf_op jit(solution)/shard_map/near_field/pallas_call | solution.py:316
  60.9 0.1 turned.1.f
  61.1 0.5 synthesis.3
  61.6 3.0 %collective-permute-start.14 = (bf16[128,512]{1,0:T(8,128)(2,1)S(1)}, bf16[128,512]{1,0:T(8,128)(2,1)S(1)}, u32[]{:S(2)}, u32[]{:S(2)}) collective-permute-start(bf16[128,512]{1,0:T(8,128)(2,1)S(1)} %get-tuple-element.59), channel_id=1, source_target_pairs={{0,4},{1,5},{2,6},{3,7},{4,0},{5,1},{6,2},{7,3},{8,12},{9,13},{10,... | collective-permute-start | bytes 393224 | tf_op jit(solution)/shard_map/ppermute | solution.py:42
  64.5 0.9 %collective-permute-start.15 = (bf16[128,512]{1,0:T(8,128)(2,1)S(1)}, bf16[128,512]{1,0:T(8,128)(2,1)S(1)}, u32[]{:S(2)}, u32[]{:S(2)}) collective-permute-start(bf16[128,512]{1,0:T(8,128)(2,1)S(1)} %get-tuple-element.60), channel_id=1, source_target_pairs={{0,3},{1,4},{2,5},{3,6},{4,7},{5,0},{6,1},{7,2},{8,11},{9,12},{10,... | collective-permute-start | bytes 393224 | tf_op jit(solution)/shard_map/ppermute | solution.py:42
  65.5 0.6 synthesis.4
  66.1 0.6 synthesis.5
  66.7 0.4 collective-permute-start.19
  67.2 3.2 %collective-permute-start.20 = (bf16[128,512]{1,0:T(8,128)(2,1)S(1)}, bf16[128,512]{1,0:T(8,128)(2,1)S(1)}, u32[]{:S(2)}, u32[]{:S(2)}) collective-permute-start(bf16[128,512]{1,0:T(8,128)(2,1)S(1)} %get-tuple-element.69), channel_id=1, source_target_pairs={{0,7},{1,0},{2,1},{3,2},{4,3},{5,4},{6,5},{7,6},{8,15},{9,8},{10,9... | collective-permute-start | bytes 393224 | tf_op jit(solution)/shard_map/ppermute | solution.py:42
  70.4 0.8 collective-permute-start.16
  71.2 1.7 %collective-permute-done.14.rest_0_ = bf16[128,512]{1,0:T(8,128)(2,1)S(1)} collective-permute-done((bf16[128,512]{1,0:T(8,128)(2,1)S(1)}, bf16[128,512]{1,0:T(8,128)(2,1)S(1)}, u32[]{:S(2)}, u32[]{:S(2)}) %collective-permute-start.14) | collective-permute-done | bytes 131104 | tf_op jit(solution)/shard_map/ppermute | solution.py:42
  72.9 0.0 collective-permute-start.17
  72.9 2.7 %collective-permute-start.18 = (bf16[128,512]{1,0:T(8,128)(2,1)S(1)}, bf16[128,512]{1,0:T(8,128)(2,1)S(1)}, u32[]{:S(2)}, u32[]{:S(2)}) collective-permute-start(bf16[128,512]{1,0:T(8,128)(2,1)S(1)} %get-tuple-element.65), channel_id=1, source_target_pairs={{0,6},{1,7},{2,0},{3,1},{4,2},{5,3},{6,4},{7,5},{8,14},{9,15},{10,... | collective-permute-start | bytes 393224 | tf_op jit(solution)/shard_map/ppermute | solution.py:42
  75.6 3.0 %collective-permute-done.16.rest_2_ = bf16[128,512]{1,0:T(8,128)(2,1)S(1)} collective-permute-done((bf16[128,512]{1,0:T(8,128)(2,1)S(1)}, bf16[128,512]{1,0:T(8,128)(2,1)S(1)}, u32[]{:S(2)}, u32[]{:S(2)}) %collective-permute-start.16) | collective-permute-done | bytes 131104 | tf_op jit(solution)/shard_map/ppermute | solution.py:42
  78.7 0.0 collective-permute-done.17.rest_3_
  78.7 3.4 %collective-permute-done.18.rest_4_ = bf16[128,512]{1,0:T(8,128)(2,1)S(1)} collective-permute-done((bf16[128,512]{1,0:T(8,128)(2,1)S(1)}, bf16[128,512]{1,0:T(8,128)(2,1)S(1)}, u32[]{:S(2)}, u32[]{:S(2)}) %collective-permute-start.18) | collective-permute-done | bytes 131104 | tf_op jit(solution)/shard_map/ppermute | solution.py:42
  82.0 0.9 %finish.1 = bf16[512,128]{1,0:T(8,128)(2,1)} custom-call(f32[8,128]{1,0:T(8,128)S(1)} %get-tuple-element.54.total, f32[512,128]{1,0:T(8,128)S(1)} %get-tuple-element.43.after.linear, bf16[128,512]{1,0:T(8,128)(2,1)S(1)} %collective-permute-done.14.rest_0_, bf16[128,512]{1,0:T(8,128)(2,1)S(1)} %collective-permute-done.15.rest_1_, ...), custom_call_target="tpu_custom_call" | custom-call | bytes 1048576 | tf_op jit(solution)/shard_map/finish/pallas_call | solution.py:331
  (15 shorter events, 0.0 us)
Async XLA Ops:
  8.9 7.9 %collective-permute-start = (bf16[1040,128]{1,0:T(8,128)(2,1)S(1)}, bf16[1040,128]{1,0:T(8,128)(2,1)S(1)}, u32[]{:S(2)}, u32[]{:S(2)}) collective-permute-start(bf16[1040,128]{1,0:T(8,128)(2,1)S(1)} %get-tuple-element.45), channel_id=1, source_target_pairs={{0,8},{8,0},{1,9},{9,1},{2,10},{10,2},{3,11},{11,3},{4,12},{12,4},... | collective-permute-start | bytes 798728 | tf_op jit(solution)/shard_map/ppermute | solution.py:42
  16.8 19.8 %copy-start = (bf16[32,2,128,128]{3,2,1,0:T(8,128)(2,1)S(1)}, bf16[32,2,128,128]{3,2,1,0:T(8,128)(2,1)}, u32[]{:S(2)}) copy-start(bf16[32,2,128,128]{3,2,1,0:T(8,128)(2,1)} %weight.1) | copy-start | bytes 6291460
  16.9 9.4 %collective-permute-start.2 = (bf16[272,128]{1,0:T(8,128)(2,1)S(1)}, bf16[272,128]{1,0:T(8,128)(2,1)S(1)}, u32[]{:S(2)}, u32[]{:S(2)}) collective-permute-start(bf16[272,128]{1,0:T(8,128)(2,1)S(1)} %get-tuple-element.48), channel_id=1, source_target_pairs={{0,128},{64,192},{128,0},{192,64},{1,129},{65,193},{129,1},{193,65... | collective-permute-start | bytes 208904 | tf_op jit(solution)/shard_map/ppermute | solution.py:42
  22.1 7.6 %collective-permute-start.3 = (bf16[272,128]{1,0:T(8,128)(2,1)S(1)}, bf16[272,128]{1,0:T(8,128)(2,1)S(1)}, u32[]{:S(2)}, u32[]{:S(2)}) collective-permute-start(bf16[272,128]{1,0:T(8,128)(2,1)S(1)} %get-tuple-element.49), channel_id=1, source_target_pairs={{0,192},{64,0},{128,64},{192,128},{1,193},{65,1},{129,65},{193,129... | collective-permute-start | bytes 208904 | tf_op jit(solution)/shard_map/ppermute | solution.py:42
  22.1 7.6 %collective-permute-start.1 = (bf16[272,128]{1,0:T(8,128)(2,1)S(1)}, bf16[272,128]{1,0:T(8,128)(2,1)S(1)}, u32[]{:S(2)}, u32[]{:S(2)}) collective-permute-start(bf16[272,128]{1,0:T(8,128)(2,1)S(1)} %get-tuple-element.46.after), channel_id=1, source_target_pairs={{0,64},{64,128},{128,192},{192,0},{1,65},{65,129},{129,193},{193,1... | collective-permute-start | bytes 208904 | tf_op jit(solution)/shard_map/ppermute | solution.py:42
  29.8 4.9 %collective-permute-start.4 = (bf16[48,256]{1,0:T(8,128)(2,1)S(1)}, bf16[48,256]{1,0:T(8,128)(2,1)S(1)}, u32[]{:S(2)}, u32[]{:S(2)}) collective-permute-start(bf16[48,256]{1,0:T(8,128)(2,1)S(1)} %get-tuple-element.51), channel_id=1, source_target_pairs={{0,16},{16,32},{32,48},{48,0},{1,17},{17,33},{33,49},{49,1},{2,18}... | collective-permute-start | bytes 73736 | tf_op jit(solution)/shard_map/ppermute | solution.py:42
  31.1 4.2 %collective-permute-start.5 = (bf16[48,256]{1,0:T(8,128)(2,1)S(1)}, bf16[48,256]{1,0:T(8,128)(2,1)S(1)}, u32[]{:S(2)}, u32[]{:S(2)}) collective-permute-start(bf16[48,256]{1,0:T(8,128)(2,1)S(1)} %get-tuple-element.52), channel_id=1, source_target_pairs={{0,32},{16,48},{32,0},{48,16},{1,33},{17,49},{33,1},{49,17},{2,34}... | collective-permute-start | bytes 73736 | tf_op jit(solution)/shard_map/ppermute | solution.py:42
  33.6 3.0 %collective-permute-start.6 = (bf16[48,256]{1,0:T(8,128)(2,1)S(1)}, bf16[48,256]{1,0:T(8,128)(2,1)S(1)}, u32[]{:S(2)}, u32[]{:S(2)}) collective-permute-start(bf16[48,256]{1,0:T(8,128)(2,1)S(1)} %get-tuple-element.53), channel_id=1, source_target_pairs={{0,48},{16,0},{32,16},{48,32},{1,49},{17,1},{33,17},{49,33},{2,50}... | collective-permute-start | bytes 73736 | tf_op jit(solution)/shard_map/ppermute | solution.py:42
  36.9 8.0 %collective-permute-start.9 = (bf16[32,256]{1,0:T(8,128)(2,1)S(1)}, bf16[32,256]{1,0:T(8,128)(2,1)S(1)}, u32[]{:S(2)}, u32[]{:S(2)}) collective-permute-start(bf16[32,256]{1,0:T(8,128)(2,1)S(1)} %get-tuple-element.55), channel_id=1, source_target_pairs={{0,64},{64,128},{128,192},{192,0},{1,65},{65,129},{129,193},{193,1... | collective-permute-start | bytes 49160 | tf_op jit(solution)/shard_map/ppermute | solution.py:42
  37.9 7.0 %collective-permute-start.8 = (bf16[32,256]{1,0:T(8,128)(2,1)S(1)}, bf16[32,256]{1,0:T(8,128)(2,1)S(1)}, u32[]{:S(2)}, u32[]{:S(2)}) collective-permute-start(bf16[32,256]{1,0:T(8,128)(2,1)S(1)} %get-tuple-element.55), channel_id=1, source_target_pairs={{0,128},{64,192},{128,0},{192,64},{1,129},{65,193},{129,1},{193,65... | collective-permute-start | bytes 49160 | tf_op jit(solution)/shard_map/ppermute | solution.py:42
  41.5 3.5 %collective-permute-start.7 = (bf16[32,256]{1,0:T(8,128)(2,1)S(1)}, bf16[32,256]{1,0:T(8,128)(2,1)S(1)}, u32[]{:S(2)}, u32[]{:S(2)}) collective-permute-start(bf16[32,256]{1,0:T(8,128)(2,1)S(1)} %get-tuple-element.55), channel_id=1, source_target_pairs={{0,192},{64,0},{128,64},{192,128},{1,193},{65,1},{129,65},{193,129... | collective-permute-start | bytes 49160 | tf_op jit(solution)/shard_map/ppermute | solution.py:42
  45.0 3.9 %collective-permute-start.10 = (bf16[128,256]{1,0:T(8,128)(2,1)S(1)}, bf16[128,256]{1,0:T(8,128)(2,1)S(1)}, u32[]{:S(2)}, u32[]{:S(2)}) collective-permute-start(bf16[128,256]{1,0:T(8,128)(2,1)S(1)} %get-tuple-element.71), channel_id=1, source_target_pairs={{0,48},{16,0},{32,16},{48,32},{1,49},{17,1},{33,17},{49,33},{2,50}... | collective-permute-start | bytes 196616 | tf_op jit(solution)/shard_map/ppermute | solution.py:42
  47.4 5.0 %collective-permute-start.12 = (bf16[128,256]{1,0:T(8,128)(2,1)S(1)}, bf16[128,256]{1,0:T(8,128)(2,1)S(1)}, u32[]{:S(2)}, u32[]{:S(2)}) collective-permute-start(bf16[128,256]{1,0:T(8,128)(2,1)S(1)} %get-tuple-element.71), channel_id=1, source_target_pairs={{0,16},{16,32},{32,48},{48,0},{1,17},{17,33},{33,49},{49,1},{2,18}... | collective-permute-start | bytes 196616 | tf_op jit(solution)/shard_map/ppermute | solution.py:42
  47.4 4.7 %collective-permute-start.11 = (bf16[128,256]{1,0:T(8,128)(2,1)S(1)}, bf16[128,256]{1,0:T(8,128)(2,1)S(1)}, u32[]{:S(2)}, u32[]{:S(2)}) collective-permute-start(bf16[128,256]{1,0:T(8,128)(2,1)S(1)} %get-tuple-element.71), channel_id=1, source_target_pairs={{0,32},{16,48},{32,0},{48,16},{1,33},{17,49},{33,1},{49,17},{2,34}... | collective-permute-start | bytes 196616 | tf_op jit(solution)/shard_map/ppermute | solution.py:42
  52.4 8.5 %collective-permute-start.13 = (bf16[512,256]{1,0:T(8,128)(2,1)S(1)}, bf16[512,256]{1,0:T(8,128)(2,1)S(1)}, u32[]{:S(2)}, u32[]{:S(2)}) collective-permute-start(bf16[512,256]{1,0:T(8,128)(2,1)S(1)} %constant_dynamic-update-slice_fusion.4.src), channel_id=1, source_target_pairs={{0,8},{8,0},{1,9},{9,1},{2,10},{10,2},{3,11},{11,3},{4,12},{12,4},... | collective-permute-start | bytes 786440 | tf_op jit(solution)/shard_map/ppermute | solution.py:42
  61.6 11.4 %collective-permute-start.14 = (bf16[128,512]{1,0:T(8,128)(2,1)S(1)}, bf16[128,512]{1,0:T(8,128)(2,1)S(1)}, u32[]{:S(2)}, u32[]{:S(2)}) collective-permute-start(bf16[128,512]{1,0:T(8,128)(2,1)S(1)} %get-tuple-element.59), channel_id=1, source_target_pairs={{0,4},{1,5},{2,6},{3,7},{4,0},{5,1},{6,2},{7,3},{8,12},{9,13},{10,... | collective-permute-start | bytes 393224 | tf_op jit(solution)/shard_map/ppermute | solution.py:42
  64.5 8.4 %collective-permute-start.15 = (bf16[128,512]{1,0:T(8,128)(2,1)S(1)}, bf16[128,512]{1,0:T(8,128)(2,1)S(1)}, u32[]{:S(2)}, u32[]{:S(2)}) collective-permute-start(bf16[128,512]{1,0:T(8,128)(2,1)S(1)} %get-tuple-element.60), channel_id=1, source_target_pairs={{0,3},{1,4},{2,5},{3,6},{4,7},{5,0},{6,1},{7,2},{8,11},{9,12},{10,... | collective-permute-start | bytes 393224 | tf_op jit(solution)/shard_map/ppermute | solution.py:42
  66.7 8.9 %collective-permute-start.19 = (bf16[128,512]{1,0:T(8,128)(2,1)S(1)}, bf16[128,512]{1,0:T(8,128)(2,1)S(1)}, u32[]{:S(2)}, u32[]{:S(2)}) collective-permute-start(bf16[128,512]{1,0:T(8,128)(2,1)S(1)} %get-tuple-element.68), channel_id=1, source_target_pairs={{0,1},{1,2},{2,3},{3,4},{4,5},{5,6},{6,7},{7,0},{8,9},{9,10},{10,1... | collective-permute-start | bytes 393224 | tf_op jit(solution)/shard_map/ppermute | solution.py:42
  67.2 8.5 %collective-permute-start.20 = (bf16[128,512]{1,0:T(8,128)(2,1)S(1)}, bf16[128,512]{1,0:T(8,128)(2,1)S(1)}, u32[]{:S(2)}, u32[]{:S(2)}) collective-permute-start(bf16[128,512]{1,0:T(8,128)(2,1)S(1)} %get-tuple-element.69), channel_id=1, source_target_pairs={{0,7},{1,0},{2,1},{3,2},{4,3},{5,4},{6,5},{7,6},{8,15},{9,8},{10,9... | collective-permute-start | bytes 393224 | tf_op jit(solution)/shard_map/ppermute | solution.py:42
  70.4 8.3 %collective-permute-start.16 = (bf16[128,512]{1,0:T(8,128)(2,1)S(1)}, bf16[128,512]{1,0:T(8,128)(2,1)S(1)}, u32[]{:S(2)}, u32[]{:S(2)}) collective-permute-start(bf16[128,512]{1,0:T(8,128)(2,1)S(1)} %get-tuple-element.63), channel_id=1, source_target_pairs={{0,5},{1,6},{2,7},{3,0},{4,1},{5,2},{6,3},{7,4},{8,13},{9,14},{10,... | collective-permute-start | bytes 393224 | tf_op jit(solution)/shard_map/ppermute | solution.py:42
  72.9 5.7 %collective-permute-start.17 = (bf16[128,512]{1,0:T(8,128)(2,1)S(1)}, bf16[128,512]{1,0:T(8,128)(2,1)S(1)}, u32[]{:S(2)}, u32[]{:S(2)}) collective-permute-start(bf16[128,512]{1,0:T(8,128)(2,1)S(1)} %get-tuple-element.64), channel_id=1, source_target_pairs={{0,2},{1,3},{2,4},{3,5},{4,6},{5,7},{6,0},{7,1},{8,10},{9,11},{10,... | collective-permute-start | bytes 393224 | tf_op jit(solution)/shard_map/ppermute | solution.py:42
  72.9 9.1 %collective-permute-start.18 = (bf16[128,512]{1,0:T(8,128)(2,1)S(1)}, bf16[128,512]{1,0:T(8,128)(2,1)S(1)}, u32[]{:S(2)}, u32[]{:S(2)}) collective-permute-start(bf16[128,512]{1,0:T(8,128)(2,1)S(1)} %get-tuple-element.65), channel_id=1, source_target_pairs={{0,6},{1,7},{2,0},{3,1},{4,2},{5,3},{6,4},{7,5},{8,14},{9,15},{10,... | collective-permute-start | bytes 393224 | tf_op jit(solution)/shard_map/ppermute | solution.py:42

commit v5 on v4

--- a/solution.py
+++ b/solution.py
@@ -12,6 +12,7 @@
 PTS = ("z_hi", "x", "core")
 GRP = ("y", "z_lo")
 ALL = PTS + GRP
+FAR_LAST = (1, 3, 2)
 C = 128
 PITCH = C + 1
 ROWS = 32
@@ -126,7 +127,7 @@
             coef[pl.ds(pl.multiple_of(s * 2 * C, 2 * C), 2 * C), :] = value
 
         def put_basis(cols, value):
-            basis[s, :, cols] = value
+            basis[pl.ds(pl.multiple_of((first % 4 + s) * 2 * C, 2 * C), 2 * C), cols] = value
 
         analyse(index, first + s, put_coef, put_basis, exy, ez, w, scr)
 
@@ -140,15 +141,15 @@
     tile, within = group // 4, lax.rem(group, 4)
     part = lax.broadcasted_iota(jnp.int32, (1, C), 1) // 32
     for flip in range(2):
-        for dz in range(4):
+        for dx in range(4):
             row = jnp.zeros((1, C), jnp.int32)
-            for dx in range(4):
+            for dz in range(4):
                 own = (lax.rem(z + dz, 4) * 4 + lax.rem(x + dx, 4)) * 2 + lax.rem(core + flip, 2)
                 v = table[:, pl.ds(pl.multiple_of(own * 256 + tile * C, C), C)]
                 k = ((v[0:1] + 8) * 16 + v[1:2] + 8) * 32 + v[2:3]
-                k = pltpu.roll(k, lax.rem(dx - within + 4, 4) * 32, 1)
-                row = jnp.where(part == dx, k, row)
-            index[pl.ds(flip * 4 + dz, 1), :] = row
+                k = pltpu.roll(k, lax.rem(dz - within + 4, 4) * 32, 1)
+                row = jnp.where(part == dz, k, row)
+            index[pl.ds(flip * 4 + dx, 1), :] = row
 
 
 def first_body(*refs):
@@ -183,7 +184,7 @@
     slabs(4, 4, held, coef, basis, exy, ez, w, quad, scr)
 
 
-def near_body(count, first, index, quad, exy, ez, w, after, coef, basis, scr):
+def near_body(count, first, index, quad, exy, ez, w, given, coef, basis, scr):
     slabs(count, first, index, coef, basis, exy, ez, w, quad, scr)
 
 
@@ -195,7 +196,7 @@
         out[pl.ds(2 * C, 16), :] = lanes3(tail)
 
 
-def z_body(own, got0, got1, got2, got3, keep, out1, out2, out3):
+def x_body(own, got0, got1, got2, got3, keep, out1, out2, out3):
     body, rest = pl.ds(0, 2 * C), pl.ds(2 * C, 16)
     summed = own[body, :].astype(F32) + got0[body, :].astype(F32)
     tail = own[rest, :].astype(F32) + got0[pl.ds(8 * C, 16), :].astype(F32)
@@ -231,34 +232,26 @@
 
 
 def turned_body(src, out):
-    for dz in range(4):
+    for dx in range(4):
         for part in range(2):
-            cols = pl.ds(part * C, C)
-            block = jnp.concatenate([src[pl.ds(dx * C + dz * 32, 32), cols].astype(F32) for dx in range(4)], axis=0)
-            out[:, pl.ds((dz * 2 + part) * C, C)] = block.T.astype(BF)
-
-
-def near_field_body(src, n0, n123, part, f):
+            block = src[pl.ds(dx * C, C), pl.ds(part * C, C)].astype(F32).T
+            out[:, pl.ds((dx * 2 + part) * C, C)] = block.astype(BF)
+
+
+def near_field_body(src, basis, part, f):
     turned_body(src, f)
 
     @pl.loop(0, 8)
     def _(k):
         at = pl.ds(pl.multiple_of(k * 512, 512), 512)
-        acc = None
-        for i, b in enumerate((n0.at[0], n123.at[0], n123.at[1], n123.at[2])):
-            term = jnp.dot(f[:, pl.ds(i * 2 * C, 2 * C)], b[:, at], preferred_element_type=F32)
-            acc = term if acc is None else acc + term
-        part[:, at] = acc
+        part[:, at] = jnp.dot(f[...], basis[:, at], preferred_element_type=F32)
 
 
 def synthesis_body(shifts, f, basis, part, *outs):
     group = lax.axis_index("y") * 2 + lax.axis_index("z_lo")
     for s, out in zip(shifts, outs[: len(shifts)], strict=True):
         at = pl.ds(pl.multiple_of(lax.rem(group + s, 8) * 512, 512), 512)
-        acc = part[:, at]
-        for i in range(4):
-            acc = acc + jnp.dot(f[:, pl.ds(i * 2 * C, 2 * C)], basis[i, :, at], preferred_element_type=F32)
-        out[...] = acc.astype(BF)
+        out[...] = (part[:, at] + jnp.dot(f[...], basis[:, at], preferred_element_type=F32)).astype(BF)
 
 
 def finish_body(total, linear, *rest):
@@ -273,8 +266,17 @@
         out[rows, :] = (0.5 * pre * (1.0 + lax.erf(pre * math.sqrt(0.5)))).astype(BF)
 
 
+def join_body(piece, *rest):
+    *got, out = rest
+    rows = piece.shape[0]
+    for s, ref in zip((0, *FAR_LAST), (piece, *got)):
+        out[pl.ds(s * rows, rows), :] = ref[...]
+
+
 def gather_over(piece, axes, n):
-    return jnp.concatenate([piece] + [send(piece, axes, n - s) for s in range(1, n)])
+    got = [send(piece, axes, n - s) for s in FAR_LAST]
+    shape = jax.ShapeDtypeStruct((n * piece.shape[0], piece.shape[1]), piece.dtype)
+    return call(join_body, n, shape, "join")(piece, *got)
 
 
 def on_device(features, coords, quad_weight, mode_table, mode_weight, lin_weight, bias):
@@ -284,7 +286,7 @@
     slab = 2 * 2 * C * pts * C
     far, far_basis, exy, ez, w, linear, quad, index = call(
         first_body, 0,
-        [pltpu.VMEM((8 * C + 16, C), BF), pltpu.VMEM((4, 2 * C, pts), BF), pltpu.VMEM((256, 2, ROWS, C), F32),
+        [pltpu.VMEM((8 * C + 16, C), BF), pltpu.VMEM((8 * C, pts), BF), pltpu.VMEM((256, 2, ROWS, C), F32),
          pltpu.VMEM((32, 2, ROWS, C), F32), pltpu.VMEM((pts, C), BF), pltpu.VMEM((pts // 8, C), F32),
          pltpu.VMEM((ROWS, C), F32), pltpu.VMEM((8, C), jnp.int32)],
         "first",
@@ -294,28 +296,28 @@
     )(coords, mode_table, quad_weight.reshape(ROWS, C), lin_weight, bias.reshape(1, C), features)
     got = send(far, ("core",), 1)
 
-    def near(count, first, after):
+    def near(count, first, given, alias):
         return call(
             functools.partial(near_body, count, first), 4,
-            [pltpu.VMEM((count * 2 * C + 16, C), BF), pltpu.VMEM((count, 2 * C, pts), BF)],
-            "near", [scr], 1, 2 * count * slab, last=[pl.ANY],
-        )(index, quad, exy, ez, w, after)
-
-    mine, n123 = near(3, 1, linear)
+            [pltpu.VMEM((count * 2 * C + 16, C), BF), pltpu.VMEM((8 * C, pts), BF)],
+            "near", [scr], 1, 2 * count * slab, last=[pltpu.VMEM if alias else pl.ANY], aliases={5: 1} if alias else {},
+        )(index, quad, exy, ez, w, given)
+
+    mine, basis = near(3, 1, linear, False)
     outs = call(pair_body, 2, [one(2 * C + 16, C, BF)] * 3, "pair")(mine, got)
-    across = {s: send(outs[s - 1], ("z_hi",), s) for s in (2, 1, 3)}
-    mine, n0 = near(1, 0, outs[0])
-    keep, *outs = call(z_body, 5, [one(48, 2 * C, F32)] + [one(48, 2 * C, BF)] * 3, "z_sum")(
-        mine, got, across[1], across[2], across[3]
+    across = {s: send(outs[s - 1], ("x",), s) for s in FAR_LAST}
+    mine, basis = near(1, 0, basis, True)
+    keep, *outs = call(x_body, 5, [one(48, 2 * C, F32)] + [one(48, 2 * C, BF)] * 3, "x_sum")(
+        mine, got, *[across[s] for s in FAR_LAST]
     )
-    got = [send(o, ("x",), s) for s, o in zip((1, 2, 3), outs)]
+    got = [send(outs[s - 1], ("z_hi",), s) for s in FAR_LAST]
     piece, total = call(filter_body, 5, [one(32, 2 * C, BF), one(8, C, F32)], "filter")(keep, *got, mode_weight)
     piece = gather_over(piece, ("z_hi",), 4)
     piece = gather_over(piece, ("x",), 4)
     other = send(piece, ("core",), 1)
     part = call(
-        near_field_body, 3, pltpu.VMEM((C, pts), F32), "near_field", [pltpu.VMEM((C, 8 * C), BF)], flops=4 * slab
-    )(piece, n0, n123)
+        near_field_body, 2, pltpu.VMEM((C, pts), F32), "near_field", [pltpu.VMEM((C, 8 * C), BF)], flops=4 * slab
+    )(piece, basis)
     f = call(turned_body, 1, one(C, 8 * C, BF), "turned")(other)
     fields = []
     for shifts in ((4, 3), (5, 2, 6), (1, 7, 0)):

time: 83 us -> 82.1 us (0.989)
  waiting for transfers between devices: 18.9 us -> 16.1 us
  starting transfers between devices: 42.6 us -> 44.5 us
    ppermute x21, waiting for transfers between devices: 18.9 us -> 16.1 us  [send(): return lax.ppermute(value, axes, [(j, (j + shift) % n) for j in range(n)])]
    ppermute x21, starting transfers between devices: 42.6 us -> 44.5 us  [send(): return lax.ppermute(value, axes, [(j, (j + shift) % n) for j in range(n)])]
    pallas_call x3 -> x5, Pallas kernels: 11.7 us -> 11.7 us  [the longest x1 8.85 us: on_device(): call(first_body, 0, [pltpu.VMEM((8 * C + 16, C), BF), pltpu.VMEM((8 * C,...]
  transfers between devices with their start and end apart: 21 -> 21, of which waited for: 9 -> 10; matrix products, arithmetic and copies ran while one was open for 0% -> 0% of each run, Pallas kernels for 13% -> 13%
where the time goes in v5:
time: 82.1 us; the launch traced here: 82 us
  starting transfers between devices  44.5 us (54%)
  Pallas kernels  21.4 us (26%)
  waiting for transfers between devices  16.1 us (20%)
    ppermute x21, starting transfers between devices, send(): return lax.ppermute(value, axes, [(j, (j + shift) % n) for j in range(n)])  44.5 us
    ppermute x21, waiting for transfers between devices, send(): return lax.ppermute(value, axes, [(j, (j + shift) % n) for j in range(n)])  16.1 us
    pallas_call x1, Pallas kernels, on_device(): call(first_body, 0, [pltpu.VMEM((8 * C + 16, C), BF), pltpu.VMEM((8 * C,...  8.85 us
    pallas_call x2, Pallas kernels, near(): call(functools.partial(near_body, count, first), 4, [pltpu.VMEM((count *...  6.43 us
    pallas_call x1, Pallas kernels, on_device(): call(near_field_body, 2, pltpu.VMEM((C, pts), F32), 'near_field', [pltpu....  2.69 us
    pallas_call x3, Pallas kernels, on_device(): call(functools.partial(synthesis_body, shifts), 3, [one(C, 512, BF)] * co...  1.76 us
  transfers between devices with their start and end apart: 21, of which 10 were waited for; matrix products, arithmetic and copies ran while one was open for 0% of the time, Pallas kernels for 13%

profile of v5, /device:TPU:1, one launch (start us, length us, event | category | flops | bytes accessed | tf_op | source)
XLA Modules:
  0.0 82.0 jit_solution(15661466006932130773)
XLA Ops:
  0.0 8.9 %first.1 = (bf16[1040,128]{1,0:T(8,128)(2,1)S(1)}, bf16[1024,4096]{1,0:T(8,128)(2,1)S(1)}, f32[256,2,32,128]{3,2,1,0:T(8,128)S(1)}, f32[32,2,32,128]{3,2,1,0:T(8...) custom-call(f32[3,4096]{1,0:T(4,128)} %refs_0_.1, ...), custom_call_target="tpu_custom_call" | custom-call | flops 2147483648 | bytes 1048576 | tf_op jit(solution)/shard_map/first/pallas_call | solution.py:287
  8.9 3.3 %collective-permute-start = (bf16[1040,128]{1,0:T(8,128)(2,1)S(1)}, bf16[1040,128]{1,0:T(8,128)(2,1)S(1)}, u32[]{:S(2)}, u32[]{:S(2)}) collective-permute-start(bf16[1040,128]{1,0:T(8,128)(2,1)S(1)} %get-tuple-element.46), channel_id=1, source_target_pairs={{0,8},{8,0},{1,9},{9,1},{2,10},{10,2},{3,11},{11,3},{4,12},{12,4},... | collective-permute-start | bytes 798728 | tf_op jit(solution)/shard_map/ppermute | solution.py:43
  12.2 4.6 %near.2 = (bf16[784,128]{1,0:T(8,128)(2,1)S(1)}, bf16[1024,4096]{1,0:T(8,128)(2,1)S(1)}) custom-call(s32[8,128]{1,0:T(8,128)S(1)} %get-tuple-element.38.index, f32[32,128]{1,0:T(8,128)S(1)} %get-tuple-element.39.quad, f32[256,2,32,128]{3,2,1,0:T(8,128)S(1)} %get-tuple-element.40.exy, f32[32,2,32,128]{3,2,1,0:T(8,128)S(1)} %get-tuple-element.41.ez, ...), custom_call_target="tpu_custom_call" | custom-call | flops 1610612736 | bytes 1048576 | tf_op jit(solution)/shard_map/near/pallas_call | solution.py:300
  16.8 0.0 collective-permute-done.got.got0
  16.8 0.1 pair.1
  16.9 0.1 collective-permute-start.1
  16.9 2.7 %collective-permute-start.2 = (bf16[272,128]{1,0:T(8,128)(2,1)S(1)}, bf16[272,128]{1,0:T(8,128)(2,1)S(1)}, u32[]{:S(2)}, u32[]{:S(2)}) collective-permute-start(bf16[272,128]{1,0:T(8,128)(2,1)S(1)} %get-tuple-element.49), channel_id=1, source_target_pairs={{0,48},{16,0},{32,16},{48,32},{1,49},{17,1},{33,17},{49,33},{2,50}... | collective-permute-start | bytes 208904 | tf_op jit(solution)/shard_map/ppermute | solution.py:43
  19.6 1.8 %near.3 = (bf16[272,128]{1,0:T(8,128)(2,1)S(1)}, bf16[1024,4096]{1,0:T(8,128)(2,1)S(1)}) custom-call(s32[8,128]{1,0:T(8,128)S(1)} %get-tuple-element.38.index, f32[32,128]{1,0:T(8,128)S(1)} %get-tuple-element.39.quad, f32[256,2,32,128]{3,2,1,0:T(8,128)S(1)} %get-tuple-element.40.exy, ...), custom_call_target="tpu_custom_call", output_to_operand_aliasing={{1}: (5, {})} | custom-call | flops 536870912 | bytes 1048576 | tf_op jit(solution)/shard_map/near/pallas_call | solution.py:300
  21.4 0.5 collective-permute-done.1.got1
  21.9 0.7 collective-permute-done.2.got2
  22.6 1.7 %collective-permute-done.3.got3 = bf16[272,128]{1,0:T(8,128)(2,1)S(1)} collective-permute-done((bf16[272,128]{1,0:T(8,128)(2,1)S(1)}, bf16[272,128]{1,0:T(8,128)(2,1)S(1)}, u32[]{:S(2)}, u32[]{:S(2)}) %collective-permute-start.3) | collective-permute-done | bytes 69664 | tf_op jit(solution)/shard_map/ppermute | solution.py:43
  24.3 0.1 x_sum.1
  24.4 1.3 %collective-permute-start.4 = (bf16[48,256]{1,0:T(8,128)(2,1)S(1)}, bf16[48,256]{1,0:T(8,128)(2,1)S(1)}, u32[]{:S(2)}, u32[]{:S(2)}) collective-permute-start(bf16[48,256]{1,0:T(8,128)(2,1)S(1)} %get-tuple-element.52), channel_id=1, source_target_pairs={{0,64},{64,128},{128,192},{192,0},{1,65},{65,129},{129,193},{193,1... | collective-permute-start | bytes 73736 | tf_op jit(solution)/shard_map/ppermute | solution.py:43
  25.7 3.1 %collective-permute-start.5 = (bf16[48,256]{1,0:T(8,128)(2,1)S(1)}, bf16[48,256]{1,0:T(8,128)(2,1)S(1)}, u32[]{:S(2)}, u32[]{:S(2)}) collective-permute-start(bf16[48,256]{1,0:T(8,128)(2,1)S(1)} %get-tuple-element.53), channel_id=1, source_target_pairs={{0,192},{64,0},{128,64},{192,128},{1,193},{65,1},{129,65},{193,129... | collective-permute-start | bytes 73736 | tf_op jit(solution)/shard_map/ppermute | solution.py:43
  28.8 4.4 %collective-permute-start.6 = (bf16[48,256]{1,0:T(8,128)(2,1)S(1)}, bf16[48,256]{1,0:T(8,128)(2,1)S(1)}, u32[]{:S(2)}, u32[]{:S(2)}) collective-permute-start(bf16[48,256]{1,0:T(8,128)(2,1)S(1)} %get-tuple-element.54), channel_id=1, source_target_pairs={{0,128},{64,192},{128,0},{192,64},{1,129},{65,193},{129,1},{193,65... | collective-permute-start | bytes 73736 | tf_op jit(solution)/shard_map/ppermute | solution.py:43
  33.2 0.0 collective-permute-done.4.got1
  33.2 0.0 collective-permute-done.5.got2
  33.2 2.2 %collective-permute-done.6.got3 = bf16[48,256]{1,0:T(8,128)(2,1)S(1)} collective-permute-done((bf16[48,256]{1,0:T(8,128)(2,1)S(1)}, bf16[48,256]{1,0:T(8,128)(2,1)S(1)}, u32[]{:S(2)}, u32[]{:S(2)}) %collective-permute-start.6) | collective-permute-done | bytes 24608 | tf_op jit(solution)/shard_map/ppermute | solution.py:43
  35.4 0.4 filter.1
  35.8 4.4 %collective-permute-start.9 = (bf16[32,256]{1,0:T(8,128)(2,1)S(1)}, bf16[32,256]{1,0:T(8,128)(2,1)S(1)}, u32[]{:S(2)}, u32[]{:S(2)}) collective-permute-start(bf16[32,256]{1,0:T(8,128)(2,1)S(1)} %get-tuple-element.56.piece), channel_id=1, source_target_pairs={{0,128},{64,192},{128,0},{192,64},{1,129},{65,193},{129,1},{193,65... | collective-permute-start | bytes 49160 | tf_op jit(solution)/shard_map/ppermute | solution.py:43
  40.3 0.0 collective-permute-start.8
  40.3 3.6 %collective-permute-start.7 = (bf16[32,256]{1,0:T(8,128)(2,1)S(1)}, bf16[32,256]{1,0:T(8,128)(2,1)S(1)}, u32[]{:S(2)}, u32[]{:S(2)}) collective-permute-start(bf16[32,256]{1,0:T(8,128)(2,1)S(1)} %get-tuple-element.56.piece), channel_id=1, source_target_pairs={{0,192},{64,0},{128,64},{192,128},{1,193},{65,1},{129,65},{193,129... | collective-permute-start | bytes 49160 | tf_op jit(solution)/shard_map/ppermute | solution.py:43
  43.8 1.3 %collective-permute-done.8.rest_1_ = bf16[32,256]{1,0:T(8,128)(2,1)S(1)} collective-permute-done((bf16[32,256]{1,0:T(8,128)(2,1)S(1)}, bf16[32,256]{1,0:T(8,128)(2,1)S(1)}, u32[]{:S(2)}, u32[]{:S(2)}) %collective-permute-start.8) | collective-permute-done | bytes 16416 | tf_op jit(solution)/shard_map/ppermute | solution.py:43
  45.1 1.6 %collective-permute-start.12 = (bf16[128,256]{1,0:T(8,128)(2,1)S(1)}, bf16[128,256]{1,0:T(8,128)(2,1)S(1)}, u32[]{:S(2)}, u32[]{:S(2)}) collective-permute-start(bf16[128,256]{1,0:T(8,128)(2,1)S(1)} %join.2.piece), channel_id=1, source_target_pairs={{0,32},{16,48},{32,0},{48,16},{1,33},{17,49},{33,1},{49,17},{2,34}... | collective-permute-start | bytes 196616 | tf_op jit(solution)/shard_map/ppermute | solution.py:43
  46.7 0.3 collective-permute-start.11
  47.0 2.4 %collective-permute-start.10 = (bf16[128,256]{1,0:T(8,128)(2,1)S(1)}, bf16[128,256]{1,0:T(8,128)(2,1)S(1)}, u32[]{:S(2)}, u32[]{:S(2)}) collective-permute-start(bf16[128,256]{1,0:T(8,128)(2,1)S(1)} %join.2.piece), channel_id=1, source_target_pairs={{0,48},{16,0},{32,16},{48,32},{1,49},{17,1},{33,17},{49,33},{2,50}... | collective-permute-start | bytes 196616 | tf_op jit(solution)/shard_map/ppermute | solution.py:43
  49.4 0.4 collective-permute-done.12.rest_2_
  49.8 1.2 %collective-permute-done.11.rest_1_ = bf16[128,256]{1,0:T(8,128)(2,1)S(1)} collective-permute-done((bf16[128,256]{1,0:T(8,128)(2,1)S(1)}, bf16[128,256]{1,0:T(8,128)(2,1)S(1)}, u32[]{:S(2)}, u32[]{:S(2)}) %collective-permute-start.11) | collective-permute-done | bytes 65568 | tf_op jit(solution)/shard_map/ppermute | solution.py:43
  51.0 0.0 collective-permute-done.10.rest_0_
  51.1 6.2 %collective-permute-start.13 = (bf16[512,256]{1,0:T(8,128)(2,1)S(1)}, bf16[512,256]{1,0:T(8,128)(2,1)S(1)}, u32[]{:S(2)}, u32[]{:S(2)}) collective-permute-start(bf16[512,256]{1,0:T(8,128)(2,1)S(1)} %join.3.src), channel_id=1, source_target_pairs={{0,8},{8,0},{1,9},{9,1},{2,10},{10,2},{3,11},{11,3},{4,12},{12,4},... | collective-permute-start | bytes 786440 | tf_op jit(solution)/shard_map/ppermute | solution.py:43
  57.3 2.7 %near_field.1.part = f32[128,4096]{1,0:T(8,128)S(1)} custom-call(bf16[512,256]{1,0:T(8,128)(2,1)S(1)} %join.3.src, bf16[1024,4096]{1,0:T(8,128)(2,1)S(1)} %get-tuple-element.58.basis), custom_call_target="tpu_custom_call" | custom-call | flops 1073741824 | bytes 1048576 | tf_op jit(solution)/shard_map/near_field/pallas_call | solution.py:318
  60.0 0.0 collective-permute-done.13.src
  60.0 0.1 turned.1.f
  60.2 0.5 synthesis.3
  60.7 3.0 %collective-permute-start.14 = (bf16[128,512]{1,0:T(8,128)(2,1)S(1)}, bf16[128,512]{1,0:T(8,128)(2,1)S(1)}, u32[]{:S(2)}, u32[]{:S(2)}) collective-permute-start(bf16[128,512]{1,0:T(8,128)(2,1)S(1)} %get-tuple-element.59), channel_id=1, source_target_pairs={{0,4},{1,5},{2,6},{3,7},{4,0},{5,1},{6,2},{7,3},{8,12},{9,13},{10,... | collective-permute-start | bytes 393224 | tf_op jit(solution)/shard_map/ppermute | solution.py:43
  63.7 0.9 %collective-permute-start.15 = (bf16[128,512]{1,0:T(8,128)(2,1)S(1)}, bf16[128,512]{1,0:T(8,128)(2,1)S(1)}, u32[]{:S(2)}, u32[]{:S(2)}) collective-permute-start(bf16[128,512]{1,0:T(8,128)(2,1)S(1)} %get-tuple-element.60), channel_id=1, source_target_pairs={{0,3},{1,4},{2,5},{3,6},{4,7},{5,0},{6,1},{7,2},{8,11},{9,12},{10,... | collective-permute-start | bytes 393224 | tf_op jit(solution)/shard_map/ppermute | solution.py:43
  64.5 0.6 synthesis.4
  65.2 0.6 synthesis.5
  65.8 0.4 collective-permute-start.19
  66.3 3.2 %collective-permute-start.20 = (bf16[128,512]{1,0:T(8,128)(2,1)S(1)}, bf16[128,512]{1,0:T(8,128)(2,1)S(1)}, u32[]{:S(2)}, u32[]{:S(2)}) collective-permute-start(bf16[128,512]{1,0:T(8,128)(2,1)S(1)} %get-tuple-element.69), channel_id=1, source_target_pairs={{0,7},{1,0},{2,1},{3,2},{4,3},{5,4},{6,5},{7,6},{8,15},{9,8},{10,9... | collective-permute-start | bytes 393224 | tf_op jit(solution)/shard_map/ppermute | solution.py:43
  69.5 0.8 %collective-permute-start.16 = (bf16[128,512]{1,0:T(8,128)(2,1)S(1)}, bf16[128,512]{1,0:T(8,128)(2,1)S(1)}, u32[]{:S(2)}, u32[]{:S(2)}) collective-permute-start(bf16[128,512]{1,0:T(8,128)(2,1)S(1)} %get-tuple-element.63), channel_id=1, source_target_pairs={{0,5},{1,6},{2,7},{3,0},{4,1},{5,2},{6,3},{7,4},{8,13},{9,14},{10,... | collective-permute-start | bytes 393224 | tf_op jit(solution)/shard_map/ppermute | solution.py:43
  70.3 1.7 %collective-permute-done.14.rest_0_ = bf16[128,512]{1,0:T(8,128)(2,1)S(1)} collective-permute-done((bf16[128,512]{1,0:T(8,128)(2,1)S(1)}, bf16[128,512]{1,0:T(8,128)(2,1)S(1)}, u32[]{:S(2)}, u32[]{:S(2)}) %collective-permute-start.14) | collective-permute-done | bytes 131104 | tf_op jit(solution)/shard_map/ppermute | solution.py:43
  72.1 2.7 %collective-permute-start.18 = (bf16[128,512]{1,0:T(8,128)(2,1)S(1)}, bf16[128,512]{1,0:T(8,128)(2,1)S(1)}, u32[]{:S(2)}, u32[]{:S(2)}) collective-permute-start(bf16[128,512]{1,0:T(8,128)(2,1)S(1)} %get-tuple-element.65), channel_id=1, source_target_pairs={{0,6},{1,7},{2,0},{3,1},{4,2},{5,3},{6,4},{7,5},{8,14},{9,15},{10,... | collective-permute-start | bytes 393224 | tf_op jit(solution)/shard_map/ppermute | solution.py:43
  74.7 0.0 collective-permute-done.19.rest_5_
  74.7 0.0 collective-permute-done.20.rest_6_
  74.7 3.0 %collective-permute-done.16.rest_2_ = bf16[128,512]{1,0:T(8,128)(2,1)S(1)} collective-permute-done((bf16[128,512]{1,0:T(8,128)(2,1)S(1)}, bf16[128,512]{1,0:T(8,128)(2,1)S(1)}, u32[]{:S(2)}, u32[]{:S(2)}) %collective-permute-start.16) | collective-permute-done | bytes 131104 | tf_op jit(solution)/shard_map/ppermute | solution.py:43
  77.7 3.4 %collective-permute-done.18.rest_4_ = bf16[128,512]{1,0:T(8,128)(2,1)S(1)} collective-permute-done((bf16[128,512]{1,0:T(8,128)(2,1)S(1)}, bf16[128,512]{1,0:T(8,128)(2,1)S(1)}, u32[]{:S(2)}, u32[]{:S(2)}) %collective-permute-start.18) | collective-permute-done | bytes 131104 | tf_op jit(solution)/shard_map/ppermute | solution.py:43
  81.1 0.9 %finish.1 = bf16[512,128]{1,0:T(8,128)(2,1)} custom-call(f32[8,128]{1,0:T(8,128)S(1)} %get-tuple-element.55.total, f32[512,128]{1,0:T(8,128)S(1)} %get-tuple-element.43.given.linear, bf16[128,512]{1,0:T(8,128)(2,1)S(1)} %collective-permute-done.14.rest_0_, bf16[128,512]{1,0:T(8,128)(2,1)S(1)} %collective-permute-done.15.rest_1_, ...), custom_call_target="tpu_custom_call" | custom-call | bytes 1048576 | tf_op jit(solution)/shard_map/finish/pallas_call | solution.py:333
  (10 shorter events, 0.0 us)
Async XLA Ops:
  8.9 7.9 %collective-permute-start = (bf16[1040,128]{1,0:T(8,128)(2,1)S(1)}, bf16[1040,128]{1,0:T(8,128)(2,1)S(1)}, u32[]{:S(2)}, u32[]{:S(2)}) collective-permute-start(bf16[1040,128]{1,0:T(8,128)(2,1)S(1)} %get-tuple-element.46), channel_id=1, source_target_pairs={{0,8},{8,0},{1,9},{9,1},{2,10},{10,2},{3,11},{11,3},{4,12},{12,4},... | collective-permute-start | bytes 798728 | tf_op jit(solution)/shard_map/ppermute | solution.py:43
  16.9 5.0 %collective-permute-start.1 = (bf16[272,128]{1,0:T(8,128)(2,1)S(1)}, bf16[272,128]{1,0:T(8,128)(2,1)S(1)}, u32[]{:S(2)}, u32[]{:S(2)}) collective-permute-start(bf16[272,128]{1,0:T(8,128)(2,1)S(1)} %get-tuple-element.48), channel_id=1, source_target_pairs={{0,16},{16,32},{32,48},{48,0},{1,17},{17,33},{33,49},{49,1},{2,18}... | collective-permute-start | bytes 208904 | tf_op jit(solution)/shard_map/ppermute | solution.py:43
  16.9 5.6 %collective-permute-start.2 = (bf16[272,128]{1,0:T(8,128)(2,1)S(1)}, bf16[272,128]{1,0:T(8,128)(2,1)S(1)}, u32[]{:S(2)}, u32[]{:S(2)}) collective-permute-start(bf16[272,128]{1,0:T(8,128)(2,1)S(1)} %get-tuple-element.49), channel_id=1, source_target_pairs={{0,48},{16,0},{32,16},{48,32},{1,49},{17,1},{33,17},{49,33},{2,50}... | collective-permute-start | bytes 208904 | tf_op jit(solution)/shard_map/ppermute | solution.py:43
  19.6 4.7 %collective-permute-start.3 = (bf16[272,128]{1,0:T(8,128)(2,1)S(1)}, bf16[272,128]{1,0:T(8,128)(2,1)S(1)}, u32[]{:S(2)}, u32[]{:S(2)}) collective-permute-start(bf16[272,128]{1,0:T(8,128)(2,1)S(1)} %get-tuple-element.50), channel_id=1, source_target_pairs={{0,32},{16,48},{32,0},{48,16},{1,33},{17,49},{33,1},{49,17},{2,34}... | collective-permute-start | bytes 208904 | tf_op jit(solution)/shard_map/ppermute | solution.py:43
  19.6 15.8 %copy-start = (bf16[32,2,128,128]{3,2,1,0:T(8,128)(2,1)S(1)}, bf16[32,2,128,128]{3,2,1,0:T(8,128)(2,1)}, u32[]{:S(2)}) copy-start(bf16[32,2,128,128]{3,2,1,0:T(8,128)(2,1)} %weight.1) | copy-start | bytes 6291460
  24.4 8.8 %collective-permute-start.4 = (bf16[48,256]{1,0:T(8,128)(2,1)S(1)}, bf16[48,256]{1,0:T(8,128)(2,1)S(1)}, u32[]{:S(2)}, u32[]{:S(2)}) collective-permute-start(bf16[48,256]{1,0:T(8,128)(2,1)S(1)} %get-tuple-element.52), channel_id=1, source_target_pairs={{0,64},{64,128},{128,192},{192,0},{1,65},{65,129},{129,193},{193,1... | collective-permute-start | bytes 73736 | tf_op jit(solution)/shard_map/ppermute | solution.py:43
  25.7 7.5 %collective-permute-start.5 = (bf16[48,256]{1,0:T(8,128)(2,1)S(1)}, bf16[48,256]{1,0:T(8,128)(2,1)S(1)}, u32[]{:S(2)}, u32[]{:S(2)}) collective-permute-start(bf16[48,256]{1,0:T(8,128)(2,1)S(1)} %get-tuple-element.53), channel_id=1, source_target_pairs={{0,192},{64,0},{128,64},{192,128},{1,193},{65,1},{129,65},{193,129... | collective-permute-start | bytes 73736 | tf_op jit(solution)/shard_map/ppermute | solution.py:43
  28.8 6.6 %collective-permute-start.6 = (bf16[48,256]{1,0:T(8,128)(2,1)S(1)}, bf16[48,256]{1,0:T(8,128)(2,1)S(1)}, u32[]{:S(2)}, u32[]{:S(2)}) collective-permute-start(bf16[48,256]{1,0:T(8,128)(2,1)S(1)} %get-tuple-element.54), channel_id=1, source_target_pairs={{0,128},{64,192},{128,0},{192,64},{1,129},{65,193},{129,1},{193,65... | collective-permute-start | bytes 73736 | tf_op jit(solution)/shard_map/ppermute | solution.py:43
  35.8 8.0 %collective-permute-start.9 = (bf16[32,256]{1,0:T(8,128)(2,1)S(1)}, bf16[32,256]{1,0:T(8,128)(2,1)S(1)}, u32[]{:S(2)}, u32[]{:S(2)}) collective-permute-start(bf16[32,256]{1,0:T(8,128)(2,1)S(1)} %get-tuple-element.56.piece), channel_id=1, source_target_pairs={{0,128},{64,192},{128,0},{192,64},{1,129},{65,193},{129,1},{193,65... | collective-permute-start | bytes 49160 | tf_op jit(solution)/shard_map/ppermute | solution.py:43
  40.3 4.8 %collective-permute-start.8 = (bf16[32,256]{1,0:T(8,128)(2,1)S(1)}, bf16[32,256]{1,0:T(8,128)(2,1)S(1)}, u32[]{:S(2)}, u32[]{:S(2)}) collective-permute-start(bf16[32,256]{1,0:T(8,128)(2,1)S(1)} %get-tuple-element.56.piece), channel_id=1, source_target_pairs={{0,64},{64,128},{128,192},{192,0},{1,65},{65,129},{129,193},{193,1... | collective-permute-start | bytes 49160 | tf_op jit(solution)/shard_map/ppermute | solution.py:43
  40.3 4.8 %collective-permute-start.7 = (bf16[32,256]{1,0:T(8,128)(2,1)S(1)}, bf16[32,256]{1,0:T(8,128)(2,1)S(1)}, u32[]{:S(2)}, u32[]{:S(2)}) collective-permute-start(bf16[32,256]{1,0:T(8,128)(2,1)S(1)} %get-tuple-element.56.piece), channel_id=1, source_target_pairs={{0,192},{64,0},{128,64},{192,128},{1,193},{65,1},{129,65},{193,129... | collective-permute-start | bytes 49160 | tf_op jit(solution)/shard_map/ppermute | solution.py:43
  45.1 4.7 %collective-permute-start.12 = (bf16[128,256]{1,0:T(8,128)(2,1)S(1)}, bf16[128,256]{1,0:T(8,128)(2,1)S(1)}, u32[]{:S(2)}, u32[]{:S(2)}) collective-permute-start(bf16[128,256]{1,0:T(8,128)(2,1)S(1)} %join.2.piece), channel_id=1, source_target_pairs={{0,32},{16,48},{32,0},{48,16},{1,33},{17,49},{33,1},{49,17},{2,34}... | collective-permute-start | bytes 196616 | tf_op jit(solution)/shard_map/ppermute | solution.py:43
  46.7 4.3 %collective-permute-start.11 = (bf16[128,256]{1,0:T(8,128)(2,1)S(1)}, bf16[128,256]{1,0:T(8,128)(2,1)S(1)}, u32[]{:S(2)}, u32[]{:S(2)}) collective-permute-start(bf16[128,256]{1,0:T(8,128)(2,1)S(1)} %join.2.piece), channel_id=1, source_target_pairs={{0,16},{16,32},{32,48},{48,0},{1,17},{17,33},{33,49},{49,1},{2,18}... | collective-permute-start | bytes 196616 | tf_op jit(solution)/shard_map/ppermute | solution.py:43
  47.0 4.0 %collective-permute-start.10 = (bf16[128,256]{1,0:T(8,128)(2,1)S(1)}, bf16[128,256]{1,0:T(8,128)(2,1)S(1)}, u32[]{:S(2)}, u32[]{:S(2)}) collective-permute-start(bf16[128,256]{1,0:T(8,128)(2,1)S(1)} %join.2.piece), channel_id=1, source_target_pairs={{0,48},{16,0},{32,16},{48,32},{1,49},{17,1},{33,17},{49,33},{2,50}... | collective-permute-start | bytes 196616 | tf_op jit(solution)/shard_map/ppermute | solution.py:43
  51.1 9.0 %collective-permute-start.13 = (bf16[512,256]{1,0:T(8,128)(2,1)S(1)}, bf16[512,256]{1,0:T(8,128)(2,1)S(1)}, u32[]{:S(2)}, u32[]{:S(2)}) collective-permute-start(bf16[512,256]{1,0:T(8,128)(2,1)S(1)} %join.3.src), channel_id=1, source_target_pairs={{0,8},{8,0},{1,9},{9,1},{2,10},{10,2},{3,11},{11,3},{4,12},{12,4},... | collective-permute-start | bytes 786440 | tf_op jit(solution)/shard_map/ppermute | solution.py:43
  60.7 11.4 %collective-permute-start.14 = (bf16[128,512]{1,0:T(8,128)(2,1)S(1)}, bf16[128,512]{1,0:T(8,128)(2,1)S(1)}, u32[]{:S(2)}, u32[]{:S(2)}) collective-permute-start(bf16[128,512]{1,0:T(8,128)(2,1)S(1)} %get-tuple-element.59), channel_id=1, source_target_pairs={{0,4},{1,5},{2,6},{3,7},{4,0},{5,1},{6,2},{7,3},{8,12},{9,13},{10,... | collective-permute-start | bytes 393224 | tf_op jit(solution)/shard_map/ppermute | solution.py:43
  63.7 8.4 %collective-permute-start.15 = (bf16[128,512]{1,0:T(8,128)(2,1)S(1)}, bf16[128,512]{1,0:T(8,128)(2,1)S(1)}, u32[]{:S(2)}, u32[]{:S(2)}) collective-permute-start(bf16[128,512]{1,0:T(8,128)(2,1)S(1)} %get-tuple-element.60), channel_id=1, source_target_pairs={{0,3},{1,4},{2,5},{3,6},{4,7},{5,0},{6,1},{7,2},{8,11},{9,12},{10,... | collective-permute-start | bytes 393224 | tf_op jit(solution)/shard_map/ppermute | solution.py:43
  65.8 8.9 %collective-permute-start.19 = (bf16[128,512]{1,0:T(8,128)(2,1)S(1)}, bf16[128,512]{1,0:T(8,128)(2,1)S(1)}, u32[]{:S(2)}, u32[]{:S(2)}) collective-permute-start(bf16[128,512]{1,0:T(8,128)(2,1)S(1)} %get-tuple-element.68), channel_id=1, source_target_pairs={{0,1},{1,2},{2,3},{3,4},{4,5},{5,6},{6,7},{7,0},{8,9},{9,10},{10,1... | collective-permute-start | bytes 393224 | tf_op jit(solution)/shard_map/ppermute | solution.py:43
  66.3 8.5 %collective-permute-start.20 = (bf16[128,512]{1,0:T(8,128)(2,1)S(1)}, bf16[128,512]{1,0:T(8,128)(2,1)S(1)}, u32[]{:S(2)}, u32[]{:S(2)}) collective-permute-start(bf16[128,512]{1,0:T(8,128)(2,1)S(1)} %get-tuple-element.69), channel_id=1, source_target_pairs={{0,7},{1,0},{2,1},{3,2},{4,3},{5,4},{6,5},{7,6},{8,15},{9,8},{10,9... | collective-permute-start | bytes 393224 | tf_op jit(solution)/shard_map/ppermute | solution.py:43
  69.5 8.2 %collective-permute-start.16 = (bf16[128,512]{1,0:T(8,128)(2,1)S(1)}, bf16[128,512]{1,0:T(8,128)(2,1)S(1)}, u32[]{:S(2)}, u32[]{:S(2)}) collective-permute-start(bf16[128,512]{1,0:T(8,128)(2,1)S(1)} %get-tuple-element.63), channel_id=1, source_target_pairs={{0,5},{1,6},{2,7},{3,0},{4,1},{5,2},{6,3},{7,4},{8,13},{9,14},{10,... | collective-permute-start | bytes 393224 | tf_op jit(solution)/shard_map/ppermute | solution.py:43
  72.0 5.7 %collective-permute-start.17 = (bf16[128,512]{1,0:T(8,128)(2,1)S(1)}, bf16[128,512]{1,0:T(8,128)(2,1)S(1)}, u32[]{:S(2)}, u32[]{:S(2)}) collective-permute-start(bf16[128,512]{1,0:T(8,128)(2,1)S(1)} %get-tuple-element.64), channel_id=1, source_target_pairs={{0,2},{1,3},{2,4},{3,5},{4,6},{5,7},{6,0},{7,1},{8,10},{9,11},{10,... | collective-permute-start | bytes 393224 | tf_op jit(solution)/shard_map/ppermute | solution.py:43
  72.1 9.1 %collective-permute-start.18 = (bf16[128,512]{1,0:T(8,128)(2,1)S(1)}, bf16[128,512]{1,0:T(8,128)(2,1)S(1)}, u32[]{:S(2)}, u32[]{:S(2)}) collective-permute-start(bf16[128,512]{1,0:T(8,128)(2,1)S(1)} %get-tuple-element.65), channel_id=1, source_target_pairs={{0,6},{1,7},{2,0},{3,1},{4,2},{5,3},{6,4},{7,5},{8,14},{9,15},{10,... | collective-permute-start | bytes 393224 | tf_op jit(solution)/shard_map/ppermute | solution.py:43

commit v6 on v5

--- a/solution.py
+++ b/solution.py
@@ -240,24 +240,30 @@
 
 def near_field_body(src, basis, part, f):
     turned_body(src, f)
-
-    @pl.loop(0, 8)
-    def _(k):
-        at = pl.ds(pl.multiple_of(k * 512, 512), 512)
+    for k in range(8):
+        at = pl.ds(k * 512, 512)
         part[:, at] = jnp.dot(f[...], basis[:, at], preferred_element_type=F32)
 
 
-def synthesis_body(shifts, f, basis, part, *outs):
-    group = lax.axis_index("y") * 2 + lax.axis_index("z_lo")
-    for s, out in zip(shifts, outs[: len(shifts)], strict=True):
-        at = pl.ds(pl.multiple_of(lax.rem(group + s, 8) * 512, 512), 512)
-        out[...] = (part[:, at] + jnp.dot(f[...], basis[:, at], preferred_element_type=F32)).astype(BF)
-
-
-def finish_body(total, linear, *rest):
+def synthesis_body(flip, steps, f, basis, part, out, *_):
+    y, z_lo = lax.axis_index("y"), lax.axis_index("z_lo")
+    for i, dy in enumerate(steps):
+        owner = lax.rem(y + dy, 4) * 2 + lax.rem(z_lo + flip, 2)
+        at = pl.ds(pl.multiple_of(owner * 512, 512), 512)
+        value = part[:, at] + jnp.dot(f[...], basis[:, at], preferred_element_type=F32)
+        out[pl.ds(i * C, C), :] = value.astype(out.dtype)
+
+
+def merge_body(own, got, *outs):
+    for i, out in enumerate(outs):
+        rows = pl.ds(i * C, C)
+        out[...] = (own[rows, :] + got[rows, :].astype(F32)).astype(BF)
+
+
+def finish_body(total, linear, own, got, *rest):
     *blocks, out = rest
-    summed = blocks[0][...].astype(F32)
-    for b in blocks[1:]:
+    summed = own[pl.ds(3 * C, C), :] + got[...].astype(F32)
+    for b in blocks:
         summed = summed + b[...].astype(F32)
     scaled = summed / total[0:1, 0:1]
     for k in range(4):
@@ -319,18 +325,23 @@
         near_field_body, 2, pltpu.VMEM((C, pts), F32), "near_field", [pltpu.VMEM((C, 8 * C), BF)], flops=4 * slab
     )(piece, basis)
     f = call(turned_body, 1, one(C, 8 * C, BF), "turned")(other)
-    fields = []
-    for shifts in ((4, 3), (5, 2, 6), (1, 7, 0)):
-        count = len(shifts)
-        chain = [pltpu.VMEM(v.shape, v.dtype) for v in (far_basis, part)] if 0 not in shifts else []
-        outs = call(
-            functools.partial(synthesis_body, shifts), 3, [one(C, 512, BF)] * count + chain, "synthesis",
-            flops=count * slab // 2, aliases={1: count, 2: count + 1} if chain else {},
-        )(f, far_basis, part)
-        if chain:
-            far_basis, part = outs[count:]
-        fields += [send(o, GRP, s) if s else o for s, o in zip(shifts, outs)]
-    return call(finish_body, 10, one(pts // 8, C, BF), "finish")(total, linear, *fields)
+    steps = (*FAR_LAST, 0)
+
+    def field(flip, steps, dtype, basis, part, last=False):
+        chain = [] if last else [pltpu.VMEM(v.shape, v.dtype) for v in (basis, part)]
+        return call(
+            functools.partial(synthesis_body, flip, steps), 3, [one(len(steps) * C, 512, dtype)] + chain, "synthesis",
+            flops=len(steps) * slab // 2, aliases={1: 1, 2: 2} if chain else {},
+        )(f, basis, part)
+
+    out, far_basis, part = field(1, steps[:3], BF, far_basis, part)
+    got0 = send(out, ("z_lo",), 1)
+    out, far_basis, part = field(1, steps[3:], BF, far_basis, part)
+    got1 = send(out, ("z_lo",), 1)
+    (own,) = field(0, steps, F32, far_basis, part, True)
+    outs = call(merge_body, 2, [one(C, 512, BF)] * 3, "merge")(own, got0)
+    fields = [send(o, ("y",), s) for o, s in zip(outs, steps)]
+    return call(finish_body, 7, one(pts // 8, C, BF), "finish")(total, linear, own, got1, *fields)
 
 
 def solution(mesh):

time: 82.1 us -> 81.9 us (level); the launches traced: 82 us -> 80.6 us
  starting transfers between devices: 44.5 us -> 39.6 us
  waiting for transfers between devices: 16.1 us -> 20.9 us
  Pallas kernels: 21.4 us -> 20 us
    ppermute x21 -> x19, starting transfers between devices: 44.5 us -> 39.6 us  [send(): return lax.ppermute(value, axes, [(j, (j + shift) % n) for j in range(n)])]
    ppermute x21 -> x19, waiting for transfers between devices: 16.1 us -> 20.9 us  [send(): return lax.ppermute(value, axes, [(j, (j + shift) % n) for j in range(n)])]
    pallas_call x1, Pallas kernels: 2.69 us -> 1.37 us  [on_device(): call(near_field_body, 2, pltpu.VMEM((C, pts), F32), 'near_field', [pltpu....]
    pallas_call x4 -> x5, Pallas kernels: 2.64 us -> 2.63 us  [the longest x3 1.72 us: field(): call(functools.partial(synthesis_body, flip, steps), 3, [one(len(steps) *...]
  transfers between devices with their start and end apart: 21 -> 19, of which waited for: 10 -> 10; matrix products, arithmetic and copies ran while one was open for 0% -> 0% of each run, Pallas kernels for 13% -> 11%
where the time goes in v6:
time: 81.9 us; the launch traced here: 80.6 us
  starting transfers between devices  39.6 us (48%)
  waiting for transfers between devices  20.9 us (26%)
  Pallas kernels  20 us (24%)
    ppermute x19, starting transfers between devices, send(): return lax.ppermute(value, axes, [(j, (j + shift) % n) for j in range(n)])  39.6 us
    ppermute x19, waiting for transfers between devices, send(): return lax.ppermute(value, axes, [(j, (j + shift) % n) for j in range(n)])  20.9 us
    pallas_call x1, Pallas kernels, on_device(): call(first_body, 0, [pltpu.VMEM((8 * C + 16, C), BF), pltpu.VMEM((8 * C,...  8.85 us
    pallas_call x2, Pallas kernels, near(): call(functools.partial(near_body, count, first), 4, [pltpu.VMEM((count *...  6.43 us
    pallas_call x3, Pallas kernels, field(): call(functools.partial(synthesis_body, flip, steps), 3, [one(len(steps) *...  1.72 us
  transfers between devices with their start and end apart: 19, of which 10 were waited for; matrix products, arithmetic and copies ran while one was open for 0% of the time, Pallas kernels for 11%

profile of v6, /device:TPU:1, one launch (start us, length us, event | category | flops | bytes accessed | tf_op | source)
XLA Modules:
  0.0 80.6 jit_solution(16102865435865238718)
XLA Ops:
  0.0 8.9 %first.1 = (bf16[1040,128]{1,0:T(8,128)(2,1)S(1)}, bf16[1024,4096]{1,0:T(8,128)(2,1)S(1)}, f32[256,2,32,128]{3,2,1,0:T(8,128)S(1)}, f32[32,2,32,128]{3,2,1,0:T(8...) custom-call(f32[3,4096]{1,0:T(4,128)} %refs_0_.1, ...), custom_call_target="tpu_custom_call" | custom-call | flops 2147483648 | bytes 1048576 | tf_op jit(solution)/shard_map/first/pallas_call | solution.py:293
  8.9 3.3 %collective-permute-start = (bf16[1040,128]{1,0:T(8,128)(2,1)S(1)}, bf16[1040,128]{1,0:T(8,128)(2,1)S(1)}, u32[]{:S(2)}, u32[]{:S(2)}) collective-permute-start(bf16[1040,128]{1,0:T(8,128)(2,1)S(1)} %get-tuple-element.43), channel_id=1, source_target_pairs={{0,8},{8,0},{1,9},{9,1},{2,10},{10,2},{3,11},{11,3},{4,12},{12,4},... | collective-permute-start | bytes 798728 | tf_op jit(solution)/shard_map/ppermute | solution.py:43
  12.2 4.6 %near.2 = (bf16[784,128]{1,0:T(8,128)(2,1)S(1)}, bf16[1024,4096]{1,0:T(8,128)(2,1)S(1)}) custom-call(s32[8,128]{1,0:T(8,128)S(1)} %get-tuple-element.35.index, f32[32,128]{1,0:T(8,128)S(1)} %get-tuple-element.36.quad, f32[256,2,32,128]{3,2,1,0:T(8,128)S(1)} %get-tuple-element.37.exy, f32[32,2,32,128]{3,2,1,0:T(8,128)S(1)} %get-tuple-element.38.ez, ...), custom_call_target="tpu_custom_call" | custom-call | flops 1610612736 | bytes 1048576 | tf_op jit(solution)/shard_map/near/pallas_call | solution.py:306
  16.8 0.0 collective-permute-done.got.got0
  16.8 0.1 pair.1
  16.9 0.1 collective-permute-start.1
  16.9 2.7 %collective-permute-start.2 = (bf16[272,128]{1,0:T(8,128)(2,1)S(1)}, bf16[272,128]{1,0:T(8,128)(2,1)S(1)}, u32[]{:S(2)}, u32[]{:S(2)}) collective-permute-start(bf16[272,128]{1,0:T(8,128)(2,1)S(1)} %get-tuple-element.46), channel_id=1, source_target_pairs={{0,48},{16,0},{32,16},{48,32},{1,49},{17,1},{33,17},{49,33},{2,50}... | collective-permute-start | bytes 208904 | tf_op jit(solution)/shard_map/ppermute | solution.py:43
  19.6 0.0 collective-permute-start.3
  19.6 1.8 %near.3 = (bf16[272,128]{1,0:T(8,128)(2,1)S(1)}, bf16[1024,4096]{1,0:T(8,128)(2,1)S(1)}) custom-call(s32[8,128]{1,0:T(8,128)S(1)} %get-tuple-element.35.index, f32[32,128]{1,0:T(8,128)S(1)} %get-tuple-element.36.quad, f32[256,2,32,128]{3,2,1,0:T(8,128)S(1)} %get-tuple-element.37.exy, ...), custom_call_target="tpu_custom_call", output_to_operand_aliasing={{1}: (5, {})} | custom-call | flops 536870912 | bytes 1048576 | tf_op jit(solution)/shard_map/near/pallas_call | solution.py:306
  21.4 0.5 collective-permute-done.1.got1
  21.9 0.7 collective-permute-done.2.got2
  22.6 1.7 %collective-permute-done.3.got3 = bf16[272,128]{1,0:T(8,128)(2,1)S(1)} collective-permute-done((bf16[272,128]{1,0:T(8,128)(2,1)S(1)}, bf16[272,128]{1,0:T(8,128)(2,1)S(1)}, u32[]{:S(2)}, u32[]{:S(2)}) %collective-permute-start.3) | collective-permute-done | bytes 69664 | tf_op jit(solution)/shard_map/ppermute | solution.py:43
  24.3 0.1 x_sum.1
  24.4 1.3 %collective-permute-start.4 = (bf16[48,256]{1,0:T(8,128)(2,1)S(1)}, bf16[48,256]{1,0:T(8,128)(2,1)S(1)}, u32[]{:S(2)}, u32[]{:S(2)}) collective-permute-start(bf16[48,256]{1,0:T(8,128)(2,1)S(1)} %get-tuple-element.49), channel_id=1, source_target_pairs={{0,64},{64,128},{128,192},{192,0},{1,65},{65,129},{129,193},{193,1... | collective-permute-start | bytes 73736 | tf_op jit(solution)/shard_map/ppermute | solution.py:43
  25.7 3.1 %collective-permute-start.5 = (bf16[48,256]{1,0:T(8,128)(2,1)S(1)}, bf16[48,256]{1,0:T(8,128)(2,1)S(1)}, u32[]{:S(2)}, u32[]{:S(2)}) collective-permute-start(bf16[48,256]{1,0:T(8,128)(2,1)S(1)} %get-tuple-element.50), channel_id=1, source_target_pairs={{0,192},{64,0},{128,64},{192,128},{1,193},{65,1},{129,65},{193,129... | collective-permute-start | bytes 73736 | tf_op jit(solution)/shard_map/ppermute | solution.py:43
  28.8 4.4 %collective-permute-start.6 = (bf16[48,256]{1,0:T(8,128)(2,1)S(1)}, bf16[48,256]{1,0:T(8,128)(2,1)S(1)}, u32[]{:S(2)}, u32[]{:S(2)}) collective-permute-start(bf16[48,256]{1,0:T(8,128)(2,1)S(1)} %get-tuple-element.51), channel_id=1, source_target_pairs={{0,128},{64,192},{128,0},{192,64},{1,129},{65,193},{129,1},{193,65... | collective-permute-start | bytes 73736 | tf_op jit(solution)/shard_map/ppermute | solution.py:43
  33.2 0.0 collective-permute-done.4.got1
  33.2 0.0 collective-permute-done.5.got2
  33.2 2.2 %collective-permute-done.6.got3 = bf16[48,256]{1,0:T(8,128)(2,1)S(1)} collective-permute-done((bf16[48,256]{1,0:T(8,128)(2,1)S(1)}, bf16[48,256]{1,0:T(8,128)(2,1)S(1)}, u32[]{:S(2)}, u32[]{:S(2)}) %collective-permute-start.6) | collective-permute-done | bytes 24608 | tf_op jit(solution)/shard_map/ppermute | solution.py:43
  35.4 0.4 filter.1
  35.8 4.4 %collective-permute-start.9 = (bf16[32,256]{1,0:T(8,128)(2,1)S(1)}, bf16[32,256]{1,0:T(8,128)(2,1)S(1)}, u32[]{:S(2)}, u32[]{:S(2)}) collective-permute-start(bf16[32,256]{1,0:T(8,128)(2,1)S(1)} %get-tuple-element.53.piece), channel_id=1, source_target_pairs={{0,128},{64,192},{128,0},{192,64},{1,129},{65,193},{129,1},{193,65... | collective-permute-start | bytes 49160 | tf_op jit(solution)/shard_map/ppermute | solution.py:43
  40.3 0.0 collective-permute-start.8
  40.3 3.6 %collective-permute-start.7 = (bf16[32,256]{1,0:T(8,128)(2,1)S(1)}, bf16[32,256]{1,0:T(8,128)(2,1)S(1)}, u32[]{:S(2)}, u32[]{:S(2)}) collective-permute-start(bf16[32,256]{1,0:T(8,128)(2,1)S(1)} %get-tuple-element.53.piece), channel_id=1, source_target_pairs={{0,192},{64,0},{128,64},{192,128},{1,193},{65,1},{129,65},{193,129... | collective-permute-start | bytes 49160 | tf_op jit(solution)/shard_map/ppermute | solution.py:43
  43.8 1.3 %collective-permute-done.8.rest_1_ = bf16[32,256]{1,0:T(8,128)(2,1)S(1)} collective-permute-done((bf16[32,256]{1,0:T(8,128)(2,1)S(1)}, bf16[32,256]{1,0:T(8,128)(2,1)S(1)}, u32[]{:S(2)}, u32[]{:S(2)}) %collective-permute-start.8) | collective-permute-done | bytes 16416 | tf_op jit(solution)/shard_map/ppermute | solution.py:43
  45.1 1.6 %collective-permute-start.12 = (bf16[128,256]{1,0:T(8,128)(2,1)S(1)}, bf16[128,256]{1,0:T(8,128)(2,1)S(1)}, u32[]{:S(2)}, u32[]{:S(2)}) collective-permute-start(bf16[128,256]{1,0:T(8,128)(2,1)S(1)} %join.2.piece), channel_id=1, source_target_pairs={{0,32},{16,48},{32,0},{48,16},{1,33},{17,49},{33,1},{49,17},{2,34}... | collective-permute-start | bytes 196616 | tf_op jit(solution)/shard_map/ppermute | solution.py:43
  46.7 0.3 collective-permute-start.11
  47.0 2.4 %collective-permute-start.10 = (bf16[128,256]{1,0:T(8,128)(2,1)S(1)}, bf16[128,256]{1,0:T(8,128)(2,1)S(1)}, u32[]{:S(2)}, u32[]{:S(2)}) collective-permute-start(bf16[128,256]{1,0:T(8,128)(2,1)S(1)} %join.2.piece), channel_id=1, source_target_pairs={{0,48},{16,0},{32,16},{48,32},{1,49},{17,1},{33,17},{49,33},{2,50}... | collective-permute-start | bytes 196616 | tf_op jit(solution)/shard_map/ppermute | solution.py:43
  49.4 0.4 collective-permute-done.12.rest_2_
  49.8 1.2 %collective-permute-done.11.rest_1_ = bf16[128,256]{1,0:T(8,128)(2,1)S(1)} collective-permute-done((bf16[128,256]{1,0:T(8,128)(2,1)S(1)}, bf16[128,256]{1,0:T(8,128)(2,1)S(1)}, u32[]{:S(2)}, u32[]{:S(2)}) %collective-permute-start.11) | collective-permute-done | bytes 65568 | tf_op jit(solution)/shard_map/ppermute | solution.py:43
  51.0 0.0 collective-permute-done.10.rest_0_
  51.1 6.2 %collective-permute-start.13 = (bf16[512,256]{1,0:T(8,128)(2,1)S(1)}, bf16[512,256]{1,0:T(8,128)(2,1)S(1)}, u32[]{:S(2)}, u32[]{:S(2)}) collective-permute-start(bf16[512,256]{1,0:T(8,128)(2,1)S(1)} %join.3.src), channel_id=1, source_target_pairs={{0,8},{8,0},{1,9},{9,1},{2,10},{10,2},{3,11},{11,3},{4,12},{12,4},... | collective-permute-start | bytes 786440 | tf_op jit(solution)/shard_map/ppermute | solution.py:43
  57.3 1.4 %near_field.1.part = f32[128,4096]{1,0:T(8,128)S(1)} custom-call(bf16[512,256]{1,0:T(8,128)(2,1)S(1)} %join.3.src, bf16[1024,4096]{1,0:T(8,128)(2,1)S(1)} %get-tuple-element.55.basis), custom_call_target="tpu_custom_call" | custom-call | flops 1073741824 | bytes 1048576 | tf_op jit(solution)/shard_map/near_field/pallas_call | solution.py:324
  58.7 0.1 turned.1.f
  58.9 0.6 synthesis.3
  59.5 0.8 %collective-permute-start.15 = (bf16[384,512]{1,0:T(8,128)(2,1)S(1)}, bf16[384,512]{1,0:T(8,128)(2,1)S(1)}, u32[]{:S(2)}, u32[]{:S(2)}) collective-permute-start(bf16[384,512]{1,0:T(8,128)(2,1)S(1)} %get-tuple-element.61), channel_id=1, source_target_pairs={{0,1},{1,0},{2,3},{3,2},{4,5},{5,4},{6,7},{7,6},{8,9},{9,8},{10,11... | collective-permute-start | bytes 1179656 | tf_op jit(solution)/shard_map/ppermute | solution.py:43
  60.3 0.3 synthesis.4
  60.7 0.8 collective-permute-start.14
  61.5 0.8 synthesis.5.own
  62.2 7.9 %collective-permute-done.15.got = bf16[384,512]{1,0:T(8,128)(2,1)S(1)} collective-permute-done((bf16[384,512]{1,0:T(8,128)(2,1)S(1)}, bf16[384,512]{1,0:T(8,128)(2,1)S(1)}, u32[]{:S(2)}, u32[]{:S(2)}) %collective-permute-start.15) | collective-permute-done | bytes 393248 | tf_op jit(solution)/shard_map/ppermute | solution.py:43
  70.1 0.1 merge.1
  70.2 1.4 %collective-permute-start.16 = (bf16[128,512]{1,0:T(8,128)(2,1)S(1)}, bf16[128,512]{1,0:T(8,128)(2,1)S(1)}, u32[]{:S(2)}, u32[]{:S(2)}) collective-permute-start(bf16[128,512]{1,0:T(8,128)(2,1)S(1)} %get-tuple-element.62), channel_id=1, source_target_pairs={{0,2},{2,4},{4,6},{6,0},{1,3},{3,5},{5,7},{7,1},{8,10},{10,12},{12... | collective-permute-start | bytes 393224 | tf_op jit(solution)/shard_map/ppermute | solution.py:43
  71.6 1.5 %collective-permute-start.17 = (bf16[128,512]{1,0:T(8,128)(2,1)S(1)}, bf16[128,512]{1,0:T(8,128)(2,1)S(1)}, u32[]{:S(2)}, u32[]{:S(2)}) collective-permute-start(bf16[128,512]{1,0:T(8,128)(2,1)S(1)} %get-tuple-element.63), channel_id=1, source_target_pairs={{0,6},{2,0},{4,2},{6,4},{1,7},{3,1},{5,3},{7,5},{8,14},{10,8},{12,... | collective-permute-start | bytes 393224 | tf_op jit(solution)/shard_map/ppermute | solution.py:43
  73.1 1.6 %collective-permute-start.18 = (bf16[128,512]{1,0:T(8,128)(2,1)S(1)}, bf16[128,512]{1,0:T(8,128)(2,1)S(1)}, u32[]{:S(2)}, u32[]{:S(2)}) collective-permute-start(bf16[128,512]{1,0:T(8,128)(2,1)S(1)} %get-tuple-element.64), channel_id=1, source_target_pairs={{0,4},{2,6},{4,0},{6,2},{1,5},{3,7},{5,1},{7,3},{8,12},{10,14},{12... | collective-permute-start | bytes 393224 | tf_op jit(solution)/shard_map/ppermute | solution.py:43
  74.7 0.0 collective-permute-done.14.got
  74.7 0.7 collective-permute-done.16.rest_0_
  75.4 0.0 collective-permute-done.17.rest_1_
  75.4 4.4 %collective-permute-done.18.rest_2_ = bf16[128,512]{1,0:T(8,128)(2,1)S(1)} collective-permute-done((bf16[128,512]{1,0:T(8,128)(2,1)S(1)}, bf16[128,512]{1,0:T(8,128)(2,1)S(1)}, u32[]{:S(2)}, u32[]{:S(2)}) %collective-permute-start.18) | collective-permute-done | bytes 131104 | tf_op jit(solution)/shard_map/ppermute | solution.py:43
  79.8 0.8 %finish.1 = bf16[512,128]{1,0:T(8,128)(2,1)} custom-call(f32[8,128]{1,0:T(8,128)S(1)} %get-tuple-element.52.total, f32[512,128]{1,0:T(8,128)S(1)} %get-tuple-element.40.given.linear, f32[512,512]{1,0:T(8,128)S(1)} %synthesis.5.own, bf16[128,512]{1,0:T(8,128)(2,1)S(1)} %collective-permute-done.14.got, bf16[128,512]{1,0:T(8,128)(2,1)S(1)} %collective-permute-done.16.rest_0_, ...), custom_call_target="tpu_custom_call" | custom-call | bytes 1048576 | tf_op jit(solution)/shard_map/finish/pallas_call | solution.py:344
  (7 shorter events, 0.0 us)
Async XLA Ops:
  8.9 7.9 %collective-permute-start = (bf16[1040,128]{1,0:T(8,128)(2,1)S(1)}, bf16[1040,128]{1,0:T(8,128)(2,1)S(1)}, u32[]{:S(2)}, u32[]{:S(2)}) collective-permute-start(bf16[1040,128]{1,0:T(8,128)(2,1)S(1)} %get-tuple-element.43), channel_id=1, source_target_pairs={{0,8},{8,0},{1,9},{9,1},{2,10},{10,2},{3,11},{11,3},{4,12},{12,4},... | collective-permute-start | bytes 798728 | tf_op jit(solution)/shard_map/ppermute | solution.py:43
  16.9 5.0 %collective-permute-start.1 = (bf16[272,128]{1,0:T(8,128)(2,1)S(1)}, bf16[272,128]{1,0:T(8,128)(2,1)S(1)}, u32[]{:S(2)}, u32[]{:S(2)}) collective-permute-start(bf16[272,128]{1,0:T(8,128)(2,1)S(1)} %get-tuple-element.45), channel_id=1, source_target_pairs={{0,16},{16,32},{32,48},{48,0},{1,17},{17,33},{33,49},{49,1},{2,18}... | collective-permute-start | bytes 208904 | tf_op jit(solution)/shard_map/ppermute | solution.py:43
  16.9 5.6 %collective-permute-start.2 = (bf16[272,128]{1,0:T(8,128)(2,1)S(1)}, bf16[272,128]{1,0:T(8,128)(2,1)S(1)}, u32[]{:S(2)}, u32[]{:S(2)}) collective-permute-start(bf16[272,128]{1,0:T(8,128)(2,1)S(1)} %get-tuple-element.46), channel_id=1, source_target_pairs={{0,48},{16,0},{32,16},{48,32},{1,49},{17,1},{33,17},{49,33},{2,50}... | collective-permute-start | bytes 208904 | tf_op jit(solution)/shard_map/ppermute | solution.py:43
  19.6 4.7 %collective-permute-start.3 = (bf16[272,128]{1,0:T(8,128)(2,1)S(1)}, bf16[272,128]{1,0:T(8,128)(2,1)S(1)}, u32[]{:S(2)}, u32[]{:S(2)}) collective-permute-start(bf16[272,128]{1,0:T(8,128)(2,1)S(1)} %get-tuple-element.47), channel_id=1, source_target_pairs={{0,32},{16,48},{32,0},{48,16},{1,33},{17,49},{33,1},{49,17},{2,34}... | collective-permute-start | bytes 208904 | tf_op jit(solution)/shard_map/ppermute | solution.py:43
  19.6 15.8 %copy-start = (bf16[32,2,128,128]{3,2,1,0:T(8,128)(2,1)S(1)}, bf16[32,2,128,128]{3,2,1,0:T(8,128)(2,1)}, u32[]{:S(2)}) copy-start(bf16[32,2,128,128]{3,2,1,0:T(8,128)(2,1)} %weight.1) | copy-start | bytes 6291460
  24.4 8.8 %collective-permute-start.4 = (bf16[48,256]{1,0:T(8,128)(2,1)S(1)}, bf16[48,256]{1,0:T(8,128)(2,1)S(1)}, u32[]{:S(2)}, u32[]{:S(2)}) collective-permute-start(bf16[48,256]{1,0:T(8,128)(2,1)S(1)} %get-tuple-element.49), channel_id=1, source_target_pairs={{0,64},{64,128},{128,192},{192,0},{1,65},{65,129},{129,193},{193,1... | collective-permute-start | bytes 73736 | tf_op jit(solution)/shard_map/ppermute | solution.py:43
  25.7 7.5 %collective-permute-start.5 = (bf16[48,256]{1,0:T(8,128)(2,1)S(1)}, bf16[48,256]{1,0:T(8,128)(2,1)S(1)}, u32[]{:S(2)}, u32[]{:S(2)}) collective-permute-start(bf16[48,256]{1,0:T(8,128)(2,1)S(1)} %get-tuple-element.50), channel_id=1, source_target_pairs={{0,192},{64,0},{128,64},{192,128},{1,193},{65,1},{129,65},{193,129... | collective-permute-start | bytes 73736 | tf_op jit(solution)/shard_map/ppermute | solution.py:43
  28.8 6.6 %collective-permute-start.6 = (bf16[48,256]{1,0:T(8,128)(2,1)S(1)}, bf16[48,256]{1,0:T(8,128)(2,1)S(1)}, u32[]{:S(2)}, u32[]{:S(2)}) collective-permute-start(bf16[48,256]{1,0:T(8,128)(2,1)S(1)} %get-tuple-element.51), channel_id=1, source_target_pairs={{0,128},{64,192},{128,0},{192,64},{1,129},{65,193},{129,1},{193,65... | collective-permute-start | bytes 73736 | tf_op jit(solution)/shard_map/ppermute | solution.py:43
  35.8 8.0 %collective-permute-start.9 = (bf16[32,256]{1,0:T(8,128)(2,1)S(1)}, bf16[32,256]{1,0:T(8,128)(2,1)S(1)}, u32[]{:S(2)}, u32[]{:S(2)}) collective-permute-start(bf16[32,256]{1,0:T(8,128)(2,1)S(1)} %get-tuple-element.53.piece), channel_id=1, source_target_pairs={{0,128},{64,192},{128,0},{192,64},{1,129},{65,193},{129,1},{193,65... | collective-permute-start | bytes 49160 | tf_op jit(solution)/shard_map/ppermute | solution.py:43
  40.3 4.8 %collective-permute-start.8 = (bf16[32,256]{1,0:T(8,128)(2,1)S(1)}, bf16[32,256]{1,0:T(8,128)(2,1)S(1)}, u32[]{:S(2)}, u32[]{:S(2)}) collective-permute-start(bf16[32,256]{1,0:T(8,128)(2,1)S(1)} %get-tuple-element.53.piece), channel_id=1, source_target_pairs={{0,64},{64,128},{128,192},{192,0},{1,65},{65,129},{129,193},{193,1... | collective-permute-start | bytes 49160 | tf_op jit(solution)/shard_map/ppermute | solution.py:43
  40.3 4.8 %collective-permute-start.7 = (bf16[32,256]{1,0:T(8,128)(2,1)S(1)}, bf16[32,256]{1,0:T(8,128)(2,1)S(1)}, u32[]{:S(2)}, u32[]{:S(2)}) collective-permute-start(bf16[32,256]{1,0:T(8,128)(2,1)S(1)} %get-tuple-element.53.piece), channel_id=1, source_target_pairs={{0,192},{64,0},{128,64},{192,128},{1,193},{65,1},{129,65},{193,129... | collective-permute-start | bytes 49160 | tf_op jit(solution)/shard_map/ppermute | solution.py:43
  45.1 4.7 %collective-permute-start.12 = (bf16[128,256]{1,0:T(8,128)(2,1)S(1)}, bf16[128,256]{1,0:T(8,128)(2,1)S(1)}, u32[]{:S(2)}, u32[]{:S(2)}) collective-permute-start(bf16[128,256]{1,0:T(8,128)(2,1)S(1)} %join.2.piece), channel_id=1, source_target_pairs={{0,32},{16,48},{32,0},{48,16},{1,33},{17,49},{33,1},{49,17},{2,34}... | collective-permute-start | bytes 196616 | tf_op jit(solution)/shard_map/ppermute | solution.py:43
  46.7 4.3 %collective-permute-start.11 = (bf16[128,256]{1,0:T(8,128)(2,1)S(1)}, bf16[128,256]{1,0:T(8,128)(2,1)S(1)}, u32[]{:S(2)}, u32[]{:S(2)}) collective-permute-start(bf16[128,256]{1,0:T(8,128)(2,1)S(1)} %join.2.piece), channel_id=1, source_target_pairs={{0,16},{16,32},{32,48},{48,0},{1,17},{17,33},{33,49},{49,1},{2,18}... | collective-permute-start | bytes 196616 | tf_op jit(solution)/shard_map/ppermute | solution.py:43
  47.0 4.0 %collective-permute-start.10 = (bf16[128,256]{1,0:T(8,128)(2,1)S(1)}, bf16[128,256]{1,0:T(8,128)(2,1)S(1)}, u32[]{:S(2)}, u32[]{:S(2)}) collective-permute-start(bf16[128,256]{1,0:T(8,128)(2,1)S(1)} %join.2.piece), channel_id=1, source_target_pairs={{0,48},{16,0},{32,16},{48,32},{1,49},{17,1},{33,17},{49,33},{2,50}... | collective-permute-start | bytes 196616 | tf_op jit(solution)/shard_map/ppermute | solution.py:43
  51.1 7.6 %collective-permute-start.13 = (bf16[512,256]{1,0:T(8,128)(2,1)S(1)}, bf16[512,256]{1,0:T(8,128)(2,1)S(1)}, u32[]{:S(2)}, u32[]{:S(2)}) collective-permute-start(bf16[512,256]{1,0:T(8,128)(2,1)S(1)} %join.3.src), channel_id=1, source_target_pairs={{0,8},{8,0},{1,9},{9,1},{2,10},{10,2},{3,11},{11,3},{4,12},{12,4},... | collective-permute-start | bytes 786440 | tf_op jit(solution)/shard_map/ppermute | solution.py:43
  59.5 10.6 %collective-permute-start.15 = (bf16[384,512]{1,0:T(8,128)(2,1)S(1)}, bf16[384,512]{1,0:T(8,128)(2,1)S(1)}, u32[]{:S(2)}, u32[]{:S(2)}) collective-permute-start(bf16[384,512]{1,0:T(8,128)(2,1)S(1)} %get-tuple-element.61), channel_id=1, source_target_pairs={{0,1},{1,0},{2,3},{3,2},{4,5},{5,4},{6,7},{7,6},{8,9},{9,8},{10,11... | collective-permute-start | bytes 1179656 | tf_op jit(solution)/shard_map/ppermute | solution.py:43
  60.7 14.0 %collective-permute-start.14 = (bf16[128,512]{1,0:T(8,128)(2,1)S(1)}, bf16[128,512]{1,0:T(8,128)(2,1)S(1)}, u32[]{:S(2)}, u32[]{:S(2)}) collective-permute-start(bf16[128,512]{1,0:T(8,128)(2,1)S(1)} %get-tuple-element.60), channel_id=1, source_target_pairs={{0,1},{1,0},{2,3},{3,2},{4,5},{5,4},{6,7},{7,6},{8,9},{9,8},{10,11... | collective-permute-start | bytes 393224 | tf_op jit(solution)/shard_map/ppermute | solution.py:43
  70.2 5.2 %collective-permute-start.16 = (bf16[128,512]{1,0:T(8,128)(2,1)S(1)}, bf16[128,512]{1,0:T(8,128)(2,1)S(1)}, u32[]{:S(2)}, u32[]{:S(2)}) collective-permute-start(bf16[128,512]{1,0:T(8,128)(2,1)S(1)} %get-tuple-element.62), channel_id=1, source_target_pairs={{0,2},{2,4},{4,6},{6,0},{1,3},{3,5},{5,7},{7,1},{8,10},{10,12},{12... | collective-permute-start | bytes 393224 | tf_op jit(solution)/shard_map/ppermute | solution.py:43
  71.6 3.8 %collective-permute-start.17 = (bf16[128,512]{1,0:T(8,128)(2,1)S(1)}, bf16[128,512]{1,0:T(8,128)(2,1)S(1)}, u32[]{:S(2)}, u32[]{:S(2)}) collective-permute-start(bf16[128,512]{1,0:T(8,128)(2,1)S(1)} %get-tuple-element.63), channel_id=1, source_target_pairs={{0,6},{2,0},{4,2},{6,4},{1,7},{3,1},{5,3},{7,5},{8,14},{10,8},{12,... | collective-permute-start | bytes 393224 | tf_op jit(solution)/shard_map/ppermute | solution.py:43
  73.1 6.6 %collective-permute-start.18 = (bf16[128,512]{1,0:T(8,128)(2,1)S(1)}, bf16[128,512]{1,0:T(8,128)(2,1)S(1)}, u32[]{:S(2)}, u32[]{:S(2)}) collective-permute-start(bf16[128,512]{1,0:T(8,128)(2,1)S(1)} %get-tuple-element.64), channel_id=1, source_target_pairs={{0,4},{2,6},{4,0},{6,2},{1,5},{3,7},{5,1},{7,3},{8,12},{10,14},{12... | collective-permute-start | bytes 393224 | tf_op jit(solution)/shard_map/ppermute | solution.py:43

commit v7 on v6

--- a/solution.py
+++ b/solution.py
@@ -245,26 +245,25 @@
         part[:, at] = jnp.dot(f[...], basis[:, at], preferred_element_type=F32)
 
 
-def synthesis_body(flip, steps, f, basis, part, out, *_):
+def synthesis_body(places, f, basis, part, out, *_):
     y, z_lo = lax.axis_index("y"), lax.axis_index("z_lo")
-    for i, dy in enumerate(steps):
+    for i, (flip, dy) in enumerate(places):
         owner = lax.rem(y + dy, 4) * 2 + lax.rem(z_lo + flip, 2)
         at = pl.ds(pl.multiple_of(owner * 512, 512), 512)
         value = part[:, at] + jnp.dot(f[...], basis[:, at], preferred_element_type=F32)
         out[pl.ds(i * C, C), :] = value.astype(out.dtype)
 
 
-def merge_body(own, got, *outs):
-    for i, out in enumerate(outs):
-        rows = pl.ds(i * C, C)
-        out[...] = (own[rows, :] + got[rows, :].astype(F32)).astype(BF)
-
-
-def finish_body(total, linear, own, got, *rest):
+def merge_body(pairs, own, got, *outs):
+    for (mine, theirs), out in zip(pairs, outs, strict=True):
+        out[...] = (own[pl.ds(mine * C, C), :] + got[pl.ds(theirs * C, C), :].astype(F32)).astype(BF)
+
+
+def finish_body(total, linear, own, *rest):
     *blocks, out = rest
-    summed = own[pl.ds(3 * C, C), :] + got[...].astype(F32)
+    summed = own[pl.ds(3 * C, C), :]
     for b in blocks:
-        summed = summed + b[...].astype(F32)
+        summed = summed + b[pl.ds(0, C), :].astype(F32)
     scaled = summed / total[0:1, 0:1]
     for k in range(4):
         rows = pl.ds(k * C, C)
@@ -275,12 +274,12 @@
 def join_body(piece, *rest):
     *got, out = rest
     rows = piece.shape[0]
-    for s, ref in zip((0, *FAR_LAST), (piece, *got)):
+    for s, ref in zip((0, 2, 3, 1), (piece, *got)):
         out[pl.ds(s * rows, rows), :] = ref[...]
 
 
 def gather_over(piece, axes, n):
-    got = [send(piece, axes, n - s) for s in FAR_LAST]
+    got = [send(piece, axes, n - s) for s in (2, 3, 1)]
     shape = jax.ShapeDtypeStruct((n * piece.shape[0], piece.shape[1]), piece.dtype)
     return call(join_body, n, shape, "join")(piece, *got)
 
@@ -325,23 +324,25 @@
         near_field_body, 2, pltpu.VMEM((C, pts), F32), "near_field", [pltpu.VMEM((C, 8 * C), BF)], flops=4 * slab
     )(piece, basis)
     f = call(turned_body, 1, one(C, 8 * C, BF), "turned")(other)
-    steps = (*FAR_LAST, 0)
-
-    def field(flip, steps, dtype, basis, part, last=False):
+    def field(places, dtype, basis, part, last=False):
         chain = [] if last else [pltpu.VMEM(v.shape, v.dtype) for v in (basis, part)]
         return call(
-            functools.partial(synthesis_body, flip, steps), 3, [one(len(steps) * C, 512, dtype)] + chain, "synthesis",
-            flops=len(steps) * slab // 2, aliases={1: 1, 2: 2} if chain else {},
+            functools.partial(synthesis_body, places), 3, [one(len(places) * C, 512, dtype)] + chain, "synthesis",
+            flops=len(places) * slab // 2, aliases={1: 1, 2: 2} if chain else {},
         )(f, basis, part)
 
-    out, far_basis, part = field(1, steps[:3], BF, far_basis, part)
-    got0 = send(out, ("z_lo",), 1)
-    out, far_basis, part = field(1, steps[3:], BF, far_basis, part)
-    got1 = send(out, ("z_lo",), 1)
-    (own,) = field(0, steps, F32, far_basis, part, True)
-    outs = call(merge_body, 2, [one(C, 512, BF)] * 3, "merge")(own, got0)
-    fields = [send(o, ("y",), s) for o, s in zip(outs, steps)]
-    return call(finish_body, 7, one(pts // 8, C, BF), "finish")(total, linear, own, got1, *fields)
+    def merge(*pairs):
+        return call(functools.partial(merge_body, pairs), 2, [one(C, 512, BF)] * len(pairs), "merge")
+
+    out, far_basis, part = field(((1, 1), (1, 3)), BF, far_basis, part)
+    beside = send(out, ("z_lo",), 1)
+    out, far_basis, part = field(((0, 2), (1, 2)), BF, far_basis, part)
+    across = send(out, ("y",), 2)
+    (own,) = field(((0, 1), (0, 3), (1, 0), (0, 0)), F32, far_basis, part, True)
+    one_step, three_steps = merge((0, 0), (1, 1))(own, beside)
+    (out,) = merge((2, 1))(own, across)
+    fields = [across, send(one_step, ("y",), 1), send(three_steps, ("y",), 3), send(out, ("z_lo",), 1)]
+    return call(finish_body, 7, one(pts // 8, C, BF), "finish")(total, linear, own, *fields)
 
 
 def solution(mesh):

time: 81.9 us -> 77.7 us (0.949)
  waiting for transfers between devices: 20.9 us -> 17.9 us
  starting transfers between devices: 39.6 us -> 38.5 us
    ppermute x19, waiting for transfers between devices: 20.9 us -> 17.9 us  [send(): return lax.ppermute(value, axes, [(j, (j + shift) % n) for j in range(n)])]
    ppermute x19, starting transfers between devices: 39.6 us -> 38.5 us  [send(): return lax.ppermute(value, axes, [(j, (j + shift) % n) for j in range(n)])]
    pallas_call x4 -> x5, Pallas kernels: 1.78 us -> 1.8 us  [the longest x3 1.73 us: field(): call(functools.partial(synthesis_body, places), 3, [one(len(places) * C,...]
  transfers between devices with their start and end apart: 19 -> 19, of which waited for: 10 -> 11; matrix products, arithmetic and copies ran while one was open for 0% -> 0% of each run, Pallas kernels for 11% -> 11%
where the time goes in v7:
time: 77.7 us; the launch traced here: 76.5 us
  starting transfers between devices  38.5 us (50%)
  Pallas kernels  20 us (26%)
  waiting for transfers between devices  17.9 us (23%)
    ppermute x19, starting transfers between devices, send(): return lax.ppermute(value, axes, [(j, (j + shift) % n) for j in range(n)])  38.5 us
    ppermute x19, waiting for transfers between devices, send(): return lax.ppermute(value, axes, [(j, (j + shift) % n) for j in range(n)])  17.9 us
    pallas_call x1, Pallas kernels, on_device(): call(first_body, 0, [pltpu.VMEM((8 * C + 16, C), BF), pltpu.VMEM((8 * C,...  8.85 us
    pallas_call x2, Pallas kernels, near(): call(functools.partial(near_body, count, first), 4, [pltpu.VMEM((count *...  6.43 us
    pallas_call x3, Pallas kernels, field(): call(functools.partial(synthesis_body, places), 3, [one(len(places) * C,...  1.73 us
  transfers between devices with their start and end apart: 19, of which 11 were waited for; matrix products, arithmetic and copies ran while one was open for 0% of the time, Pallas kernels for 11%

profile of v7, /device:TPU:1, one launch (start us, length us, event | category | flops | bytes accessed | tf_op | source)
XLA Modules:
  0.0 76.5 jit_solution(3432717097830709259)
XLA Ops:
  0.0 8.9 %first.1 = (bf16[1040,128]{1,0:T(8,128)(2,1)S(1)}, bf16[1024,4096]{1,0:T(8,128)(2,1)S(1)}, f32[256,2,32,128]{3,2,1,0:T(8,128)S(1)}, f32[32,2,32,128]{3,2,1,0:T(8...) custom-call(f32[3,4096]{1,0:T(4,128)} %refs_0_.1, ...), custom_call_target="tpu_custom_call" | custom-call | flops 2147483648 | bytes 1048576 | tf_op jit(solution)/shard_map/first/pallas_call | solution.py:292
  8.9 3.3 %collective-permute-start = (bf16[1040,128]{1,0:T(8,128)(2,1)S(1)}, bf16[1040,128]{1,0:T(8,128)(2,1)S(1)}, u32[]{:S(2)}, u32[]{:S(2)}) collective-permute-start(bf16[1040,128]{1,0:T(8,128)(2,1)S(1)} %get-tuple-element.42), channel_id=1, source_target_pairs={{0,8},{8,0},{1,9},{9,1},{2,10},{10,2},{3,11},{11,3},{4,12},{12,4},... | collective-permute-start | bytes 798728 | tf_op jit(solution)/shard_map/ppermute | solution.py:43
  12.2 4.6 %near.2 = (bf16[784,128]{1,0:T(8,128)(2,1)S(1)}, bf16[1024,4096]{1,0:T(8,128)(2,1)S(1)}) custom-call(s32[8,128]{1,0:T(8,128)S(1)} %get-tuple-element.34.index, f32[32,128]{1,0:T(8,128)S(1)} %get-tuple-element.35.quad, f32[256,2,32,128]{3,2,1,0:T(8,128)S(1)} %get-tuple-element.36.exy, f32[32,2,32,128]{3,2,1,0:T(8,128)S(1)} %get-tuple-element.37.ez, ...), custom_call_target="tpu_custom_call" | custom-call | flops 1610612736 | bytes 1048576 | tf_op jit(solution)/shard_map/near/pallas_call | solution.py:305
  16.8 0.0 collective-permute-done.got.got0
  16.8 0.1 pair.1
  16.9 0.1 collective-permute-start.1
  16.9 2.7 %collective-permute-start.2 = (bf16[272,128]{1,0:T(8,128)(2,1)S(1)}, bf16[272,128]{1,0:T(8,128)(2,1)S(1)}, u32[]{:S(2)}, u32[]{:S(2)}) collective-permute-start(bf16[272,128]{1,0:T(8,128)(2,1)S(1)} %get-tuple-element.45), channel_id=1, source_target_pairs={{0,48},{16,0},{32,16},{48,32},{1,49},{17,1},{33,17},{49,33},{2,50}... | collective-permute-start | bytes 208904 | tf_op jit(solution)/shard_map/ppermute | solution.py:43
  19.6 0.0 collective-permute-start.3
  19.6 1.8 %near.3 = (bf16[272,128]{1,0:T(8,128)(2,1)S(1)}, bf16[1024,4096]{1,0:T(8,128)(2,1)S(1)}) custom-call(s32[8,128]{1,0:T(8,128)S(1)} %get-tuple-element.34.index, f32[32,128]{1,0:T(8,128)S(1)} %get-tuple-element.35.quad, f32[256,2,32,128]{3,2,1,0:T(8,128)S(1)} %get-tuple-element.36.exy, ...), custom_call_target="tpu_custom_call", output_to_operand_aliasing={{1}: (5, {})} | custom-call | flops 536870912 | bytes 1048576 | tf_op jit(solution)/shard_map/near/pallas_call | solution.py:305
  21.4 0.5 collective-permute-done.1.got1
  21.9 0.7 collective-permute-done.2.got2
  22.6 1.7 %collective-permute-done.3.got3 = bf16[272,128]{1,0:T(8,128)(2,1)S(1)} collective-permute-done((bf16[272,128]{1,0:T(8,128)(2,1)S(1)}, bf16[272,128]{1,0:T(8,128)(2,1)S(1)}, u32[]{:S(2)}, u32[]{:S(2)}) %collective-permute-start.3) | collective-permute-done | bytes 69664 | tf_op jit(solution)/shard_map/ppermute | solution.py:43
  24.3 0.1 x_sum.1
  24.4 1.3 %collective-permute-start.4 = (bf16[48,256]{1,0:T(8,128)(2,1)S(1)}, bf16[48,256]{1,0:T(8,128)(2,1)S(1)}, u32[]{:S(2)}, u32[]{:S(2)}) collective-permute-start(bf16[48,256]{1,0:T(8,128)(2,1)S(1)} %get-tuple-element.48), channel_id=1, source_target_pairs={{0,64},{64,128},{128,192},{192,0},{1,65},{65,129},{129,193},{193,1... | collective-permute-start | bytes 73736 | tf_op jit(solution)/shard_map/ppermute | solution.py:43
  25.7 3.1 %collective-permute-start.5 = (bf16[48,256]{1,0:T(8,128)(2,1)S(1)}, bf16[48,256]{1,0:T(8,128)(2,1)S(1)}, u32[]{:S(2)}, u32[]{:S(2)}) collective-permute-start(bf16[48,256]{1,0:T(8,128)(2,1)S(1)} %get-tuple-element.49), channel_id=1, source_target_pairs={{0,192},{64,0},{128,64},{192,128},{1,193},{65,1},{129,65},{193,129... | collective-permute-start | bytes 73736 | tf_op jit(solution)/shard_map/ppermute | solution.py:43
  28.8 4.4 %collective-permute-start.6 = (bf16[48,256]{1,0:T(8,128)(2,1)S(1)}, bf16[48,256]{1,0:T(8,128)(2,1)S(1)}, u32[]{:S(2)}, u32[]{:S(2)}) collective-permute-start(bf16[48,256]{1,0:T(8,128)(2,1)S(1)} %get-tuple-element.50), channel_id=1, source_target_pairs={{0,128},{64,192},{128,0},{192,64},{1,129},{65,193},{129,1},{193,65... | collective-permute-start | bytes 73736 | tf_op jit(solution)/shard_map/ppermute | solution.py:43
  33.2 0.0 collective-permute-done.4.got1
  33.2 0.0 collective-permute-done.5.got2
  33.2 2.2 %collective-permute-done.6.got3 = bf16[48,256]{1,0:T(8,128)(2,1)S(1)} collective-permute-done((bf16[48,256]{1,0:T(8,128)(2,1)S(1)}, bf16[48,256]{1,0:T(8,128)(2,1)S(1)}, u32[]{:S(2)}, u32[]{:S(2)}) %collective-permute-start.6) | collective-permute-done | bytes 24608 | tf_op jit(solution)/shard_map/ppermute | solution.py:43
  35.4 0.4 filter.1
  35.8 2.3 %collective-permute-start.9 = (bf16[32,256]{1,0:T(8,128)(2,1)S(1)}, bf16[32,256]{1,0:T(8,128)(2,1)S(1)}, u32[]{:S(2)}, u32[]{:S(2)}) collective-permute-start(bf16[32,256]{1,0:T(8,128)(2,1)S(1)} %get-tuple-element.52.piece), channel_id=1, source_target_pairs={{0,192},{64,0},{128,64},{192,128},{1,193},{65,1},{129,65},{193,129... | collective-permute-start | bytes 49160 | tf_op jit(solution)/shard_map/ppermute | solution.py:43
  38.1 0.1 collective-permute-start.8
  38.2 4.4 %collective-permute-start.7 = (bf16[32,256]{1,0:T(8,128)(2,1)S(1)}, bf16[32,256]{1,0:T(8,128)(2,1)S(1)}, u32[]{:S(2)}, u32[]{:S(2)}) collective-permute-start(bf16[32,256]{1,0:T(8,128)(2,1)S(1)} %get-tuple-element.52.piece), channel_id=1, source_target_pairs={{0,128},{64,192},{128,0},{192,64},{1,129},{65,193},{129,1},{193,65... | collective-permute-start | bytes 49160 | tf_op jit(solution)/shard_map/ppermute | solution.py:43
  42.6 0.2 collective-permute-done.8.rest_1_
  42.8 1.9 %collective-permute-done.7.rest_0_ = bf16[32,256]{1,0:T(8,128)(2,1)S(1)} collective-permute-done((bf16[32,256]{1,0:T(8,128)(2,1)S(1)}, bf16[32,256]{1,0:T(8,128)(2,1)S(1)}, u32[]{:S(2)}, u32[]{:S(2)}) %collective-permute-start.7) | collective-permute-done | bytes 16416 | tf_op jit(solution)/shard_map/ppermute | solution.py:43
  44.7 1.3 %collective-permute-start.12 = (bf16[128,256]{1,0:T(8,128)(2,1)S(1)}, bf16[128,256]{1,0:T(8,128)(2,1)S(1)}, u32[]{:S(2)}, u32[]{:S(2)}) collective-permute-start(bf16[128,256]{1,0:T(8,128)(2,1)S(1)} %join.2.piece), channel_id=1, source_target_pairs={{0,48},{16,0},{32,16},{48,32},{1,49},{17,1},{33,17},{49,33},{2,50}... | collective-permute-start | bytes 196616 | tf_op jit(solution)/shard_map/ppermute | solution.py:43
  46.0 0.2 collective-permute-start.11
  46.2 1.5 %collective-permute-start.10 = (bf16[128,256]{1,0:T(8,128)(2,1)S(1)}, bf16[128,256]{1,0:T(8,128)(2,1)S(1)}, u32[]{:S(2)}, u32[]{:S(2)}) collective-permute-start(bf16[128,256]{1,0:T(8,128)(2,1)S(1)} %join.2.piece), channel_id=1, source_target_pairs={{0,32},{16,48},{32,0},{48,16},{1,33},{17,49},{33,1},{49,17},{2,34}... | collective-permute-start | bytes 196616 | tf_op jit(solution)/shard_map/ppermute | solution.py:43
  47.7 0.4 collective-permute-done.12.rest_2_
  48.2 2.9 %collective-permute-done.11.rest_1_ = bf16[128,256]{1,0:T(8,128)(2,1)S(1)} collective-permute-done((bf16[128,256]{1,0:T(8,128)(2,1)S(1)}, bf16[128,256]{1,0:T(8,128)(2,1)S(1)}, u32[]{:S(2)}, u32[]{:S(2)}) %collective-permute-start.11) | collective-permute-done | bytes 65568 | tf_op jit(solution)/shard_map/ppermute | solution.py:43
  51.1 6.5 %collective-permute-start.13 = (bf16[512,256]{1,0:T(8,128)(2,1)S(1)}, bf16[512,256]{1,0:T(8,128)(2,1)S(1)}, u32[]{:S(2)}, u32[]{:S(2)}) collective-permute-start(bf16[512,256]{1,0:T(8,128)(2,1)S(1)} %join.3.src), channel_id=1, source_target_pairs={{0,8},{8,0},{1,9},{9,1},{2,10},{10,2},{3,11},{11,3},{4,12},{12,4},... | collective-permute-start | bytes 786440 | tf_op jit(solution)/shard_map/ppermute | solution.py:43
  57.5 1.4 %near_field.1.part = f32[128,4096]{1,0:T(8,128)S(1)} custom-call(bf16[512,256]{1,0:T(8,128)(2,1)S(1)} %join.3.src, bf16[1024,4096]{1,0:T(8,128)(2,1)S(1)} %get-tuple-element.54.basis), custom_call_target="tpu_custom_call" | custom-call | flops 1073741824 | bytes 1048576 | tf_op jit(solution)/shard_map/near_field/pallas_call | solution.py:323
  58.9 0.0 collective-permute-done.13.src
  58.9 0.1 turned.1.f
  59.1 0.5 synthesis.3
  59.5 0.5 synthesis.4
  60.0 3.0 %collective-permute-start.14 = (bf16[256,512]{1,0:T(8,128)(2,1)S(1)}, bf16[256,512]{1,0:T(8,128)(2,1)S(1)}, u32[]{:S(2)}, u32[]{:S(2)}) collective-permute-start(bf16[256,512]{1,0:T(8,128)(2,1)S(1)} %get-tuple-element.59), channel_id=1, source_target_pairs={{0,4},{2,6},{4,0},{6,2},{1,5},{3,7},{5,1},{7,3},{8,12},{10,14},{12... | collective-permute-start | bytes 786440 | tf_op jit(solution)/shard_map/ppermute | solution.py:43
  63.0 0.7 collective-permute-start.15
  63.8 0.8 %synthesis.5.own = f32[512,512]{1,0:T(8,128)S(1)} custom-call(bf16[128,1024]{1,0:T(8,128)(2,1)S(1)} %turned.1.f, bf16[1024,4096]{1,0:T(8,128)(2,1)S(1)} %get-tuple-element.57.basis, f32[128,4096]{1,0:T(8,128)S(1)} %get-tuple-element.58.part), custom_call_target="tpu_custom_call" | custom-call | flops 536870912 | bytes 1048576 | tf_op jit(solution)/shard_map/synthesis/pallas_call | solution.py:329
  64.5 4.8 %collective-permute-done.14.got.rest_0_ = bf16[256,512]{1,0:T(8,128)(2,1)S(1)} collective-permute-done((bf16[256,512]{1,0:T(8,128)(2,1)S(1)}, bf16[256,512]{1,0:T(8,128)(2,1)S(1)}, u32[]{:S(2)}, u32[]{:S(2)}) %collective-permute-start.14) | collective-permute-done | bytes 262176 | tf_op jit(solution)/shard_map/ppermute | solution.py:43
  69.4 0.8 %collective-permute-start.18 = (bf16[128,512]{1,0:T(8,128)(2,1)S(1)}, bf16[128,512]{1,0:T(8,128)(2,1)S(1)}, u32[]{:S(2)}, u32[]{:S(2)}) collective-permute-start(bf16[128,512]{1,0:T(8,128)(2,1)S(1)} %merge.3), channel_id=1, source_target_pairs={{0,1},{1,0},{2,3},{3,2},{4,5},{5,4},{6,7},{7,6},{8,9},{9,8},{10,11... | collective-permute-start | bytes 393224 | tf_op jit(solution)/shard_map/ppermute | solution.py:43
  70.2 0.2 collective-permute-done.15.got
  70.5 1.1 %collective-permute-start.16 = (bf16[128,512]{1,0:T(8,128)(2,1)S(1)}, bf16[128,512]{1,0:T(8,128)(2,1)S(1)}, u32[]{:S(2)}, u32[]{:S(2)}) collective-permute-start(bf16[128,512]{1,0:T(8,128)(2,1)S(1)} %get-tuple-element.61), channel_id=1, source_target_pairs={{0,2},{2,4},{4,6},{6,0},{1,3},{3,5},{5,7},{7,1},{8,10},{10,12},{12... | collective-permute-start | bytes 393224 | tf_op jit(solution)/shard_map/ppermute | solution.py:43
  71.7 1.6 %collective-permute-start.17 = (bf16[128,512]{1,0:T(8,128)(2,1)S(1)}, bf16[128,512]{1,0:T(8,128)(2,1)S(1)}, u32[]{:S(2)}, u32[]{:S(2)}) collective-permute-start(bf16[128,512]{1,0:T(8,128)(2,1)S(1)} %get-tuple-element.62), channel_id=1, source_target_pairs={{0,6},{2,0},{4,2},{6,4},{1,7},{3,1},{5,3},{7,5},{8,14},{10,8},{12,... | collective-permute-start | bytes 393224 | tf_op jit(solution)/shard_map/ppermute | solution.py:43
  73.3 0.0 collective-permute-done.18.rest_3_
  73.3 2.3 %collective-permute-done.16.rest_1_ = bf16[128,512]{1,0:T(8,128)(2,1)S(1)} collective-permute-done((bf16[128,512]{1,0:T(8,128)(2,1)S(1)}, bf16[128,512]{1,0:T(8,128)(2,1)S(1)}, u32[]{:S(2)}, u32[]{:S(2)}) %collective-permute-start.16) | collective-permute-done | bytes 131104 | tf_op jit(solution)/shard_map/ppermute | solution.py:43
  75.6 0.0 collective-permute-done.17.rest_2_
  75.6 0.8 %finish.1 = bf16[512,128]{1,0:T(8,128)(2,1)} custom-call(f32[8,128]{1,0:T(8,128)S(1)} %get-tuple-element.51.total, f32[512,128]{1,0:T(8,128)S(1)} %get-tuple-element.39.given.linear, f32[512,512]{1,0:T(8,128)S(1)} %synthesis.5.own, bf16[256,512]{1,0:T(8,128)(2,1)S(1)} %collective-permute-done.14.got.rest_0_, ...), custom_call_target="tpu_custom_call" | custom-call | bytes 1048576 | tf_op jit(solution)/shard_map/finish/pallas_call | solution.py:345
  (8 shorter events, 0.1 us)
Async XLA Ops:
  8.9 7.9 %collective-permute-start = (bf16[1040,128]{1,0:T(8,128)(2,1)S(1)}, bf16[1040,128]{1,0:T(8,128)(2,1)S(1)}, u32[]{:S(2)}, u32[]{:S(2)}) collective-permute-start(bf16[1040,128]{1,0:T(8,128)(2,1)S(1)} %get-tuple-element.42), channel_id=1, source_target_pairs={{0,8},{8,0},{1,9},{9,1},{2,10},{10,2},{3,11},{11,3},{4,12},{12,4},... | collective-permute-start | bytes 798728 | tf_op jit(solution)/shard_map/ppermute | solution.py:43
  16.9 5.0 %collective-permute-start.1 = (bf16[272,128]{1,0:T(8,128)(2,1)S(1)}, bf16[272,128]{1,0:T(8,128)(2,1)S(1)}, u32[]{:S(2)}, u32[]{:S(2)}) collective-permute-start(bf16[272,128]{1,0:T(8,128)(2,1)S(1)} %get-tuple-element.44), channel_id=1, source_target_pairs={{0,16},{16,32},{32,48},{48,0},{1,17},{17,33},{33,49},{49,1},{2,18}... | collective-permute-start | bytes 208904 | tf_op jit(solution)/shard_map/ppermute | solution.py:43
  16.9 5.6 %collective-permute-start.2 = (bf16[272,128]{1,0:T(8,128)(2,1)S(1)}, bf16[272,128]{1,0:T(8,128)(2,1)S(1)}, u32[]{:S(2)}, u32[]{:S(2)}) collective-permute-start(bf16[272,128]{1,0:T(8,128)(2,1)S(1)} %get-tuple-element.45), channel_id=1, source_target_pairs={{0,48},{16,0},{32,16},{48,32},{1,49},{17,1},{33,17},{49,33},{2,50}... | collective-permute-start | bytes 208904 | tf_op jit(solution)/shard_map/ppermute | solution.py:43
  19.6 4.7 %collective-permute-start.3 = (bf16[272,128]{1,0:T(8,128)(2,1)S(1)}, bf16[272,128]{1,0:T(8,128)(2,1)S(1)}, u32[]{:S(2)}, u32[]{:S(2)}) collective-permute-start(bf16[272,128]{1,0:T(8,128)(2,1)S(1)} %get-tuple-element.46), channel_id=1, source_target_pairs={{0,32},{16,48},{32,0},{48,16},{1,33},{17,49},{33,1},{49,17},{2,34}... | collective-permute-start | bytes 208904 | tf_op jit(solution)/shard_map/ppermute | solution.py:43
  19.6 15.8 %copy-start = (bf16[32,2,128,128]{3,2,1,0:T(8,128)(2,1)S(1)}, bf16[32,2,128,128]{3,2,1,0:T(8,128)(2,1)}, u32[]{:S(2)}) copy-start(bf16[32,2,128,128]{3,2,1,0:T(8,128)(2,1)} %weight.1) | copy-start | bytes 6291460
  24.4 8.8 %collective-permute-start.4 = (bf16[48,256]{1,0:T(8,128)(2,1)S(1)}, bf16[48,256]{1,0:T(8,128)(2,1)S(1)}, u32[]{:S(2)}, u32[]{:S(2)}) collective-permute-start(bf16[48,256]{1,0:T(8,128)(2,1)S(1)} %get-tuple-element.48), channel_id=1, source_target_pairs={{0,64},{64,128},{128,192},{192,0},{1,65},{65,129},{129,193},{193,1... | collective-permute-start | bytes 73736 | tf_op jit(solution)/shard_map/ppermute | solution.py:43
  25.7 7.5 %collective-permute-start.5 = (bf16[48,256]{1,0:T(8,128)(2,1)S(1)}, bf16[48,256]{1,0:T(8,128)(2,1)S(1)}, u32[]{:S(2)}, u32[]{:S(2)}) collective-permute-start(bf16[48,256]{1,0:T(8,128)(2,1)S(1)} %get-tuple-element.49), channel_id=1, source_target_pairs={{0,192},{64,0},{128,64},{192,128},{1,193},{65,1},{129,65},{193,129... | collective-permute-start | bytes 73736 | tf_op jit(solution)/shard_map/ppermute | solution.py:43
  28.8 6.6 %collective-permute-start.6 = (bf16[48,256]{1,0:T(8,128)(2,1)S(1)}, bf16[48,256]{1,0:T(8,128)(2,1)S(1)}, u32[]{:S(2)}, u32[]{:S(2)}) collective-permute-start(bf16[48,256]{1,0:T(8,128)(2,1)S(1)} %get-tuple-element.50), channel_id=1, source_target_pairs={{0,128},{64,192},{128,0},{192,64},{1,129},{65,193},{129,1},{193,65... | collective-permute-start | bytes 73736 | tf_op jit(solution)/shard_map/ppermute | solution.py:43
  35.8 6.8 %collective-permute-start.9 = (bf16[32,256]{1,0:T(8,128)(2,1)S(1)}, bf16[32,256]{1,0:T(8,128)(2,1)S(1)}, u32[]{:S(2)}, u32[]{:S(2)}) collective-permute-start(bf16[32,256]{1,0:T(8,128)(2,1)S(1)} %get-tuple-element.52.piece), channel_id=1, source_target_pairs={{0,192},{64,0},{128,64},{192,128},{1,193},{65,1},{129,65},{193,129... | collective-permute-start | bytes 49160 | tf_op jit(solution)/shard_map/ppermute | solution.py:43
  38.1 4.7 %collective-permute-start.8 = (bf16[32,256]{1,0:T(8,128)(2,1)S(1)}, bf16[32,256]{1,0:T(8,128)(2,1)S(1)}, u32[]{:S(2)}, u32[]{:S(2)}) collective-permute-start(bf16[32,256]{1,0:T(8,128)(2,1)S(1)} %get-tuple-element.52.piece), channel_id=1, source_target_pairs={{0,64},{64,128},{128,192},{192,0},{1,65},{65,129},{129,193},{193,1... | collective-permute-start | bytes 49160 | tf_op jit(solution)/shard_map/ppermute | solution.py:43
  38.2 6.5 %collective-permute-start.7 = (bf16[32,256]{1,0:T(8,128)(2,1)S(1)}, bf16[32,256]{1,0:T(8,128)(2,1)S(1)}, u32[]{:S(2)}, u32[]{:S(2)}) collective-permute-start(bf16[32,256]{1,0:T(8,128)(2,1)S(1)} %get-tuple-element.52.piece), channel_id=1, source_target_pairs={{0,128},{64,192},{128,0},{192,64},{1,129},{65,193},{129,1},{193,65... | collective-permute-start | bytes 49160 | tf_op jit(solution)/shard_map/ppermute | solution.py:43
  44.7 3.4 %collective-permute-start.12 = (bf16[128,256]{1,0:T(8,128)(2,1)S(1)}, bf16[128,256]{1,0:T(8,128)(2,1)S(1)}, u32[]{:S(2)}, u32[]{:S(2)}) collective-permute-start(bf16[128,256]{1,0:T(8,128)(2,1)S(1)} %join.2.piece), channel_id=1, source_target_pairs={{0,48},{16,0},{32,16},{48,32},{1,49},{17,1},{33,17},{49,33},{2,50}... | collective-permute-start | bytes 196616 | tf_op jit(solution)/shard_map/ppermute | solution.py:43
  46.0 5.0 %collective-permute-start.11 = (bf16[128,256]{1,0:T(8,128)(2,1)S(1)}, bf16[128,256]{1,0:T(8,128)(2,1)S(1)}, u32[]{:S(2)}, u32[]{:S(2)}) collective-permute-start(bf16[128,256]{1,0:T(8,128)(2,1)S(1)} %join.2.piece), channel_id=1, source_target_pairs={{0,16},{16,32},{32,48},{48,0},{1,17},{17,33},{33,49},{49,1},{2,18}... | collective-permute-start | bytes 196616 | tf_op jit(solution)/shard_map/ppermute | solution.py:43
  46.2 4.8 %collective-permute-start.10 = (bf16[128,256]{1,0:T(8,128)(2,1)S(1)}, bf16[128,256]{1,0:T(8,128)(2,1)S(1)}, u32[]{:S(2)}, u32[]{:S(2)}) collective-permute-start(bf16[128,256]{1,0:T(8,128)(2,1)S(1)} %join.2.piece), channel_id=1, source_target_pairs={{0,32},{16,48},{32,0},{48,16},{1,33},{17,49},{33,1},{49,17},{2,34}... | collective-permute-start | bytes 196616 | tf_op jit(solution)/shard_map/ppermute | solution.py:43
  51.1 7.8 %collective-permute-start.13 = (bf16[512,256]{1,0:T(8,128)(2,1)S(1)}, bf16[512,256]{1,0:T(8,128)(2,1)S(1)}, u32[]{:S(2)}, u32[]{:S(2)}) collective-permute-start(bf16[512,256]{1,0:T(8,128)(2,1)S(1)} %join.3.src), channel_id=1, source_target_pairs={{0,8},{8,0},{1,9},{9,1},{2,10},{10,2},{3,11},{11,3},{4,12},{12,4},... | collective-permute-start | bytes 786440 | tf_op jit(solution)/shard_map/ppermute | solution.py:43
  60.0 9.3 %collective-permute-start.14 = (bf16[256,512]{1,0:T(8,128)(2,1)S(1)}, bf16[256,512]{1,0:T(8,128)(2,1)S(1)}, u32[]{:S(2)}, u32[]{:S(2)}) collective-permute-start(bf16[256,512]{1,0:T(8,128)(2,1)S(1)} %get-tuple-element.59), channel_id=1, source_target_pairs={{0,4},{2,6},{4,0},{6,2},{1,5},{3,7},{5,1},{7,3},{8,12},{10,14},{12... | collective-permute-start | bytes 786440 | tf_op jit(solution)/shard_map/ppermute | solution.py:43
  63.0 7.4 %collective-permute-start.15 = (bf16[256,512]{1,0:T(8,128)(2,1)S(1)}, bf16[256,512]{1,0:T(8,128)(2,1)S(1)}, u32[]{:S(2)}, u32[]{:S(2)}) collective-permute-start(bf16[256,512]{1,0:T(8,128)(2,1)S(1)} %get-tuple-element.60), channel_id=1, source_target_pairs={{0,1},{1,0},{2,3},{3,2},{4,5},{5,4},{6,7},{7,6},{8,9},{9,8},{10,11... | collective-permute-start | bytes 786440 | tf_op jit(solution)/shard_map/ppermute | solution.py:43
  69.4 3.9 %collective-permute-start.18 = (bf16[128,512]{1,0:T(8,128)(2,1)S(1)}, bf16[128,512]{1,0:T(8,128)(2,1)S(1)}, u32[]{:S(2)}, u32[]{:S(2)}) collective-permute-start(bf16[128,512]{1,0:T(8,128)(2,1)S(1)} %merge.3), channel_id=1, source_target_pairs={{0,1},{1,0},{2,3},{3,2},{4,5},{5,4},{6,7},{7,6},{8,9},{9,8},{10,11... | collective-permute-start | bytes 393224 | tf_op jit(solution)/shard_map/ppermute | solution.py:43
  70.5 5.1 %collective-permute-start.16 = (bf16[128,512]{1,0:T(8,128)(2,1)S(1)}, bf16[128,512]{1,0:T(8,128)(2,1)S(1)}, u32[]{:S(2)}, u32[]{:S(2)}) collective-permute-start(bf16[128,512]{1,0:T(8,128)(2,1)S(1)} %get-tuple-element.61), channel_id=1, source_target_pairs={{0,2},{2,4},{4,6},{6,0},{1,3},{3,5},{5,7},{7,1},{8,10},{10,12},{12... | collective-permute-start | bytes 393224 | tf_op jit(solution)/shard_map/ppermute | solution.py:43
  71.7 4.0 %collective-permute-start.17 = (bf16[128,512]{1,0:T(8,128)(2,1)S(1)}, bf16[128,512]{1,0:T(8,128)(2,1)S(1)}, u32[]{:S(2)}, u32[]{:S(2)}) collective-permute-start(bf16[128,512]{1,0:T(8,128)(2,1)S(1)} %get-tuple-element.62), channel_id=1, source_target_pairs={{0,6},{2,0},{4,2},{6,4},{1,7},{3,1},{5,3},{7,5},{8,14},{10,8},{12,... | collective-permute-start | bytes 393224 | tf_op jit(solution)/shard_map/ppermute | solution.py:43

commit v8 on v7

--- a/solution.py
+++ b/solution.py
@@ -274,12 +274,12 @@
 def join_body(piece, *rest):
     *got, out = rest
     rows = piece.shape[0]
-    for s, ref in zip((0, 2, 3, 1), (piece, *got)):
+    for s, ref in zip((0, *FAR_LAST), (piece, *got)):
         out[pl.ds(s * rows, rows), :] = ref[...]
 
 
 def gather_over(piece, axes, n):
-    got = [send(piece, axes, n - s) for s in (2, 3, 1)]
+    got = [send(piece, axes, n - s) for s in FAR_LAST]
     shape = jax.ShapeDtypeStruct((n * piece.shape[0], piece.shape[1]), piece.dtype)
     return call(join_body, n, shape, "join")(piece, *got)
 
@@ -315,7 +315,7 @@
     keep, *outs = call(x_body, 5, [one(48, 2 * C, F32)] + [one(48, 2 * C, BF)] * 3, "x_sum")(
         mine, got, *[across[s] for s in FAR_LAST]
     )
-    got = [send(outs[s - 1], ("z_hi",), s) for s in FAR_LAST]
+    got = [send(outs[s - 1], ("z_hi",), s) for s in (2, 1, 3)]
     piece, total = call(filter_body, 5, [one(32, 2 * C, BF), one(8, C, F32)], "filter")(keep, *got, mode_weight)
     piece = gather_over(piece, ("z_hi",), 4)
     piece = gather_over(piece, ("x",), 4)

time: 77.7 us -> 77.3 us (level)
  the two profiles are of different devices: /device:TPU:1 before, /device:TPU:30 now
where the time goes in v8:
time: 77.3 us; the launch traced here: 77.2 us
  starting transfers between devices  30.6 us (40%)
  waiting for transfers between devices  26.4 us (34%)
  Pallas kernels  20.1 us (26%)
    ppermute x19, starting transfers between devices, send(): return lax.ppermute(value, axes, [(j, (j + shift) % n) for j in range(n)])  30.6 us
    ppermute x19, waiting for transfers between devices, send(): return lax.ppermute(value, axes, [(j, (j + shift) % n) for j in range(n)])  26.4 us
    pallas_call x1, Pallas kernels, on_device(): call(first_body, 0, [pltpu.VMEM((8 * C + 16, C), BF), pltpu.VMEM((8 * C,...  8.85 us
    pallas_call x2, Pallas kernels, near(): call(functools.partial(near_body, count, first), 4, [pltpu.VMEM((count *...  6.44 us
    pallas_call x3, Pallas kernels, field(): call(functools.partial(synthesis_body, places), 3, [one(len(places) * C,...  1.72 us
  transfers between devices with their start and end apart: 19, of which 14 were waited for; matrix products, arithmetic and copies ran while one was open for 0% of the time, Pallas kernels for 11%

profile of v8, /device:TPU:30, one launch (start us, length us, event | category | flops | bytes accessed | tf_op | source)
XLA Modules:
  0.0 77.2 jit_solution(2143637210975198839)
XLA Ops:
  0.0 8.8 %first.1 = (bf16[1040,128]{1,0:T(8,128)(2,1)S(1)}, bf16[1024,4096]{1,0:T(8,128)(2,1)S(1)}, f32[256,2,32,128]{3,2,1,0:T(8,128)S(1)}, f32[32,2,32,128]{3,2,1,0:T(8...) custom-call(f32[3,4096]{1,0:T(4,128)} %refs_0_.1, ...), custom_call_target="tpu_custom_call" | custom-call | flops 2147483648 | bytes 1048576 | tf_op jit(solution)/shard_map/first/pallas_call | solution.py:292
  8.9 0.1 collective-permute-start
  9.0 4.6 %near.2 = (bf16[784,128]{1,0:T(8,128)(2,1)S(1)}, bf16[1024,4096]{1,0:T(8,128)(2,1)S(1)}) custom-call(s32[8,128]{1,0:T(8,128)S(1)} %get-tuple-element.34.index, f32[32,128]{1,0:T(8,128)S(1)} %get-tuple-element.35.quad, f32[256,2,32,128]{3,2,1,0:T(8,128)S(1)} %get-tuple-element.36.exy, f32[32,2,32,128]{3,2,1,0:T(8,128)S(1)} %get-tuple-element.37.ez, ...), custom_call_target="tpu_custom_call" | custom-call | flops 1610612736 | bytes 1048576 | tf_op jit(solution)/shard_map/near/pallas_call | solution.py:305
  13.6 0.0 collective-permute-done.got.got0
  13.6 0.1 pair.1
  13.7 0.5 collective-permute-start.1
  14.2 1.5 %collective-permute-start.2 = (bf16[272,128]{1,0:T(8,128)(2,1)S(1)}, bf16[272,128]{1,0:T(8,128)(2,1)S(1)}, u32[]{:S(2)}, u32[]{:S(2)}) collective-permute-start(bf16[272,128]{1,0:T(8,128)(2,1)S(1)} %get-tuple-element.45), channel_id=1, source_target_pairs={{0,48},{16,0},{32,16},{48,32},{1,49},{17,1},{33,17},{49,33},{2,50}... | collective-permute-start | bytes 208904 | tf_op jit(solution)/shard_map/ppermute | solution.py:43
  15.7 1.4 %collective-permute-start.3 = (bf16[272,128]{1,0:T(8,128)(2,1)S(1)}, bf16[272,128]{1,0:T(8,128)(2,1)S(1)}, u32[]{:S(2)}, u32[]{:S(2)}) collective-permute-start(bf16[272,128]{1,0:T(8,128)(2,1)S(1)} %get-tuple-element.46), channel_id=1, source_target_pairs={{0,32},{16,48},{32,0},{48,16},{1,33},{17,49},{33,1},{49,17},{2,34}... | collective-permute-start | bytes 208904 | tf_op jit(solution)/shard_map/ppermute | solution.py:43
  17.1 1.8 %near.3 = (bf16[272,128]{1,0:T(8,128)(2,1)S(1)}, bf16[1024,4096]{1,0:T(8,128)(2,1)S(1)}) custom-call(s32[8,128]{1,0:T(8,128)S(1)} %get-tuple-element.34.index, f32[32,128]{1,0:T(8,128)S(1)} %get-tuple-element.35.quad, f32[256,2,32,128]{3,2,1,0:T(8,128)S(1)} %get-tuple-element.36.exy, ...), custom_call_target="tpu_custom_call", output_to_operand_aliasing={{1}: (5, {})} | custom-call | flops 536870912 | bytes 1048576 | tf_op jit(solution)/shard_map/near/pallas_call | solution.py:305
  19.0 0.0 collective-permute-done.1.got1
  19.0 0.7 collective-permute-done.2.got2
  19.7 1.8 %collective-permute-done.3.got3 = bf16[272,128]{1,0:T(8,128)(2,1)S(1)} collective-permute-done((bf16[272,128]{1,0:T(8,128)(2,1)S(1)}, bf16[272,128]{1,0:T(8,128)(2,1)S(1)}, u32[]{:S(2)}, u32[]{:S(2)}) %collective-permute-start.3) | collective-permute-done | bytes 69664 | tf_op jit(solution)/shard_map/ppermute | solution.py:43
  21.6 0.1 x_sum.1
  21.7 7.3 %collective-permute-start.4 = (bf16[48,256]{1,0:T(8,128)(2,1)S(1)}, bf16[48,256]{1,0:T(8,128)(2,1)S(1)}, u32[]{:S(2)}, u32[]{:S(2)}) collective-permute-start(bf16[48,256]{1,0:T(8,128)(2,1)S(1)} %get-tuple-element.48), channel_id=1, source_target_pairs={{0,128},{64,192},{128,0},{192,64},{1,129},{65,193},{129,1},{193,65... | collective-permute-start | bytes 73736 | tf_op jit(solution)/shard_map/ppermute | solution.py:43
  28.9 1.5 %collective-permute-start.5 = (bf16[48,256]{1,0:T(8,128)(2,1)S(1)}, bf16[48,256]{1,0:T(8,128)(2,1)S(1)}, u32[]{:S(2)}, u32[]{:S(2)}) collective-permute-start(bf16[48,256]{1,0:T(8,128)(2,1)S(1)} %get-tuple-element.49), channel_id=1, source_target_pairs={{0,64},{64,128},{128,192},{192,0},{1,65},{65,129},{129,193},{193,1... | collective-permute-start | bytes 73736 | tf_op jit(solution)/shard_map/ppermute | solution.py:43
  30.4 2.6 %collective-permute-start.6 = (bf16[48,256]{1,0:T(8,128)(2,1)S(1)}, bf16[48,256]{1,0:T(8,128)(2,1)S(1)}, u32[]{:S(2)}, u32[]{:S(2)}) collective-permute-start(bf16[48,256]{1,0:T(8,128)(2,1)S(1)} %get-tuple-element.50), channel_id=1, source_target_pairs={{0,192},{64,0},{128,64},{192,128},{1,193},{65,1},{129,65},{193,129... | collective-permute-start | bytes 73736 | tf_op jit(solution)/shard_map/ppermute | solution.py:43
  33.1 1.8 %collective-permute-done.5.got2 = bf16[48,256]{1,0:T(8,128)(2,1)S(1)} collective-permute-done((bf16[48,256]{1,0:T(8,128)(2,1)S(1)}, bf16[48,256]{1,0:T(8,128)(2,1)S(1)}, u32[]{:S(2)}, u32[]{:S(2)}) %collective-permute-start.5) | collective-permute-done | bytes 24608 | tf_op jit(solution)/shard_map/ppermute | solution.py:43
  34.9 0.3 collective-permute-done.6.got3
  35.2 0.4 filter.1
  35.5 2.3 %collective-permute-start.9 = (bf16[32,256]{1,0:T(8,128)(2,1)S(1)}, bf16[32,256]{1,0:T(8,128)(2,1)S(1)}, u32[]{:S(2)}, u32[]{:S(2)}) collective-permute-start(bf16[32,256]{1,0:T(8,128)(2,1)S(1)} %get-tuple-element.52.piece), channel_id=1, source_target_pairs={{0,128},{64,192},{128,0},{192,64},{1,129},{65,193},{129,1},{193,65... | collective-permute-start | bytes 49160 | tf_op jit(solution)/shard_map/ppermute | solution.py:43
  37.9 4.0 %collective-permute-start.8 = (bf16[32,256]{1,0:T(8,128)(2,1)S(1)}, bf16[32,256]{1,0:T(8,128)(2,1)S(1)}, u32[]{:S(2)}, u32[]{:S(2)}) collective-permute-start(bf16[32,256]{1,0:T(8,128)(2,1)S(1)} %get-tuple-element.52.piece), channel_id=1, source_target_pairs={{0,64},{64,128},{128,192},{192,0},{1,65},{65,129},{129,193},{193,1... | collective-permute-start | bytes 49160 | tf_op jit(solution)/shard_map/ppermute | solution.py:43
  41.8 0.2 collective-permute-start.7
  42.0 1.3 %collective-permute-done.9.rest_2_ = bf16[32,256]{1,0:T(8,128)(2,1)S(1)} collective-permute-done((bf16[32,256]{1,0:T(8,128)(2,1)S(1)}, bf16[32,256]{1,0:T(8,128)(2,1)S(1)}, u32[]{:S(2)}, u32[]{:S(2)}) %collective-permute-start.9) | collective-permute-done | bytes 16416 | tf_op jit(solution)/shard_map/ppermute | solution.py:43
  43.3 0.4 collective-permute-done.8.rest_1_
  43.7 2.8 %collective-permute-done.7.rest_0_ = bf16[32,256]{1,0:T(8,128)(2,1)S(1)} collective-permute-done((bf16[32,256]{1,0:T(8,128)(2,1)S(1)}, bf16[32,256]{1,0:T(8,128)(2,1)S(1)}, u32[]{:S(2)}, u32[]{:S(2)}) %collective-permute-start.7) | collective-permute-done | bytes 16416 | tf_op jit(solution)/shard_map/ppermute | solution.py:43
  46.5 1.5 %collective-permute-start.12 = (bf16[128,256]{1,0:T(8,128)(2,1)S(1)}, bf16[128,256]{1,0:T(8,128)(2,1)S(1)}, u32[]{:S(2)}, u32[]{:S(2)}) collective-permute-start(bf16[128,256]{1,0:T(8,128)(2,1)S(1)} %join.2.piece), channel_id=1, source_target_pairs={{0,32},{16,48},{32,0},{48,16},{1,33},{17,49},{33,1},{49,17},{2,34}... | collective-permute-start | bytes 196616 | tf_op jit(solution)/shard_map/ppermute | solution.py:43
  48.0 2.0 %collective-permute-start.11 = (bf16[128,256]{1,0:T(8,128)(2,1)S(1)}, bf16[128,256]{1,0:T(8,128)(2,1)S(1)}, u32[]{:S(2)}, u32[]{:S(2)}) collective-permute-start(bf16[128,256]{1,0:T(8,128)(2,1)S(1)} %join.2.piece), channel_id=1, source_target_pairs={{0,16},{16,32},{32,48},{48,0},{1,17},{17,33},{33,49},{49,1},{2,18}... | collective-permute-start | bytes 196616 | tf_op jit(solution)/shard_map/ppermute | solution.py:43
  50.0 0.0 collective-permute-start.10
  50.0 2.3 %collective-permute-done.12.rest_2_ = bf16[128,256]{1,0:T(8,128)(2,1)S(1)} collective-permute-done((bf16[128,256]{1,0:T(8,128)(2,1)S(1)}, bf16[128,256]{1,0:T(8,128)(2,1)S(1)}, u32[]{:S(2)}, u32[]{:S(2)}) %collective-permute-start.12) | collective-permute-done | bytes 65568 | tf_op jit(solution)/shard_map/ppermute | solution.py:43
  52.2 0.0 collective-permute-done.11.rest_1_
  52.2 3.2 %collective-permute-done.10.rest_0_ = bf16[128,256]{1,0:T(8,128)(2,1)S(1)} collective-permute-done((bf16[128,256]{1,0:T(8,128)(2,1)S(1)}, bf16[128,256]{1,0:T(8,128)(2,1)S(1)}, u32[]{:S(2)}, u32[]{:S(2)}) %collective-permute-start.10) | collective-permute-done | bytes 65568 | tf_op jit(solution)/shard_map/ppermute | solution.py:43
  55.5 0.1 collective-permute-start.13
  55.6 1.4 %near_field.1.part = f32[128,4096]{1,0:T(8,128)S(1)} custom-call(bf16[512,256]{1,0:T(8,128)(2,1)S(1)} %join.3.src, bf16[1024,4096]{1,0:T(8,128)(2,1)S(1)} %get-tuple-element.54.basis), custom_call_target="tpu_custom_call" | custom-call | flops 1073741824 | bytes 1048576 | tf_op jit(solution)/shard_map/near_field/pallas_call | solution.py:323
  57.0 0.1 collective-permute-done.13.src
  57.1 0.1 turned.1.f
  57.2 0.5 synthesis.3
  57.7 0.5 synthesis.4
  58.2 1.3 %collective-permute-start.14 = (bf16[256,512]{1,0:T(8,128)(2,1)S(1)}, bf16[256,512]{1,0:T(8,128)(2,1)S(1)}, u32[]{:S(2)}, u32[]{:S(2)}) collective-permute-start(bf16[256,512]{1,0:T(8,128)(2,1)S(1)} %get-tuple-element.59), channel_id=1, source_target_pairs={{0,4},{2,6},{4,0},{6,2},{1,5},{3,7},{5,1},{7,3},{8,12},{10,14},{12... | collective-permute-start | bytes 786440 | tf_op jit(solution)/shard_map/ppermute | solution.py:43
  59.5 1.0 %collective-permute-start.15 = (bf16[256,512]{1,0:T(8,128)(2,1)S(1)}, bf16[256,512]{1,0:T(8,128)(2,1)S(1)}, u32[]{:S(2)}, u32[]{:S(2)}) collective-permute-start(bf16[256,512]{1,0:T(8,128)(2,1)S(1)} %get-tuple-element.60), channel_id=1, source_target_pairs={{0,1},{1,0},{2,3},{3,2},{4,5},{5,4},{6,7},{7,6},{8,9},{9,8},{10,11... | collective-permute-start | bytes 786440 | tf_op jit(solution)/shard_map/ppermute | solution.py:43
  60.6 0.8 synthesis.5.own
  61.4 7.0 %collective-permute-done.14.got.rest_0_ = bf16[256,512]{1,0:T(8,128)(2,1)S(1)} collective-permute-done((bf16[256,512]{1,0:T(8,128)(2,1)S(1)}, bf16[256,512]{1,0:T(8,128)(2,1)S(1)}, u32[]{:S(2)}, u32[]{:S(2)}) %collective-permute-start.14) | collective-permute-done | bytes 262176 | tf_op jit(solution)/shard_map/ppermute | solution.py:43
  68.4 1.1 %collective-permute-start.18 = (bf16[128,512]{1,0:T(8,128)(2,1)S(1)}, bf16[128,512]{1,0:T(8,128)(2,1)S(1)}, u32[]{:S(2)}, u32[]{:S(2)}) collective-permute-start(bf16[128,512]{1,0:T(8,128)(2,1)S(1)} %merge.3), channel_id=1, source_target_pairs={{0,1},{1,0},{2,3},{3,2},{4,5},{5,4},{6,7},{7,6},{8,9},{9,8},{10,11... | collective-permute-start | bytes 393224 | tf_op jit(solution)/shard_map/ppermute | solution.py:43
  69.6 0.6 collective-permute-start.16
  70.1 1.5 %collective-permute-start.17 = (bf16[128,512]{1,0:T(8,128)(2,1)S(1)}, bf16[128,512]{1,0:T(8,128)(2,1)S(1)}, u32[]{:S(2)}, u32[]{:S(2)}) collective-permute-start(bf16[128,512]{1,0:T(8,128)(2,1)S(1)} %get-tuple-element.62), channel_id=1, source_target_pairs={{0,6},{2,0},{4,2},{6,4},{1,7},{3,1},{5,3},{7,5},{8,14},{10,8},{12,... | collective-permute-start | bytes 393224 | tf_op jit(solution)/shard_map/ppermute | solution.py:43
  71.7 1.8 %collective-permute-done.18.rest_3_ = bf16[128,512]{1,0:T(8,128)(2,1)S(1)} collective-permute-done((bf16[128,512]{1,0:T(8,128)(2,1)S(1)}, bf16[128,512]{1,0:T(8,128)(2,1)S(1)}, u32[]{:S(2)}, u32[]{:S(2)}) %collective-permute-start.18) | collective-permute-done | bytes 131104 | tf_op jit(solution)/shard_map/ppermute | solution.py:43
  73.5 1.2 %collective-permute-done.16.rest_1_ = bf16[128,512]{1,0:T(8,128)(2,1)S(1)} collective-permute-done((bf16[128,512]{1,0:T(8,128)(2,1)S(1)}, bf16[128,512]{1,0:T(8,128)(2,1)S(1)}, u32[]{:S(2)}, u32[]{:S(2)}) %collective-permute-start.16) | collective-permute-done | bytes 131104 | tf_op jit(solution)/shard_map/ppermute | solution.py:43
  74.6 1.7 %collective-permute-done.17.rest_2_ = bf16[128,512]{1,0:T(8,128)(2,1)S(1)} collective-permute-done((bf16[128,512]{1,0:T(8,128)(2,1)S(1)}, bf16[128,512]{1,0:T(8,128)(2,1)S(1)}, u32[]{:S(2)}, u32[]{:S(2)}) %collective-permute-start.17) | collective-permute-done | bytes 131104 | tf_op jit(solution)/shard_map/ppermute | solution.py:43
  76.3 0.8 %finish.1 = bf16[512,128]{1,0:T(8,128)(2,1)} custom-call(f32[8,128]{1,0:T(8,128)S(1)} %get-tuple-element.51.total, f32[512,128]{1,0:T(8,128)S(1)} %get-tuple-element.39.given.linear, f32[512,512]{1,0:T(8,128)S(1)} %synthesis.5.own, bf16[256,512]{1,0:T(8,128)(2,1)S(1)} %collective-permute-done.14.got.rest_0_, ...), custom_call_target="tpu_custom_call" | custom-call | bytes 1048576 | tf_op jit(solution)/shard_map/finish/pallas_call | solution.py:345
  (8 shorter events, 0.1 us)
Async XLA Ops:
  8.9 4.7 %collective-permute-start = (bf16[1040,128]{1,0:T(8,128)(2,1)S(1)}, bf16[1040,128]{1,0:T(8,128)(2,1)S(1)}, u32[]{:S(2)}, u32[]{:S(2)}) collective-permute-start(bf16[1040,128]{1,0:T(8,128)(2,1)S(1)} %get-tuple-element.42), channel_id=1, source_target_pairs={{0,8},{8,0},{1,9},{9,1},{2,10},{10,2},{3,11},{11,3},{4,12},{12,4},... | collective-permute-start | bytes 798728 | tf_op jit(solution)/shard_map/ppermute | solution.py:43
  13.7 5.3 %collective-permute-start.1 = (bf16[272,128]{1,0:T(8,128)(2,1)S(1)}, bf16[272,128]{1,0:T(8,128)(2,1)S(1)}, u32[]{:S(2)}, u32[]{:S(2)}) collective-permute-start(bf16[272,128]{1,0:T(8,128)(2,1)S(1)} %get-tuple-element.44), channel_id=1, source_target_pairs={{0,16},{16,32},{32,48},{48,0},{1,17},{17,33},{33,49},{49,1},{2,18}... | collective-permute-start | bytes 208904 | tf_op jit(solution)/shard_map/ppermute | solution.py:43
  14.2 5.5 %collective-permute-start.2 = (bf16[272,128]{1,0:T(8,128)(2,1)S(1)}, bf16[272,128]{1,0:T(8,128)(2,1)S(1)}, u32[]{:S(2)}, u32[]{:S(2)}) collective-permute-start(bf16[272,128]{1,0:T(8,128)(2,1)S(1)} %get-tuple-element.45), channel_id=1, source_target_pairs={{0,48},{16,0},{32,16},{48,32},{1,49},{17,1},{33,17},{49,33},{2,50}... | collective-permute-start | bytes 208904 | tf_op jit(solution)/shard_map/ppermute | solution.py:43
  15.7 5.8 %collective-permute-start.3 = (bf16[272,128]{1,0:T(8,128)(2,1)S(1)}, bf16[272,128]{1,0:T(8,128)(2,1)S(1)}, u32[]{:S(2)}, u32[]{:S(2)}) collective-permute-start(bf16[272,128]{1,0:T(8,128)(2,1)S(1)} %get-tuple-element.46), channel_id=1, source_target_pairs={{0,32},{16,48},{32,0},{48,16},{1,33},{17,49},{33,1},{49,17},{2,34}... | collective-permute-start | bytes 208904 | tf_op jit(solution)/shard_map/ppermute | solution.py:43
  17.1 18.0 %copy-start = (bf16[32,2,128,128]{3,2,1,0:T(8,128)(2,1)S(1)}, bf16[32,2,128,128]{3,2,1,0:T(8,128)(2,1)}, u32[]{:S(2)}) copy-start(bf16[32,2,128,128]{3,2,1,0:T(8,128)(2,1)} %weight.1) | copy-start | bytes 6291460
  21.7 11.4 %collective-permute-start.4 = (bf16[48,256]{1,0:T(8,128)(2,1)S(1)}, bf16[48,256]{1,0:T(8,128)(2,1)S(1)}, u32[]{:S(2)}, u32[]{:S(2)}) collective-permute-start(bf16[48,256]{1,0:T(8,128)(2,1)S(1)} %get-tuple-element.48), channel_id=1, source_target_pairs={{0,128},{64,192},{128,0},{192,64},{1,129},{65,193},{129,1},{193,65... | collective-permute-start | bytes 73736 | tf_op jit(solution)/shard_map/ppermute | solution.py:43
  28.9 5.9 %collective-permute-start.5 = (bf16[48,256]{1,0:T(8,128)(2,1)S(1)}, bf16[48,256]{1,0:T(8,128)(2,1)S(1)}, u32[]{:S(2)}, u32[]{:S(2)}) collective-permute-start(bf16[48,256]{1,0:T(8,128)(2,1)S(1)} %get-tuple-element.49), channel_id=1, source_target_pairs={{0,64},{64,128},{128,192},{192,0},{1,65},{65,129},{129,193},{193,1... | collective-permute-start | bytes 73736 | tf_op jit(solution)/shard_map/ppermute | solution.py:43
  30.4 4.7 %collective-permute-start.6 = (bf16[48,256]{1,0:T(8,128)(2,1)S(1)}, bf16[48,256]{1,0:T(8,128)(2,1)S(1)}, u32[]{:S(2)}, u32[]{:S(2)}) collective-permute-start(bf16[48,256]{1,0:T(8,128)(2,1)S(1)} %get-tuple-element.50), channel_id=1, source_target_pairs={{0,192},{64,0},{128,64},{192,128},{1,193},{65,1},{129,65},{193,129... | collective-permute-start | bytes 73736 | tf_op jit(solution)/shard_map/ppermute | solution.py:43
  35.5 7.8 %collective-permute-start.9 = (bf16[32,256]{1,0:T(8,128)(2,1)S(1)}, bf16[32,256]{1,0:T(8,128)(2,1)S(1)}, u32[]{:S(2)}, u32[]{:S(2)}) collective-permute-start(bf16[32,256]{1,0:T(8,128)(2,1)S(1)} %get-tuple-element.52.piece), channel_id=1, source_target_pairs={{0,128},{64,192},{128,0},{192,64},{1,129},{65,193},{129,1},{193,65... | collective-permute-start | bytes 49160 | tf_op jit(solution)/shard_map/ppermute | solution.py:43
  37.9 5.8 %collective-permute-start.8 = (bf16[32,256]{1,0:T(8,128)(2,1)S(1)}, bf16[32,256]{1,0:T(8,128)(2,1)S(1)}, u32[]{:S(2)}, u32[]{:S(2)}) collective-permute-start(bf16[32,256]{1,0:T(8,128)(2,1)S(1)} %get-tuple-element.52.piece), channel_id=1, source_target_pairs={{0,64},{64,128},{128,192},{192,0},{1,65},{65,129},{129,193},{193,1... | collective-permute-start | bytes 49160 | tf_op jit(solution)/shard_map/ppermute | solution.py:43
  41.8 4.6 %collective-permute-start.7 = (bf16[32,256]{1,0:T(8,128)(2,1)S(1)}, bf16[32,256]{1,0:T(8,128)(2,1)S(1)}, u32[]{:S(2)}, u32[]{:S(2)}) collective-permute-start(bf16[32,256]{1,0:T(8,128)(2,1)S(1)} %get-tuple-element.52.piece), channel_id=1, source_target_pairs={{0,192},{64,0},{128,64},{192,128},{1,193},{65,1},{129,65},{193,129... | collective-permute-start | bytes 49160 | tf_op jit(solution)/shard_map/ppermute | solution.py:43
  46.5 5.8 %collective-permute-start.12 = (bf16[128,256]{1,0:T(8,128)(2,1)S(1)}, bf16[128,256]{1,0:T(8,128)(2,1)S(1)}, u32[]{:S(2)}, u32[]{:S(2)}) collective-permute-start(bf16[128,256]{1,0:T(8,128)(2,1)S(1)} %join.2.piece), channel_id=1, source_target_pairs={{0,32},{16,48},{32,0},{48,16},{1,33},{17,49},{33,1},{49,17},{2,34}... | collective-permute-start | bytes 196616 | tf_op jit(solution)/shard_map/ppermute | solution.py:43
  48.0 4.3 %collective-permute-start.11 = (bf16[128,256]{1,0:T(8,128)(2,1)S(1)}, bf16[128,256]{1,0:T(8,128)(2,1)S(1)}, u32[]{:S(2)}, u32[]{:S(2)}) collective-permute-start(bf16[128,256]{1,0:T(8,128)(2,1)S(1)} %join.2.piece), channel_id=1, source_target_pairs={{0,16},{16,32},{32,48},{48,0},{1,17},{17,33},{33,49},{49,1},{2,18}... | collective-permute-start | bytes 196616 | tf_op jit(solution)/shard_map/ppermute | solution.py:43
  50.0 5.5 %collective-permute-start.10 = (bf16[128,256]{1,0:T(8,128)(2,1)S(1)}, bf16[128,256]{1,0:T(8,128)(2,1)S(1)}, u32[]{:S(2)}, u32[]{:S(2)}) collective-permute-start(bf16[128,256]{1,0:T(8,128)(2,1)S(1)} %join.2.piece), channel_id=1, source_target_pairs={{0,48},{16,0},{32,16},{48,32},{1,49},{17,1},{33,17},{49,33},{2,50}... | collective-permute-start | bytes 196616 | tf_op jit(solution)/shard_map/ppermute | solution.py:43
  55.5 1.6 %collective-permute-start.13 = (bf16[512,256]{1,0:T(8,128)(2,1)S(1)}, bf16[512,256]{1,0:T(8,128)(2,1)S(1)}, u32[]{:S(2)}, u32[]{:S(2)}) collective-permute-start(bf16[512,256]{1,0:T(8,128)(2,1)S(1)} %join.3.src), channel_id=1, source_target_pairs={{0,8},{8,0},{1,9},{9,1},{2,10},{10,2},{3,11},{11,3},{4,12},{12,4},... | collective-permute-start | bytes 786440 | tf_op jit(solution)/shard_map/ppermute | solution.py:43
  58.2 10.2 %collective-permute-start.14 = (bf16[256,512]{1,0:T(8,128)(2,1)S(1)}, bf16[256,512]{1,0:T(8,128)(2,1)S(1)}, u32[]{:S(2)}, u32[]{:S(2)}) collective-permute-start(bf16[256,512]{1,0:T(8,128)(2,1)S(1)} %get-tuple-element.59), channel_id=1, source_target_pairs={{0,4},{2,6},{4,0},{6,2},{1,5},{3,7},{5,1},{7,3},{8,12},{10,14},{12... | collective-permute-start | bytes 786440 | tf_op jit(solution)/shard_map/ppermute | solution.py:43
  59.5 10.0 %collective-permute-start.15 = (bf16[256,512]{1,0:T(8,128)(2,1)S(1)}, bf16[256,512]{1,0:T(8,128)(2,1)S(1)}, u32[]{:S(2)}, u32[]{:S(2)}) collective-permute-start(bf16[256,512]{1,0:T(8,128)(2,1)S(1)} %get-tuple-element.60), channel_id=1, source_target_pairs={{0,1},{1,0},{2,3},{3,2},{4,5},{5,4},{6,7},{7,6},{8,9},{9,8},{10,11... | collective-permute-start | bytes 786440 | tf_op jit(solution)/shard_map/ppermute | solution.py:43
  68.4 5.1 %collective-permute-start.18 = (bf16[128,512]{1,0:T(8,128)(2,1)S(1)}, bf16[128,512]{1,0:T(8,128)(2,1)S(1)}, u32[]{:S(2)}, u32[]{:S(2)}) collective-permute-start(bf16[128,512]{1,0:T(8,128)(2,1)S(1)} %merge.3), channel_id=1, source_target_pairs={{0,1},{1,0},{2,3},{3,2},{4,5},{5,4},{6,7},{7,6},{8,9},{9,8},{10,11... | collective-permute-start | bytes 393224 | tf_op jit(solution)/shard_map/ppermute | solution.py:43
  69.6 5.0 %collective-permute-start.16 = (bf16[128,512]{1,0:T(8,128)(2,1)S(1)}, bf16[128,512]{1,0:T(8,128)(2,1)S(1)}, u32[]{:S(2)}, u32[]{:S(2)}) collective-permute-start(bf16[128,512]{1,0:T(8,128)(2,1)S(1)} %get-tuple-element.61), channel_id=1, source_target_pairs={{0,2},{2,4},{4,6},{6,0},{1,3},{3,5},{5,7},{7,1},{8,10},{10,12},{12... | collective-permute-start | bytes 393224 | tf_op jit(solution)/shard_map/ppermute | solution.py:43
  70.1 6.2 %collective-permute-start.17 = (bf16[128,512]{1,0:T(8,128)(2,1)S(1)}, bf16[128,512]{1,0:T(8,128)(2,1)S(1)}, u32[]{:S(2)}, u32[]{:S(2)}) collective-permute-start(bf16[128,512]{1,0:T(8,128)(2,1)S(1)} %get-tuple-element.62), channel_id=1, source_target_pairs={{0,6},{2,0},{4,2},{6,4},{1,7},{3,1},{5,3},{7,5},{8,14},{10,8},{12,... | collective-permute-start | bytes 393224 | tf_op jit(solution)/shard_map/ppermute | solution.py:43

commit v9 on v8

--- a/solution.py
+++ b/solution.py
@@ -310,10 +310,10 @@
 
     mine, basis = near(3, 1, linear, False)
     outs = call(pair_body, 2, [one(2 * C + 16, C, BF)] * 3, "pair")(mine, got)
-    across = {s: send(outs[s - 1], ("x",), s) for s in FAR_LAST}
+    across = {s: send(outs[s - 1], ("x",), s) for s in (2, 1, 3)}
     mine, basis = near(1, 0, basis, True)
     keep, *outs = call(x_body, 5, [one(48, 2 * C, F32)] + [one(48, 2 * C, BF)] * 3, "x_sum")(
-        mine, got, *[across[s] for s in FAR_LAST]
+        mine, got, *[across[s] for s in (2, 1, 3)]
     )
     got = [send(outs[s - 1], ("z_hi",), s) for s in (2, 1, 3)]
     piece, total = call(filter_body, 5, [one(32, 2 * C, BF), one(8, C, F32)], "filter")(keep, *got, mode_weight)
@@ -334,10 +334,10 @@
     def merge(*pairs):
         return call(functools.partial(merge_body, pairs), 2, [one(C, 512, BF)] * len(pairs), "merge")
 
+    out, far_basis, part = field(((0, 2), (1, 2)), BF, far_basis, part)
+    across = send(out, ("y",), 2)
     out, far_basis, part = field(((1, 1), (1, 3)), BF, far_basis, part)
     beside = send(out, ("z_lo",), 1)
-    out, far_basis, part = field(((0, 2), (1, 2)), BF, far_basis, part)
-    across = send(out, ("y",), 2)
     (own,) = field(((0, 1), (0, 3), (1, 0), (0, 0)), F32, far_basis, part, True)
     one_step, three_steps = merge((0, 0), (1, 1))(own, beside)
     (out,) = merge((2, 1))(own, across)

time: 77.3 us -> 75.6 us (0.978)
  the two profiles are of different devices: /device:TPU:30 before, /device:TPU:1 now
where the time goes in v9:
time: 75.6 us; the launch traced here: 75.5 us
  starting transfers between devices  39.7 us (53%)
  Pallas kernels  20 us (26%)
  waiting for transfers between devices  15.7 us (21%)
    ppermute x19, starting transfers between devices, send(): return lax.ppermute(value, axes, [(j, (j + shift) % n) for j in range(n)])  39.7 us
    ppermute x19, waiting for transfers between devices, send(): return lax.ppermute(value, axes, [(j, (j + shift) % n) for j in range(n)])  15.7 us
    pallas_call x1, Pallas kernels, on_device(): call(first_body, 0, [pltpu.VMEM((8 * C + 16, C), BF), pltpu.VMEM((8 * C,...  8.85 us
    pallas_call x2, Pallas kernels, near(): call(functools.partial(near_body, count, first), 4, [pltpu.VMEM((count *...  6.43 us
    pallas_call x3, Pallas kernels, field(): call(functools.partial(synthesis_body, places), 3, [one(len(places) * C,...  1.72 us
  transfers between devices with their start and end apart: 19, of which 13 were waited for; matrix products, arithmetic and copies ran while one was open for 0% of the time, Pallas kernels for 11%

profile of v9, /device:TPU:1, one launch (start us, length us, event | category | flops | bytes accessed | tf_op | source)
XLA Modules:
  0.0 75.5 jit_solution(2213514173730099361)
XLA Ops:
  0.0 8.9 %first.1 = (bf16[1040,128]{1,0:T(8,128)(2,1)S(1)}, bf16[1024,4096]{1,0:T(8,128)(2,1)S(1)}, f32[256,2,32,128]{3,2,1,0:T(8,128)S(1)}, f32[32,2,32,128]{3,2,1,0:T(8...) custom-call(f32[3,4096]{1,0:T(4,128)} %refs_0_.1, ...), custom_call_target="tpu_custom_call" | custom-call | flops 2147483648 | bytes 1048576 | tf_op jit(solution)/shard_map/first/pallas_call | solution.py:292
  8.9 3.3 %collective-permute-start = (bf16[1040,128]{1,0:T(8,128)(2,1)S(1)}, bf16[1040,128]{1,0:T(8,128)(2,1)S(1)}, u32[]{:S(2)}, u32[]{:S(2)}) collective-permute-start(bf16[1040,128]{1,0:T(8,128)(2,1)S(1)} %get-tuple-element.42), channel_id=1, source_target_pairs={{0,8},{8,0},{1,9},{9,1},{2,10},{10,2},{3,11},{11,3},{4,12},{12,4},... | collective-permute-start | bytes 798728 | tf_op jit(solution)/shard_map/ppermute | solution.py:43
  12.2 4.6 %near.2 = (bf16[784,128]{1,0:T(8,128)(2,1)S(1)}, bf16[1024,4096]{1,0:T(8,128)(2,1)S(1)}) custom-call(s32[8,128]{1,0:T(8,128)S(1)} %get-tuple-element.34.index, f32[32,128]{1,0:T(8,128)S(1)} %get-tuple-element.35.quad, f32[256,2,32,128]{3,2,1,0:T(8,128)S(1)} %get-tuple-element.36.exy, f32[32,2,32,128]{3,2,1,0:T(8,128)S(1)} %get-tuple-element.37.ez, ...), custom_call_target="tpu_custom_call" | custom-call | flops 1610612736 | bytes 1048576 | tf_op jit(solution)/shard_map/near/pallas_call | solution.py:305
  16.8 0.0 collective-permute-done.got.got0
  16.8 0.1 pair.1
  16.9 1.1 %collective-permute-start.1 = (bf16[272,128]{1,0:T(8,128)(2,1)S(1)}, bf16[272,128]{1,0:T(8,128)(2,1)S(1)}, u32[]{:S(2)}, u32[]{:S(2)}) collective-permute-start(bf16[272,128]{1,0:T(8,128)(2,1)S(1)} %get-tuple-element.44), channel_id=1, source_target_pairs={{0,32},{16,48},{32,0},{48,16},{1,33},{17,49},{33,1},{49,17},{2,34}... | collective-permute-start | bytes 208904 | tf_op jit(solution)/shard_map/ppermute | solution.py:43
  17.9 0.3 collective-permute-start.2
  18.3 2.4 %collective-permute-start.3 = (bf16[272,128]{1,0:T(8,128)(2,1)S(1)}, bf16[272,128]{1,0:T(8,128)(2,1)S(1)}, u32[]{:S(2)}, u32[]{:S(2)}) collective-permute-start(bf16[272,128]{1,0:T(8,128)(2,1)S(1)} %get-tuple-element.46), channel_id=1, source_target_pairs={{0,48},{16,0},{32,16},{48,32},{1,49},{17,1},{33,17},{49,33},{2,50}... | collective-permute-start | bytes 208904 | tf_op jit(solution)/shard_map/ppermute | solution.py:43
  20.6 1.8 %near.3 = (bf16[272,128]{1,0:T(8,128)(2,1)S(1)}, bf16[1024,4096]{1,0:T(8,128)(2,1)S(1)}) custom-call(s32[8,128]{1,0:T(8,128)S(1)} %get-tuple-element.34.index, f32[32,128]{1,0:T(8,128)S(1)} %get-tuple-element.35.quad, f32[256,2,32,128]{3,2,1,0:T(8,128)S(1)} %get-tuple-element.36.exy, ...), custom_call_target="tpu_custom_call", output_to_operand_aliasing={{1}: (5, {})} | custom-call | flops 536870912 | bytes 1048576 | tf_op jit(solution)/shard_map/near/pallas_call | solution.py:305
  22.5 0.0 collective-permute-done.1.got1
  22.5 1.4 %collective-permute-done.2.got2 = bf16[272,128]{1,0:T(8,128)(2,1)S(1)} collective-permute-done((bf16[272,128]{1,0:T(8,128)(2,1)S(1)}, bf16[272,128]{1,0:T(8,128)(2,1)S(1)}, u32[]{:S(2)}, u32[]{:S(2)}) %collective-permute-start.2) | collective-permute-done | bytes 69664 | tf_op jit(solution)/shard_map/ppermute | solution.py:43
  23.9 0.0 collective-permute-done.3.got3
  23.9 0.1 x_sum.1
  24.0 5.6 %collective-permute-start.4 = (bf16[48,256]{1,0:T(8,128)(2,1)S(1)}, bf16[48,256]{1,0:T(8,128)(2,1)S(1)}, u32[]{:S(2)}, u32[]{:S(2)}) collective-permute-start(bf16[48,256]{1,0:T(8,128)(2,1)S(1)} %get-tuple-element.48), channel_id=1, source_target_pairs={{0,128},{64,192},{128,0},{192,64},{1,129},{65,193},{129,1},{193,65... | collective-permute-start | bytes 73736 | tf_op jit(solution)/shard_map/ppermute | solution.py:43
  29.6 1.2 %collective-permute-start.5 = (bf16[48,256]{1,0:T(8,128)(2,1)S(1)}, bf16[48,256]{1,0:T(8,128)(2,1)S(1)}, u32[]{:S(2)}, u32[]{:S(2)}) collective-permute-start(bf16[48,256]{1,0:T(8,128)(2,1)S(1)} %get-tuple-element.49), channel_id=1, source_target_pairs={{0,64},{64,128},{128,192},{192,0},{1,65},{65,129},{129,193},{193,1... | collective-permute-start | bytes 73736 | tf_op jit(solution)/shard_map/ppermute | solution.py:43
  30.8 2.4 %collective-permute-start.6 = (bf16[48,256]{1,0:T(8,128)(2,1)S(1)}, bf16[48,256]{1,0:T(8,128)(2,1)S(1)}, u32[]{:S(2)}, u32[]{:S(2)}) collective-permute-start(bf16[48,256]{1,0:T(8,128)(2,1)S(1)} %get-tuple-element.50), channel_id=1, source_target_pairs={{0,192},{64,0},{128,64},{192,128},{1,193},{65,1},{129,65},{193,129... | collective-permute-start | bytes 73736 | tf_op jit(solution)/shard_map/ppermute | solution.py:43
  33.2 0.0 collective-permute-done.4.got1
  33.2 1.2 %collective-permute-done.5.got2 = bf16[48,256]{1,0:T(8,128)(2,1)S(1)} collective-permute-done((bf16[48,256]{1,0:T(8,128)(2,1)S(1)}, bf16[48,256]{1,0:T(8,128)(2,1)S(1)}, u32[]{:S(2)}, u32[]{:S(2)}) %collective-permute-start.5) | collective-permute-done | bytes 24608 | tf_op jit(solution)/shard_map/ppermute | solution.py:43
  34.4 0.1 collective-permute-done.6.got3
  34.5 0.4 filter.1
  34.9 2.4 %collective-permute-start.9 = (bf16[32,256]{1,0:T(8,128)(2,1)S(1)}, bf16[32,256]{1,0:T(8,128)(2,1)S(1)}, u32[]{:S(2)}, u32[]{:S(2)}) collective-permute-start(bf16[32,256]{1,0:T(8,128)(2,1)S(1)} %get-tuple-element.52.piece), channel_id=1, source_target_pairs={{0,128},{64,192},{128,0},{192,64},{1,129},{65,193},{129,1},{193,65... | collective-permute-start | bytes 49160 | tf_op jit(solution)/shard_map/ppermute | solution.py:43
  37.2 3.3 %collective-permute-start.8 = (bf16[32,256]{1,0:T(8,128)(2,1)S(1)}, bf16[32,256]{1,0:T(8,128)(2,1)S(1)}, u32[]{:S(2)}, u32[]{:S(2)}) collective-permute-start(bf16[32,256]{1,0:T(8,128)(2,1)S(1)} %get-tuple-element.52.piece), channel_id=1, source_target_pairs={{0,64},{64,128},{128,192},{192,0},{1,65},{65,129},{129,193},{193,1... | collective-permute-start | bytes 49160 | tf_op jit(solution)/shard_map/ppermute | solution.py:43
  40.5 0.3 collective-permute-start.7
  40.8 0.6 collective-permute-done.9.rest_2_
  41.4 0.5 collective-permute-done.8.rest_1_
  42.0 2.3 %collective-permute-done.7.rest_0_ = bf16[32,256]{1,0:T(8,128)(2,1)S(1)} collective-permute-done((bf16[32,256]{1,0:T(8,128)(2,1)S(1)}, bf16[32,256]{1,0:T(8,128)(2,1)S(1)}, u32[]{:S(2)}, u32[]{:S(2)}) %collective-permute-start.7) | collective-permute-done | bytes 16416 | tf_op jit(solution)/shard_map/ppermute | solution.py:43
  44.3 1.3 %collective-permute-start.12 = (bf16[128,256]{1,0:T(8,128)(2,1)S(1)}, bf16[128,256]{1,0:T(8,128)(2,1)S(1)}, u32[]{:S(2)}, u32[]{:S(2)}) collective-permute-start(bf16[128,256]{1,0:T(8,128)(2,1)S(1)} %join.2.piece), channel_id=1, source_target_pairs={{0,32},{16,48},{32,0},{48,16},{1,33},{17,49},{33,1},{49,17},{2,34}... | collective-permute-start | bytes 196616 | tf_op jit(solution)/shard_map/ppermute | solution.py:43
  45.6 2.4 %collective-permute-start.11 = (bf16[128,256]{1,0:T(8,128)(2,1)S(1)}, bf16[128,256]{1,0:T(8,128)(2,1)S(1)}, u32[]{:S(2)}, u32[]{:S(2)}) collective-permute-start(bf16[128,256]{1,0:T(8,128)(2,1)S(1)} %join.2.piece), channel_id=1, source_target_pairs={{0,16},{16,32},{32,48},{48,0},{1,17},{17,33},{33,49},{49,1},{2,18}... | collective-permute-start | bytes 196616 | tf_op jit(solution)/shard_map/ppermute | solution.py:43
  48.0 0.3 collective-permute-start.10
  48.3 0.6 collective-permute-done.12.rest_2_
  48.9 1.0 %collective-permute-done.11.rest_1_ = bf16[128,256]{1,0:T(8,128)(2,1)S(1)} collective-permute-done((bf16[128,256]{1,0:T(8,128)(2,1)S(1)}, bf16[128,256]{1,0:T(8,128)(2,1)S(1)}, u32[]{:S(2)}, u32[]{:S(2)}) %collective-permute-start.11) | collective-permute-done | bytes 65568 | tf_op jit(solution)/shard_map/ppermute | solution.py:43
  49.9 1.2 %collective-permute-done.10.rest_0_ = bf16[128,256]{1,0:T(8,128)(2,1)S(1)} collective-permute-done((bf16[128,256]{1,0:T(8,128)(2,1)S(1)}, bf16[128,256]{1,0:T(8,128)(2,1)S(1)}, u32[]{:S(2)}, u32[]{:S(2)}) %collective-permute-start.10) | collective-permute-done | bytes 65568 | tf_op jit(solution)/shard_map/ppermute | solution.py:43
  51.1 6.0 %collective-permute-start.13 = (bf16[512,256]{1,0:T(8,128)(2,1)S(1)}, bf16[512,256]{1,0:T(8,128)(2,1)S(1)}, u32[]{:S(2)}, u32[]{:S(2)}) collective-permute-start(bf16[512,256]{1,0:T(8,128)(2,1)S(1)} %join.3.src), channel_id=1, source_target_pairs={{0,8},{8,0},{1,9},{9,1},{2,10},{10,2},{3,11},{11,3},{4,12},{12,4},... | collective-permute-start | bytes 786440 | tf_op jit(solution)/shard_map/ppermute | solution.py:43
  57.2 1.4 %near_field.1.part = f32[128,4096]{1,0:T(8,128)S(1)} custom-call(bf16[512,256]{1,0:T(8,128)(2,1)S(1)} %join.3.src, bf16[1024,4096]{1,0:T(8,128)(2,1)S(1)} %get-tuple-element.54.basis), custom_call_target="tpu_custom_call" | custom-call | flops 1073741824 | bytes 1048576 | tf_op jit(solution)/shard_map/near_field/pallas_call | solution.py:323
  58.6 0.1 turned.1.f
  58.7 0.5 synthesis.3
  59.2 0.5 synthesis.4
  59.7 0.9 %collective-permute-start.15 = (bf16[256,512]{1,0:T(8,128)(2,1)S(1)}, bf16[256,512]{1,0:T(8,128)(2,1)S(1)}, u32[]{:S(2)}, u32[]{:S(2)}) collective-permute-start(bf16[256,512]{1,0:T(8,128)(2,1)S(1)} %get-tuple-element.60), channel_id=1, source_target_pairs={{0,1},{1,0},{2,3},{3,2},{4,5},{5,4},{6,7},{7,6},{8,9},{9,8},{10,11... | collective-permute-start | bytes 786440 | tf_op jit(solution)/shard_map/ppermute | solution.py:43
  60.5 2.9 %collective-permute-start.14 = (bf16[256,512]{1,0:T(8,128)(2,1)S(1)}, bf16[256,512]{1,0:T(8,128)(2,1)S(1)}, u32[]{:S(2)}, u32[]{:S(2)}) collective-permute-start(bf16[256,512]{1,0:T(8,128)(2,1)S(1)} %get-tuple-element.59), channel_id=1, source_target_pairs={{0,4},{2,6},{4,0},{6,2},{1,5},{3,7},{5,1},{7,3},{8,12},{10,14},{12... | collective-permute-start | bytes 786440 | tf_op jit(solution)/shard_map/ppermute | solution.py:43
  63.4 0.8 %synthesis.5.own = f32[512,512]{1,0:T(8,128)S(1)} custom-call(bf16[128,1024]{1,0:T(8,128)(2,1)S(1)} %turned.1.f, bf16[1024,4096]{1,0:T(8,128)(2,1)S(1)} %get-tuple-element.57.basis, f32[128,4096]{1,0:T(8,128)S(1)} %get-tuple-element.58.part), custom_call_target="tpu_custom_call" | custom-call | flops 536870912 | bytes 1048576 | tf_op jit(solution)/shard_map/synthesis/pallas_call | solution.py:329
  64.2 3.3 %collective-permute-done.15.got = bf16[256,512]{1,0:T(8,128)(2,1)S(1)} collective-permute-done((bf16[256,512]{1,0:T(8,128)(2,1)S(1)}, bf16[256,512]{1,0:T(8,128)(2,1)S(1)}, u32[]{:S(2)}, u32[]{:S(2)}) %collective-permute-start.15) | collective-permute-done | bytes 262176 | tf_op jit(solution)/shard_map/ppermute | solution.py:43
  67.6 1.4 %collective-permute-start.16 = (bf16[128,512]{1,0:T(8,128)(2,1)S(1)}, bf16[128,512]{1,0:T(8,128)(2,1)S(1)}, u32[]{:S(2)}, u32[]{:S(2)}) collective-permute-start(bf16[128,512]{1,0:T(8,128)(2,1)S(1)} %get-tuple-element.61), channel_id=1, source_target_pairs={{0,2},{2,4},{4,6},{6,0},{1,3},{3,5},{5,7},{7,1},{8,10},{10,12},{12... | collective-permute-start | bytes 393224 | tf_op jit(solution)/shard_map/ppermute | solution.py:43
  68.9 1.5 %collective-permute-start.17 = (bf16[128,512]{1,0:T(8,128)(2,1)S(1)}, bf16[128,512]{1,0:T(8,128)(2,1)S(1)}, u32[]{:S(2)}, u32[]{:S(2)}) collective-permute-start(bf16[128,512]{1,0:T(8,128)(2,1)S(1)} %get-tuple-element.62), channel_id=1, source_target_pairs={{0,6},{2,0},{4,2},{6,4},{1,7},{3,1},{5,3},{7,5},{8,14},{10,8},{12,... | collective-permute-start | bytes 393224 | tf_op jit(solution)/shard_map/ppermute | solution.py:43
  70.5 0.8 %collective-permute-start.18 = (bf16[128,512]{1,0:T(8,128)(2,1)S(1)}, bf16[128,512]{1,0:T(8,128)(2,1)S(1)}, u32[]{:S(2)}, u32[]{:S(2)}) collective-permute-start(bf16[128,512]{1,0:T(8,128)(2,1)S(1)} %merge.3), channel_id=1, source_target_pairs={{0,1},{1,0},{2,3},{3,2},{4,5},{5,4},{6,7},{7,6},{8,9},{9,8},{10,11... | collective-permute-start | bytes 393224 | tf_op jit(solution)/shard_map/ppermute | solution.py:43
  71.4 1.4 %collective-permute-done.16.rest_1_ = bf16[128,512]{1,0:T(8,128)(2,1)S(1)} collective-permute-done((bf16[128,512]{1,0:T(8,128)(2,1)S(1)}, bf16[128,512]{1,0:T(8,128)(2,1)S(1)}, u32[]{:S(2)}, u32[]{:S(2)}) %collective-permute-start.16) | collective-permute-done | bytes 131104 | tf_op jit(solution)/shard_map/ppermute | solution.py:43
  72.7 0.3 collective-permute-done.17.rest_2_
  73.1 1.6 %collective-permute-done.18.rest_3_ = bf16[128,512]{1,0:T(8,128)(2,1)S(1)} collective-permute-done((bf16[128,512]{1,0:T(8,128)(2,1)S(1)}, bf16[128,512]{1,0:T(8,128)(2,1)S(1)}, u32[]{:S(2)}, u32[]{:S(2)}) %collective-permute-start.18) | collective-permute-done | bytes 131104 | tf_op jit(solution)/shard_map/ppermute | solution.py:43
  74.7 0.8 %finish.1 = bf16[512,128]{1,0:T(8,128)(2,1)} custom-call(f32[8,128]{1,0:T(8,128)S(1)} %get-tuple-element.51.total, f32[512,128]{1,0:T(8,128)S(1)} %get-tuple-element.39.given.linear, f32[512,512]{1,0:T(8,128)S(1)} %synthesis.5.own, bf16[256,512]{1,0:T(8,128)(2,1)S(1)} %collective-permute-done.14.got.rest_0_, ...), custom_call_target="tpu_custom_call" | custom-call | bytes 1048576 | tf_op jit(solution)/shard_map/finish/pallas_call | solution.py:345
  (8 shorter events, 0.1 us)
Async XLA Ops:
  8.9 7.9 %collective-permute-start = (bf16[1040,128]{1,0:T(8,128)(2,1)S(1)}, bf16[1040,128]{1,0:T(8,128)(2,1)S(1)}, u32[]{:S(2)}, u32[]{:S(2)}) collective-permute-start(bf16[1040,128]{1,0:T(8,128)(2,1)S(1)} %get-tuple-element.42), channel_id=1, source_target_pairs={{0,8},{8,0},{1,9},{9,1},{2,10},{10,2},{3,11},{11,3},{4,12},{12,4},... | collective-permute-start | bytes 798728 | tf_op jit(solution)/shard_map/ppermute | solution.py:43
  16.9 5.6 %collective-permute-start.1 = (bf16[272,128]{1,0:T(8,128)(2,1)S(1)}, bf16[272,128]{1,0:T(8,128)(2,1)S(1)}, u32[]{:S(2)}, u32[]{:S(2)}) collective-permute-start(bf16[272,128]{1,0:T(8,128)(2,1)S(1)} %get-tuple-element.44), channel_id=1, source_target_pairs={{0,32},{16,48},{32,0},{48,16},{1,33},{17,49},{33,1},{49,17},{2,34}... | collective-permute-start | bytes 208904 | tf_op jit(solution)/shard_map/ppermute | solution.py:43
  17.9 6.0 %collective-permute-start.2 = (bf16[272,128]{1,0:T(8,128)(2,1)S(1)}, bf16[272,128]{1,0:T(8,128)(2,1)S(1)}, u32[]{:S(2)}, u32[]{:S(2)}) collective-permute-start(bf16[272,128]{1,0:T(8,128)(2,1)S(1)} %get-tuple-element.45), channel_id=1, source_target_pairs={{0,16},{16,32},{32,48},{48,0},{1,17},{17,33},{33,49},{49,1},{2,18}... | collective-permute-start | bytes 208904 | tf_op jit(solution)/shard_map/ppermute | solution.py:43
  18.3 5.7 %collective-permute-start.3 = (bf16[272,128]{1,0:T(8,128)(2,1)S(1)}, bf16[272,128]{1,0:T(8,128)(2,1)S(1)}, u32[]{:S(2)}, u32[]{:S(2)}) collective-permute-start(bf16[272,128]{1,0:T(8,128)(2,1)S(1)} %get-tuple-element.46), channel_id=1, source_target_pairs={{0,48},{16,0},{32,16},{48,32},{1,49},{17,1},{33,17},{49,33},{2,50}... | collective-permute-start | bytes 208904 | tf_op jit(solution)/shard_map/ppermute | solution.py:43
  20.6 13.8 %copy-start = (bf16[32,2,128,128]{3,2,1,0:T(8,128)(2,1)S(1)}, bf16[32,2,128,128]{3,2,1,0:T(8,128)(2,1)}, u32[]{:S(2)}) copy-start(bf16[32,2,128,128]{3,2,1,0:T(8,128)(2,1)} %weight.1) | copy-start | bytes 6291460
  24.0 9.2 %collective-permute-start.4 = (bf16[48,256]{1,0:T(8,128)(2,1)S(1)}, bf16[48,256]{1,0:T(8,128)(2,1)S(1)}, u32[]{:S(2)}, u32[]{:S(2)}) collective-permute-start(bf16[48,256]{1,0:T(8,128)(2,1)S(1)} %get-tuple-element.48), channel_id=1, source_target_pairs={{0,128},{64,192},{128,0},{192,64},{1,129},{65,193},{129,1},{193,65... | collective-permute-start | bytes 73736 | tf_op jit(solution)/shard_map/ppermute | solution.py:43
  29.6 4.8 %collective-permute-start.5 = (bf16[48,256]{1,0:T(8,128)(2,1)S(1)}, bf16[48,256]{1,0:T(8,128)(2,1)S(1)}, u32[]{:S(2)}, u32[]{:S(2)}) collective-permute-start(bf16[48,256]{1,0:T(8,128)(2,1)S(1)} %get-tuple-element.49), channel_id=1, source_target_pairs={{0,64},{64,128},{128,192},{192,0},{1,65},{65,129},{129,193},{193,1... | collective-permute-start | bytes 73736 | tf_op jit(solution)/shard_map/ppermute | solution.py:43
  30.8 3.7 %collective-permute-start.6 = (bf16[48,256]{1,0:T(8,128)(2,1)S(1)}, bf16[48,256]{1,0:T(8,128)(2,1)S(1)}, u32[]{:S(2)}, u32[]{:S(2)}) collective-permute-start(bf16[48,256]{1,0:T(8,128)(2,1)S(1)} %get-tuple-element.50), channel_id=1, source_target_pairs={{0,192},{64,0},{128,64},{192,128},{1,193},{65,1},{129,65},{193,129... | collective-permute-start | bytes 73736 | tf_op jit(solution)/shard_map/ppermute | solution.py:43
  34.9 6.6 %collective-permute-start.9 = (bf16[32,256]{1,0:T(8,128)(2,1)S(1)}, bf16[32,256]{1,0:T(8,128)(2,1)S(1)}, u32[]{:S(2)}, u32[]{:S(2)}) collective-permute-start(bf16[32,256]{1,0:T(8,128)(2,1)S(1)} %get-tuple-element.52.piece), channel_id=1, source_target_pairs={{0,128},{64,192},{128,0},{192,64},{1,129},{65,193},{129,1},{193,65... | collective-permute-start | bytes 49160 | tf_op jit(solution)/shard_map/ppermute | solution.py:43
  37.2 4.7 %collective-permute-start.8 = (bf16[32,256]{1,0:T(8,128)(2,1)S(1)}, bf16[32,256]{1,0:T(8,128)(2,1)S(1)}, u32[]{:S(2)}, u32[]{:S(2)}) collective-permute-start(bf16[32,256]{1,0:T(8,128)(2,1)S(1)} %get-tuple-element.52.piece), channel_id=1, source_target_pairs={{0,64},{64,128},{128,192},{192,0},{1,65},{65,129},{129,193},{193,1... | collective-permute-start | bytes 49160 | tf_op jit(solution)/shard_map/ppermute | solution.py:43
  40.5 3.8 %collective-permute-start.7 = (bf16[32,256]{1,0:T(8,128)(2,1)S(1)}, bf16[32,256]{1,0:T(8,128)(2,1)S(1)}, u32[]{:S(2)}, u32[]{:S(2)}) collective-permute-start(bf16[32,256]{1,0:T(8,128)(2,1)S(1)} %get-tuple-element.52.piece), channel_id=1, source_target_pairs={{0,192},{64,0},{128,64},{192,128},{1,193},{65,1},{129,65},{193,129... | collective-permute-start | bytes 49160 | tf_op jit(solution)/shard_map/ppermute | solution.py:43
  44.3 4.6 %collective-permute-start.12 = (bf16[128,256]{1,0:T(8,128)(2,1)S(1)}, bf16[128,256]{1,0:T(8,128)(2,1)S(1)}, u32[]{:S(2)}, u32[]{:S(2)}) collective-permute-start(bf16[128,256]{1,0:T(8,128)(2,1)S(1)} %join.2.piece), channel_id=1, source_target_pairs={{0,32},{16,48},{32,0},{48,16},{1,33},{17,49},{33,1},{49,17},{2,34}... | collective-permute-start | bytes 196616 | tf_op jit(solution)/shard_map/ppermute | solution.py:43
  45.6 4.3 %collective-permute-start.11 = (bf16[128,256]{1,0:T(8,128)(2,1)S(1)}, bf16[128,256]{1,0:T(8,128)(2,1)S(1)}, u32[]{:S(2)}, u32[]{:S(2)}) collective-permute-start(bf16[128,256]{1,0:T(8,128)(2,1)S(1)} %join.2.piece), channel_id=1, source_target_pairs={{0,16},{16,32},{32,48},{48,0},{1,17},{17,33},{33,49},{49,1},{2,18}... | collective-permute-start | bytes 196616 | tf_op jit(solution)/shard_map/ppermute | solution.py:43
  48.0 3.1 %collective-permute-start.10 = (bf16[128,256]{1,0:T(8,128)(2,1)S(1)}, bf16[128,256]{1,0:T(8,128)(2,1)S(1)}, u32[]{:S(2)}, u32[]{:S(2)}) collective-permute-start(bf16[128,256]{1,0:T(8,128)(2,1)S(1)} %join.2.piece), channel_id=1, source_target_pairs={{0,48},{16,0},{32,16},{48,32},{1,49},{17,1},{33,17},{49,33},{2,50}... | collective-permute-start | bytes 196616 | tf_op jit(solution)/shard_map/ppermute | solution.py:43
  51.1 7.4 %collective-permute-start.13 = (bf16[512,256]{1,0:T(8,128)(2,1)S(1)}, bf16[512,256]{1,0:T(8,128)(2,1)S(1)}, u32[]{:S(2)}, u32[]{:S(2)}) collective-permute-start(bf16[512,256]{1,0:T(8,128)(2,1)S(1)} %join.3.src), channel_id=1, source_target_pairs={{0,8},{8,0},{1,9},{9,1},{2,10},{10,2},{3,11},{11,3},{4,12},{12,4},... | collective-permute-start | bytes 786440 | tf_op jit(solution)/shard_map/ppermute | solution.py:43
  59.7 7.8 %collective-permute-start.15 = (bf16[256,512]{1,0:T(8,128)(2,1)S(1)}, bf16[256,512]{1,0:T(8,128)(2,1)S(1)}, u32[]{:S(2)}, u32[]{:S(2)}) collective-permute-start(bf16[256,512]{1,0:T(8,128)(2,1)S(1)} %get-tuple-element.60), channel_id=1, source_target_pairs={{0,1},{1,0},{2,3},{3,2},{4,5},{5,4},{6,7},{7,6},{8,9},{9,8},{10,11... | collective-permute-start | bytes 786440 | tf_op jit(solution)/shard_map/ppermute | solution.py:43
  60.5 10.0 %collective-permute-start.14 = (bf16[256,512]{1,0:T(8,128)(2,1)S(1)}, bf16[256,512]{1,0:T(8,128)(2,1)S(1)}, u32[]{:S(2)}, u32[]{:S(2)}) collective-permute-start(bf16[256,512]{1,0:T(8,128)(2,1)S(1)} %get-tuple-element.59), channel_id=1, source_target_pairs={{0,4},{2,6},{4,0},{6,2},{1,5},{3,7},{5,1},{7,3},{8,12},{10,14},{12... | collective-permute-start | bytes 786440 | tf_op jit(solution)/shard_map/ppermute | solution.py:43
  67.6 5.2 %collective-permute-start.16 = (bf16[128,512]{1,0:T(8,128)(2,1)S(1)}, bf16[128,512]{1,0:T(8,128)(2,1)S(1)}, u32[]{:S(2)}, u32[]{:S(2)}) collective-permute-start(bf16[128,512]{1,0:T(8,128)(2,1)S(1)} %get-tuple-element.61), channel_id=1, source_target_pairs={{0,2},{2,4},{4,6},{6,0},{1,3},{3,5},{5,7},{7,1},{8,10},{10,12},{12... | collective-permute-start | bytes 393224 | tf_op jit(solution)/shard_map/ppermute | solution.py:43
  68.9 4.1 %collective-permute-start.17 = (bf16[128,512]{1,0:T(8,128)(2,1)S(1)}, bf16[128,512]{1,0:T(8,128)(2,1)S(1)}, u32[]{:S(2)}, u32[]{:S(2)}) collective-permute-start(bf16[128,512]{1,0:T(8,128)(2,1)S(1)} %get-tuple-element.62), channel_id=1, source_target_pairs={{0,6},{2,0},{4,2},{6,4},{1,7},{3,1},{5,3},{7,5},{8,14},{10,8},{12,... | collective-permute-start | bytes 393224 | tf_op jit(solution)/shard_map/ppermute | solution.py:43
  70.5 4.2 %collective-permute-start.18 = (bf16[128,512]{1,0:T(8,128)(2,1)S(1)}, bf16[128,512]{1,0:T(8,128)(2,1)S(1)}, u32[]{:S(2)}, u32[]{:S(2)}) collective-permute-start(bf16[128,512]{1,0:T(8,128)(2,1)S(1)} %merge.3), channel_id=1, source_target_pairs={{0,1},{1,0},{2,3},{3,2},{4,5},{5,4},{6,7},{7,6},{8,9},{9,8},{10,11... | collective-permute-start | bytes 393224 | tf_op jit(solution)/shard_map/ppermute | solution.py:43

commit v10 on v9

--- a/solution.py
+++ b/solution.py
@@ -94,10 +94,10 @@
 
 
 def analyse(index, row, put_coef, put_basis, exy, ez, w, scr):
-    @pl.loop(0, C // 16)
+    @pl.loop(0, C // 32)
     def _(it):
-        for u in range(16):
-            m = it * 16 + u
+        for u in range(32):
+            m = it * 32 + u
             k = index[row, m]
             ixy, iz = lax.shift_right_logical(k, 5), lax.bitwise_and(k, 31)
             for j in range(ROWS // 8):

time: 75.6 us -> 75.3 us (level)
  no operation moved by 1% of the time
where the time goes in v10:
time: 75.3 us; the launch traced here: 75.2 us
  starting transfers between devices  39.6 us (53%)
  Pallas kernels  19.7 us (26%)
  waiting for transfers between devices  15.8 us (21%)
    ppermute x19, starting transfers between devices, send(): return lax.ppermute(value, axes, [(j, (j + shift) % n) for j in range(n)])  39.6 us
    ppermute x19, waiting for transfers between devices, send(): return lax.ppermute(value, axes, [(j, (j + shift) % n) for j in range(n)])  15.8 us
    pallas_call x1, Pallas kernels, on_device(): call(first_body, 0, [pltpu.VMEM((8 * C + 16, C), BF), pltpu.VMEM((8 * C,...  8.66 us
    pallas_call x2, Pallas kernels, near(): call(functools.partial(near_body, count, first), 4, [pltpu.VMEM((count *...  6.28 us
    pallas_call x3, Pallas kernels, field(): call(functools.partial(synthesis_body, places), 3, [one(len(places) * C,...  1.72 us
  transfers between devices with their start and end apart: 19, of which 13 were waited for; matrix products, arithmetic and copies ran while one was open for 0% of the time, Pallas kernels for 11%

profile of v10, /device:TPU:1, one launch (start us, length us, event | category | flops | bytes accessed | tf_op | source)
XLA Modules:
  0.0 75.2 jit_solution(1554576566307271387)
XLA Ops:
  0.0 8.7 %first.1 = (bf16[1040,128]{1,0:T(8,128)(2,1)S(1)}, bf16[1024,4096]{1,0:T(8,128)(2,1)S(1)}, f32[256,2,32,128]{3,2,1,0:T(8,128)S(1)}, f32[32,2,32,128]{3,2,1,0:T(8...) custom-call(f32[3,4096]{1,0:T(4,128)} %refs_0_.1, ...), custom_call_target="tpu_custom_call" | custom-call | flops 2147483648 | bytes 1048576 | tf_op jit(solution)/shard_map/first/pallas_call | solution.py:292
  8.7 3.3 %collective-permute-start = (bf16[1040,128]{1,0:T(8,128)(2,1)S(1)}, bf16[1040,128]{1,0:T(8,128)(2,1)S(1)}, u32[]{:S(2)}, u32[]{:S(2)}) collective-permute-start(bf16[1040,128]{1,0:T(8,128)(2,1)S(1)} %get-tuple-element.42), channel_id=1, source_target_pairs={{0,8},{8,0},{1,9},{9,1},{2,10},{10,2},{3,11},{11,3},{4,12},{12,4},... | collective-permute-start | bytes 798728 | tf_op jit(solution)/shard_map/ppermute | solution.py:43
  12.0 4.5 %near.2 = (bf16[784,128]{1,0:T(8,128)(2,1)S(1)}, bf16[1024,4096]{1,0:T(8,128)(2,1)S(1)}) custom-call(s32[8,128]{1,0:T(8,128)S(1)} %get-tuple-element.34.index, f32[32,128]{1,0:T(8,128)S(1)} %get-tuple-element.35.quad, f32[256,2,32,128]{3,2,1,0:T(8,128)S(1)} %get-tuple-element.36.exy, f32[32,2,32,128]{3,2,1,0:T(8,128)S(1)} %get-tuple-element.37.ez, ...), custom_call_target="tpu_custom_call" | custom-call | flops 1610612736 | bytes 1048576 | tf_op jit(solution)/shard_map/near/pallas_call | solution.py:305
  16.5 0.0 collective-permute-done.got.got0
  16.5 0.1 pair.1
  16.6 1.1 %collective-permute-start.1 = (bf16[272,128]{1,0:T(8,128)(2,1)S(1)}, bf16[272,128]{1,0:T(8,128)(2,1)S(1)}, u32[]{:S(2)}, u32[]{:S(2)}) collective-permute-start(bf16[272,128]{1,0:T(8,128)(2,1)S(1)} %get-tuple-element.44), channel_id=1, source_target_pairs={{0,32},{16,48},{32,0},{48,16},{1,33},{17,49},{33,1},{49,17},{2,34}... | collective-permute-start | bytes 208904 | tf_op jit(solution)/shard_map/ppermute | solution.py:43
  17.6 0.3 collective-permute-start.2
  18.0 2.4 %collective-permute-start.3 = (bf16[272,128]{1,0:T(8,128)(2,1)S(1)}, bf16[272,128]{1,0:T(8,128)(2,1)S(1)}, u32[]{:S(2)}, u32[]{:S(2)}) collective-permute-start(bf16[272,128]{1,0:T(8,128)(2,1)S(1)} %get-tuple-element.46), channel_id=1, source_target_pairs={{0,48},{16,0},{32,16},{48,32},{1,49},{17,1},{33,17},{49,33},{2,50}... | collective-permute-start | bytes 208904 | tf_op jit(solution)/shard_map/ppermute | solution.py:43
  20.3 1.8 %near.3 = (bf16[272,128]{1,0:T(8,128)(2,1)S(1)}, bf16[1024,4096]{1,0:T(8,128)(2,1)S(1)}) custom-call(s32[8,128]{1,0:T(8,128)S(1)} %get-tuple-element.34.index, f32[32,128]{1,0:T(8,128)S(1)} %get-tuple-element.35.quad, f32[256,2,32,128]{3,2,1,0:T(8,128)S(1)} %get-tuple-element.36.exy, ...), custom_call_target="tpu_custom_call", output_to_operand_aliasing={{1}: (5, {})} | custom-call | flops 536870912 | bytes 1048576 | tf_op jit(solution)/shard_map/near/pallas_call | solution.py:305
  22.1 1.5 %collective-permute-done.2.got2 = bf16[272,128]{1,0:T(8,128)(2,1)S(1)} collective-permute-done((bf16[272,128]{1,0:T(8,128)(2,1)S(1)}, bf16[272,128]{1,0:T(8,128)(2,1)S(1)}, u32[]{:S(2)}, u32[]{:S(2)}) %collective-permute-start.2) | collective-permute-done | bytes 69664 | tf_op jit(solution)/shard_map/ppermute | solution.py:43
  23.6 0.0 collective-permute-done.3.got3
  23.6 0.1 x_sum.1
  23.8 5.5 %collective-permute-start.4 = (bf16[48,256]{1,0:T(8,128)(2,1)S(1)}, bf16[48,256]{1,0:T(8,128)(2,1)S(1)}, u32[]{:S(2)}, u32[]{:S(2)}) collective-permute-start(bf16[48,256]{1,0:T(8,128)(2,1)S(1)} %get-tuple-element.48), channel_id=1, source_target_pairs={{0,128},{64,192},{128,0},{192,64},{1,129},{65,193},{129,1},{193,65... | collective-permute-start | bytes 73736 | tf_op jit(solution)/shard_map/ppermute | solution.py:43
  29.3 1.2 %collective-permute-start.5 = (bf16[48,256]{1,0:T(8,128)(2,1)S(1)}, bf16[48,256]{1,0:T(8,128)(2,1)S(1)}, u32[]{:S(2)}, u32[]{:S(2)}) collective-permute-start(bf16[48,256]{1,0:T(8,128)(2,1)S(1)} %get-tuple-element.49), channel_id=1, source_target_pairs={{0,64},{64,128},{128,192},{192,0},{1,65},{65,129},{129,193},{193,1... | collective-permute-start | bytes 73736 | tf_op jit(solution)/shard_map/ppermute | solution.py:43
  30.5 2.4 %collective-permute-start.6 = (bf16[48,256]{1,0:T(8,128)(2,1)S(1)}, bf16[48,256]{1,0:T(8,128)(2,1)S(1)}, u32[]{:S(2)}, u32[]{:S(2)}) collective-permute-start(bf16[48,256]{1,0:T(8,128)(2,1)S(1)} %get-tuple-element.50), channel_id=1, source_target_pairs={{0,192},{64,0},{128,64},{192,128},{1,193},{65,1},{129,65},{193,129... | collective-permute-start | bytes 73736 | tf_op jit(solution)/shard_map/ppermute | solution.py:43
  32.9 0.0 collective-permute-done.4.got1
  32.9 1.2 %collective-permute-done.5.got2 = bf16[48,256]{1,0:T(8,128)(2,1)S(1)} collective-permute-done((bf16[48,256]{1,0:T(8,128)(2,1)S(1)}, bf16[48,256]{1,0:T(8,128)(2,1)S(1)}, u32[]{:S(2)}, u32[]{:S(2)}) %collective-permute-start.5) | collective-permute-done | bytes 24608 | tf_op jit(solution)/shard_map/ppermute | solution.py:43
  34.1 0.1 collective-permute-done.6.got3
  34.2 0.4 filter.1
  34.6 2.4 %collective-permute-start.9 = (bf16[32,256]{1,0:T(8,128)(2,1)S(1)}, bf16[32,256]{1,0:T(8,128)(2,1)S(1)}, u32[]{:S(2)}, u32[]{:S(2)}) collective-permute-start(bf16[32,256]{1,0:T(8,128)(2,1)S(1)} %get-tuple-element.52.piece), channel_id=1, source_target_pairs={{0,128},{64,192},{128,0},{192,64},{1,129},{65,193},{129,1},{193,65... | collective-permute-start | bytes 49160 | tf_op jit(solution)/shard_map/ppermute | solution.py:43
  36.9 3.3 %collective-permute-start.8 = (bf16[32,256]{1,0:T(8,128)(2,1)S(1)}, bf16[32,256]{1,0:T(8,128)(2,1)S(1)}, u32[]{:S(2)}, u32[]{:S(2)}) collective-permute-start(bf16[32,256]{1,0:T(8,128)(2,1)S(1)} %get-tuple-element.52.piece), channel_id=1, source_target_pairs={{0,64},{64,128},{128,192},{192,0},{1,65},{65,129},{129,193},{193,1... | collective-permute-start | bytes 49160 | tf_op jit(solution)/shard_map/ppermute | solution.py:43
  40.2 0.3 collective-permute-start.7
  40.5 0.6 collective-permute-done.9.rest_2_
  41.1 0.5 collective-permute-done.8.rest_1_
  41.6 2.3 %collective-permute-done.7.rest_0_ = bf16[32,256]{1,0:T(8,128)(2,1)S(1)} collective-permute-done((bf16[32,256]{1,0:T(8,128)(2,1)S(1)}, bf16[32,256]{1,0:T(8,128)(2,1)S(1)}, u32[]{:S(2)}, u32[]{:S(2)}) %collective-permute-start.7) | collective-permute-done | bytes 16416 | tf_op jit(solution)/shard_map/ppermute | solution.py:43
  44.0 1.3 %collective-permute-start.12 = (bf16[128,256]{1,0:T(8,128)(2,1)S(1)}, bf16[128,256]{1,0:T(8,128)(2,1)S(1)}, u32[]{:S(2)}, u32[]{:S(2)}) collective-permute-start(bf16[128,256]{1,0:T(8,128)(2,1)S(1)} %join.2.piece), channel_id=1, source_target_pairs={{0,32},{16,48},{32,0},{48,16},{1,33},{17,49},{33,1},{49,17},{2,34}... | collective-permute-start | bytes 196616 | tf_op jit(solution)/shard_map/ppermute | solution.py:43
  45.3 2.4 %collective-permute-start.11 = (bf16[128,256]{1,0:T(8,128)(2,1)S(1)}, bf16[128,256]{1,0:T(8,128)(2,1)S(1)}, u32[]{:S(2)}, u32[]{:S(2)}) collective-permute-start(bf16[128,256]{1,0:T(8,128)(2,1)S(1)} %join.2.piece), channel_id=1, source_target_pairs={{0,16},{16,32},{32,48},{48,0},{1,17},{17,33},{33,49},{49,1},{2,18}... | collective-permute-start | bytes 196616 | tf_op jit(solution)/shard_map/ppermute | solution.py:43
  47.7 0.3 collective-permute-start.10
  48.0 0.6 collective-permute-done.12.rest_2_
  48.6 1.0 %collective-permute-done.11.rest_1_ = bf16[128,256]{1,0:T(8,128)(2,1)S(1)} collective-permute-done((bf16[128,256]{1,0:T(8,128)(2,1)S(1)}, bf16[128,256]{1,0:T(8,128)(2,1)S(1)}, u32[]{:S(2)}, u32[]{:S(2)}) %collective-permute-start.11) | collective-permute-done | bytes 65568 | tf_op jit(solution)/shard_map/ppermute | solution.py:43
  49.6 1.2 %collective-permute-done.10.rest_0_ = bf16[128,256]{1,0:T(8,128)(2,1)S(1)} collective-permute-done((bf16[128,256]{1,0:T(8,128)(2,1)S(1)}, bf16[128,256]{1,0:T(8,128)(2,1)S(1)}, u32[]{:S(2)}, u32[]{:S(2)}) %collective-permute-start.10) | collective-permute-done | bytes 65568 | tf_op jit(solution)/shard_map/ppermute | solution.py:43
  50.9 6.0 %collective-permute-start.13 = (bf16[512,256]{1,0:T(8,128)(2,1)S(1)}, bf16[512,256]{1,0:T(8,128)(2,1)S(1)}, u32[]{:S(2)}, u32[]{:S(2)}) collective-permute-start(bf16[512,256]{1,0:T(8,128)(2,1)S(1)} %join.3.src), channel_id=1, source_target_pairs={{0,8},{8,0},{1,9},{9,1},{2,10},{10,2},{3,11},{11,3},{4,12},{12,4},... | collective-permute-start | bytes 786440 | tf_op jit(solution)/shard_map/ppermute | solution.py:43
  56.9 1.4 %near_field.1.part = f32[128,4096]{1,0:T(8,128)S(1)} custom-call(bf16[512,256]{1,0:T(8,128)(2,1)S(1)} %join.3.src, bf16[1024,4096]{1,0:T(8,128)(2,1)S(1)} %get-tuple-element.54.basis), custom_call_target="tpu_custom_call" | custom-call | flops 1073741824 | bytes 1048576 | tf_op jit(solution)/shard_map/near_field/pallas_call | solution.py:323
  58.3 0.0 collective-permute-done.13.src
  58.3 0.1 turned.1.f
  58.4 0.5 synthesis.3
  58.9 0.5 synthesis.4
  59.4 0.8 %collective-permute-start.15 = (bf16[256,512]{1,0:T(8,128)(2,1)S(1)}, bf16[256,512]{1,0:T(8,128)(2,1)S(1)}, u32[]{:S(2)}, u32[]{:S(2)}) collective-permute-start(bf16[256,512]{1,0:T(8,128)(2,1)S(1)} %get-tuple-element.60), channel_id=1, source_target_pairs={{0,1},{1,0},{2,3},{3,2},{4,5},{5,4},{6,7},{7,6},{8,9},{9,8},{10,11... | collective-permute-start | bytes 786440 | tf_op jit(solution)/shard_map/ppermute | solution.py:43
  60.2 2.9 %collective-permute-start.14 = (bf16[256,512]{1,0:T(8,128)(2,1)S(1)}, bf16[256,512]{1,0:T(8,128)(2,1)S(1)}, u32[]{:S(2)}, u32[]{:S(2)}) collective-permute-start(bf16[256,512]{1,0:T(8,128)(2,1)S(1)} %get-tuple-element.59), channel_id=1, source_target_pairs={{0,4},{2,6},{4,0},{6,2},{1,5},{3,7},{5,1},{7,3},{8,12},{10,14},{12... | collective-permute-start | bytes 786440 | tf_op jit(solution)/shard_map/ppermute | solution.py:43
  63.1 0.8 %synthesis.5.own = f32[512,512]{1,0:T(8,128)S(1)} custom-call(bf16[128,1024]{1,0:T(8,128)(2,1)S(1)} %turned.1.f, bf16[1024,4096]{1,0:T(8,128)(2,1)S(1)} %get-tuple-element.57.basis, f32[128,4096]{1,0:T(8,128)S(1)} %get-tuple-element.58.part), custom_call_target="tpu_custom_call" | custom-call | flops 536870912 | bytes 1048576 | tf_op jit(solution)/shard_map/synthesis/pallas_call | solution.py:329
  63.9 3.3 %collective-permute-done.15.got = bf16[256,512]{1,0:T(8,128)(2,1)S(1)} collective-permute-done((bf16[256,512]{1,0:T(8,128)(2,1)S(1)}, bf16[256,512]{1,0:T(8,128)(2,1)S(1)}, u32[]{:S(2)}, u32[]{:S(2)}) %collective-permute-start.15) | collective-permute-done | bytes 262176 | tf_op jit(solution)/shard_map/ppermute | solution.py:43
  67.3 1.4 %collective-permute-start.16 = (bf16[128,512]{1,0:T(8,128)(2,1)S(1)}, bf16[128,512]{1,0:T(8,128)(2,1)S(1)}, u32[]{:S(2)}, u32[]{:S(2)}) collective-permute-start(bf16[128,512]{1,0:T(8,128)(2,1)S(1)} %get-tuple-element.61), channel_id=1, source_target_pairs={{0,2},{2,4},{4,6},{6,0},{1,3},{3,5},{5,7},{7,1},{8,10},{10,12},{12... | collective-permute-start | bytes 393224 | tf_op jit(solution)/shard_map/ppermute | solution.py:43
  68.7 1.5 %collective-permute-start.17 = (bf16[128,512]{1,0:T(8,128)(2,1)S(1)}, bf16[128,512]{1,0:T(8,128)(2,1)S(1)}, u32[]{:S(2)}, u32[]{:S(2)}) collective-permute-start(bf16[128,512]{1,0:T(8,128)(2,1)S(1)} %get-tuple-element.62), channel_id=1, source_target_pairs={{0,6},{2,0},{4,2},{6,4},{1,7},{3,1},{5,3},{7,5},{8,14},{10,8},{12,... | collective-permute-start | bytes 393224 | tf_op jit(solution)/shard_map/ppermute | solution.py:43
  70.2 0.8 %collective-permute-start.18 = (bf16[128,512]{1,0:T(8,128)(2,1)S(1)}, bf16[128,512]{1,0:T(8,128)(2,1)S(1)}, u32[]{:S(2)}, u32[]{:S(2)}) collective-permute-start(bf16[128,512]{1,0:T(8,128)(2,1)S(1)} %merge.3), channel_id=1, source_target_pairs={{0,1},{1,0},{2,3},{3,2},{4,5},{5,4},{6,7},{7,6},{8,9},{9,8},{10,11... | collective-permute-start | bytes 393224 | tf_op jit(solution)/shard_map/ppermute | solution.py:43
  71.0 1.4 %collective-permute-done.16.rest_1_ = bf16[128,512]{1,0:T(8,128)(2,1)S(1)} collective-permute-done((bf16[128,512]{1,0:T(8,128)(2,1)S(1)}, bf16[128,512]{1,0:T(8,128)(2,1)S(1)}, u32[]{:S(2)}, u32[]{:S(2)}) %collective-permute-start.16) | collective-permute-done | bytes 131104 | tf_op jit(solution)/shard_map/ppermute | solution.py:43
  72.4 0.3 collective-permute-done.17.rest_2_
  72.8 1.6 %collective-permute-done.18.rest_3_ = bf16[128,512]{1,0:T(8,128)(2,1)S(1)} collective-permute-done((bf16[128,512]{1,0:T(8,128)(2,1)S(1)}, bf16[128,512]{1,0:T(8,128)(2,1)S(1)}, u32[]{:S(2)}, u32[]{:S(2)}) %collective-permute-start.18) | collective-permute-done | bytes 131104 | tf_op jit(solution)/shard_map/ppermute | solution.py:43
  74.4 0.8 %finish.1 = bf16[512,128]{1,0:T(8,128)(2,1)} custom-call(f32[8,128]{1,0:T(8,128)S(1)} %get-tuple-element.51.total, f32[512,128]{1,0:T(8,128)S(1)} %get-tuple-element.39.given.linear, f32[512,512]{1,0:T(8,128)S(1)} %synthesis.5.own, bf16[256,512]{1,0:T(8,128)(2,1)S(1)} %collective-permute-done.14.got.rest_0_, ...), custom_call_target="tpu_custom_call" | custom-call | bytes 1048576 | tf_op jit(solution)/shard_map/finish/pallas_call | solution.py:345
  (8 shorter events, 0.1 us)
Async XLA Ops:
  8.7 7.8 %collective-permute-start = (bf16[1040,128]{1,0:T(8,128)(2,1)S(1)}, bf16[1040,128]{1,0:T(8,128)(2,1)S(1)}, u32[]{:S(2)}, u32[]{:S(2)}) collective-permute-start(bf16[1040,128]{1,0:T(8,128)(2,1)S(1)} %get-tuple-element.42), channel_id=1, source_target_pairs={{0,8},{8,0},{1,9},{9,1},{2,10},{10,2},{3,11},{11,3},{4,12},{12,4},... | collective-permute-start | bytes 798728 | tf_op jit(solution)/shard_map/ppermute | solution.py:43
  16.6 5.6 %collective-permute-start.1 = (bf16[272,128]{1,0:T(8,128)(2,1)S(1)}, bf16[272,128]{1,0:T(8,128)(2,1)S(1)}, u32[]{:S(2)}, u32[]{:S(2)}) collective-permute-start(bf16[272,128]{1,0:T(8,128)(2,1)S(1)} %get-tuple-element.44), channel_id=1, source_target_pairs={{0,32},{16,48},{32,0},{48,16},{1,33},{17,49},{33,1},{49,17},{2,34}... | collective-permute-start | bytes 208904 | tf_op jit(solution)/shard_map/ppermute | solution.py:43
  17.6 6.0 %collective-permute-start.2 = (bf16[272,128]{1,0:T(8,128)(2,1)S(1)}, bf16[272,128]{1,0:T(8,128)(2,1)S(1)}, u32[]{:S(2)}, u32[]{:S(2)}) collective-permute-start(bf16[272,128]{1,0:T(8,128)(2,1)S(1)} %get-tuple-element.45), channel_id=1, source_target_pairs={{0,16},{16,32},{32,48},{48,0},{1,17},{17,33},{33,49},{49,1},{2,18}... | collective-permute-start | bytes 208904 | tf_op jit(solution)/shard_map/ppermute | solution.py:43
  18.0 5.7 %collective-permute-start.3 = (bf16[272,128]{1,0:T(8,128)(2,1)S(1)}, bf16[272,128]{1,0:T(8,128)(2,1)S(1)}, u32[]{:S(2)}, u32[]{:S(2)}) collective-permute-start(bf16[272,128]{1,0:T(8,128)(2,1)S(1)} %get-tuple-element.46), channel_id=1, source_target_pairs={{0,48},{16,0},{32,16},{48,32},{1,49},{17,1},{33,17},{49,33},{2,50}... | collective-permute-start | bytes 208904 | tf_op jit(solution)/shard_map/ppermute | solution.py:43
  20.3 13.8 %copy-start = (bf16[32,2,128,128]{3,2,1,0:T(8,128)(2,1)S(1)}, bf16[32,2,128,128]{3,2,1,0:T(8,128)(2,1)}, u32[]{:S(2)}) copy-start(bf16[32,2,128,128]{3,2,1,0:T(8,128)(2,1)} %weight.1) | copy-start | bytes 6291460
  23.8 9.1 %collective-permute-start.4 = (bf16[48,256]{1,0:T(8,128)(2,1)S(1)}, bf16[48,256]{1,0:T(8,128)(2,1)S(1)}, u32[]{:S(2)}, u32[]{:S(2)}) collective-permute-start(bf16[48,256]{1,0:T(8,128)(2,1)S(1)} %get-tuple-element.48), channel_id=1, source_target_pairs={{0,128},{64,192},{128,0},{192,64},{1,129},{65,193},{129,1},{193,65... | collective-permute-start | bytes 73736 | tf_op jit(solution)/shard_map/ppermute | solution.py:43
  29.3 4.8 %collective-permute-start.5 = (bf16[48,256]{1,0:T(8,128)(2,1)S(1)}, bf16[48,256]{1,0:T(8,128)(2,1)S(1)}, u32[]{:S(2)}, u32[]{:S(2)}) collective-permute-start(bf16[48,256]{1,0:T(8,128)(2,1)S(1)} %get-tuple-element.49), channel_id=1, source_target_pairs={{0,64},{64,128},{128,192},{192,0},{1,65},{65,129},{129,193},{193,1... | collective-permute-start | bytes 73736 | tf_op jit(solution)/shard_map/ppermute | solution.py:43
  30.5 3.7 %collective-permute-start.6 = (bf16[48,256]{1,0:T(8,128)(2,1)S(1)}, bf16[48,256]{1,0:T(8,128)(2,1)S(1)}, u32[]{:S(2)}, u32[]{:S(2)}) collective-permute-start(bf16[48,256]{1,0:T(8,128)(2,1)S(1)} %get-tuple-element.50), channel_id=1, source_target_pairs={{0,192},{64,0},{128,64},{192,128},{1,193},{65,1},{129,65},{193,129... | collective-permute-start | bytes 73736 | tf_op jit(solution)/shard_map/ppermute | solution.py:43
  34.6 6.6 %collective-permute-start.9 = (bf16[32,256]{1,0:T(8,128)(2,1)S(1)}, bf16[32,256]{1,0:T(8,128)(2,1)S(1)}, u32[]{:S(2)}, u32[]{:S(2)}) collective-permute-start(bf16[32,256]{1,0:T(8,128)(2,1)S(1)} %get-tuple-element.52.piece), channel_id=1, source_target_pairs={{0,128},{64,192},{128,0},{192,64},{1,129},{65,193},{129,1},{193,65... | collective-permute-start | bytes 49160 | tf_op jit(solution)/shard_map/ppermute | solution.py:43
  36.9 4.7 %collective-permute-start.8 = (bf16[32,256]{1,0:T(8,128)(2,1)S(1)}, bf16[32,256]{1,0:T(8,128)(2,1)S(1)}, u32[]{:S(2)}, u32[]{:S(2)}) collective-permute-start(bf16[32,256]{1,0:T(8,128)(2,1)S(1)} %get-tuple-element.52.piece), channel_id=1, source_target_pairs={{0,64},{64,128},{128,192},{192,0},{1,65},{65,129},{129,193},{193,1... | collective-permute-start | bytes 49160 | tf_op jit(solution)/shard_map/ppermute | solution.py:43
  40.2 3.8 %collective-permute-start.7 = (bf16[32,256]{1,0:T(8,128)(2,1)S(1)}, bf16[32,256]{1,0:T(8,128)(2,1)S(1)}, u32[]{:S(2)}, u32[]{:S(2)}) collective-permute-start(bf16[32,256]{1,0:T(8,128)(2,1)S(1)} %get-tuple-element.52.piece), channel_id=1, source_target_pairs={{0,192},{64,0},{128,64},{192,128},{1,193},{65,1},{129,65},{193,129... | collective-permute-start | bytes 49160 | tf_op jit(solution)/shard_map/ppermute | solution.py:43
  44.0 4.6 %collective-permute-start.12 = (bf16[128,256]{1,0:T(8,128)(2,1)S(1)}, bf16[128,256]{1,0:T(8,128)(2,1)S(1)}, u32[]{:S(2)}, u32[]{:S(2)}) collective-permute-start(bf16[128,256]{1,0:T(8,128)(2,1)S(1)} %join.2.piece), channel_id=1, source_target_pairs={{0,32},{16,48},{32,0},{48,16},{1,33},{17,49},{33,1},{49,17},{2,34}... | collective-permute-start | bytes 196616 | tf_op jit(solution)/shard_map/ppermute | solution.py:43
  45.3 4.3 %collective-permute-start.11 = (bf16[128,256]{1,0:T(8,128)(2,1)S(1)}, bf16[128,256]{1,0:T(8,128)(2,1)S(1)}, u32[]{:S(2)}, u32[]{:S(2)}) collective-permute-start(bf16[128,256]{1,0:T(8,128)(2,1)S(1)} %join.2.piece), channel_id=1, source_target_pairs={{0,16},{16,32},{32,48},{48,0},{1,17},{17,33},{33,49},{49,1},{2,18}... | collective-permute-start | bytes 196616 | tf_op jit(solution)/shard_map/ppermute | solution.py:43
  47.7 3.1 %collective-permute-start.10 = (bf16[128,256]{1,0:T(8,128)(2,1)S(1)}, bf16[128,256]{1,0:T(8,128)(2,1)S(1)}, u32[]{:S(2)}, u32[]{:S(2)}) collective-permute-start(bf16[128,256]{1,0:T(8,128)(2,1)S(1)} %join.2.piece), channel_id=1, source_target_pairs={{0,48},{16,0},{32,16},{48,32},{1,49},{17,1},{33,17},{49,33},{2,50}... | collective-permute-start | bytes 196616 | tf_op jit(solution)/shard_map/ppermute | solution.py:43
  50.9 7.4 %collective-permute-start.13 = (bf16[512,256]{1,0:T(8,128)(2,1)S(1)}, bf16[512,256]{1,0:T(8,128)(2,1)S(1)}, u32[]{:S(2)}, u32[]{:S(2)}) collective-permute-start(bf16[512,256]{1,0:T(8,128)(2,1)S(1)} %join.3.src), channel_id=1, source_target_pairs={{0,8},{8,0},{1,9},{9,1},{2,10},{10,2},{3,11},{11,3},{4,12},{12,4},... | collective-permute-start | bytes 786440 | tf_op jit(solution)/shard_map/ppermute | solution.py:43
  59.4 7.9 %collective-permute-start.15 = (bf16[256,512]{1,0:T(8,128)(2,1)S(1)}, bf16[256,512]{1,0:T(8,128)(2,1)S(1)}, u32[]{:S(2)}, u32[]{:S(2)}) collective-permute-start(bf16[256,512]{1,0:T(8,128)(2,1)S(1)} %get-tuple-element.60), channel_id=1, source_target_pairs={{0,1},{1,0},{2,3},{3,2},{4,5},{5,4},{6,7},{7,6},{8,9},{9,8},{10,11... | collective-permute-start | bytes 786440 | tf_op jit(solution)/shard_map/ppermute | solution.py:43
  60.2 10.0 %collective-permute-start.14 = (bf16[256,512]{1,0:T(8,128)(2,1)S(1)}, bf16[256,512]{1,0:T(8,128)(2,1)S(1)}, u32[]{:S(2)}, u32[]{:S(2)}) collective-permute-start(bf16[256,512]{1,0:T(8,128)(2,1)S(1)} %get-tuple-element.59), channel_id=1, source_target_pairs={{0,4},{2,6},{4,0},{6,2},{1,5},{3,7},{5,1},{7,3},{8,12},{10,14},{12... | collective-permute-start | bytes 786440 | tf_op jit(solution)/shard_map/ppermute | solution.py:43
  67.3 5.2 %collective-permute-start.16 = (bf16[128,512]{1,0:T(8,128)(2,1)S(1)}, bf16[128,512]{1,0:T(8,128)(2,1)S(1)}, u32[]{:S(2)}, u32[]{:S(2)}) collective-permute-start(bf16[128,512]{1,0:T(8,128)(2,1)S(1)} %get-tuple-element.61), channel_id=1, source_target_pairs={{0,2},{2,4},{4,6},{6,0},{1,3},{3,5},{5,7},{7,1},{8,10},{10,12},{12... | collective-permute-start | bytes 393224 | tf_op jit(solution)/shard_map/ppermute | solution.py:43
  68.7 4.1 %collective-permute-start.17 = (bf16[128,512]{1,0:T(8,128)(2,1)S(1)}, bf16[128,512]{1,0:T(8,128)(2,1)S(1)}, u32[]{:S(2)}, u32[]{:S(2)}) collective-permute-start(bf16[128,512]{1,0:T(8,128)(2,1)S(1)} %get-tuple-element.62), channel_id=1, source_target_pairs={{0,6},{2,0},{4,2},{6,4},{1,7},{3,1},{5,3},{7,5},{8,14},{10,8},{12,... | collective-permute-start | bytes 393224 | tf_op jit(solution)/shard_map/ppermute | solution.py:43
  70.2 4.2 %collective-permute-start.18 = (bf16[128,512]{1,0:T(8,128)(2,1)S(1)}, bf16[128,512]{1,0:T(8,128)(2,1)S(1)}, u32[]{:S(2)}, u32[]{:S(2)}) collective-permute-start(bf16[128,512]{1,0:T(8,128)(2,1)S(1)} %merge.3), channel_id=1, source_target_pairs={{0,1},{1,0},{2,3},{3,2},{4,5},{5,4},{6,7},{7,6},{8,9},{9,8},{10,11... | collective-permute-start | bytes 393224 | tf_op jit(solution)/shard_map/ppermute | solution.py:43
